TPU v7x, 32 devices: a whole 2x2x4 slice. The times are simulated.
32 devices in a mesh: batch: 4 (over y, x), tm: 8 (over z, core).
Axes of the slice: x: 2, y: 2, z: 4, core: 2. Of those that a mesh axis runs over, the one named last changes fastest.
Arguments:
- tokens: bfloat16 [16, 2048, 512], P('batch', 'tm'), may hold values from -80 to 80
- starts: int32 [16, 16], P('batch'), may hold values from 0 to 2047, as said below
- lengths: int32 [16], P('batch'), may hold values from 1024 to 2048
- cotangent: bfloat16 [16, 2048, 512], P('batch', 'tm'), may hold values from -6 to 6
- norm_gain: float32 [2, 512], replicated, may hold values from 0.5 to 1.5
- norm_shift: float32 [2, 512], replicated, may hold values from -1.75 to 1.75
- b_proj: bfloat16 [2, 512, 768], replicated, may hold values from -0.25 to 0.25
- log_rate: float32 [2, 384], replicated, may hold values from -20 to -3
- rotation: float32 [2, 384], replicated, may hold values from -3.140625 to 3.140625
- c_proj: bfloat16 [2, 768, 512], replicated, may hold values from -0.21875 to 0.21875
- skip_gain: float32 [2, 512], replicated, may hold values from -3 to 3
- w_gate: bfloat16 [2, 512, 512], replicated, may hold values from -0.25 to 0.25
- gate_bias: float32 [2, 512], replicated, may hold values from -3 to 3
- run_mean: float32 [2, 512], replicated, may hold values from -3 to 3
- run_var: float32 [2, 512], replicated, may hold values from 0.5 to 4
Outputs:
- output: bfloat16 [16, 2048, 512], P('batch', 'tm')
- tokens_grad: float32 [16, 2048, 512], P('batch', 'tm')
- grad_norm_gain: float32 [2, 512], replicated
- grad_norm_shift: float32 [2, 512], replicated
- grad_b_proj: float32 [2, 512, 768], replicated
- grad_log_rate: float32 [2, 384], replicated
- grad_rotation: float32 [2, 384], replicated
- grad_c_proj: float32 [2, 768, 512], replicated
- grad_skip_gain: float32 [2, 512], replicated
- grad_w_gate: float32 [2, 512, 512], replicated
- grad_gate_bias: float32 [2, 512], replicated
- new_mean: float32 [2, 512], replicated
- new_var: float32 [2, 512], replicated
Inputs may be any that keep to these rules, and one draw needn't show every extreme that they name: starts[i,0] is 0 and starts may repeat; among the 4 rows of each index of batch one row has all its starts below 128 and length 2048.
All inputs are finite; a program needn't handle non-finite values.
Results may differ from a plain program's by a relative error of at most 0.009.
Values sent between devices are 32-bit elements; how exact they have to be, the bound alone decides.
No kernel may reach another device: no remote copies, remote signals or barrier semaphores. Data moves between devices by JAX's collectives and lax.ppermute only.
A program may use at most 192 MiB of HBM per device.

v0:
```python
import math

import jax
import jax.numpy as jnp
from jax import lax
from jax.sharding import PartitionSpec as P

ROWS_DEV = 2
MICRO = 2


epsilon = 1e-05
momentum = 0.1


def passed_along(block, axis, distance):
    devices = range(lax.axis_size(axis))
    route = [(i - distance, i) for i in devices if i - distance in devices]
    return lax.ppermute(block, axis, route)


def complex_times(ar, ai, br, bi):
    return (ar * br - ai * bi, ar * bi + ai * br)


def combine(earlier, later):
    coef_re, coef_im = complex_times(later[0], later[1], earlier[0], earlier[1])
    state_re, state_im = complex_times(later[0], later[1], earlier[2], earlier[3])
    return (coef_re, coef_im, state_re + later[2], state_im + later[3])


def gelu_slope(values):
    return (
        0.5 * (1.0 + lax.erf(values * 0.7071067811865476))
        + values * jnp.exp(-0.5 * values * values) * 0.3989422804014327
    )


def local_scan(coef_re, coef_im, drive_re, drive_im, reverse):
    rows, length, width = drive_re.shape
    block = math.gcd(length, 16)
    count = length // block

    def arrange(values):
        full = values.reshape((rows, count, block, width))
        return jnp.moveaxis(full, 2, 0)

    def restore(values):
        return jnp.moveaxis(values, 0, 2).reshape((rows, length, width))

    unit_ones = jnp.ones((rows, count, width), jnp.float32)
    zero_part = jnp.zeros((rows, count, width), jnp.float32)

    def inner_step(carry, item):
        joined = combine(carry, item)
        return (joined, joined)

    members = (arrange(coef_re), arrange(coef_im), arrange(drive_re), arrange(drive_im))
    unused, inner = lax.scan(
        inner_step, (unit_ones, zero_part, zero_part, zero_part), members, reverse=reverse
    )
    border = 0 if reverse else block - 1
    summary = tuple((jnp.moveaxis(member[border], 1, 0) for member in inner))

    def outer_step(carry, item):
        return (combine(carry, item), carry)

    row_ones = jnp.ones((rows, width), jnp.float32)
    row_zero = jnp.zeros((rows, width), jnp.float32)
    unused_total, entering = lax.scan(
        outer_step, (row_ones, row_zero, row_zero, row_zero), summary, reverse=reverse
    )
    entering = tuple((jnp.moveaxis(member, 0, 1)[None] for member in entering))
    fixed = combine(entering, inner)
    return tuple((restore(member) for member in fixed))


def recurrence(coef_re, coef_im, drive_re, drive_im, reverse):
    inside = local_scan(coef_re, coef_im, drive_re, drive_im, reverse)
    border = 0 if reverse else -1
    summary = tuple((member[:, border] for member in inside))

    def advance(counter, carried):
        out_re, out_im = complex_times(summary[0], summary[1], carried[0], carried[1])
        outgoing = jnp.stack((out_re + summary[2], out_im + summary[3]))
        if reverse:
            return passed_along(outgoing, "tm", -1)
        return passed_along(outgoing, "tm", 1)

    initial = jnp.zeros((2,) + summary[0].shape, jnp.float32)
    carried = lax.fori_loop(0, lax.axis_size("tm") - 1, advance, initial)
    carried_re, carried_im = (carried[0], carried[1])
    lift_re, lift_im = complex_times(inside[0], inside[1], carried_re[:, None], carried_im[:, None])
    return (inside[2] + lift_re, inside[3] + lift_im, carried_re, carried_im)


def moments(current, valid_mask):
    count_here = jnp.sum(valid_mask)
    counted, summed, squares = lax.psum(
        (
            count_here,
            jnp.sum(valid_mask * current, axis=(0, 1)),
            jnp.sum(valid_mask * current * current, axis=(0, 1)),
        ),
        ("batch", "tm"),
    )
    center = summed / counted
    spread = squares / counted - center * center
    return (counted, center, spread)


def prepare(
    layer_index,
    norm_gain,
    norm_shift,
    b_proj,
    log_rate,
    rotation,
    c_proj,
    skip_gain,
    w_gate,
    gate_bias,
):
    decay_rate = jnp.exp(log_rate[layer_index])
    magnitude = jnp.exp(-decay_rate)
    norm_in = jnp.sqrt(-jnp.expm1(-2.0 * decay_rate))
    return {
        "gain": norm_gain[layer_index],
        "shift": norm_shift[layer_index],
        "b_proj": b_proj[layer_index],
        "decay_rate": decay_rate,
        "lam_re": magnitude * jnp.cos(rotation[layer_index]),
        "lam_im": magnitude * jnp.sin(rotation[layer_index]),
        "norm_in": norm_in,
        "norm_both": jnp.concatenate((norm_in, norm_in)),
        "c_proj": c_proj[layer_index],
        "skip_gain": skip_gain[layer_index],
        "w_gate": w_gate[layer_index],
        "gate_bias": gate_bias[layer_index],
    }


def layer_forward(current, valid_mask, keep_mask, weights, reverse):
    states = weights["lam_re"].shape[0]
    counted, center, spread = moments(current, valid_mask)
    scaling = lax.rsqrt(spread + epsilon)
    normed = (current - center) * scaling
    masked = valid_mask * (normed * weights["gain"] + weights["shift"])
    masked_low = masked.astype(jnp.bfloat16)
    driven = jnp.einsum(
        "rth,hs->rts", masked_low, weights["b_proj"], preferred_element_type=jnp.float32
    )
    state_re, state_im, carried_re, carried_im = recurrence(
        keep_mask * weights["lam_re"],
        keep_mask * weights["lam_im"],
        weights["norm_in"] * driven[..., :states],
        weights["norm_in"] * driven[..., states:],
        reverse,
    )
    state_low = jnp.concatenate((state_re, state_im), axis=-1).astype(jnp.bfloat16)
    mixed_out = (
        jnp.einsum("rts,sh->rth", state_low, weights["c_proj"], preferred_element_type=jnp.float32)
        + weights["skip_gain"] * masked
    )
    active = jax.nn.gelu(mixed_out, approximate=False)
    active_low = active.astype(jnp.bfloat16)
    gate_pre = (
        jnp.einsum("rth,hk->rtk", active_low, weights["w_gate"], preferred_element_type=jnp.float32)
        + weights["gate_bias"]
    )
    result = current + valid_mask * active * jax.nn.sigmoid(gate_pre)
    saved = {
        "counted": counted,
        "center": center,
        "spread": spread,
        "scaling": scaling,
        "normed": normed,
        "masked": masked,
        "masked_low": masked_low,
        "driven": driven,
        "state_re": state_re,
        "state_im": state_im,
        "carried_re": carried_re,
        "carried_im": carried_im,
        "state_low": state_low,
        "mixed_out": mixed_out,
        "active": active,
        "active_low": active_low,
        "gate_pre": gate_pre,
    }
    return (result, saved)


def layer_backward(grad_out, valid_mask, keep_adjoint, keep_mask, weights, saved, reverse):
    states = weights["lam_re"].shape[0]
    lam_re = weights["lam_re"]
    lam_im = weights["lam_im"]
    sigmoid_gate = jax.nn.sigmoid(saved["gate_pre"])
    upstream = valid_mask * grad_out
    gate_grad = (upstream * saved["active"] * sigmoid_gate * (1.0 - sigmoid_gate)).astype(
        jnp.bfloat16
    )
    grad_w = jnp.einsum(
        "rth,rtk->hk", saved["active_low"], gate_grad, preferred_element_type=jnp.float32
    )
    grad_bias = jnp.sum(gate_grad.astype(jnp.float32), axis=(0, 1))
    act_grad = upstream * sigmoid_gate + jnp.einsum(
        "rtk,hk->rth", gate_grad, weights["w_gate"], preferred_element_type=jnp.float32
    )
    mix_grad = (act_grad * gelu_slope(saved["mixed_out"])).astype(jnp.bfloat16)
    mix_wide = mix_grad.astype(jnp.float32)
    grad_c = jnp.einsum(
        "rts,rth->sh", saved["state_low"], mix_grad, preferred_element_type=jnp.float32
    )
    grad_skip = jnp.sum(mix_wide * saved["masked"], axis=(0, 1))
    state_grad = jnp.einsum(
        "rth,sh->rts", mix_grad, weights["c_proj"], preferred_element_type=jnp.float32
    )
    adj_re, adj_im, unused_re, unused_im = recurrence(
        keep_adjoint * lam_re,
        -keep_adjoint * lam_im,
        state_grad[..., :states],
        state_grad[..., states:],
        not reverse,
    )
    state_re = saved["state_re"]
    state_im = saved["state_im"]
    if reverse:
        before_re = jnp.concatenate((state_re[:, 1:], saved["carried_re"][:, None]), axis=1)
        before_im = jnp.concatenate((state_im[:, 1:], saved["carried_im"][:, None]), axis=1)
    else:
        before_re = jnp.concatenate((saved["carried_re"][:, None], state_re[:, :-1]), axis=1)
        before_im = jnp.concatenate((saved["carried_im"][:, None], state_im[:, :-1]), axis=1)
    lam_grad_re = jnp.sum(keep_mask * (adj_re * before_re + adj_im * before_im), axis=(0, 1))
    lam_grad_im = jnp.sum(keep_mask * (adj_im * before_re - adj_re * before_im), axis=(0, 1))
    driven = saved["driven"]
    norm_grad = jnp.sum(adj_re * driven[..., :states] + adj_im * driven[..., states:], axis=(0, 1))
    grad_rotation = lam_re * lam_grad_im - lam_im * lam_grad_re
    decay_rate = weights["decay_rate"]
    rate_grad = (
        -(lam_re * lam_grad_re + lam_im * lam_grad_im)
        + norm_grad * jnp.exp(-2.0 * decay_rate) / weights["norm_in"]
    )
    grad_rate = decay_rate * rate_grad
    drive_grad = (jnp.concatenate((adj_re, adj_im), axis=-1) * weights["norm_both"]).astype(
        jnp.bfloat16
    )
    grad_b = jnp.einsum(
        "rth,rts->hs", saved["masked_low"], drive_grad, preferred_element_type=jnp.float32
    )
    masked_grad = (
        jnp.einsum("rts,hs->rth", drive_grad, weights["b_proj"], preferred_element_type=jnp.float32)
        + weights["skip_gain"] * mix_wide
    )
    z_grad = valid_mask * masked_grad
    normed = saved["normed"]
    grad_gain = jnp.sum(z_grad * normed, axis=(0, 1))
    grad_shift = jnp.sum(z_grad, axis=(0, 1))
    normed_grad = z_grad * weights["gain"]
    first_sum, second_sum = lax.psum(
        (jnp.sum(normed_grad, axis=(0, 1)), jnp.sum(normed_grad * normed, axis=(0, 1))),
        ("batch", "tm"),
    )
    counted = saved["counted"]
    input_grad = grad_out + valid_mask * saved["scaling"] * (
        normed_grad - first_sum / counted - normed * second_sum / counted
    )
    return (
        input_grad,
        (
            grad_gain,
            grad_shift,
            grad_b,
            grad_rate,
            grad_rotation,
            grad_c,
            grad_skip,
            grad_w,
            grad_bias,
        ),
    )


def add_tuples(first_tuple, second_tuple):
    if first_tuple is None:
        return second_tuple
    return tuple((left + right for left, right in zip(first_tuple, second_tuple)))


def local(
    tokens,
    starts,
    lengths,
    cotangent,
    norm_gain,
    norm_shift,
    b_proj,
    log_rate,
    rotation,
    c_proj,
    skip_gain,
    w_gate,
    gate_bias,
    run_mean,
    run_var,
):
    cycle_size = lax.axis_size("tm")
    length = tokens.shape[1]
    offset = lax.axis_index("tm") * length
    places = offset + jnp.arange(length + 1, dtype=jnp.int32)
    resets = jnp.any(starts[:, :, None] == places[None, None, :], axis=1).astype(jnp.float32)
    keeping = 1.0 - resets
    keep_here = keeping[:, :length, None]
    keep_next = (keeping[:, 1:] * (places[None, 1:] < cycle_size * length).astype(jnp.float32))[
        :, :, None
    ]
    valid_mask = (places[None, :length] < lengths[:, None]).astype(jnp.float32)[:, :, None]
    lower = prepare(
        0, norm_gain, norm_shift, b_proj, log_rate, rotation, c_proj, skip_gain, w_gate, gate_bias
    )
    upper = prepare(
        1, norm_gain, norm_shift, b_proj, log_rate, rotation, c_proj, skip_gain, w_gate, gate_bias
    )
    inputs = tokens.astype(jnp.float32)
    results = []
    records = []
    new_mean = run_mean
    new_var = run_var
    for micro_index in range(MICRO):
        lower_row = micro_index * ROWS_DEV
        upper_row = lower_row + ROWS_DEV
        current = inputs[lower_row:upper_row]
        valid_rows = valid_mask[lower_row:upper_row]
        current, saved_a = layer_forward(
            current, valid_rows, keep_here[lower_row:upper_row], lower, False
        )
        current, saved_b = layer_forward(
            current, valid_rows, keep_next[lower_row:upper_row], upper, True
        )
        results.append(current.astype(jnp.bfloat16))
        records.append((saved_a, saved_b))
        new_mean = (1.0 - momentum) * new_mean + momentum * jnp.stack(
            (saved_a["center"], saved_b["center"])
        )
        new_var = (1.0 - momentum) * new_var + momentum * jnp.stack(
            (saved_a["spread"], saved_b["spread"])
        )
    lower_total = None
    upper_total = None
    input_grads = []
    for micro_index in range(MICRO):
        lower_row = micro_index * ROWS_DEV
        upper_row = lower_row + ROWS_DEV
        valid_rows = valid_mask[lower_row:upper_row]
        here_rows = keep_here[lower_row:upper_row]
        next_rows = keep_next[lower_row:upper_row]
        saved_a, saved_b = records[micro_index]
        grad_flow = cotangent[lower_row:upper_row].astype(jnp.float32)
        grad_flow, grads_b = layer_backward(
            grad_flow, valid_rows, here_rows, next_rows, upper, saved_b, True
        )
        upper_total = add_tuples(upper_total, grads_b)
        grad_flow, grads_a = layer_backward(
            grad_flow, valid_rows, next_rows, here_rows, lower, saved_a, False
        )
        lower_total = add_tuples(lower_total, grads_a)
        input_grads.append(grad_flow)
    gradients = lax.psum(
        tuple((jnp.stack((left, right)) for left, right in zip(lower_total, upper_total))),
        ("batch", "tm"),
    )
    output = jnp.concatenate(results, axis=0)
    tokens_grad = jnp.concatenate(input_grads, axis=0)
    return (
        output,
        tokens_grad,
        gradients[0],
        gradients[1],
        gradients[2],
        gradients[3],
        gradients[4],
        gradients[5],
        gradients[6],
        gradients[7],
        gradients[8],
        new_mean,
        new_var,
    )


def solution(mesh):
    return jax.shard_map(
        local,
        mesh=mesh,
        in_specs=(
            P("batch", "tm", None),
            P("batch", None),
            P("batch"),
            P("batch", "tm", None),
            P(),
            P(),
            P(),
            P(),
            P(),
            P(),
            P(),
            P(),
            P(),
            P(),
            P(),
        ),
        out_specs=(
            P("batch", "tm", None),
            P("batch", "tm", None),
            P(),
            P(),
            P(),
            P(),
            P(),
            P(),
            P(),
            P(),
            P(),
            P(),
            P(),
        ),
        check_vma=False,
    )
```

profile of v0, /device:TPU:0, one launch (start us, length us, event | category | flops | bytes accessed | tf_op | source)
XLA Modules:
  0.0 1344.5 jit_solution(3472620517341484114)
XLA Ops:
  12.2 42.4 %all-reduce.3 = (f32[512]{0:T(512)S(1)}, f32[]{:T(128)}, f32[512]{0:T(512)S(1)}, f32[512]{0:T(512)S(1)}, f32[]{:T(128)}, /*index=5*/f32[512]{0:T(512)S(1)}) all-reduce(f32[512]{0:T(512)S(1)} %get-tuple-element.3662, f32[]{:T(128)} %get-tuple-element.3687, ...), channel_id=1, replica_groups=mesh['batch'=4,'tm'=8] {'batch','tm'}, use_global_device_ids=true, to_apply=%region_28.29 | all-reduce | flops 2050 | bytes 16400 | tf_op jit(solution)/shard_map/psum | solution.py:99
  67.0 5.1 broadcast_multiply_fusion.4
  75.1 25.1 %while.524 = (s32[]{:T(128)}, f32[2,16,384]{2,1,0:T(8,128)S(1)}, f32[2,16,384]{2,1,0:T(8,128)S(1)}, f32[2,16,384]{2,1,0:T(8,128)S(1)}, f32[2,16,384]{2,1,0:T(8,1...) while((s32[]{:T(128)}, f32[2,16,384]{2,1,0:T(8,128)S(1)}, ...), condition=%wide.region_30.31_spmd.clone, body=%wide.region_29.30_spmd.clone.sunk | while | flops 221187 | bytes 787095 | solution.py:59
  110.5 31.9 %while.514 = (s32[]{:T(128)}, f32[2,2,384]{2,1,0:T(2,128)S(1)}, f32[2,384]{1,0:T(2,128)S(1)}, f32[2,384]{1,0:T(2,128)S(1)}, f32[2,384]{1,0:T(2,128)S(1)}, /*index=5*/f32[2,384]{1,0:T(2,128)S(1)}, s32[]{:T(128)}) while((s32[]{:T(128)}, f32[2,2,384]{2,1,0:T(2,128)S(1)}, f32[2,384]{1,0:T(2,128)S(1)}, f32[2,384]{1,0:T(2,128)S(1)}, ...), condition=%wide.region_34.35_spmd, body=%wide.region_33.34_spmd.sunk | while | flops 7682 | bytes 61557 | solution.py:91
  112.6 4.1 collective-permute-start.2
  117.6 4.1 collective-permute-start.2
  122.5 4.1 collective-permute-start.2
  127.5 4.1 collective-permute-start.2
  132.4 4.1 collective-permute-start.2
  137.4 4.1 collective-permute-start.2
  151.7 25.0 %while.520 = (s32[]{:T(128)}, f32[2,16,384]{2,1,0:T(8,128)S(1)}, f32[2,16,384]{2,1,0:T(8,128)S(1)}, f32[2,16,384]{2,1,0:T(8,128)S(1)}, f32[2,16,384]{2,1,0:T(8,1...) while((s32[]{:T(128)}, f32[2,16,384]{2,1,0:T(8,128)S(1)}, ...), condition=%wide.region_8.9_spmd.clone, body=%wide.region_7.8_spmd.clone.sunk | while | flops 221187 | bytes 787095 | solution.py:59
  187.4 34.8 %while.512 = (s32[]{:T(128)}, f32[2,2,384]{2,1,0:T(2,128)S(1)}, f32[2,384]{1,0:T(2,128)S(1)}, f32[2,384]{1,0:T(2,128)S(1)}, f32[2,384]{1,0:T(2,128)S(1)}, /*index=5*/f32[2,384]{1,0:T(2,128)S(1)}, s32[]{:T(128)}) while((s32[]{:T(128)}, f32[2,2,384]{2,1,0:T(2,128)S(1)}, f32[2,384]{1,0:T(2,128)S(1)}, f32[2,384]{1,0:T(2,128)S(1)}, ...), condition=%wide.region_12.13_spmd, body=%wide.region_11.12_spmd.sunk | while | flops 7682 | bytes 61557 | solution.py:91
  187.4 4.1 collective-permute-start
  192.3 4.1 collective-permute-start
  197.3 4.1 collective-permute-start
  202.3 4.1 collective-permute-start
  207.2 4.1 collective-permute-start
  212.2 4.1 collective-permute-start
  217.2 4.1 collective-permute-start
  239.3 43.8 %all-reduce.2 = (f32[512]{0:T(512)}, f32[512]{0:T(512)}, f32[512]{0:T(512)}, f32[512]{0:T(512)}) all-reduce(f32[512]{0:T(512)} %get-tuple-element.4513, f32[512]{0:T(512)} %get-tuple-element.4514, f32[512]{0:T(512)} %get-tuple-element.3671, f32[512]{0:T(512)} %get-tuple-element.3670), channel_id=1, replica_groups=mesh['batch'=4,'tm'=8] {'batch','tm'}, use_global_device_ids=true, to_apply=%region_38.39 | all-reduce | flops 2048 | bytes 16384 | tf_op jit(solution)/shard_map/psum | solution.py:99
  296.8 27.9 %while.522 = (s32[]{:T(128)}, f32[2,16,384]{2,1,0:T(8,128)}, f32[2,16,384]{2,1,0:T(8,128)}, f32[2,16,384]{2,1,0:T(8,128)}, f32[2,16,384]{2,1,0:T(8,128)}, /*inde...) while((s32[]{:T(128)}, f32[2,16,384]{2,1,0:T(8,128)}, ...), condition=%wide.region_18.19_spmd.clone, body=%wide.region_17.18_spmd.clone.sunk | while | flops 221188 | bytes 786607 | solution.py:59
  332.7 31.0 %while.523 = (s32[]{:T(128)}, f32[2,384]{1,0:T(2,128)S(1)}, f32[2,384]{1,0:T(2,128)S(1)}, f32[2,384]{1,0:T(2,128)S(1)}, f32[2,384]{1,0:T(2,128)S(1)}, /*index=5*...) while((s32[]{:T(128)}, f32[2,384]{1,0:T(2,128)S(1)}, ...), condition=%wide.region_20.21_spmd.clone, body=%wide.region_19.20_spmd.clone.sunk | while | flops 16900 | bytes 86201 | solution.py:70
  374.6 36.7 %while.513 = (s32[]{:T(128)}, f32[2,2,384]{2,1,0:T(2,128)S(1)}, f32[2,384]{1,0:T(2,128)}, f32[2,384]{1,0:T(2,128)}, f32[2,384]{1,0:T(2,128)}, /*index=5*/f32[2,384]{1,0:T(2,128)}, s32[]{:T(128)}) while((s32[]{:T(128)}, f32[2,2,384]{2,1,0:T(2,128)S(1)}, f32[2,384]{1,0:T(2,128)}, f32[2,384]{1,0:T(2,128)}, f32[2,384]{1,0:T(2,128)}, ...), condition=%wide.region_22.23_spmd, body=%wide.region_21.22_spmd.sunk | while | flops 7682 | bytes 61557 | solution.py:91
  384.9 3.6 collective-permute-done.1
  390.6 3.6 collective-permute-done.1
  420.5 28.0 %while.526 = (s32[]{:T(128)}, f32[2,16,384]{2,1,0:T(8,128)}, f32[2,16,384]{2,1,0:T(8,128)}, f32[2,16,384]{2,1,0:T(8,128)}, f32[2,16,384]{2,1,0:T(8,128)}, /*inde...) while((s32[]{:T(128)}, f32[2,16,384]{2,1,0:T(8,128)}, ...), condition=%wide.region_40.41_spmd.clone, body=%wide.region_39.40_spmd.clone.sunk | while | flops 221188 | bytes 786607 | solution.py:59
  456.5 31.3 %while.527 = (s32[]{:T(128)}, f32[2,384]{1,0:T(2,128)S(1)}, f32[2,384]{1,0:T(2,128)S(1)}, f32[2,384]{1,0:T(2,128)S(1)}, f32[2,384]{1,0:T(2,128)S(1)}, /*index=5*...) while((s32[]{:T(128)}, f32[2,384]{1,0:T(2,128)S(1)}, ...), condition=%wide.region_42.43_spmd.clone, body=%wide.region_41.42_spmd.clone.sunk | while | flops 16900 | bytes 86201 | solution.py:70
  498.7 39.9 %while.515 = (s32[]{:T(128)}, f32[2,2,384]{2,1,0:T(2,128)S(1)}, f32[2,384]{1,0:T(2,128)}, f32[2,384]{1,0:T(2,128)}, f32[2,384]{1,0:T(2,128)}, /*index=5*/f32[2,384]{1,0:T(2,128)}, s32[]{:T(128)}) while((s32[]{:T(128)}, f32[2,2,384]{2,1,0:T(2,128)S(1)}, f32[2,384]{1,0:T(2,128)}, f32[2,384]{1,0:T(2,128)}, f32[2,384]{1,0:T(2,128)}, ...), condition=%wide.region_44.45_spmd, body=%wide.region_43.44_spmd.sunk | while | flops 7682 | bytes 61557 | solution.py:91
  550.8 7.6 convert_reduce_fusion.1
  571.1 27.9 %while.528 = (s32[]{:T(128)}, f32[2,16,384]{2,1,0:T(8,128)}, f32[2,16,384]{2,1,0:T(8,128)}, f32[2,16,384]{2,1,0:T(8,128)}, f32[2,16,384]{2,1,0:T(8,128)}, /*inde...) while((s32[]{:T(128)}, f32[2,16,384]{2,1,0:T(8,128)}, ...), condition=%wide.region_46.47_spmd.clone, body=%wide.region_45.46_spmd.clone.sunk | while | flops 221187 | bytes 787095 | solution.py:59
  607.0 30.9 %while.529 = (s32[]{:T(128)}, f32[2,384]{1,0:T(2,128)S(1)}, f32[2,384]{1,0:T(2,128)S(1)}, f32[2,384]{1,0:T(2,128)S(1)}, f32[2,384]{1,0:T(2,128)S(1)}, /*index=5*...) while((s32[]{:T(128)}, f32[2,384]{1,0:T(2,128)S(1)}, ...), condition=%wide.region_48.49_spmd.clone, body=%wide.region_47.48_spmd.clone.sunk | while | flops 16899 | bytes 87197 | solution.py:70
  649.2 37.6 %while.516 = (s32[]{:T(128)}, f32[2,2,384]{2,1,0:T(2,128)S(1)}, f32[2,384]{1,0:T(2,128)}, f32[2,384]{1,0:T(2,128)}, f32[2,384]{1,0:T(2,128)}, /*index=5*/f32[2,384]{1,0:T(2,128)}, s32[]{:T(128)}) while((s32[]{:T(128)}, f32[2,2,384]{2,1,0:T(2,128)S(1)}, f32[2,384]{1,0:T(2,128)}, f32[2,384]{1,0:T(2,128)}, f32[2,384]{1,0:T(2,128)}, ...), condition=%wide.region_50.51_spmd, body=%wide.region_49.50_spmd.sunk | while | flops 7682 | bytes 61557 | solution.py:91
  649.9 4.3 collective-permute-start.4
  659.5 3.8 collective-permute-start.4
  664.8 4.1 collective-permute-start.4
  670.5 4.1 collective-permute-start.4
  676.2 4.1 collective-permute-start.4
  681.8 4.1 collective-permute-start.4
  695.6 28.2 %while.532 = (s32[]{:T(128)}, f32[2,16,384]{2,1,0:T(8,128)}, f32[2,16,384]{2,1,0:T(8,128)}, f32[2,16,384]{2,1,0:T(8,128)}, f32[2,16,384]{2,1,0:T(8,128)}, /*inde...) while((s32[]{:T(128)}, f32[2,16,384]{2,1,0:T(8,128)}, ...), condition=%wide.region_66.67_spmd.clone, body=%wide.region_65.66_spmd.clone.sunk | while | flops 221187 | bytes 787095 | solution.py:59
  731.8 31.2 %while.533 = (s32[]{:T(128)}, f32[2,384]{1,0:T(2,128)S(1)}, f32[2,384]{1,0:T(2,128)S(1)}, f32[2,384]{1,0:T(2,128)S(1)}, f32[2,384]{1,0:T(2,128)S(1)}, /*index=5*...) while((s32[]{:T(128)}, f32[2,384]{1,0:T(2,128)S(1)}, ...), condition=%wide.region_68.69_spmd.clone, body=%wide.region_67.68_spmd.clone.sunk | while | flops 16899 | bytes 87197 | solution.py:70
  774.2 39.7 %while.518 = (s32[]{:T(128)}, f32[2,2,384]{2,1,0:T(2,128)S(1)}, f32[2,384]{1,0:T(2,128)}, f32[2,384]{1,0:T(2,128)}, f32[2,384]{1,0:T(2,128)}, /*index=5*/f32[2,384]{1,0:T(2,128)}, s32[]{:T(128)}) while((s32[]{:T(128)}, f32[2,2,384]{2,1,0:T(2,128)S(1)}, f32[2,384]{1,0:T(2,128)}, f32[2,384]{1,0:T(2,128)}, f32[2,384]{1,0:T(2,128)}, ...), condition=%wide.region_70.71_spmd, body=%wide.region_69.70_spmd.sunk | while | flops 7682 | bytes 61557 | solution.py:91
  774.9 4.1 collective-permute-start.6
  780.6 4.1 collective-permute-start.6
  786.2 4.1 collective-permute-start.6
  791.9 4.1 collective-permute-start.6
  797.6 4.1 collective-permute-start.6
  803.3 4.1 collective-permute-start.6
  808.9 4.1 collective-permute-start.6
  824.1 44.0 %all-reduce.1 = (f32[512]{0:T(512)}, f32[512]{0:T(512)}, f32[512]{0:T(512)}, f32[512]{0:T(512)}) all-reduce(f32[512]{0:T(512)} %get-tuple-element.4668, f32[512]{0:T(512)} %get-tuple-element.4666, f32[512]{0:T(512)} %get-tuple-element.3657, f32[512]{0:T(512)} %get-tuple-element.3667), channel_id=1, replica_groups=mesh['batch'=4,'tm'=8] {'batch','tm'}, use_global_device_ids=true, to_apply=%region_74.75 | all-reduce | flops 2048 | bytes 16384 | tf_op jit(solution)/shard_map/psum | solution.py:260
  869.3 6.3 convert_reduce_fusion.3
  881.7 3.7 fusion.271
  886.1 5.4 convert_reduce_fusion.2
  895.4 3.7 fusion.115
  913.0 25.6 %while.530 = (s32[]{:T(128)}, f32[2,16,384]{2,1,0:T(8,128)S(1)}, f32[2,16,384]{2,1,0:T(8,128)S(1)}, f32[2,16,384]{2,1,0:T(8,128)S(1)}, f32[2,16,384]{2,1,0:T(8,1...) while((s32[]{:T(128)}, f32[2,16,384]{2,1,0:T(8,128)S(1)}, ...), condition=%wide.region_56.57_spmd.clone, body=%wide.region_55.56_spmd.clone.sunk | while | flops 221188 | bytes 786607 | solution.py:59
  942.0 53.8 %while.531 = (s32[]{:T(128)}, f32[2,384]{1,0:T(2,128)}, f32[2,384]{1,0:T(2,128)}, f32[2,384]{1,0:T(2,128)}, f32[2,384]{1,0:T(2,128)}, /*index=5*/f32[16,2,384]{2...) while((s32[]{:T(128)}, f32[2,384]{1,0:T(2,128)}, ...), condition=%wide.region_58.59_spmd.clone, body=%wide.region_57.58_spmd.clone.sunk | while | flops 16900 | bytes 86201 | solution.py:70
  1001.5 32.5 %while.517 = (s32[]{:T(128)}, f32[2,2,384]{2,1,0:T(2,128)S(1)}, f32[2,384]{1,0:T(2,128)S(1)}, f32[2,384]{1,0:T(2,128)S(1)}, f32[2,384]{1,0:T(2,128)S(1)}, /*index=5*/f32[2,384]{1,0:T(2,128)S(1)}, s32[]{:T(128)}) while((s32[]{:T(128)}, f32[2,2,384]{2,1,0:T(2,128)S(1)}, f32[2,384]{1,0:T(2,128)S(1)}, f32[2,384]{1,0:T(2,128)S(1)}, ...), condition=%wide.region_60.61_spmd, body=%wide.region_59.60_spmd.sunk | while | flops 7682 | bytes 61557 | solution.py:91
  1042.3 25.3 %while.534 = (s32[]{:T(128)}, f32[2,16,384]{2,1,0:T(8,128)S(1)}, f32[2,16,384]{2,1,0:T(8,128)S(1)}, f32[2,16,384]{2,1,0:T(8,128)S(1)}, f32[2,16,384]{2,1,0:T(8,1...) while((s32[]{:T(128)}, f32[2,16,384]{2,1,0:T(8,128)S(1)}, ...), condition=%wide.region_76.77_spmd.clone, body=%wide.region_75.76_spmd.clone.sunk | while | flops 221188 | bytes 786607 | solution.py:59
  1070.9 21.1 %while.535 = (s32[]{:T(128)}, f32[2,384]{1,0:T(2,128)S(1)}, f32[2,384]{1,0:T(2,128)S(1)}, f32[2,384]{1,0:T(2,128)S(1)}, f32[2,384]{1,0:T(2,128)}, /*index=5*/f32...) while((s32[]{:T(128)}, f32[2,384]{1,0:T(2,128)S(1)}, ...), condition=%wide.region_78.79_spmd.clone, body=%wide.region_77.78_spmd.clone.sunk | while | flops 16900 | bytes 86201 | solution.py:70
  1097.8 34.9 %while.519 = (s32[]{:T(128)}, f32[2,2,384]{2,1,0:T(2,128)S(1)}, f32[2,384]{1,0:T(2,128)S(1)}, f32[2,384]{1,0:T(2,128)S(1)}, f32[2,384]{1,0:T(2,128)S(1)}, /*index=5*/f32[2,384]{1,0:T(2,128)S(1)}, s32[]{:T(128)}) while((s32[]{:T(128)}, f32[2,2,384]{2,1,0:T(2,128)S(1)}, f32[2,384]{1,0:T(2,128)S(1)}, f32[2,384]{1,0:T(2,128)S(1)}, ...), condition=%wide.region_80.81_spmd, body=%wide.region_79.80_spmd.sunk | while | flops 7682 | bytes 61557 | solution.py:91
  1154.2 3.7 subtract_add_fusion.2
  1158.1 5.3 multiply_reduce_fusion.6
  1177.6 42.6 %all-reduce = (f32[512]{0:T(512)S(1)}, f32[512]{0:T(512)S(1)}, f32[512]{0:T(512)S(1)}, f32[512]{0:T(512)S(1)}, f32[2,512]{1,0:T(2,128)}, /*index=5*/f32[2,512]{1...) all-reduce(f32[512]{0:T(512)S(1)} %get-tuple-element.3646, ...), channel_id=1, replica_groups=mesh['batch'=4,'tm'=8] {'batch','tm'}, use_global_device_ids=true, to_apply=%region_84.85 | all-reduce | flops 7680 | bytes 61440 | tf_op jit(solution)/shard_map/psum | solution.py:260
  1230.4 99.1 %all-reduce.7.cloned.1.call-done = (f32[2,512,768]{2,1,0:T(8,128)}, f32[2,768,512]{2,1,0:T(8,128)}, f32[2,512,512]{2,1,0:T(8,128)}) async-done(((f32[2,512,768]{2,1,0:T(8,128)}, f32[2,768,512]{2,1,0:T(8,128)}, f32[2,512,512]{2,1,0:T(8,128)}), (f32[2,512,768]{2,1,0:T(8,128)}, f32[2,768,512]{2,1,0:T(8,128)}, f32[2,512,512]{2,1,0:T(8,128)})) %all-reduce.7.cloned.1.call-update) | async-done | bytes 8388624 | tf_op jit(solution)/shard_map/psum | solution.py:368
  1329.5 3.9 copy.1224
  (2444 shorter events, 892.7 us)
Async XLA Ops:
  7.2 1322.3 %all-reduce.7.cloned.1.call-start = ((), (), s32[]{:S(2)}) async-start(), calls=%async_computation | async-start | bytes 16777216 | tf_op jit(solution)/shard_map/psum | solution.py:368
  9.1 50.0 %copy-start.237 = (f32[2,256]{1,0:T(2,128)}, f32[2,256]{1,0:T(2,128)S(1)}, u32[]{:S(2)}) copy-start(f32[2,256]{1,0:T(2,128)S(1)} %get-tuple-element.4679) | copy-start | bytes 6148
  9.1 276.7 %copy-start.211 = (f32[2,256]{1,0:T(2,128)}, f32[2,256]{1,0:T(2,128)S(1)}, u32[]{:S(2)}) copy-start(f32[2,256]{1,0:T(2,128)S(1)} %get-tuple-element.4678) | copy-start | bytes 6148
  11.2 47.8 %copy-start.267 = (f32[1,512]{1,0:T(1,128)}, f32[1,512]{1,0:T(1,128)S(1)}, u32[]{:S(2)}) copy-start(f32[1,512]{1,0:T(1,128)S(1)} %get-tuple-element.4671) | copy-start | bytes 6148
  11.8 47.2 %copy-start.305 = (f32[1,512]{1,0:T(1,128)}, f32[1,512]{1,0:T(1,128)S(1)}, u32[]{:S(2)}) copy-start(f32[1,512]{1,0:T(1,128)S(1)} %get-tuple-element.4673) | copy-start | bytes 6148
  109.1 38.5 %copy-start.147 = (f32[2,256,384]{2,1,0:T(8,128)S(1)}, f32[2,256,384]{2,1,0:T(8,128)}, u32[]{:S(2)}) copy-start(f32[2,256,384]{2,1,0:T(8,128)} %get-tuple-element.4569) | copy-start | bytes 2359300
  110.5 2.1 collective-permute-start.2
  112.6 4.9 collective-permute-start.2
  117.6 4.9 collective-permute-start.2
  122.5 4.9 collective-permute-start.2
  127.5 4.9 collective-permute-start.2
  132.4 4.9 collective-permute-start.2
  137.4 4.9 collective-permute-start.2
  185.4 37.9 %copy-start.111 = (f32[2,16,16,384]{3,2,1,0:T(8,128)S(1)}, f32[2,16,16,384]{3,2,1,0:T(8,128)}, u32[]{:S(2)}) copy-start(f32[2,16,16,384]{3,2,1,0:T(8,128)} %copy-done.110) | copy-start | bytes 2359300
  187.4 5.0 collective-permute-start
  192.3 4.9 collective-permute-start
  197.3 4.9 collective-permute-start
  202.3 4.9 collective-permute-start
  207.2 4.9 collective-permute-start
  212.2 4.9 collective-permute-start
  217.2 4.9 collective-permute-start
  375.3 3.1 collective-permute-start.1
  379.1 3.7 collective-permute-start.1
  383.6 4.9 collective-permute-start.1
  389.3 4.9 collective-permute-start.1
  395.0 4.9 collective-permute-start.1
  400.6 4.9 collective-permute-start.1
  406.3 4.9 collective-permute-start.1
  499.4 4.9 collective-permute-start.3
  505.1 4.9 collective-permute-start.3
  510.8 4.9 collective-permute-start.3
  516.5 4.9 collective-permute-start.3
  522.2 4.9 collective-permute-start.3
  527.9 4.9 collective-permute-start.3
  533.6 4.9 collective-permute-start.3
  649.9 5.1 collective-permute-start.4
  655.7 3.1 collective-permute-start.4
  659.5 4.6 collective-permute-start.4
  664.8 4.9 collective-permute-start.4
  670.5 4.9 collective-permute-start.4
  676.2 4.9 collective-permute-start.4
  681.8 4.9 collective-permute-start.4
  774.9 4.9 collective-permute-start.6
  780.6 5.0 collective-permute-start.6
  786.2 4.9 collective-permute-start.6
  791.9 4.9 collective-permute-start.6
  797.6 4.9 collective-permute-start.6
  803.3 4.9 collective-permute-start.6
  808.9 4.9 collective-permute-start.6
  1001.5 3.1 collective-permute-start.5
  1004.6 4.5 collective-permute-start.5
  1009.1 4.9 collective-permute-start.5
  1014.1 4.9 collective-permute-start.5
  1019.1 4.9 collective-permute-start.5
  1024.0 4.9 collective-permute-start.5
  1029.0 4.9 collective-permute-start.5
  1097.8 4.9 collective-permute-start.7
  1102.8 4.9 collective-permute-start.7
  1107.7 4.9 collective-permute-start.7
  1112.7 4.9 collective-permute-start.7
  1117.7 4.9 collective-permute-start.7
  1122.6 4.9 collective-permute-start.7
  1127.6 4.9 collective-permute-start.7
  1177.4 46.6 %copy-start.73 = (f32[2,256,512]{2,1,0:T(8,128)S(1)}, f32[2,256,512]{2,1,0:T(8,128)}, u32[]{:S(2)}) copy-start(f32[2,256,512]{2,1,0:T(8,128)} %copy-done.72) | copy-start | bytes 3145732
  (348 other events, 1139.9 us)
Sparse Core Ops, SparseCore 0:
  1148.5 180.8 all-reduce.6
where the time goes:
time: 1370 us; the launch traced here: 1340 us
  other arithmetic  475 us (35%)
  local copies, waits for them, and re-layouts  241 us (18%)
  waiting for transfers between devices  218 us (16%)
  blocking collectives  173 us (13%)
  starting transfers between devices  147 us (11%)
  matrix products  65.4 us (5%)
  between operations  19.2 us (1%)
    dynamic_update_slice x128, other arithmetic, local_scan(): lax.scan(inner_step, (unit_ones, zero_part, zero_part, zero_part), member...  213 us
    ppermute x56, starting transfers between devices, passed_along(): return lax.ppermute(block, axis, route)  147 us
    ppermute x56, waiting for transfers between devices, passed_along(): return lax.ppermute(block, axis, route)  119 us
    psum x1, waiting for transfers between devices, local(): lax.psum(tuple((jnp.stack((left, right)) for left, right in zip(lower_tot...  99.1 us
    psum x2, blocking collectives, layer_backward(): lax.psum((jnp.sum(normed_grad, axis=(0, 1)), jnp.sum(normed_grad * normed...  86.6 us
    psum x2, blocking collectives, moments(): lax.psum((count_here, jnp.sum(valid_mask * current, axis=(0, 1)), jnp.sum...  86.2 us
    dynamic_update_slice x256, other arithmetic, local_scan(): lax.scan(outer_step, (row_ones, row_zero, row_zero, row_zero), summary, r...  78.5 us
    add x128, other arithmetic, combine(): return (coef_re, coef_im, state_re + later[2], state_im + later[3])  66 us
  transfers between devices with their start and end apart: 57, of which 57 were waited for; matrix products, arithmetic and copies ran while one was open for 2% of the time, Pallas kernels for 0%

commit v1 on v0

v1 whole, which is shorter than its diff:
```python
import functools

import jax
import jax.numpy as jnp
from jax import lax
from jax.experimental import pallas as pl
from jax.experimental.pallas import tpu as pltpu
from jax.sharding import PartitionSpec as P

epsilon = 1e-05
momentum = 0.1
F32 = jnp.float32
BF16 = jnp.bfloat16

SUB = 8
LANE = 128
TILE = 256


def in_vmem(count):
    return [pl.BlockSpec(memory_space=pltpu.VMEM)] * count


def call(name, body, outs, args, scratch=(), scalars=0):
    specs = [pl.BlockSpec(memory_space=pltpu.SMEM)] * scalars + in_vmem(len(args) - scalars)
    return pl.pallas_call(
        body,
        name=name,
        out_shape=outs,
        in_specs=specs,
        out_specs=in_vmem(len(outs)),
        scratch_shapes=list(scratch),
        compiler_params=pltpu.CompilerParams(vmem_limit_bytes=56 * 1024 * 1024),
    )(*args)


def shaped(shape, dtype=F32):
    return jax.ShapeDtypeStruct(shape, dtype)


def tile_mask(lim_ref, i):
    steps = TILE // SUB
    t = lax.broadcasted_iota(jnp.int32, (steps,) + lim_ref.shape, 0) + i * steps
    return t < lim_ref[...][None]


def folded(values):
    return values.reshape((values.shape[0] // SUB, SUB, values.shape[1]))


def flat(values):
    return values.reshape((values.shape[0] * SUB, values.shape[2]))


def times(ar, ai, br, bi):
    return (ar * br - ai * bi, ar * bi + ai * br)


def scan(d_ref, keep_ref, par_ref, start, reverse, conj, visit=None, extra=(), unroll=8):
    width = par_ref.shape[1]
    count = d_ref.shape[0] // SUB
    tiles = width // LANE
    lam = []
    for j in range(tiles):
        lanes = slice(j * LANE, (j + 1) * LANE)
        lr = jnp.broadcast_to(par_ref[0:1, lanes], (SUB, LANE))
        li = jnp.broadcast_to(par_ref[1:2, lanes], (SUB, LANE))
        lam.append((lr, -li if conj else li))
    state = tuple(
        (start[0][:, j * LANE : (j + 1) * LANE], start[1][:, j * LANE : (j + 1) * LANE])
        for j in range(tiles)
    )

    def step(i, carry):
        state, extra = carry
        t = count - 1 - i if reverse else i
        at = pl.ds(pl.multiple_of(t * SUB, SUB), SUB)
        keep = keep_ref[at, :]
        fresh = []
        for j in range(tiles):
            re, im = state[j]
            a = keep * lam[j][0]
            b = keep * lam[j][1]
            dr = d_ref[at, j * LANE : (j + 1) * LANE]
            di = d_ref[at, width + j * LANE : width + (j + 1) * LANE]
            fresh.append((a * re - b * im + dr, a * im + b * re + di))
        fresh = tuple(fresh)
        if visit is not None:
            extra = visit(t, keep, fresh, extra)
        return (fresh, extra)

    state, extra = lax.fori_loop(0, count, step, (state, tuple(extra)), unroll=unroll)
    re = jnp.concatenate([part[0] for part in state], axis=1)
    im = jnp.concatenate([part[1] for part in state], axis=1)
    return re, im, extra


def wide(values, width):
    return jnp.concatenate([values] * (width // LANE), axis=1)


def chunk_end(ends, kp_ref, par_ref, reverse, conj):
    width = par_ref.shape[1]
    re, im = ends
    shift = SUB - 1 if reverse else 1
    pr, pi = pltpu.roll(re, shift, 0), pltpu.roll(im, shift, 0)
    keep = wide(kp_ref[...], width)
    lr = keep * par_ref[2:3, :]
    li = keep * par_ref[3:4, :]
    li = -li if conj else li
    qr, qi = times(lr, li, pr, pi)
    odd = lax.broadcasted_iota(jnp.int32, (SUB, width), 0) % 2
    last = odd == (0 if reverse else 1)
    return jnp.where(last, qr + re, re), jnp.where(last, qi + im, im)


def enter(me_ref, got_ref, kd_ref, kp_ref, par_ref, reverse, conj):
    width = par_ref.shape[1]
    n = got_ref.shape[0]
    me = me_ref[0, 0]
    lr = jnp.broadcast_to(par_ref[4:5, :], (SUB, width))
    li = jnp.broadcast_to(par_ref[5:6, :], (SUB, width))
    li = -li if conj else li

    def step(i, x):
        j = n - 1 - i if reverse else i
        keep = wide(kd_ref[j], width)
        qr, qi = times(keep * lr, keep * li, x[0], x[1])
        use = (j > me) if reverse else (j < me)
        use = jnp.where(use, 1.0, 0.0)
        nr = qr + got_ref[j, :, :width]
        ni = qi + got_ref[j, :, width:]
        return (x[0] + use * (nr - x[0]), x[1] + use * (ni - x[1]))

    zero = jnp.zeros((SUB, width), F32)
    xr, xi = lax.fori_loop(0, n, step, (zero, zero), unroll=n <= 8)
    own_r = got_ref[me, :, :width]
    own_i = got_ref[me, :, width:]
    near, far = (1, SUB - 1) if reverse else (SUB - 1, 1)
    sr, si = pltpu.roll(xr, near, 0), pltpu.roll(xi, near, 0)
    keep = wide(kp_ref[...], width)
    hr = keep * par_ref[2:3, :]
    hi = keep * par_ref[3:4, :]
    hi = -hi if conj else hi
    tr, ti = times(hr, hi, sr, si)
    tr, ti = pltpu.roll(tr + own_r, far, 0), pltpu.roll(ti + own_i, far, 0)
    odd = lax.broadcasted_iota(jnp.int32, (SUB, width), 0) % 2
    second = odd == (0 if reverse else 1)
    return jnp.where(second, tr, sr), jnp.where(second, ti, si)


def put_ends(e_ref, ends):
    e_ref[...] = jnp.concatenate(ends, axis=1)


def zeros_state(par_ref):
    zero = jnp.zeros((SUB, par_ref.shape[1]), F32)
    return (zero, zero)


def per_micro(values):
    return (
        jnp.sum(values[0:4], axis=0, keepdims=True),
        jnp.sum(values[4:8], axis=0, keepdims=True),
    )


def pack_rows(out_ref, rows):
    at = 0
    for row in rows:
        for j in range(row.shape[1] // LANE):
            out_ref[at : at + 1, :] = row[:, j * LANE : (j + 1) * LANE]
            at += 1


def unpack_rows(values, count, width):
    tiles = width // LANE
    return [
        jnp.concatenate(
            [values[r * tiles + j : r * tiles + j + 1, :] for j in range(tiles)], axis=1
        )
        for r in range(count)
    ]


def by_micro(first, second):
    sub = lax.broadcasted_iota(jnp.int32, (SUB, first.shape[1]), 0)
    return jnp.where(sub < 4, jnp.broadcast_to(first, sub.shape), jnp.broadcast_to(second, sub.shape))


def dot(a, b):
    return jnp.dot(a, b, preferred_element_type=F32)


def dot_nt(a, b):
    return lax.dot_general(a, b, (((1,), (1,)), ((), ())), preferred_element_type=F32)


def dot_tn(a, b):
    return lax.dot_general(a, b, (((0,), (0,)), ((), ())), preferred_element_type=F32)


def normed_tile(u_ref, stat_ref, i):
    x = folded(u_ref[pl.ds(pl.multiple_of(i * TILE, TILE), TILE), :])
    return (x - stat_ref[0:8, :][None]) * stat_ref[8:16, :][None]


def masked_tile(u_ref, stat_ref, vec_ref, lim_ref, i):
    normed = normed_tile(u_ref, stat_ref, i)
    z = normed * vec_ref[0:1, :][None] + vec_ref[1:2, :][None]
    return jnp.where(tile_mask(lim_ref, i), z, 0.0)


def rows_at(i):
    return pl.ds(pl.multiple_of(i * TILE, TILE), TILE)


def spread_in(src_ref, dst_ref, lines_ref):
    half = src_ref.shape[1] // 2
    tiles = src_ref.shape[2] // LANE
    for s in range(SUB):
        part = src_ref[s // 2, (s % 2) * half : (s % 2 + 1) * half, :].astype(F32)
        for j in range(tiles):
            lines_ref[j, pl.ds(s, half, stride=SUB), :] = part[:, j * LANE : (j + 1) * LANE]
    for j in range(tiles):
        dst_ref[:, j * LANE : (j + 1) * LANE] = lines_ref[j]


def spread_out(lines_ref, dst_ref):
    half = dst_ref.shape[1] // 2
    tiles = dst_ref.shape[2] // LANE
    for s in range(SUB):
        for j in range(tiles):
            part = lines_ref[j, pl.ds(s, half, stride=SUB), :]
            dst_ref[s // 2, (s % 2) * half : (s % 2 + 1) * half, j * LANE : (j + 1) * LANE] = part.astype(dst_ref.dtype)


def put_lines(lines_ref, i, values):
    for j in range(lines_ref.shape[0]):
        lines_ref[j, rows_at(i), :] = values[:, j * LANE : (j + 1) * LANE]


def moment_sums(u_ref, lim_ref, upto):
    def step(i, sums):
        x = jnp.where(tile_mask(lim_ref, i), folded(u_ref[rows_at(i), :]), 0.0)
        return (sums[0] + jnp.sum(x, axis=0), sums[1] + jnp.sum(x * x, axis=0))

    zero = jnp.zeros(lim_ref.shape, F32)
    return lax.fori_loop(0, upto, step, (zero, zero))


def k_input(tokens_ref, lim_ref, u_ref, st_ref, lines_ref):
    spread_in(tokens_ref, u_ref, lines_ref)
    half = tokens_ref.shape[1] // 2
    sums, squares = moment_sums(u_ref, lim_ref, u_ref.shape[0] // TILE)
    a, b = per_micro(sums)
    c, d = per_micro(squares)
    st_ref[...] = jnp.zeros(st_ref.shape, F32)
    pack_rows(st_ref, (a, c, b, d))
    counts = jnp.clip(lim_ref[:, :LANE], 0, half).astype(F32)
    a, b = per_micro(counts)
    st_ref[16:17, :] = a
    st_ref[17:18, :] = b


def k_drive(reverse, st_ref, cnt_ref, u_ref, lim_ref, vec_ref, par_ref, b_ref, keep_ref, kp_ref,
            d_ref, ml_ref, stat_ref, e_ref):
    total = jnp.sum(st_ref[...], axis=0)
    a, c, b, d = unpack_rows(total, 4, u_ref.shape[1])
    if cnt_ref is None:
        counts = (total[16:17, :], total[17:18, :])
    else:
        counts = (cnt_ref[0:1, :], cnt_ref[1:2, :])
    parts = []
    for summed, squares, count in ((a, c, counts[0]), (b, d, counts[1])):
        inverse = 1.0 / wide(count, u_ref.shape[1])
        center = summed * inverse
        spread = squares * inverse - center * center
        parts.append((center, spread, lax.rsqrt(spread + epsilon), inverse))
    stat_ref[0:8, :] = by_micro(parts[0][0], parts[1][0])
    stat_ref[8:16, :] = by_micro(parts[0][2], parts[1][2])
    stat_ref[16:24, :] = by_micro(parts[0][3], parts[1][3])
    stat_ref[24:25, :] = parts[0][0]
    stat_ref[25:26, :] = parts[1][0]
    stat_ref[26:27, :] = parts[0][1]
    stat_ref[27:28, :] = parts[1][1]
    stat_ref[28:29, :] = wide(counts[0], u_ref.shape[1])
    stat_ref[29:30, :] = wide(counts[1], u_ref.shape[1])
    stat_ref[30:32, :] = jnp.zeros((2, u_ref.shape[1]), F32)
    both = jnp.concatenate((par_ref[6:7, :], par_ref[6:7, :]), axis=1)

    def step(i, unused):
        low = flat(masked_tile(u_ref, stat_ref, vec_ref, lim_ref, i)).astype(BF16)
        ml_ref[rows_at(i), :] = low
        d_ref[rows_at(i), :] = dot(low, b_ref[...]) * both
        return unused

    lax.fori_loop(0, u_ref.shape[0] // TILE, step, 0)
    re, im, unused = scan(d_ref, keep_ref, par_ref, zeros_state(par_ref), reverse, False)
    put_ends(e_ref, chunk_end((re, im), kp_ref, par_ref, reverse, False))


def k_drive_first(reverse, st_ref, *refs):
    k_drive(reverse, st_ref, None, *refs)


def run_states(me_ref, got_ref, d_ref, keep_ref, kp_ref, kd_ref, par_ref, s_ref, reverse):
    width = par_ref.shape[1]
    first = 0 if reverse else SUB
    start = enter(me_ref, got_ref, kd_ref, kp_ref, par_ref, reverse, False)
    s_ref[(s_ref.shape[0] - SUB if reverse else 0) : (s_ref.shape[0] if reverse else SUB), :] = (
        jnp.concatenate(start, axis=1)
    )

    def visit(t, keep, states, extra):
        at = pl.ds(pl.multiple_of(t * SUB + first, SUB), SUB)
        for j, (re, im) in enumerate(states):
            s_ref[at, j * LANE : (j + 1) * LANE] = re
            s_ref[at, width + j * LANE : width + (j + 1) * LANE] = im
        return extra

    scan(d_ref, keep_ref, par_ref, start, reverse, False, visit)
    return first


def gelu_parts(x):
    cdf = 0.5 * (1.0 + lax.erf(x * 0.7071067811865476))
    return x * cdf, cdf + x * jnp.exp(-0.5 * x * x) * 0.3989422804014327


def states_low(s_ref, first, i):
    return s_ref[pl.ds(pl.multiple_of(i * TILE + first, SUB), TILE), :].astype(BF16)


def k_finish_first(me_ref, got_ref, d_ref, u_ref, stat_ref, lim_ref, vec_ref, par_ref, keep_ref, kp_ref, kd_ref,
                   c_ref, w_ref, s_ref, al_ref, sig_ref, q_ref, slope_ref, next_ref, st_ref):
    first = run_states(me_ref, got_ref, d_ref, keep_ref, kp_ref, kd_ref, par_ref, s_ref, False)

    def step(i, sums):
        at = rows_at(i)
        valid = tile_mask(lim_ref, i)
        masked = masked_tile(u_ref, stat_ref, vec_ref, lim_ref, i)
        mixed = dot(states_low(s_ref, first, i), c_ref[...]) + vec_ref[2:3, :] * flat(masked)
        active, slope = gelu_parts(mixed)
        low = active.astype(BF16)
        sig = jax.nn.sigmoid(dot(low, w_ref[...]) + vec_ref[3:4, :])
        gated = active * sig
        al_ref[at, :] = low
        sig_ref[at, :] = sig
        slope_ref[at, :] = slope
        q_ref[at, :] = gated * (1.0 - sig)
        fresh = folded(u_ref[at, :]) + jnp.where(valid, folded(gated), 0.0)
        next_ref[at, :] = flat(fresh)
        x = jnp.where(valid, fresh, 0.0)
        return (sums[0] + jnp.sum(x, axis=0), sums[1] + jnp.sum(x * x, axis=0))

    zero = jnp.zeros(lim_ref.shape, F32)
    sums, squares = lax.fori_loop(0, u_ref.shape[0] // TILE, step, (zero, zero))
    a, b = per_micro(sums)
    c, d = per_micro(squares)
    pack_rows(st_ref, (a, c, b, d))


def gate_backward(upstream, q, sig, slope, low, masked, s_low, state, c_ref, w_ref, mix_ref, sg_ref, gw_ref, gc_ref, i):
    at = rows_at(i)
    gate = (upstream * q).astype(BF16)
    gw_ref[...] += dot_tn(low, gate)
    act = upstream * sig + dot_nt(gate, w_ref[...])
    mix = (act * slope).astype(BF16)
    mix_ref[at, :] = mix
    gc_ref[...] += dot_tn(s_low, mix)
    sg = dot_nt(mix, c_ref[...])
    sg_ref[at, :] = sg
    wide_sum = jnp.sum(folded(sg * state), axis=0)
    half = wide_sum.shape[1] // 2
    return (
        jnp.sum(folded(gate.astype(F32)), axis=0),
        jnp.sum(folded(mix.astype(F32) * masked), axis=0),
        wide_sum[:, :half] + wide_sum[:, half:],
    )


def put_sums(sums_ref, sums):
    sums_ref[...] = jnp.zeros(sums_ref.shape, F32)
    pack_rows(sums_ref, [jnp.sum(part, axis=0, keepdims=True) for part in sums])


def zero_sums(width, states):
    return (jnp.zeros((SUB, width), F32), jnp.zeros((SUB, width), F32), jnp.zeros((SUB, states), F32))


def k_middle(me_ref, got_ref, d_ref, u_ref, stat_ref, lim_ref, vec_ref, par_ref, keep_ref, kp_ref, kd_ref,
             keep_adj_ref, kp_adj_ref, c_ref, w_ref, cot_ref,
             out_ref, s_ref, cot32_ref, mix_ref, sg_ref, gw_ref, gc_ref, sums_ref, e_ref, lines_ref):
    spread_in(cot_ref, cot32_ref, lines_ref)
    first = run_states(me_ref, got_ref, d_ref, keep_ref, kp_ref, kd_ref, par_ref, s_ref, True)
    gw_ref[...] = jnp.zeros(gw_ref.shape, F32)
    gc_ref[...] = jnp.zeros(gc_ref.shape, F32)

    def step(i, sums):
        at = rows_at(i)
        valid = tile_mask(lim_ref, i)
        masked = flat(masked_tile(u_ref, stat_ref, vec_ref, lim_ref, i))
        state = s_ref[pl.ds(pl.multiple_of(i * TILE + first, SUB), TILE), :]
        s_low = state.astype(BF16)
        mixed = dot(s_low, c_ref[...]) + vec_ref[2:3, :] * masked
        active, slope = gelu_parts(mixed)
        low = active.astype(BF16)
        sig = jax.nn.sigmoid(dot(low, w_ref[...]) + vec_ref[3:4, :])
        gated = active * sig
        put_lines(lines_ref, i, flat(folded(u_ref[at, :]) + jnp.where(valid, folded(gated), 0.0)))
        upstream = flat(jnp.where(valid, folded(cot32_ref[at, :]), 0.0))
        more = gate_backward(upstream, gated * (1.0 - sig), sig, slope, low, masked, s_low, state,
                             c_ref, w_ref, mix_ref, sg_ref, gw_ref, gc_ref, i)
        return tuple(x + y for x, y in zip(sums, more))

    sums = lax.fori_loop(0, u_ref.shape[0] // TILE, step, zero_sums(u_ref.shape[1], par_ref.shape[1]))
    put_sums(sums_ref, sums)
    spread_out(lines_ref, out_ref)
    re, im, unused = scan(sg_ref, keep_adj_ref, par_ref, zeros_state(par_ref), False, True)
    put_ends(e_ref, chunk_end((re, im), kp_adj_ref, par_ref, False, True))


def k_lower(st_ref, z_ref, cot32_ref, u1_ref, stat1_ref, vec1_ref, lim_ref,
            s_ref, al_ref, sig_ref, q_ref, slope_ref, u_ref, stat_ref, vec_ref, par_ref, c_ref, w_ref,
            keep_adj_ref, kp_adj_ref,
            grad_ref, mix_ref, sg_ref, gw_ref, gc_ref, sums_ref, e_ref, bn_ref):
    first = SUB
    c1, c2 = norm_sums(st_ref, stat1_ref, vec1_ref, bn_ref)
    gw_ref[...] = jnp.zeros(gw_ref.shape, F32)
    gc_ref[...] = jnp.zeros(gc_ref.shape, F32)

    def step(i, sums):
        at = rows_at(i)
        valid = tile_mask(lim_ref, i)
        extra = norm_backward(z_ref, u1_ref, stat1_ref, vec1_ref, c1, c2, valid, i)
        grad = folded(cot32_ref[at, :]) + extra
        grad_ref[at, :] = flat(grad)
        upstream = flat(jnp.where(valid, grad, 0.0))
        masked = flat(masked_tile(u_ref, stat_ref, vec_ref, lim_ref, i))
        state = s_ref[pl.ds(pl.multiple_of(i * TILE + first, SUB), TILE), :]
        more = gate_backward(upstream, q_ref[at, :], sig_ref[at, :], slope_ref[at, :], al_ref[at, :], masked,
                             state.astype(BF16), state, c_ref, w_ref, mix_ref, sg_ref, gw_ref, gc_ref, i)
        return tuple(x + y for x, y in zip(sums, more))

    sums = lax.fori_loop(0, u_ref.shape[0] // TILE, step, zero_sums(u_ref.shape[1], par_ref.shape[1]))
    put_sums(sums_ref, sums)
    re, im, unused = scan(sg_ref, keep_adj_ref, par_ref, zeros_state(par_ref), True, True)
    put_ends(e_ref, chunk_end((re, im), kp_adj_ref, par_ref, True, True))


def norm_sums(st_ref, stat_ref, vec_ref, bn_ref):
    width = vec_ref.shape[1]
    a, c, b, d = unpack_rows(jnp.sum(st_ref[...], axis=0), 4, width)
    bn_ref[...] = jnp.concatenate((a + b, c + d, jnp.zeros((6, width), F32)), axis=0)
    gain = vec_ref[0:1, :]
    inverse = stat_ref[16:24, :]
    return by_micro(a * gain, b * gain) * inverse, by_micro(c * gain, d * gain) * inverse


def norm_backward(z_ref, u_ref, stat_ref, vec_ref, c1, c2, valid, i):
    normed = normed_tile(u_ref, stat_ref, i)
    z = folded(z_ref[rows_at(i), :]) * vec_ref[0:1, :][None]
    return jnp.where(valid, stat_ref[8:16, :][None] * (z - c1[None] - normed * c2[None]), 0.0)


def k_adjoint(reverse, me_ref, got_ref, sg_ref, s_ref, mix_ref, ml_ref, u_ref, stat_ref, lim_ref, vec_ref, par_ref,
              keep_adj_ref, kp_adj_ref, kd_adj_ref, keep_ref, b_ref,
              z_ref, gb_ref, lg_ref, st_ref, a_ref):
    width = par_ref.shape[1]
    tiles = width // LANE
    behind = 0 if reverse else SUB
    start = enter(me_ref, got_ref, kd_adj_ref, kp_adj_ref, par_ref, reverse, True)
    scale = [jnp.broadcast_to(par_ref[6:7, j * LANE : (j + 1) * LANE], (SUB, LANE)) for j in range(tiles)]

    def visit(t, unused, adjoint, sums):
        at = pl.ds(pl.multiple_of(t * SUB, SUB), SUB)
        before = pl.ds(pl.multiple_of(t * SUB + behind, SUB), SUB)
        keep = keep_ref[at, :]
        fresh = []
        for j, (re, im) in enumerate(adjoint):
            a_ref[at, j * LANE : (j + 1) * LANE] = re * scale[j]
            a_ref[at, width + j * LANE : width + (j + 1) * LANE] = im * scale[j]
            pr = s_ref[before, j * LANE : (j + 1) * LANE]
            pi = s_ref[before, width + j * LANE : width + (j + 1) * LANE]
            kr, ki = keep * re, keep * im
            fresh.append((sums[j][0] + (kr * pr + ki * pi), sums[j][1] + (ki * pr - kr * pi)))
        return tuple(fresh)

    zero = jnp.zeros((SUB, LANE), F32)
    unused, unused, sums = scan(sg_ref, keep_adj_ref, par_ref, start, reverse, True, visit,
                                tuple((zero, zero) for j in range(tiles)))
    lg_ref[...] = jnp.zeros(lg_ref.shape, F32)
    pack_rows(lg_ref, [
        jnp.sum(jnp.concatenate([part[k] for part in sums], axis=1), axis=0, keepdims=True) for k in range(2)
    ])
    gb_ref[...] = jnp.zeros(gb_ref.shape, F32)

    def step(i, sums):
        at = rows_at(i)
        drive = a_ref[at, :].astype(BF16)
        gb_ref[...] += dot_tn(ml_ref[at, :], drive)
        back = dot_nt(drive, b_ref[...]) + vec_ref[2:3, :] * mix_ref[at, :].astype(F32)
        z = jnp.where(tile_mask(lim_ref, i), folded(back), 0.0)
        z_ref[at, :] = flat(z)
        return (sums[0] + jnp.sum(z, axis=0), sums[1] + jnp.sum(z * normed_tile(u_ref, stat_ref, i), axis=0))

    zero = jnp.zeros(lim_ref.shape, F32)
    sums = lax.fori_loop(0, u_ref.shape[0] // TILE, step, (zero, zero))
    a, b = per_micro(sums[0])
    c, d = per_micro(sums[1])
    pack_rows(st_ref, (a, c, b, d))


def k_output(st_ref, z_ref, grad_ref, u_ref, stat_ref, vec_ref, lim_ref, out_ref, bn_ref, lines_ref):
    c1, c2 = norm_sums(st_ref, stat_ref, vec_ref, bn_ref)

    def step(i, unused):
        extra = norm_backward(z_ref, u_ref, stat_ref, vec_ref, c1, c2, tile_mask(lim_ref, i), i)
        put_lines(lines_ref, i, grad_ref[rows_at(i), :] + flat(extra))
        return unused

    lax.fori_loop(0, u_ref.shape[0] // TILE, step, 0)
    spread_out(lines_ref, out_ref)


BOTH = ("batch", "tm")


def index_bits():
    nb, nt = lax.axis_size("batch"), lax.axis_size("tm")
    core = ("tm", 1, 1)
    outer = [("batch", 1 << k, nt << k) for k in range(nb.bit_length() - 1)]
    line = [("tm", 1 << k, 1 << k) for k in range(1, nt.bit_length() - 1)]
    return core, outer, line


def swap(block, distance):
    total = lax.axis_size("batch") * lax.axis_size("tm")
    return lax.ppermute(block, BOTH, [(i, i ^ distance) for i in range(total)])


def swap_by_core(block, even, odd):
    total = lax.axis_size("batch") * lax.axis_size("tm")
    return lax.ppermute(block, BOTH, [(i, i ^ (odd if i & 1 else even)) for i in range(total)])


def sums_of_all(block):
    block = block + swap(block, 1)
    total = lax.axis_size("batch") * lax.axis_size("tm")
    groups = [list(range(0, total, 2)), list(range(1, total, 2))]
    spread = jnp.broadcast_to(block[None], (total // 2,) + block.shape)
    return lax.all_to_all(spread, BOTH, 0, 0, axis_index_groups=groups)


def blocks_of_row(block):
    n = lax.axis_size("tm")
    return lax.all_to_all(jnp.broadcast_to(block[None], (n,) + block.shape), "tm", 0, 0)


def bit_of(axis, bit):
    return jnp.where((lax.axis_index(axis) & bit) != 0, 1, 0)


def plan():
    core, outer, line = index_bits()
    is_odd = bit_of("tm", 1)
    steps = [(is_odd, lambda block: swap(block, 1))]
    turned = outer[::-1]
    for even, odd in zip(outer, turned):
        side = jnp.where(is_odd == 1, bit_of(odd[0], odd[1]), bit_of(even[0], even[1]))
        steps.append((side, functools.partial(swap_by_core, even=even[2], odd=odd[2])))
    for axis, bit, distance in line:
        steps.append((bit_of(axis, bit), functools.partial(swap, distance=distance)))
    return steps


def sum_large(block):
    steps = plan()
    for side, exchange in steps:
        half = block.shape[0] // 2
        given = lax.dynamic_slice_in_dim(block, (1 - side) * half, half, 0)
        kept = lax.dynamic_slice_in_dim(block, side * half, half, 0)
        block = kept + exchange(given)
    for side, exchange in steps[::-1]:
        other = exchange(block)
        low = jnp.where(side == 1, other, block)
        high = jnp.where(side == 1, block, other)
        block = jnp.concatenate((low, high), axis=0)
    return block


def power(re, im, doublings):
    for unused in range(doublings):
        re, im = times(re, im, re, im)
    return re, im


def local(tokens, starts, lengths, cotangent, norm_gain, norm_shift, b_proj, log_rate, rotation, c_proj, skip_gain,
          w_gate, gate_bias, run_mean, run_var):
    rows, length, width = tokens.shape
    states = log_rate.shape[1]
    half = length // 2
    count = rows * length
    n = lax.axis_size("tm")
    me = lax.axis_index("tm")
    offset = me * length

    places = offset + jnp.arange(length + 1, dtype=jnp.int32)
    resets = jnp.any(starts[:, :, None] == places[None, None, :], axis=1)
    keeping = 1.0 - resets.astype(F32)
    here = keeping[:, :length].reshape((SUB, half))
    following = (keeping[:, 1:] * (places[None, 1:] < n * length).astype(F32)).reshape((SUB, half))

    def over_lanes(values):
        return jnp.broadcast_to(values[..., None], values.shape + (LANE,))

    def by_tile(values):
        return over_lanes(values.T).reshape((count, LANE))

    keep_f, keep_r = by_tile(here), by_tile(following)
    kp_f, kp_r = over_lanes(jnp.min(here, axis=1)), over_lanes(jnp.min(following, axis=1))
    devices = jnp.arange(n, dtype=jnp.int32)[:, None, None]

    def whole(first):
        hit = jnp.any((first[None] >= devices * length) & (first[None] < (devices + 1) * length), axis=2)
        return over_lanes(jnp.repeat(1.0 - hit.astype(F32), 2, axis=1))

    kd_f, kd_r = whole(starts), whole(starts - 1)
    halves = jnp.arange(SUB, dtype=jnp.int32) % 2
    lim = jnp.broadcast_to(
        (jnp.repeat(lengths, 2) - offset - halves * half)[:, None], (SUB, width)
    )

    decay = jnp.exp(log_rate)
    magnitude = jnp.exp(-decay)
    lam_re, lam_im = magnitude * jnp.cos(rotation), magnitude * jnp.sin(rotation)
    norm_in = jnp.sqrt(-jnp.expm1(-2.0 * decay))
    doublings = half.bit_length() - 1
    half_re, half_im = power(lam_re, lam_im, doublings)
    full_re, full_im = times(half_re, half_im, half_re, half_im)
    par = jnp.stack((lam_re, lam_im, half_re, half_im, full_re, full_im, norm_in, norm_in), axis=1)
    vec = jnp.stack((norm_gain, norm_shift, skip_gain, gate_bias) * 2, axis=1)
    place = me.astype(jnp.int32).reshape((1, 1))

    big = lambda w, dtype=F32: shaped((count, w), dtype)
    ends = shaped((SUB, 2 * states))
    kept = shaped((count + SUB, 2 * states))
    small = shaped((16, LANE))
    lines = pltpu.VMEM((width // LANE, count, LANE), F32)

    u0, st = call("enter", k_input, [big(width), shaped((24, LANE))], [tokens, lim], scratch=[lines])
    st = sums_of_all(st)
    d0, ml0, stat0, e = call(
        "drive0", functools.partial(k_drive_first, False),
        [big(2 * states), big(width, BF16), shaped((32, width)), ends],
        [st, u0, lim, vec[0], par[0], b_proj[0], keep_f, kp_f],
    )
    got = blocks_of_row(e)
    s0, al0, sig0, q0, slope0, u1, st = call(
        "finish0", k_finish_first,
        [kept, big(width, BF16), big(width), big(width), big(width), big(width), small],
        [place, got, d0, u0, stat0, lim, vec[0], par[0], keep_f, kp_f, kd_f, c_proj[0], w_gate[0]],
        scalars=1,
    )
    st = sums_of_all(st)
    counts = stat0[28:30, :LANE]
    d1, ml1, stat1, e = call(
        "drive1", functools.partial(k_drive, True),
        [big(2 * states), big(width, BF16), shaped((32, width)), ends],
        [st, counts, u1, lim, vec[1], par[1], b_proj[1], keep_r, kp_r],
    )
    got = blocks_of_row(e)
    grads = [shaped((width, width)), shaped((2 * states, width)), shaped((16, LANE)), ends]
    output, s1, cot32, mix1, sg1, gw1, gc1, sums1, e = call(
        "middle", k_middle,
        [shaped(tokens.shape, BF16), kept, big(width), big(width, BF16), big(2 * states)] + grads,
        [place, got, d1, u1, stat1, lim, vec[1], par[1], keep_r, kp_r, kd_r, keep_f, kp_f, c_proj[1], w_gate[1],
         cotangent],
        scratch=[lines], scalars=1,
    )
    got = blocks_of_row(e)
    wc1 = sum_large(jnp.concatenate((gw1, gc1), axis=0))
    adjoint = [big(width), shaped((width, 2 * states)), shaped((8, LANE)), small]
    z1, gb1, lg1, st = call(
        "adjoint1", functools.partial(k_adjoint, False), adjoint,
        [place, got, sg1, s1, mix1, ml1, u1, stat1, lim, vec[1], par[1], keep_f, kp_f, kd_f, keep_r, b_proj[1]],
        scratch=[pltpu.VMEM((count, 2 * states), F32)], scalars=1,
    )
    st = sums_of_all(st)
    b1 = sum_large(gb1)
    g0, mix0, sg0, gw0, gc0, sums0, e, bn1 = call(
        "lower", k_lower,
        [big(width), big(width, BF16), big(2 * states)] + grads + [shaped((8, width))],
        [st, z1, cot32, u1, stat1, vec[1], lim, s0, al0, sig0, q0, slope0, u0, stat0, vec[0], par[0],
         c_proj[0], w_gate[0], keep_r, kp_r],
    )
    got = blocks_of_row(e)
    wc0 = sum_large(jnp.concatenate((gw0, gc0), axis=0))
    z0, gb0, lg0, st = call(
        "adjoint0", functools.partial(k_adjoint, True), adjoint,
        [place, got, sg0, s0, mix0, ml0, u0, stat0, lim, vec[0], par[0], keep_r, kp_r, kd_r, keep_f, b_proj[0]],
        scratch=[pltpu.VMEM((count, 2 * states), F32)], scalars=1,
    )
    st = sums_of_all(jnp.concatenate((st, sums0, lg0, sums1, lg1), axis=0))
    b0 = sum_large(gb0)
    tokens_grad, bn0 = call(
        "leave", k_output, [shaped(tokens.shape), shaped((8, width))],
        [st, z0, g0, u0, stat0, vec[0], lim],
        scratch=[lines],
    )
    sums = jnp.sum(st[:, 16:], axis=0).reshape((2, 24, LANE))
    per = width // LANE
    per_state = states // LANE

    def taken(first, lines):
        return sums[:, first : first + lines].reshape((2, lines * LANE))

    grad_bias = taken(0, per)
    grad_skip = taken(per, per)
    product = taken(2 * per, per_state)
    lam_grad_re, lam_grad_im = taken(16, per_state), taken(16 + per_state, per_state)
    grad_rotation = lam_re * lam_grad_im - lam_im * lam_grad_re
    grad_rate = decay * (
        -(lam_re * lam_grad_re + lam_im * lam_grad_im)
        + product * jnp.exp(-2.0 * decay) / (norm_in * norm_in)
    )
    new_mean, new_var = run_mean, run_var
    for micro in range(2):
        center = jnp.stack((stat0[24 + micro], stat1[24 + micro]))
        spread = jnp.stack((stat0[26 + micro], stat1[26 + micro]))
        new_mean = (1.0 - momentum) * new_mean + momentum * center
        new_var = (1.0 - momentum) * new_var + momentum * spread
    return (
        output,
        tokens_grad,
        jnp.stack((bn0[1], bn1[1])),
        jnp.stack((bn0[0], bn1[0])),
        jnp.stack((b0, b1)),
        grad_rate,
        grad_rotation,
        jnp.stack((wc0[width:], wc1[width:])),
        grad_skip,
        jnp.stack((wc0[:width], wc1[:width])),
        grad_bias,
        new_mean,
        new_var,
    )


def solution(mesh):
    tokens_spec = P("batch", "tm", None)
    return jax.shard_map(
        local,
        mesh=mesh,
        in_specs=(tokens_spec, P("batch", None), P("batch"), tokens_spec) + (P(),) * 11,
        out_specs=(tokens_spec, tokens_spec) + (P(),) * 11,
        check_vma=False,
    )
```

time: 1370 us -> 347 us (0.25); the launches traced: 1340 us -> 345 us
  other arithmetic: 475 us -> 25.4 us
  local copies, waits for them, and re-layouts: 241 us -> 43.1 us
  blocking collectives: 173 us -> 0 us
  waiting for transfers between devices: 218 us -> 109 us
  Pallas kernels: 0 us -> 91 us
  starting transfers between devices: 147 us -> 75.2 us
  matrix products: 65.4 us -> 0 us
  between operations: 19.2 us -> 1.83 us
    dynamic_update_slice x384 -> x0, other arithmetic: 291 us -> none  [the longest x128 213 us: local_scan(): lax.scan(inner_step, (unit_ones, zero_part, zero_part, zero_part), member...]
    psum x4 -> x0, blocking collectives: 173 us -> none  [the longest x2 86.6 us: layer_backward(): lax.psum((jnp.sum(normed_grad, axis=(0, 1)), jnp.sum(normed_grad * normed...]
    ppermute x56 -> x44, starting transfers between devices: 147 us -> 42.4 us  [the longest x28 23.2 us: swap(): return lax.ppermute(block, BOTH, [(i, i ^ distance) for i in range(total)])]
    psum x1 -> x0, waiting for transfers between devices: 99.1 us -> none  [local(): lax.psum(tuple((jnp.stack((left, right)) for left, right in zip(lower_tot...]
    pallas_call x0 -> x9, Pallas kernels: none -> 91 us  [call(): pl.pallas_call(body, name=name, out_shape=outs, in_specs=specs, out_specs...]
    add x201 -> x26, other arithmetic: 97.2 us -> 10.8 us  [the longest x20 8.86 us: sum_large(): block = kept + exchange(given)]
    while x548 -> x0, local copies, waits for them, and re-layouts: 77.8 us -> none
    dot_general x36 -> x0, matrix products: 65.4 us -> none  [the longest x4 12.2 us: layer_backward(): jnp.einsum('rts,hs->rth', drive_grad, weights['b_proj'], preferred_elemen...]
  transfers between devices with their start and end apart: 57 -> 52, of which waited for: 57 -> 31; matrix products, arithmetic and copies ran while one was open for 2% -> 14% of each run, Pallas kernels for 0% -> 9%
where the time goes in v1:
time: 347 us; the launch traced here: 345 us
  waiting for transfers between devices  109 us (31%)
  Pallas kernels  91 us (26%)
  starting transfers between devices  75.2 us (22%)
  local copies, waits for them, and re-layouts  43.1 us (12%)
  other arithmetic  25.4 us (7%)
    pallas_call x9, Pallas kernels, call(): pl.pallas_call(body, name=name, out_shape=outs, in_specs=specs, out_specs...  91 us
    ppermute x28, waiting for transfers between devices, swap(): return lax.ppermute(block, BOTH, [(i, i ^ distance) for i in range(total)])  34.4 us
    ppermute x16, waiting for transfers between devices, swap_by_core(): lax.ppermute(block, BOTH, [(i, i ^ (odd if i & 1 else even)) for i in ran...  30.9 us
    all_to_all x4, waiting for transfers between devices, blocks_of_row(): lax.all_to_all(jnp.broadcast_to(block[None], (n,) + block.shape), 'tm', 0...  24.4 us
    ppermute x28, starting transfers between devices, swap(): return lax.ppermute(block, BOTH, [(i, i ^ distance) for i in range(total)])  23.2 us
    ppermute x16, starting transfers between devices, swap_by_core(): lax.ppermute(block, BOTH, [(i, i ^ (odd if i & 1 else even)) for i in ran...  19.1 us
    all_to_all x4, waiting for transfers between devices, sums_of_all(): return lax.all_to_all(spread, BOTH, 0, 0, axis_index_groups=groups)  19 us
    all_to_all x4, starting transfers between devices, sums_of_all(): return lax.all_to_all(spread, BOTH, 0, 0, axis_index_groups=groups)  18.6 us
  transfers between devices with their start and end apart: 52, of which 31 were waited for; matrix products, arithmetic and copies ran while one was open for 14% of the time, Pallas kernels for 9%

profile of v1, /device:TPU:0, one launch (start us, length us, event | category | flops | bytes accessed | tf_op | source)
XLA Modules:
  0.0 345.2 jit_solution(2489114755200555004)
XLA Ops:
  2.2 3.8 %enter.1 = (f32[1024,512]{1,0:T(8,128)}, f32[24,128]{1,0:T(8,128)}) custom-call(bf16[4,256,512]{2,1,0:T(8,128)(2,1)} %tokens_ref.1, s32[8,512]{1,0:T(8,128)} %broadcast_in_dim.45.lim_ref.refs_1_), custom_call_target="tpu_custom_call" | custom-call | tf_op jit(solution)/shard_map/enter/pallas_call | solution.py:26
  15.2 7.9 %all-to-all-start = ((f32[16,24,128]{2,1,0:T(8,128)}), f32[16,24,128]{2,1,0:T(8,128)S(1)}, u32[]{:S(2)}, u32[]{:S(2)}) async-start(f32[16,24,128]{2,1,0:T(8,128)} %broadcast_in_dim.46), calls=%async_computation | async-start | bytes 393216 | tf_op jit(solution)/shard_map/all_to_all | solution.py:553
  24.7 8.3 %all-to-all-done.st_ref = f32[16,24,128]{2,1,0:T(8,128)S(1)} async-done(((f32[16,24,128]{2,1,0:T(8,128)}), f32[16,24,128]{2,1,0:T(8,128)S(1)}, u32[]{:S(2)}, u32[]{:S(2)}) %all-to-all-start) | async-done | bytes 196640 | tf_op jit(solution)/shard_map/all_to_all | solution.py:553
  34.6 6.5 %drive0.1 = (f32[1024,768]{1,0:T(8,128)}, bf16[1024,512]{1,0:T(8,128)(2,1)}, f32[32,512]{1,0:T(8,128)}, f32[8,768]{1,0:T(8,128)}) custom-call(f32[16,24,128]{2,1,0:T(8,128)} %copy-done.14, f32[1024,512]{1,0:T(8,128)} %get-tuple-element.58.refs_0_.u_ref, s32[8,512]{1,0:T(8,128)} %broadcast_in_dim.45.lim_ref.refs_1_, ...), custom_call_target="tpu_custom_call" | custom-call | tf_op jit(solution)/shard_map/drive0/pallas_call | solution.py:26
  41.1 1.4 broadcast_in_dim.50
  42.6 3.4 all-to-all-start.1
  47.3 6.9 %all-to-all-done.1.got_ref = f32[8,8,768]{2,1,0:T(8,128)S(1)} async-done(((f32[8,8,768]{2,1,0:T(8,128)}), f32[8,8,768]{2,1,0:T(8,128)S(1)}, u32[]{:S(2)}, u32[]{:S(2)}) %all-to-all-start.1) | async-done | bytes 196640 | tf_op jit(solution)/shard_map/all_to_all | solution.py:558
  54.9 12.2 %finish0.1 = (f32[1032,768]{1,0:T(8,128)}, bf16[1024,512]{1,0:T(8,128)(2,1)}, f32[1024,512]{1,0:T(8,128)}, f32[1024,512]{1,0:T(8,128)}, f32[1024,512]{1,0:T(8,12...) custom-call(s32[1,1]{1,0:T(1,128)} %bitcast.me_ref, f32[8,8,768]{2,1,0:T(8,128)} %copy-done.17, ...), custom_call_target="tpu_custom_call" | custom-call | tf_op jit(solution)/shard_map/finish0/pallas_call | solution.py:26
  67.1 1.4 collective-permute-done.1
  69.9 3.5 %all-to-all-start.2 = ((f32[16,16,128]{2,1,0:T(8,128)}), f32[16,16,128]{2,1,0:T(8,128)S(1)}, u32[]{:S(2)}, u32[]{:S(2)}) async-start(f32[16,16,128]{2,1,0:T(8,128)} %broadcast_in_dim.54), calls=%async_computation.2 | async-start | bytes 262144 | tf_op jit(solution)/shard_map/all_to_all | solution.py:553
  76.0 5.7 %all-to-all-done.2.st_ref = f32[16,16,128]{2,1,0:T(8,128)S(1)} async-done(((f32[16,16,128]{2,1,0:T(8,128)}), f32[16,16,128]{2,1,0:T(8,128)S(1)}, u32[]{:S(2)}, u32[]{:S(2)}) %all-to-all-start.2) | async-done | bytes 131104 | tf_op jit(solution)/shard_map/all_to_all | solution.py:553
  83.3 6.4 %drive1.1 = (f32[1024,768]{1,0:T(8,128)}, bf16[1024,512]{1,0:T(8,128)(2,1)}, f32[32,512]{1,0:T(8,128)}, f32[8,768]{1,0:T(8,128)}) custom-call(f32[16,16,128]{2,1,0:T(8,128)} %copy-done.19, f32[2,128]{1,0:T(2,128)} %slice.130.cnt_ref, f32[1024,512]{1,0:T(8,128)} %get-tuple-element.63.u_ref.u1_ref, s32[8,512]{1,0:T(8,128)} %broadcast_in_dim.45.lim_ref.refs_1_, ...), custom_call_target="tpu_custom_call" | custom-call | tf_op jit(solution)/shard_map/drive1/pallas_call | solution.py:26
  89.7 1.4 broadcast_in_dim.58
  91.2 3.4 all-to-all-start.3
  96.1 6.8 %all-to-all-done.3.got_ref = f32[8,8,768]{2,1,0:T(8,128)S(1)} async-done(((f32[8,8,768]{2,1,0:T(8,128)}), f32[8,8,768]{2,1,0:T(8,128)S(1)}, u32[]{:S(2)}, u32[]{:S(2)}) %all-to-all-start.3) | async-done | bytes 196640 | tf_op jit(solution)/shard_map/all_to_all | solution.py:558
  103.5 19.0 %middle.1 = (bf16[4,256,512]{2,1,0:T(8,128)(2,1)}, f32[1032,768]{1,0:T(8,128)}, f32[1024,512]{1,0:T(8,128)}, bf16[1024,512]{1,0:T(8,128)(2,1)}, f32[1024,768]{1,...) custom-call(s32[1,1]{1,0:T(1,128)} %bitcast.me_ref, ...), custom_call_target="tpu_custom_call" | custom-call | tf_op jit(solution)/shard_map/middle/pallas_call | solution.py:26
  122.5 1.4 broadcast_in_dim.62
  124.0 3.4 all-to-all-start.4
  129.3 6.3 %all-to-all-done.4.got_ref = f32[8,8,768]{2,1,0:T(8,128)S(1)} async-done(((f32[8,8,768]{2,1,0:T(8,128)}), f32[8,8,768]{2,1,0:T(8,128)S(1)}, u32[]{:S(2)}, u32[]{:S(2)}) %all-to-all-start.4) | async-done | bytes 196640 | tf_op jit(solution)/shard_map/all_to_all | solution.py:558
  136.3 10.5 %adjoint1.1 = (f32[1024,512]{1,0:T(8,128)}, f32[512,768]{1,0:T(8,128)}, f32[8,128]{1,0:T(8,128)}, f32[16,128]{1,0:T(8,128)}) custom-call(s32[1,1]{1,0:T(1,128)} %bitcast.me_ref, f32[8,8,768]{2,1,0:T(8,128)} %copy-done.16, f32[1024,768]{1,0:T(8,128)} %get-tuple-element.69.sg_ref, f32[1032,768]{1,0:T(8,128)} %get-tuple-element.70.s_ref, ...), custom_call_target="tpu_custom_call" | custom-call | tf_op jit(solution)/shard_map/adjoint1/pallas_call | solution.py:26
  148.9 3.7 %all-to-all-start.5 = ((f32[16,16,128]{2,1,0:T(8,128)}), f32[16,16,128]{2,1,0:T(8,128)S(1)}, u32[]{:S(2)}, u32[]{:S(2)}) async-start(f32[16,16,128]{2,1,0:T(8,128)} %broadcast_in_dim.63), calls=%async_computation.5 | async-start | bytes 262144 | tf_op jit(solution)/shard_map/all_to_all | solution.py:553
  155.6 5.1 %all-to-all-done.5.st_ref = f32[16,16,128]{2,1,0:T(8,128)S(1)} async-done(((f32[16,16,128]{2,1,0:T(8,128)}), f32[16,16,128]{2,1,0:T(8,128)S(1)}, u32[]{:S(2)}, u32[]{:S(2)}) %all-to-all-start.5) | async-done | bytes 131104 | tf_op jit(solution)/shard_map/all_to_all | solution.py:553
  161.3 16.3 %lower.1 = (f32[1024,512]{1,0:T(8,128)}, bf16[1024,512]{1,0:T(8,128)(2,1)}, f32[1024,768]{1,0:T(8,128)}, f32[512,512]{1,0:T(8,128)}, f32[768,512]{1,0:T(8,128)},...) custom-call(f32[16,16,128]{2,1,0:T(8,128)} %copy-done.18, f32[1024,512]{1,0:T(8,128)} %get-tuple-element.74.z_ref, ...), custom_call_target="tpu_custom_call" | custom-call | tf_op jit(solution)/shard_map/lower/pallas_call | solution.py:26
  179.7 4.0 %all-to-all-start.6 = ((f32[8,8,768]{2,1,0:T(8,128)}), f32[8,8,768]{2,1,0:T(8,128)}, u32[]{:S(2)}, u32[]{:S(2)}) async-start(f32[8,8,768]{2,1,0:T(8,128)} %broadcast_in_dim.64), calls=%async_computation.6 | async-start | bytes 393216 | tf_op jit(solution)/shard_map/all_to_all | solution.py:558
  183.7 1.5 constant_dynamic-update-slice_fusion.5
  187.7 4.3 %all-to-all-done.6.got_ref = f32[8,8,768]{2,1,0:T(8,128)} async-done(((f32[8,8,768]{2,1,0:T(8,128)}), f32[8,8,768]{2,1,0:T(8,128)}, u32[]{:S(2)}, u32[]{:S(2)}) %all-to-all-start.6) | async-done | bytes 196640 | tf_op jit(solution)/shard_map/all_to_all | solution.py:558
  192.1 10.6 %adjoint0.1 = (f32[1024,512]{1,0:T(8,128)}, f32[512,768]{1,0:T(8,128)}, f32[8,128]{1,0:T(8,128)}, f32[16,128]{1,0:T(8,128)}) custom-call(s32[1,1]{1,0:T(1,128)} %bitcast.me_ref, f32[8,8,768]{2,1,0:T(8,128)} %all-to-all-done.6.got_ref, f32[1024,768]{1,0:T(8,128)} %get-tuple-element.82.sg_ref, f32[1032,768]{1,0:T(8,128)} %get-tuple-element.76.s_ref, ...), custom_call_target="tpu_custom_call" | custom-call | tf_op jit(solution)/shard_map/adjoint0/pallas_call | solution.py:26
  206.6 3.6 %all-to-all-start.7 = ((f32[16,64,128]{2,1,0:T(8,128)}), f32[16,64,128]{2,1,0:T(8,128)S(1)}, u32[]{:S(2)}, u32[]{:S(2)}) async-start(f32[16,64,128]{2,1,0:T(8,128)} %broadcast_in_dim.65), calls=%async_computation.7 | async-start | bytes 1048576 | tf_op jit(solution)/shard_map/all_to_all | solution.py:553
  212.2 2.0 dynamic-slice_add_fusion
  215.1 1.5 collective-permute-start.35
  216.6 5.2 %collective-permute-done.16 = f32[64,768]{1,0:T(8,128)S(1)} collective-permute-done((f32[64,768]{1,0:T(8,128)S(1)}, f32[64,768]{1,0:T(8,128)S(1)}, u32[]{:S(2)}, u32[]{:S(2)}) %collective-permute-start.16) | collective-permute-done | bytes 196640 | tf_op jit(solution)/shard_map/ppermute | solution.py:545
  222.0 1.4 dynamic-slice_add_fusion.3
  223.4 3.2 collective-permute-done.17
  226.6 3.2 collective-permute-start.18
  231.8 3.0 collective-permute-start.19
  234.8 1.6 dynamic-slice_add_fusion.1
  238.3 2.5 collective-permute-start.20
  241.6 5.7 %leave.1 = (f32[4,256,512]{2,1,0:T(8,128)}, f32[8,512]{1,0:T(8,128)}) custom-call(f32[16,64,128]{2,1,0:T(8,128)} %copy-done.3, f32[1024,512]{1,0:T(8,128)} %get-tuple-element.90.z_ref, f32[1024,512]{1,0:T(8,128)} %get-tuple-element.91.grad_ref, f32[1024,512]{1,0:T(8,128)} %get-tuple-element.58.refs_0_.u_ref, f32[32,512]{1,0:T(8,128)} %get-tuple-element.61.stat_ref, ...), custom_call_target="tpu_custom_call" | custom-call | tf_op jit(solution)/shard_map/leave/pallas_call | solution.py:26
  253.6 2.1 collective-permute-start.21
  256.8 5.9 %collective-permute-done.21 = f32[64,768]{1,0:T(8,128)S(1)} collective-permute-done((f32[64,768]{1,0:T(8,128)S(1)}, f32[64,768]{1,0:T(8,128)S(1)}, u32[]{:S(2)}, u32[]{:S(2)}) %collective-permute-start.21) | collective-permute-done | bytes 196640 | tf_op jit(solution)/shard_map/ppermute | solution.py:545
  263.5 2.8 collective-permute-done.6
  266.5 2.1 collective-permute-start.37
  268.5 3.0 collective-permute-done.7
  273.4 3.9 %collective-permute-done.8 = f32[16,768]{1,0:T(8,128)S(1)} collective-permute-done((f32[16,768]{1,0:T(8,128)S(1)}, f32[16,768]{1,0:T(8,128)S(1)}, u32[]{:S(2)}, u32[]{:S(2)}) %collective-permute-start.8) | collective-permute-done | bytes 49184 | tf_op jit(solution)/shard_map/ppermute | solution.py:540
  278.3 2.0 collective-permute-start.38
  280.3 3.5 %collective-permute-done.9 = f32[16,768]{1,0:T(8,128)S(1)} collective-permute-done((f32[16,768]{1,0:T(8,128)S(1)}, f32[16,768]{1,0:T(8,128)S(1)}, u32[]{:S(2)}, u32[]{:S(2)}) %collective-permute-start.9) | collective-permute-done | bytes 49184 | tf_op jit(solution)/shard_map/ppermute | solution.py:540
  283.9 1.7 collective-permute-done.38
  289.4 2.3 collective-permute-done.39
  291.8 2.3 collective-permute-done.26
  294.8 2.7 collective-permute-done.40
  298.0 1.6 collective-permute-done.27
  299.6 3.0 collective-permute-start.28
  302.6 3.4 collective-permute-done.28
  306.0 3.0 collective-permute-start.29
  310.3 1.9 collective-permute-done.29
  312.5 3.3 collective-permute-start.42
  315.8 1.9 collective-permute-done.30
  317.7 1.5 collective-permute-start.31
  319.4 5.5 %collective-permute-done.31 = f32[160,512]{1,0:T(8,128)S(1)} collective-permute-done((f32[160,512]{1,0:T(8,128)S(1)}, f32[160,512]{1,0:T(8,128)S(1)}, u32[]{:S(2)}, u32[]{:S(2)}) %collective-permute-start.31) | collective-permute-done | bytes 327712 | tf_op jit(solution)/shard_map/ppermute | solution.py:545
  325.0 4.2 %collective-permute-start.32 = (f32[320,512]{1,0:T(8,128)S(1)}, f32[320,512]{1,0:T(8,128)S(1)}, u32[]{:S(2)}, u32[]{:S(2)}) collective-permute-start(f32[320,512]{1,0:T(8,128)S(1)} %pad_maximum_fusion.9), channel_id=1, source_target_pairs={{0,8},{1,17},{2,10},{3,19},{4,12},{5,21},{6,14},{7,23},{8,0},{9,25... | collective-permute-start | bytes 1966088 | tf_op jit(solution)/shard_map/ppermute | solution.py:545
  329.7 8.0 %collective-permute-done.32 = f32[320,512]{1,0:T(8,128)S(1)} collective-permute-done((f32[320,512]{1,0:T(8,128)S(1)}, f32[320,512]{1,0:T(8,128)S(1)}, u32[]{:S(2)}, u32[]{:S(2)}) %collective-permute-start.32) | collective-permute-done | bytes 655392 | tf_op jit(solution)/shard_map/ppermute | solution.py:545
  338.3 1.9 pad_maximum_fusion
  341.7 1.5 pad_maximum_fusion.2
  343.2 2.0 pad_maximum_fusion.1
  (286 shorter events, 68.7 us)
Async XLA Ops:
  0.6 12.4 %copy-start.13 = (bf16[2,512,512]{2,1,0:T(8,128)(2,1)S(1)}, bf16[2,512,512]{2,1,0:T(8,128)(2,1)}, u32[]{:S(2)}) copy-start(bf16[2,512,512]{2,1,0:T(8,128)(2,1)} %param.26) | copy-start | bytes 3145732
  6.0 8.5 %collective-permute-start = (f32[24,128]{1,0:T(8,128)}, f32[24,128]{1,0:T(8,128)S(1)}, u32[]{:S(2)}, u32[]{:S(2)}) collective-permute-start(f32[24,128]{1,0:T(8,128)} %get-tuple-element.57), channel_id=1, source_target_pairs={{0,1},{1,0},{2,3},{3,2},{4,5},{5,4},{6,7},{7,6},{8,9},{9,8},{10,11... | collective-permute-start | bytes 36872 | tf_op jit(solution)/shard_map/ppermute | solution.py:540
  9.0 14.1 %copy-start.21 = (s32[4,16]{1,0:T(4,128)S(1)}, s32[4,16]{1,0:T(4,128)}, u32[]{:S(2)}) copy-start(s32[4,16]{1,0:T(4,128)} %param.16) | copy-start | bytes 772
  9.0 14.4 %copy-start.6 = (bf16[2,512,768]{2,1,0:T(8,128)(2,1)S(1)}, bf16[2,512,768]{2,1,0:T(8,128)(2,1)}, u32[]{:S(2)}) copy-start(bf16[2,512,768]{2,1,0:T(8,128)(2,1)} %param.21) | copy-start | bytes 4718596
  15.2 17.7 %all-to-all-start = ((f32[16,24,128]{2,1,0:T(8,128)}), f32[16,24,128]{2,1,0:T(8,128)S(1)}, u32[]{:S(2)}, u32[]{:S(2)}) async-start(f32[16,24,128]{2,1,0:T(8,128)} %broadcast_in_dim.46), calls=%async_computation | async-start | bytes 393216 | tf_op jit(solution)/shard_map/all_to_all | solution.py:553
  34.6 11.4 %copy-start.7 = (bf16[2,768,512]{2,1,0:T(8,128)(2,1)S(1)}, bf16[2,768,512]{2,1,0:T(8,128)(2,1)}, u32[]{:S(2)}) copy-start(bf16[2,768,512]{2,1,0:T(8,128)(2,1)} %param.24) | copy-start | bytes 4718596
  42.6 11.7 %all-to-all-start.1 = ((f32[8,8,768]{2,1,0:T(8,128)}), f32[8,8,768]{2,1,0:T(8,128)S(1)}, u32[]{:S(2)}, u32[]{:S(2)}) async-start(f32[8,8,768]{2,1,0:T(8,128)} %broadcast_in_dim.50), calls=%async_computation.1 | async-start | bytes 393216 | tf_op jit(solution)/shard_map/all_to_all | solution.py:558
  67.1 1.4 collective-permute-start.1
  69.9 11.8 %all-to-all-start.2 = ((f32[16,16,128]{2,1,0:T(8,128)}), f32[16,16,128]{2,1,0:T(8,128)S(1)}, u32[]{:S(2)}, u32[]{:S(2)}) async-start(f32[16,16,128]{2,1,0:T(8,128)} %broadcast_in_dim.54), calls=%async_computation.2 | async-start | bytes 262144 | tf_op jit(solution)/shard_map/all_to_all | solution.py:553
  83.3 12.1 %copy-start.29 = (f32[2,512]{1,0:T(2,128)S(1)}, f32[2,512]{1,0:T(2,128)}, u32[]{:S(2)}) copy-start(f32[2,512]{1,0:T(2,128)} %param.28) | copy-start | bytes 12292
  91.2 11.7 %all-to-all-start.3 = ((f32[8,8,768]{2,1,0:T(8,128)}), f32[8,8,768]{2,1,0:T(8,128)S(1)}, u32[]{:S(2)}, u32[]{:S(2)}) async-start(f32[8,8,768]{2,1,0:T(8,128)} %broadcast_in_dim.58), calls=%async_computation.3 | async-start | bytes 393216 | tf_op jit(solution)/shard_map/all_to_all | solution.py:558
  103.5 23.8 %copy-start.30 = (f32[2,512]{1,0:T(2,128)S(1)}, f32[2,512]{1,0:T(2,128)}, u32[]{:S(2)}) copy-start(f32[2,512]{1,0:T(2,128)} %param.29) | copy-start | bytes 12292
  124.0 11.7 %all-to-all-start.4 = ((f32[8,8,768]{2,1,0:T(8,128)}), f32[8,8,768]{2,1,0:T(8,128)S(1)}, u32[]{:S(2)}, u32[]{:S(2)}) async-start(f32[8,8,768]{2,1,0:T(8,128)} %broadcast_in_dim.62), calls=%async_computation.4 | async-start | bytes 393216 | tf_op jit(solution)/shard_map/all_to_all | solution.py:558
  136.3 10.6 %copy-start.12 = (f32[768,512]{1,0:T(8,128)S(1)}, f32[768,512]{1,0:T(8,128)}, u32[]{:S(2)}) copy-start(f32[768,512]{1,0:T(8,128)} %get-tuple-element.100) | copy-start | bytes 4718596
  146.8 1.4 collective-permute-start.2
  148.9 11.8 %all-to-all-start.5 = ((f32[16,16,128]{2,1,0:T(8,128)}), f32[16,16,128]{2,1,0:T(8,128)S(1)}, u32[]{:S(2)}, u32[]{:S(2)}) async-start(f32[16,16,128]{2,1,0:T(8,128)} %broadcast_in_dim.63), calls=%async_computation.5 | async-start | bytes 262144 | tf_op jit(solution)/shard_map/all_to_all | solution.py:553
  153.8 58.4 %collective-permute-start.34 = (f32[640,512]{1,0:T(8,128)}, f32[640,512]{1,0:T(8,128)}, u32[]{:S(2)}, u32[]{:S(2)}) collective-permute-start(f32[640,512]{1,0:T(8,128)} %constant_dynamic-slice_fusion.4), channel_id=1, source_target_pairs={{0,1},{1,0},{2,3},{3,2},{4,5},{5,4},{6,7},{7,6},{8,9},{9,8},{10,11... | collective-permute-start | bytes 3932168 | tf_op jit(solution)/shard_map/ppermute | solution.py:540
  155.4 48.0 %collective-permute-start.14 = (f32[256,768]{1,0:T(8,128)}, f32[256,768]{1,0:T(8,128)S(1)}, u32[]{:S(2)}, u32[]{:S(2)}) collective-permute-start(f32[256,768]{1,0:T(8,128)} %constant_dynamic-slice_fusion.14), channel_id=1, source_target_pairs={{0,1},{1,0},{2,3},{3,2},{4,5},{5,4},{6,7},{7,6},{8,9},{9,8},{10,11... | collective-permute-start | bytes 2359304 | tf_op jit(solution)/shard_map/ppermute | solution.py:540
  179.7 12.4 %all-to-all-start.6 = ((f32[8,8,768]{2,1,0:T(8,128)}), f32[8,8,768]{2,1,0:T(8,128)}, u32[]{:S(2)}, u32[]{:S(2)}) async-start(f32[8,8,768]{2,1,0:T(8,128)} %broadcast_in_dim.64), calls=%async_computation.6 | async-start | bytes 393216 | tf_op jit(solution)/shard_map/all_to_all | solution.py:558
  185.3 17.4 %copy-start.1 = (f32[1280,512]{1,0:T(8,128)}, f32[1280,512]{1,0:T(8,128)S(1)}, u32[]{:S(2)}) copy-start(f32[1280,512]{1,0:T(8,128)S(1)} %constant_dynamic-update-slice_fusion.5) | copy-start | bytes 7864324
  186.6 48.3 %collective-permute-start.24 = (f32[640,512]{1,0:T(8,128)}, f32[640,512]{1,0:T(8,128)}, u32[]{:S(2)}, u32[]{:S(2)}) collective-permute-start(f32[640,512]{1,0:T(8,128)} %constant_dynamic-slice_fusion.9), channel_id=1, source_target_pairs={{0,1},{1,0},{2,3},{3,2},{4,5},{5,4},{6,7},{7,6},{8,9},{9,8},{10,11... | collective-permute-start | bytes 3932168 | tf_op jit(solution)/shard_map/ppermute | solution.py:540
  192.1 11.3 %copy-start.26 = (f32[16,128]{1,0:T(8,128)S(1)}, f32[16,128]{1,0:T(8,128)}, u32[]{:S(2)}) copy-start(f32[16,128]{1,0:T(8,128)} %get-tuple-element.86) | copy-start | bytes 24580
  192.1 11.3 %copy-start.9 = (f32[512,768]{1,0:T(8,128)S(1)}, f32[512,768]{1,0:T(8,128)}, u32[]{:S(2)}) copy-start(f32[512,768]{1,0:T(8,128)} %get-tuple-element.96) | copy-start | bytes 4718596
  203.6 7.8 %collective-permute-start.15 = (f32[128,768]{1,0:T(8,128)S(1)}, f32[128,768]{1,0:T(8,128)S(1)}, u32[]{:S(2)}, u32[]{:S(2)}) collective-permute-start(f32[128,768]{1,0:T(8,128)S(1)} %constant_dynamic-slice_fusion.13), channel_id=1, source_target_pairs={{0,8},{1,17},{2,10},{3,19},{4,12},{5,21},{6,14},{7,23},{8,0},{9,25... | collective-permute-start | bytes 1179656 | tf_op jit(solution)/shard_map/ppermute | solution.py:545
  204.1 1.6 collective-permute-start.3
  205.8 16.2 %collective-permute-start.4 = (f32[256,768]{1,0:T(8,128)}, f32[256,768]{1,0:T(8,128)}, u32[]{:S(2)}, u32[]{:S(2)}) collective-permute-start(f32[256,768]{1,0:T(8,128)} %constant_dynamic-slice_fusion.19), channel_id=1, source_target_pairs={{0,1},{1,0},{2,3},{3,2},{4,5},{5,4},{6,7},{7,6},{8,9},{9,8},{10,11... | collective-permute-start | bytes 2359304 | tf_op jit(solution)/shard_map/ppermute | solution.py:540
  206.6 34.2 %all-to-all-start.7 = ((f32[16,64,128]{2,1,0:T(8,128)}), f32[16,64,128]{2,1,0:T(8,128)S(1)}, u32[]{:S(2)}, u32[]{:S(2)}) async-start(f32[16,64,128]{2,1,0:T(8,128)} %broadcast_in_dim.65), calls=%async_computation.7 | async-start | bytes 1048576 | tf_op jit(solution)/shard_map/all_to_all | solution.py:553
  211.5 10.3 %collective-permute-start.16 = (f32[64,768]{1,0:T(8,128)S(1)}, f32[64,768]{1,0:T(8,128)S(1)}, u32[]{:S(2)}, u32[]{:S(2)}) collective-permute-start(f32[64,768]{1,0:T(8,128)S(1)} %constant_dynamic-slice_fusion.12), channel_id=1, source_target_pairs={{0,16},{1,9},{2,18},{3,11},{4,20},{5,13},{6,22},{7,15},{8,24},{9,1... | collective-permute-start | bytes 589832 | tf_op jit(solution)/shard_map/ppermute | solution.py:545
  215.1 37.1 %collective-permute-start.35 = (f32[320,512]{1,0:T(8,128)}, f32[320,512]{1,0:T(8,128)}, u32[]{:S(2)}, u32[]{:S(2)}) collective-permute-start(f32[320,512]{1,0:T(8,128)} %constant_dynamic-slice_fusion.3), channel_id=1, source_target_pairs={{0,8},{1,17},{2,10},{3,19},{4,12},{5,21},{6,14},{7,23},{8,0},{9,25... | collective-permute-start | bytes 1966088 | tf_op jit(solution)/shard_map/ppermute | solution.py:545
  221.9 13.0 %copy-start.2 = (f32[1280,512]{1,0:T(8,128)S(1)}, f32[1280,512]{1,0:T(8,128)}, u32[]{:S(2)}) copy-start(f32[1280,512]{1,0:T(8,128)} %copy-done.1) | copy-start | bytes 7864324
  221.9 4.7 %collective-permute-start.17 = (f32[32,768]{1,0:T(8,128)S(1)}, f32[32,768]{1,0:T(8,128)S(1)}, u32[]{:S(2)}, u32[]{:S(2)}) collective-permute-start(f32[32,768]{1,0:T(8,128)S(1)} %constant_dynamic-slice_fusion.11), channel_id=1, source_target_pairs={{0,2},{1,3},{2,0},{3,1},{4,6},{5,7},{6,4},{7,5},{8,10},{9,11},{10,... | collective-permute-start | bytes 294920 | tf_op jit(solution)/shard_map/ppermute | solution.py:540
  223.3 11.5 %copy-start.4 = (f32[256,768]{1,0:T(8,128)}, f32[256,768]{1,0:T(8,128)S(1)}, u32[]{:S(2)}) copy-start(f32[256,768]{1,0:T(8,128)S(1)} %dynamic-slice_add_fusion.3) | copy-start | bytes 2359300
  226.6 5.2 %collective-permute-start.18 = (f32[16,768]{1,0:T(8,128)S(1)}, f32[16,768]{1,0:T(8,128)S(1)}, u32[]{:S(2)}, u32[]{:S(2)}) collective-permute-start(f32[16,768]{1,0:T(8,128)S(1)} %constant_dynamic-slice_fusion.10), channel_id=1, source_target_pairs={{0,4},{1,5},{2,6},{3,7},{4,0},{5,1},{6,2},{7,3},{8,12},{9,13},{10,... | collective-permute-start | bytes 147464 | tf_op jit(solution)/shard_map/ppermute | solution.py:540
  230.5 25.1 %collective-permute-start.5 = (f32[128,768]{1,0:T(8,128)}, f32[128,768]{1,0:T(8,128)}, u32[]{:S(2)}, u32[]{:S(2)}) collective-permute-start(f32[128,768]{1,0:T(8,128)} %constant_dynamic-slice_fusion.18), channel_id=1, source_target_pairs={{0,8},{1,17},{2,10},{3,19},{4,12},{5,21},{6,14},{7,23},{8,0},{9,25... | collective-permute-start | bytes 1179656 | tf_op jit(solution)/shard_map/ppermute | solution.py:545
  231.8 6.4 %collective-permute-start.19 = (f32[16,768]{1,0:T(8,128)S(1)}, f32[16,768]{1,0:T(8,128)S(1)}, u32[]{:S(2)}, u32[]{:S(2)}) collective-permute-start(f32[16,768]{1,0:T(8,128)S(1)} %dynamic-slice_add_fusion.18), channel_id=1, source_target_pairs={{0,4},{1,5},{2,6},{3,7},{4,0},{5,1},{6,2},{7,3},{8,12},{9,13},{10,... | collective-permute-start | bytes 147464 | tf_op jit(solution)/shard_map/ppermute | solution.py:540
  237.3 48.4 %collective-permute-start.25 = (f32[320,512]{1,0:T(8,128)}, f32[320,512]{1,0:T(8,128)}, u32[]{:S(2)}, u32[]{:S(2)}) collective-permute-start(f32[320,512]{1,0:T(8,128)} %constant_dynamic-slice_fusion.8), channel_id=1, source_target_pairs={{0,8},{1,17},{2,10},{3,19},{4,12},{5,21},{6,14},{7,23},{8,0},{9,25... | collective-permute-start | bytes 1966088 | tf_op jit(solution)/shard_map/ppermute | solution.py:545
  238.3 15.2 %collective-permute-start.20 = (f32[32,768]{1,0:T(8,128)S(1)}, f32[32,768]{1,0:T(8,128)S(1)}, u32[]{:S(2)}, u32[]{:S(2)}) collective-permute-start(f32[32,768]{1,0:T(8,128)S(1)} %pad_maximum_fusion.20), channel_id=1, source_target_pairs={{0,2},{1,3},{2,0},{3,1},{4,6},{5,7},{6,4},{7,5},{8,10},{9,11},{10,... | collective-permute-start | bytes 294920 | tf_op jit(solution)/shard_map/ppermute | solution.py:540
  253.5 10.0 %collective-permute-start.36 = (f32[160,512]{1,0:T(8,128)S(1)}, f32[160,512]{1,0:T(8,128)S(1)}, u32[]{:S(2)}, u32[]{:S(2)}) collective-permute-start(f32[160,512]{1,0:T(8,128)S(1)} %constant_dynamic-slice_fusion.2), channel_id=1, source_target_pairs={{0,16},{1,9},{2,18},{3,11},{4,20},{5,13},{6,22},{7,15},{8,24},{9,1... | collective-permute-start | bytes 983048 | tf_op jit(solution)/shard_map/ppermute | solution.py:545
  253.6 9.1 %collective-permute-start.21 = (f32[64,768]{1,0:T(8,128)S(1)}, f32[64,768]{1,0:T(8,128)S(1)}, u32[]{:S(2)}, u32[]{:S(2)}) collective-permute-start(f32[64,768]{1,0:T(8,128)S(1)} %pad_maximum_fusion.16), channel_id=1, source_target_pairs={{0,16},{1,9},{2,18},{3,11},{4,20},{5,13},{6,22},{7,15},{8,24},{9,1... | collective-permute-start | bytes 589832 | tf_op jit(solution)/shard_map/ppermute | solution.py:545
  256.7 9.6 %collective-permute-start.6 = (f32[64,768]{1,0:T(8,128)S(1)}, f32[64,768]{1,0:T(8,128)S(1)}, u32[]{:S(2)}, u32[]{:S(2)}) collective-permute-start(f32[64,768]{1,0:T(8,128)S(1)} %constant_dynamic-slice_fusion.17), channel_id=1, source_target_pairs={{0,16},{1,9},{2,18},{3,11},{4,20},{5,13},{6,22},{7,15},{8,24},{9,1... | collective-permute-start | bytes 589832 | tf_op jit(solution)/shard_map/ppermute | solution.py:545
  262.8 24.6 %collective-permute-start.22 = (f32[128,768]{1,0:T(8,128)S(1)}, f32[128,768]{1,0:T(8,128)S(1)}, u32[]{:S(2)}, u32[]{:S(2)}) collective-permute-start(f32[128,768]{1,0:T(8,128)S(1)} %pad_maximum_fusion.12), channel_id=1, source_target_pairs={{0,8},{1,17},{2,10},{3,19},{4,12},{5,21},{6,14},{7,23},{8,0},{9,25... | collective-permute-start | bytes 1179656 | tf_op jit(solution)/shard_map/ppermute | solution.py:545
  266.4 5.2 %collective-permute-start.7 = (f32[32,768]{1,0:T(8,128)S(1)}, f32[32,768]{1,0:T(8,128)S(1)}, u32[]{:S(2)}, u32[]{:S(2)}) collective-permute-start(f32[32,768]{1,0:T(8,128)S(1)} %constant_dynamic-slice_fusion.16), channel_id=1, source_target_pairs={{0,2},{1,3},{2,0},{3,1},{4,6},{5,7},{6,4},{7,5},{8,10},{9,11},{10,... | collective-permute-start | bytes 294920 | tf_op jit(solution)/shard_map/ppermute | solution.py:540
  266.5 6.9 %collective-permute-start.37 = (f32[80,512]{1,0:T(8,128)S(1)}, f32[80,512]{1,0:T(8,128)S(1)}, u32[]{:S(2)}, u32[]{:S(2)}) collective-permute-start(f32[80,512]{1,0:T(8,128)S(1)} %constant_dynamic-slice_fusion.1), channel_id=1, source_target_pairs={{0,2},{1,3},{2,0},{3,1},{4,6},{5,7},{6,4},{7,5},{8,10},{9,11},{10,... | collective-permute-start | bytes 491528 | tf_op jit(solution)/shard_map/ppermute | solution.py:540
  271.6 5.6 %collective-permute-start.8 = (f32[16,768]{1,0:T(8,128)S(1)}, f32[16,768]{1,0:T(8,128)S(1)}, u32[]{:S(2)}, u32[]{:S(2)}) collective-permute-start(f32[16,768]{1,0:T(8,128)S(1)} %constant_dynamic-slice_fusion.15), channel_id=1, source_target_pairs={{0,4},{1,5},{2,6},{3,7},{4,0},{5,1},{6,2},{7,3},{8,12},{9,13},{10,... | collective-permute-start | bytes 147464 | tf_op jit(solution)/shard_map/ppermute | solution.py:540
  277.3 6.5 %collective-permute-start.9 = (f32[16,768]{1,0:T(8,128)S(1)}, f32[16,768]{1,0:T(8,128)S(1)}, u32[]{:S(2)}, u32[]{:S(2)}) collective-permute-start(f32[16,768]{1,0:T(8,128)S(1)} %dynamic-slice_add_fusion.19), channel_id=1, source_target_pairs={{0,4},{1,5},{2,6},{3,7},{4,0},{5,1},{6,2},{7,3},{8,12},{9,13},{10,... | collective-permute-start | bytes 147464 | tf_op jit(solution)/shard_map/ppermute | solution.py:540
  278.3 7.3 %collective-permute-start.38 = (f32[40,512]{1,0:T(8,128)S(1)}, f32[40,512]{1,0:T(8,128)S(1)}, u32[]{:S(2)}, u32[]{:S(2)}) collective-permute-start(f32[40,512]{1,0:T(8,128)S(1)} %constant_dynamic-slice_fusion), channel_id=1, source_target_pairs={{0,4},{1,5},{2,6},{3,7},{4,0},{5,1},{6,2},{7,3},{8,12},{9,13},{10,... | collective-permute-start | bytes 245768 | tf_op jit(solution)/shard_map/ppermute | solution.py:540
  283.8 4.7 %collective-permute-start.10 = (f32[32,768]{1,0:T(8,128)S(1)}, f32[32,768]{1,0:T(8,128)S(1)}, u32[]{:S(2)}, u32[]{:S(2)}) collective-permute-start(f32[32,768]{1,0:T(8,128)S(1)} %pad_maximum_fusion.19), channel_id=1, source_target_pairs={{0,2},{1,3},{2,0},{3,1},{4,6},{5,7},{6,4},{7,5},{8,10},{9,11},{10,... | collective-permute-start | bytes 294920 | tf_op jit(solution)/shard_map/ppermute | solution.py:540
  285.6 6.0 %collective-permute-start.39 = (f32[40,512]{1,0:T(8,128)S(1)}, f32[40,512]{1,0:T(8,128)S(1)}, u32[]{:S(2)}, u32[]{:S(2)}) collective-permute-start(f32[40,512]{1,0:T(8,128)S(1)} %dynamic-slice_add_fusion.16), channel_id=1, source_target_pairs={{0,4},{1,5},{2,6},{3,7},{4,0},{5,1},{6,2},{7,3},{8,12},{9,13},{10,... | collective-permute-start | bytes 245768 | tf_op jit(solution)/shard_map/ppermute | solution.py:540
  287.0 7.1 %collective-permute-start.26 = (f32[160,512]{1,0:T(8,128)S(1)}, f32[160,512]{1,0:T(8,128)S(1)}, u32[]{:S(2)}, u32[]{:S(2)}) collective-permute-start(f32[160,512]{1,0:T(8,128)S(1)} %constant_dynamic-slice_fusion.7), channel_id=1, source_target_pairs={{0,16},{1,9},{2,18},{3,11},{4,20},{5,13},{6,22},{7,15},{8,24},{9,1... | collective-permute-start | bytes 983048 | tf_op jit(solution)/shard_map/ppermute | solution.py:545
  287.5 42.0 %collective-permute-start.23 = (f32[256,768]{1,0:T(8,128)S(1)}, f32[256,768]{1,0:T(8,128)S(1)}, u32[]{:S(2)}, u32[]{:S(2)}) collective-permute-start(f32[256,768]{1,0:T(8,128)S(1)} %pad_maximum_fusion.8), channel_id=1, source_target_pairs={{0,1},{1,0},{2,3},{3,2},{4,5},{5,4},{6,7},{7,6},{8,9},{9,8},{10,11... | collective-permute-start | bytes 2359304 | tf_op jit(solution)/shard_map/ppermute | solution.py:540
  288.6 14.0 %collective-permute-start.11 = (f32[64,768]{1,0:T(8,128)S(1)}, f32[64,768]{1,0:T(8,128)S(1)}, u32[]{:S(2)}, u32[]{:S(2)}) collective-permute-start(f32[64,768]{1,0:T(8,128)S(1)} %pad_maximum_fusion.15), channel_id=1, source_target_pairs={{0,16},{1,9},{2,18},{3,11},{4,20},{5,13},{6,22},{7,15},{8,24},{9,1... | collective-permute-start | bytes 589832 | tf_op jit(solution)/shard_map/ppermute | solution.py:545
  291.7 5.7 %collective-permute-start.40 = (f32[80,512]{1,0:T(8,128)S(1)}, f32[80,512]{1,0:T(8,128)S(1)}, u32[]{:S(2)}, u32[]{:S(2)}) collective-permute-start(f32[80,512]{1,0:T(8,128)S(1)} %pad_maximum_fusion.18), channel_id=1, source_target_pairs={{0,2},{1,3},{2,0},{3,1},{4,6},{5,7},{6,4},{7,5},{8,10},{9,11},{10,... | collective-permute-start | bytes 491528 | tf_op jit(solution)/shard_map/ppermute | solution.py:540
  294.2 5.4 %collective-permute-start.27 = (f32[80,512]{1,0:T(8,128)S(1)}, f32[80,512]{1,0:T(8,128)S(1)}, u32[]{:S(2)}, u32[]{:S(2)}) collective-permute-start(f32[80,512]{1,0:T(8,128)S(1)} %constant_dynamic-slice_fusion.6), channel_id=1, source_target_pairs={{0,2},{1,3},{2,0},{3,1},{4,6},{5,7},{6,4},{7,5},{8,10},{9,11},{10,... | collective-permute-start | bytes 491528 | tf_op jit(solution)/shard_map/ppermute | solution.py:540
  297.5 14.8 %collective-permute-start.41 = (f32[160,512]{1,0:T(8,128)S(1)}, f32[160,512]{1,0:T(8,128)S(1)}, u32[]{:S(2)}, u32[]{:S(2)}) collective-permute-start(f32[160,512]{1,0:T(8,128)S(1)} %pad_maximum_fusion.14), channel_id=1, source_target_pairs={{0,16},{1,9},{2,18},{3,11},{4,20},{5,13},{6,22},{7,15},{8,24},{9,1... | collective-permute-start | bytes 983048 | tf_op jit(solution)/shard_map/ppermute | solution.py:545
  299.6 6.4 %collective-permute-start.28 = (f32[40,512]{1,0:T(8,128)S(1)}, f32[40,512]{1,0:T(8,128)S(1)}, u32[]{:S(2)}, u32[]{:S(2)}) collective-permute-start(f32[40,512]{1,0:T(8,128)S(1)} %constant_dynamic-slice_fusion.5), channel_id=1, source_target_pairs={{0,4},{1,5},{2,6},{3,7},{4,0},{5,1},{6,2},{7,3},{8,12},{9,13},{10,... | collective-permute-start | bytes 245768 | tf_op jit(solution)/shard_map/ppermute | solution.py:540
  306.0 6.2 %collective-permute-start.29 = (f32[40,512]{1,0:T(8,128)S(1)}, f32[40,512]{1,0:T(8,128)S(1)}, u32[]{:S(2)}, u32[]{:S(2)}) collective-permute-start(f32[40,512]{1,0:T(8,128)S(1)} %dynamic-slice_add_fusion.17), channel_id=1, source_target_pairs={{0,4},{1,5},{2,6},{3,7},{4,0},{5,1},{6,2},{7,3},{8,12},{9,13},{10,... | collective-permute-start | bytes 245768 | tf_op jit(solution)/shard_map/ppermute | solution.py:540
  309.0 10.2 %collective-permute-start.12 = (f32[128,768]{1,0:T(8,128)S(1)}, f32[128,768]{1,0:T(8,128)S(1)}, u32[]{:S(2)}, u32[]{:S(2)}) collective-permute-start(f32[128,768]{1,0:T(8,128)S(1)} %pad_maximum_fusion.11), channel_id=1, source_target_pairs={{0,8},{1,17},{2,10},{3,19},{4,12},{5,21},{6,14},{7,23},{8,0},{9,25... | collective-permute-start | bytes 1179656 | tf_op jit(solution)/shard_map/ppermute | solution.py:545
  312.3 5.4 %collective-permute-start.30 = (f32[80,512]{1,0:T(8,128)S(1)}, f32[80,512]{1,0:T(8,128)S(1)}, u32[]{:S(2)}, u32[]{:S(2)}) collective-permute-start(f32[80,512]{1,0:T(8,128)S(1)} %pad_maximum_fusion.17), channel_id=1, source_target_pairs={{0,2},{1,3},{2,0},{3,1},{4,6},{5,7},{6,4},{7,5},{8,10},{9,11},{10,... | collective-permute-start | bytes 491528 | tf_op jit(solution)/shard_map/ppermute | solution.py:540
  312.5 16.7 %collective-permute-start.42 = (f32[320,512]{1,0:T(8,128)S(1)}, f32[320,512]{1,0:T(8,128)S(1)}, u32[]{:S(2)}, u32[]{:S(2)}) collective-permute-start(f32[320,512]{1,0:T(8,128)S(1)} %pad_maximum_fusion.10), channel_id=1, source_target_pairs={{0,8},{1,17},{2,10},{3,19},{4,12},{5,21},{6,14},{7,23},{8,0},{9,25... | collective-permute-start | bytes 1966088 | tf_op jit(solution)/shard_map/ppermute | solution.py:545
  317.7 7.1 %collective-permute-start.31 = (f32[160,512]{1,0:T(8,128)S(1)}, f32[160,512]{1,0:T(8,128)S(1)}, u32[]{:S(2)}, u32[]{:S(2)}) collective-permute-start(f32[160,512]{1,0:T(8,128)S(1)} %pad_maximum_fusion.13), channel_id=1, source_target_pairs={{0,16},{1,9},{2,18},{3,11},{4,20},{5,13},{6,22},{7,15},{8,24},{9,1... | collective-permute-start | bytes 983048 | tf_op jit(solution)/shard_map/ppermute | solution.py:545
  319.3 18.8 %collective-permute-start.13 = (f32[256,768]{1,0:T(8,128)S(1)}, f32[256,768]{1,0:T(8,128)S(1)}, u32[]{:S(2)}, u32[]{:S(2)}) collective-permute-start(f32[256,768]{1,0:T(8,128)S(1)} %pad_maximum_fusion.7), channel_id=1, source_target_pairs={{0,1},{1,0},{2,3},{3,2},{4,5},{5,4},{6,7},{7,6},{8,9},{9,8},{10,11... | collective-permute-start | bytes 2359304 | tf_op jit(solution)/shard_map/ppermute | solution.py:540
  325.0 12.7 %collective-permute-start.32 = (f32[320,512]{1,0:T(8,128)S(1)}, f32[320,512]{1,0:T(8,128)S(1)}, u32[]{:S(2)}, u32[]{:S(2)}) collective-permute-start(f32[320,512]{1,0:T(8,128)S(1)} %pad_maximum_fusion.9), channel_id=1, source_target_pairs={{0,8},{1,17},{2,10},{3,19},{4,12},{5,21},{6,14},{7,23},{8,0},{9,25... | collective-permute-start | bytes 1966088 | tf_op jit(solution)/shard_map/ppermute | solution.py:545
  329.4 10.8 %collective-permute-start.43 = (f32[640,512]{1,0:T(8,128)S(1)}, f32[640,512]{1,0:T(8,128)S(1)}, u32[]{:S(2)}, u32[]{:S(2)}) collective-permute-start(f32[640,512]{1,0:T(8,128)S(1)} %pad_maximum_fusion.6), channel_id=1, source_target_pairs={{0,1},{1,0},{2,3},{3,2},{4,5},{5,4},{6,7},{7,6},{8,9},{9,8},{10,11... | collective-permute-start | bytes 3932168 | tf_op jit(solution)/shard_map/ppermute | solution.py:540
  338.0 3.1 collective-permute-start.33
  (19 other events, 53.2 us)

commit v2 on v1

v2 whole, which is shorter than its diff:
```python
import functools
import math

import jax
import jax.numpy as jnp
from jax import lax
from jax.experimental import pallas as pl
from jax.experimental.pallas import tpu as pltpu
from jax.sharding import PartitionSpec as P

epsilon = 1e-05
momentum = 0.1
F32 = jnp.float32
BF16 = jnp.bfloat16

SUB = 8
LANE = 128
TILE = 256


def in_vmem(count):
    return [pl.BlockSpec(memory_space=pltpu.VMEM)] * count


def call(name, body, outs, args, scratch=(), scalars=0, results=0):
    room = 6 * 1024 * 1024 + sum(4 * math.prod(item.shape) for item in list(scratch) + list(outs[:results]))
    specs = [pl.BlockSpec(memory_space=pltpu.SMEM)] * scalars + in_vmem(len(args) - scalars)
    return pl.pallas_call(
        body,
        name=name,
        out_shape=outs,
        in_specs=specs,
        out_specs=in_vmem(len(outs)),
        scratch_shapes=list(scratch),
        compiler_params=pltpu.CompilerParams(vmem_limit_bytes=room),
    )(*args)


def shaped(shape, dtype=F32):
    return jax.ShapeDtypeStruct(shape, dtype)


def tile_mask(lim_ref, i):
    steps = TILE // SUB
    t = lax.broadcasted_iota(jnp.int32, (steps,) + lim_ref.shape, 0) + i * steps
    return t < lim_ref[...][None]


def folded(values):
    return values.reshape((values.shape[0] // SUB, SUB, values.shape[1]))


def flat(values):
    return values.reshape((values.shape[0] * SUB, values.shape[2]))


def times(ar, ai, br, bi):
    return (ar * br - ai * bi, ar * bi + ai * br)


def scan(d_ref, keep_ref, par_ref, start, reverse, conj, visit=None, extra=(), unroll=8):
    width = par_ref.shape[1]
    count = d_ref.shape[0] // SUB
    tiles = width // LANE
    lam = []
    for j in range(tiles):
        lanes = slice(j * LANE, (j + 1) * LANE)
        lr = jnp.broadcast_to(par_ref[0:1, lanes], (SUB, LANE))
        li = jnp.broadcast_to(par_ref[1:2, lanes], (SUB, LANE))
        lam.append((lr, -li if conj else li))
    state = tuple(
        (start[0][:, j * LANE : (j + 1) * LANE], start[1][:, j * LANE : (j + 1) * LANE])
        for j in range(tiles)
    )

    def step(i, carry):
        state, extra = carry
        t = count - 1 - i if reverse else i
        at = pl.ds(pl.multiple_of(t * SUB, SUB), SUB)
        keep = keep_ref[at, :]
        fresh = []
        for j in range(tiles):
            re, im = state[j]
            a = keep * lam[j][0]
            b = keep * lam[j][1]
            dr = d_ref[at, j * LANE : (j + 1) * LANE]
            di = d_ref[at, width + j * LANE : width + (j + 1) * LANE]
            fresh.append((a * re - b * im + dr, a * im + b * re + di))
        fresh = tuple(fresh)
        if visit is not None:
            extra = visit(t, keep, fresh, extra)
        return (fresh, extra)

    state, extra = lax.fori_loop(0, count, step, (state, tuple(extra)), unroll=unroll)
    re = jnp.concatenate([part[0] for part in state], axis=1)
    im = jnp.concatenate([part[1] for part in state], axis=1)
    return re, im, extra


def wide(values, width):
    return jnp.concatenate([values] * (width // LANE), axis=1)


def chunk_end(ends, kp_ref, par_ref, reverse, conj):
    width = par_ref.shape[1]
    re, im = ends
    shift = SUB - 1 if reverse else 1
    pr, pi = pltpu.roll(re, shift, 0), pltpu.roll(im, shift, 0)
    keep = wide(kp_ref[...], width)
    lr = keep * par_ref[2:3, :]
    li = keep * par_ref[3:4, :]
    li = -li if conj else li
    qr, qi = times(lr, li, pr, pi)
    odd = lax.broadcasted_iota(jnp.int32, (SUB, width), 0) % 2
    last = odd == (0 if reverse else 1)
    return jnp.where(last, qr + re, re), jnp.where(last, qi + im, im)


def chip_and_core():
    me = lax.axis_index("tm")
    return me // 2, me % 2


def enter(got_refs, e_ref, other_ref, all_ref, kd_ref, kp_ref, par_ref, reverse, conj):
    width = par_ref.shape[1]
    chips = all_ref.shape[0]
    chip, core = chip_and_core()
    sign = -1.0 if conj else 1.0
    at = 0
    for ref in got_refs:
        for k in range(ref.shape[0] // SUB):
            all_ref[at] = ref[k * SUB : (k + 1) * SUB, :]
            at += 1
    lr, li = par_ref[4:5, :], sign * par_ref[5:6, :]
    cr, ci = times(lr, li, lr, li)
    lr, li, cr, ci = (jnp.broadcast_to(x, (SUB, width)) for x in (lr, li, cr, ci))

    def step(i, x):
        j = chips - 1 - i if reverse else i
        keep = wide(kd_ref[2 * j] * kd_ref[2 * j + 1], width)
        qr, qi = times(keep * cr, keep * ci, x[0], x[1])
        use = (j > chip) if reverse else (j < chip)
        use = jnp.where(use, 1.0, 0.0)
        k = jnp.bitwise_xor(j, chip)
        nr = qr + all_ref[k, :, :width]
        ni = qi + all_ref[k, :, width:]
        return (x[0] + use * (nr - x[0]), x[1] + use * (ni - x[1]))

    zero = jnp.zeros((SUB, width), F32)
    xr, xi = lax.fori_loop(0, chips, step, (zero, zero), unroll=chips <= 4)
    first = 1 if reverse else 0
    keep = wide(kd_ref[2 * chip + first], width)
    qr, qi = times(keep * lr, keep * li, xr, xi)
    use = jnp.where(core == first, 0.0, 1.0)
    xr = xr + use * (qr + other_ref[:, :width] - xr)
    xi = xi + use * (qi + other_ref[:, width:] - xi)
    near, far = (1, SUB - 1) if reverse else (SUB - 1, 1)
    sr, si = pltpu.roll(xr, near, 0), pltpu.roll(xi, near, 0)
    keep = wide(kp_ref[...], width)
    hr = keep * par_ref[2:3, :]
    hi = sign * keep * par_ref[3:4, :]
    tr, ti = times(hr, hi, sr, si)
    tr = pltpu.roll(tr + e_ref[:, :width], far, 0)
    ti = pltpu.roll(ti + e_ref[:, width:], far, 0)
    odd = lax.broadcasted_iota(jnp.int32, (SUB, width), 0) % 2
    second = odd == (0 if reverse else 1)
    return jnp.where(second, tr, sr), jnp.where(second, ti, si)


def put_ends(e_ref, ends):
    e_ref[...] = jnp.concatenate(ends, axis=1)


def zeros_state(par_ref):
    zero = jnp.zeros((SUB, par_ref.shape[1]), F32)
    return (zero, zero)


def per_micro(values):
    return (
        jnp.sum(values[0:4], axis=0, keepdims=True),
        jnp.sum(values[4:8], axis=0, keepdims=True),
    )


def pack_rows(out_ref, rows):
    at = 0
    for row in rows:
        for j in range(row.shape[1] // LANE):
            out_ref[at : at + 1, :] = row[:, j * LANE : (j + 1) * LANE]
            at += 1


def unpack_rows(values, count, width):
    tiles = width // LANE
    return [
        jnp.concatenate(
            [values[r * tiles + j : r * tiles + j + 1, :] for j in range(tiles)], axis=1
        )
        for r in range(count)
    ]


def by_micro(first, second):
    sub = lax.broadcasted_iota(jnp.int32, (SUB, first.shape[1]), 0)
    return jnp.where(sub < 4, jnp.broadcast_to(first, sub.shape), jnp.broadcast_to(second, sub.shape))


def dot(a, b):
    return jnp.dot(a, b, preferred_element_type=F32)


def dot_nt(a, b):
    return lax.dot_general(a, b, (((1,), (1,)), ((), ())), preferred_element_type=F32)


def dot_tn(a, b):
    return lax.dot_general(a, b, (((0,), (0,)), ((), ())), preferred_element_type=F32)


def normed_tile(u_ref, stat_ref, i):
    x = folded(u_ref[pl.ds(pl.multiple_of(i * TILE, TILE), TILE), :])
    return (x - stat_ref[0:8, :][None]) * stat_ref[8:16, :][None]


def masked_tile(u_ref, stat_ref, vec_ref, lim_ref, i):
    normed = normed_tile(u_ref, stat_ref, i)
    z = normed * vec_ref[0:1, :][None] + vec_ref[1:2, :][None]
    return jnp.where(tile_mask(lim_ref, i), z, 0.0)


def rows_at(i):
    return pl.ds(pl.multiple_of(i * TILE, TILE), TILE)


def spread_in(src_ref, dst_ref, lines_ref):
    half = src_ref.shape[1] // 2
    tiles = src_ref.shape[2] // LANE
    for s in range(SUB):
        part = src_ref[s // 2, (s % 2) * half : (s % 2 + 1) * half, :].astype(F32)
        for j in range(tiles):
            lines_ref[j, pl.ds(s, half, stride=SUB), :] = part[:, j * LANE : (j + 1) * LANE]
    for j in range(tiles):
        dst_ref[:, j * LANE : (j + 1) * LANE] = lines_ref[j]


def spread_out(lines_ref, dst_ref):
    half = dst_ref.shape[1] // 2
    tiles = dst_ref.shape[2] // LANE
    for s in range(SUB):
        for j in range(tiles):
            part = lines_ref[j, pl.ds(s, half, stride=SUB), :]
            dst_ref[s // 2, (s % 2) * half : (s % 2 + 1) * half, j * LANE : (j + 1) * LANE] = part.astype(dst_ref.dtype)


def put_lines(lines_ref, i, values):
    for j in range(lines_ref.shape[0]):
        lines_ref[j, rows_at(i), :] = values[:, j * LANE : (j + 1) * LANE]


def moment_sums(u_ref, lim_ref, upto):
    def step(i, sums):
        x = jnp.where(tile_mask(lim_ref, i), folded(u_ref[rows_at(i), :]), 0.0)
        return (sums[0] + jnp.sum(x, axis=0), sums[1] + jnp.sum(x * x, axis=0))

    zero = jnp.zeros(lim_ref.shape, F32)
    return lax.fori_loop(0, upto, step, (zero, zero))


def fill_lim(lengths_ref, lim_ref, half):
    sub = lax.broadcasted_iota(jnp.int32, lim_ref.shape, 0)
    length = jnp.zeros(lim_ref.shape, jnp.int32)
    for r in range(lengths_ref.shape[0]):
        length = jnp.where(sub // 2 == r, lengths_ref[r], length)
    lim_ref[...] = length - lax.axis_index("tm") * (2 * half) - (sub % 2) * half


def k_input(lengths_ref, tokens_ref, u_ref, st_ref, lim_ref, lines_ref):
    half = tokens_ref.shape[1] // 2
    fill_lim(lengths_ref, lim_ref, half)
    spread_in(tokens_ref, u_ref, lines_ref)
    sums, squares = moment_sums(u_ref, lim_ref, u_ref.shape[0] // TILE)
    a, b = per_micro(sums)
    c, d = per_micro(squares)
    st_ref[...] = jnp.zeros(st_ref.shape, F32)
    pack_rows(st_ref, (a, c, b, d))
    counts = jnp.clip(lim_ref[:, :LANE], 0, half).astype(F32)
    a, b = per_micro(counts)
    st_ref[16:17, :] = a
    st_ref[17:18, :] = b


def one_minus_exp(x):
    series = jnp.full(x.shape, 1.0 / 9.0, F32)
    for k in range(8, 0, -1):
        series = (1.0 - x * series) / k if k > 1 else 1.0 - x * series
    return jnp.where(x < 0.5, x * series, 1.0 - jnp.exp(-x))


def k_prepare(starts_ref, rate_ref, rotation_ref, gain_ref, shift_ref, skip_ref, bias_ref,
              keep_f_ref, keep_r_ref, kp_f_ref, kp_r_ref, kd_f_ref, kd_r_ref, par_ref, vec_ref):
    rows, segments = starts_ref.shape
    steps = keep_f_ref.shape[0] // SUB
    n = kd_f_ref.shape[0]
    length = 2 * steps
    sub = lax.broadcasted_iota(jnp.int32, (SUB, LANE), 0)
    starts = []
    for k in range(segments):
        start = jnp.zeros((SUB, LANE), jnp.int32)
        for r in range(rows):
            start = jnp.where(sub // 2 == r, starts_ref[r, k], start)
        starts.append(start)
    base = lax.axis_index("tm") * length + (sub % 2) * steps
    block = 8

    def fill(i, least):
        t = lax.broadcasted_iota(jnp.int32, (block, SUB, LANE), 0) + i * block
        place = t + base[None]
        here = starts[0][None] == place
        following = starts[0][None] == place + 1
        for start in starts[1:]:
            here = here | (start[None] == place)
            following = following | (start[None] == place + 1)
        following = following | (place == n * length - 1)
        here = jnp.where(here, 0.0, 1.0)
        following = jnp.where(following, 0.0, 1.0)
        at = pl.ds(pl.multiple_of(i * block * SUB, SUB), block * SUB)
        keep_f_ref[at, :] = flat(here)
        keep_r_ref[at, :] = flat(following)
        return (jnp.minimum(least[0], jnp.min(here, axis=0)), jnp.minimum(least[1], jnp.min(following, axis=0)))

    ones = jnp.ones((SUB, LANE), F32)
    least = lax.fori_loop(0, steps // block, fill, (ones, ones))
    kp_f_ref[...], kp_r_ref[...] = least

    def fill_devices(j, unused):
        first = j * length
        forward = jnp.zeros((SUB, LANE), jnp.bool_)
        backward = jnp.zeros((SUB, LANE), jnp.bool_)
        for start in starts:
            forward = forward | ((start >= first) & (start < first + length))
            backward = backward | ((start > first) & (start <= first + length))
        kd_f_ref[j] = jnp.where(forward, 0.0, 1.0)
        kd_r_ref[j] = jnp.where(backward, 0.0, 1.0)
        return unused

    lax.fori_loop(0, n, fill_devices, 0)
    for layer in range(2):
        decay = jnp.exp(rate_ref[layer : layer + 1, :])
        magnitude = jnp.exp(-decay)
        angle = rotation_ref[layer : layer + 1, :]
        re, im = magnitude * jnp.cos(angle), magnitude * jnp.sin(angle)
        at = layer * SUB
        norm_in = jnp.sqrt(one_minus_exp(2.0 * decay))
        par_ref[at : at + 1, :] = re
        par_ref[at + 1 : at + 2, :] = im
        for unused in range(steps.bit_length() - 1):
            re, im = times(re, im, re, im)
        par_ref[at + 2 : at + 3, :] = re
        par_ref[at + 3 : at + 4, :] = im
        re, im = times(re, im, re, im)
        par_ref[at + 4 : at + 5, :] = re
        par_ref[at + 5 : at + 6, :] = im
        par_ref[at + 6 : at + 7, :] = norm_in
        par_ref[at + 7 : at + 8, :] = decay
        vec_ref[at : at + SUB, :] = jnp.zeros((SUB, vec_ref.shape[1]), F32)
        for k, ref in enumerate((gain_ref, shift_ref, skip_ref, bias_ref)):
            vec_ref[at + k : at + k + 1, :] = ref[layer : layer + 1, :]


def of_layer(ref, layer):
    return ref.at[layer * SUB : (layer + 1) * SUB]


def k_combine(layer, reverse, conj, e_ref, other_ref, kd_ref, par_ref, out_ref):
    par_ref = of_layer(par_ref, layer)
    width = par_ref.shape[1]
    chip, core = chip_and_core()
    keep = wide(kd_ref[2 * chip + (0 if reverse else 1)], width)
    lr = keep * par_ref[4:5, :]
    li = keep * par_ref[5:6, :] * (-1.0 if conj else 1.0)
    is_first = core == (1 if reverse else 0)
    e, other = e_ref[...], other_ref[...]
    pick = jnp.where(is_first, 1.0, 0.0)
    first = other + pick * (e - other)
    last = e + pick * (other - e)
    qr, qi = times(lr, li, first[:, :width], first[:, width:])
    out_ref[...] = jnp.concatenate((qr, qi), axis=1) + last


def k_drive(layer, reverse, st_ref, cnt_ref, u_ref, lim_ref, vec_ref, par_ref, b_ref, keep_ref, kp_ref,
            d_ref, ml_ref, stat_ref, e_ref):
    vec_ref, par_ref = of_layer(vec_ref, layer), of_layer(par_ref, layer)
    total = st_ref[...]
    a, c, b, d = unpack_rows(total, 4, u_ref.shape[1])
    if cnt_ref is None:
        counts = (total[16:17, :], total[17:18, :])
    else:
        counts = (cnt_ref[28:29, :LANE], cnt_ref[29:30, :LANE])
    parts = []
    for summed, squares, count in ((a, c, counts[0]), (b, d, counts[1])):
        inverse = 1.0 / wide(count, u_ref.shape[1])
        center = summed * inverse
        spread = squares * inverse - center * center
        parts.append((center, spread, lax.rsqrt(spread + epsilon), inverse))
    stat_ref[0:8, :] = by_micro(parts[0][0], parts[1][0])
    stat_ref[8:16, :] = by_micro(parts[0][2], parts[1][2])
    stat_ref[16:24, :] = by_micro(parts[0][3], parts[1][3])
    stat_ref[24:25, :] = parts[0][0]
    stat_ref[25:26, :] = parts[1][0]
    stat_ref[26:27, :] = parts[0][1]
    stat_ref[27:28, :] = parts[1][1]
    stat_ref[28:29, :] = wide(counts[0], u_ref.shape[1])
    stat_ref[29:30, :] = wide(counts[1], u_ref.shape[1])
    stat_ref[30:32, :] = jnp.zeros((2, u_ref.shape[1]), F32)
    both = jnp.concatenate((par_ref[6:7, :], par_ref[6:7, :]), axis=1)

    def step(i, unused):
        low = flat(masked_tile(u_ref, stat_ref, vec_ref, lim_ref, i)).astype(BF16)
        ml_ref[rows_at(i), :] = low
        d_ref[rows_at(i), :] = dot(low, b_ref[layer]) * both
        return unused

    lax.fori_loop(0, u_ref.shape[0] // TILE, step, 0)
    re, im, unused = scan(d_ref, keep_ref, par_ref, zeros_state(par_ref), reverse, False)
    put_ends(e_ref, chunk_end((re, im), kp_ref, par_ref, reverse, False))


def k_drive_first(layer, reverse, st_ref, *refs):
    k_drive(layer, reverse, st_ref, None, *refs)


def run_states(carry, d_ref, keep_ref, kp_ref, kd_ref, par_ref, s_ref, reverse):
    width = par_ref.shape[1]
    first = 0 if reverse else SUB
    start = enter(*carry, kd_ref, kp_ref, par_ref, reverse, False)
    s_ref[(s_ref.shape[0] - SUB if reverse else 0) : (s_ref.shape[0] if reverse else SUB), :] = (
        jnp.concatenate(start, axis=1)
    )

    def visit(t, keep, states, extra):
        at = pl.ds(pl.multiple_of(t * SUB + first, SUB), SUB)
        for j, (re, im) in enumerate(states):
            s_ref[at, j * LANE : (j + 1) * LANE] = re
            s_ref[at, width + j * LANE : width + (j + 1) * LANE] = im
        return extra

    scan(d_ref, keep_ref, par_ref, start, reverse, False, visit)
    return first


def gelu_parts(x):
    cdf = 0.5 * (1.0 + lax.erf(x * 0.7071067811865476))
    return x * cdf, cdf + x * jnp.exp(-0.5 * x * x) * 0.3989422804014327


def states_low(s_ref, first, i):
    return s_ref[pl.ds(pl.multiple_of(i * TILE + first, SUB), TILE), :].astype(BF16)


def take_carry(refs, parts):
    return (refs[:parts], refs[parts], refs[parts + 1], refs[-1]), refs[parts + 2 : -1]


def k_finish_first(layer, parts, *refs):
    carry, refs = take_carry(refs, parts)
    (d_ref, u_ref, stat_ref, lim_ref, vec_ref, par_ref, keep_ref, kp_ref, kd_ref, c_ref, w_ref,
     s_ref, al_ref, sig_ref, q_ref, slope_ref, next_ref, st_ref) = refs
    vec_ref, par_ref = of_layer(vec_ref, layer), of_layer(par_ref, layer)
    first = run_states(carry, d_ref, keep_ref, kp_ref, kd_ref, par_ref, s_ref, False)

    def step(i, sums):
        at = rows_at(i)
        valid = tile_mask(lim_ref, i)
        masked = masked_tile(u_ref, stat_ref, vec_ref, lim_ref, i)
        mixed = dot(states_low(s_ref, first, i), c_ref[layer]) + vec_ref[2:3, :] * flat(masked)
        active, slope = gelu_parts(mixed)
        low = active.astype(BF16)
        sig = jax.nn.sigmoid(dot(low, w_ref[layer]) + vec_ref[3:4, :])
        gated = active * sig
        al_ref[at, :] = low
        sig_ref[at, :] = sig
        slope_ref[at, :] = slope
        q_ref[at, :] = gated * (1.0 - sig)
        fresh = folded(u_ref[at, :]) + jnp.where(valid, folded(gated), 0.0)
        next_ref[at, :] = flat(fresh)
        x = jnp.where(valid, fresh, 0.0)
        return (sums[0] + jnp.sum(x, axis=0), sums[1] + jnp.sum(x * x, axis=0))

    zero = jnp.zeros(lim_ref.shape, F32)
    sums, squares = lax.fori_loop(0, u_ref.shape[0] // TILE, step, (zero, zero))
    a, b = per_micro(sums)
    c, d = per_micro(squares)
    pack_rows(st_ref, (a, c, b, d))


def gate_backward(layer, upstream, q, sig, slope, low, masked, s_low, state, c_ref, w_ref, mix_ref, sg_ref, wc_ref, i):
    at = rows_at(i)
    gate = (upstream * q).astype(BF16)
    wc_ref[: gate.shape[1], :] += dot_tn(low, gate)
    act = upstream * sig + dot_nt(gate, w_ref[layer])
    mix = (act * slope).astype(BF16)
    mix_ref[at, :] = mix
    wc_ref[gate.shape[1] :, :] += dot_tn(s_low, mix)
    sg = dot_nt(mix, c_ref[layer])
    sg_ref[at, :] = sg
    wide_sum = jnp.sum(folded(sg * state), axis=0)
    half = wide_sum.shape[1] // 2
    return (
        jnp.sum(folded(gate.astype(F32)), axis=0),
        jnp.sum(folded(mix.astype(F32) * masked), axis=0),
        wide_sum[:, :half] + wide_sum[:, half:],
    )


def put_sums(sums_ref, sums):
    sums_ref[...] = jnp.zeros(sums_ref.shape, F32)
    pack_rows(sums_ref, [jnp.sum(part, axis=0, keepdims=True) for part in sums])


def zero_sums(width, states):
    return (jnp.zeros((SUB, width), F32), jnp.zeros((SUB, width), F32), jnp.zeros((SUB, states), F32))


def k_middle(layer, parts, *refs):
    carry, refs = take_carry(refs, parts)
    (d_ref, u_ref, stat_ref, lim_ref, vec_ref, par_ref, keep_ref, kp_ref, kd_ref,
     keep_adj_ref, kp_adj_ref, c_ref, w_ref, cot_ref,
     out_ref, s_ref, cot32_ref, mix_ref, sg_ref, wc_ref, sums_ref, e_ref, lines_ref) = refs
    vec_ref, par_ref = of_layer(vec_ref, layer), of_layer(par_ref, layer)
    spread_in(cot_ref, cot32_ref, lines_ref)
    first = run_states(carry, d_ref, keep_ref, kp_ref, kd_ref, par_ref, s_ref, True)
    wc_ref[...] = jnp.zeros(wc_ref.shape, F32)

    def step(i, sums):
        at = rows_at(i)
        valid = tile_mask(lim_ref, i)
        masked = flat(masked_tile(u_ref, stat_ref, vec_ref, lim_ref, i))
        state = s_ref[pl.ds(pl.multiple_of(i * TILE + first, SUB), TILE), :]
        s_low = state.astype(BF16)
        mixed = dot(s_low, c_ref[layer]) + vec_ref[2:3, :] * masked
        active, slope = gelu_parts(mixed)
        low = active.astype(BF16)
        sig = jax.nn.sigmoid(dot(low, w_ref[layer]) + vec_ref[3:4, :])
        gated = active * sig
        put_lines(lines_ref, i, flat(folded(u_ref[at, :]) + jnp.where(valid, folded(gated), 0.0)))
        upstream = flat(jnp.where(valid, folded(cot32_ref[at, :]), 0.0))
        more = gate_backward(layer, upstream, gated * (1.0 - sig), sig, slope, low, masked, s_low, state,
                             c_ref, w_ref, mix_ref, sg_ref, wc_ref, i)
        return tuple(x + y for x, y in zip(sums, more))

    sums = lax.fori_loop(0, u_ref.shape[0] // TILE, step, zero_sums(u_ref.shape[1], par_ref.shape[1]))
    put_sums(sums_ref, sums)
    spread_out(lines_ref, out_ref)
    re, im, unused = scan(sg_ref, keep_adj_ref, par_ref, zeros_state(par_ref), False, True)
    put_ends(e_ref, chunk_end((re, im), kp_adj_ref, par_ref, False, True))


def k_lower(layer, st_ref, z_ref, cot32_ref, u1_ref, stat1_ref, lim_ref,
            s_ref, al_ref, sig_ref, q_ref, slope_ref, u_ref, stat_ref, vec_ref, par_ref, c_ref, w_ref,
            keep_adj_ref, kp_adj_ref,
            grad_ref, mix_ref, sg_ref, wc_ref, sums_ref, e_ref, bn_ref):
    vec1_ref = of_layer(vec_ref, layer + 1)
    vec_ref, par_ref = of_layer(vec_ref, layer), of_layer(par_ref, layer)
    first = SUB
    c1, c2 = norm_sums(st_ref, stat1_ref, vec1_ref, bn_ref)
    wc_ref[...] = jnp.zeros(wc_ref.shape, F32)

    def step(i, sums):
        at = rows_at(i)
        valid = tile_mask(lim_ref, i)
        extra = norm_backward(z_ref, u1_ref, stat1_ref, vec1_ref, c1, c2, valid, i)
        grad = folded(cot32_ref[at, :]) + extra
        grad_ref[at, :] = flat(grad)
        upstream = flat(jnp.where(valid, grad, 0.0))
        masked = flat(masked_tile(u_ref, stat_ref, vec_ref, lim_ref, i))
        state = s_ref[pl.ds(pl.multiple_of(i * TILE + first, SUB), TILE), :]
        more = gate_backward(layer, upstream, q_ref[at, :], sig_ref[at, :], slope_ref[at, :], al_ref[at, :], masked,
                             state.astype(BF16), state, c_ref, w_ref, mix_ref, sg_ref, wc_ref, i)
        return tuple(x + y for x, y in zip(sums, more))

    sums = lax.fori_loop(0, u_ref.shape[0] // TILE, step, zero_sums(u_ref.shape[1], par_ref.shape[1]))
    put_sums(sums_ref, sums)
    re, im, unused = scan(sg_ref, keep_adj_ref, par_ref, zeros_state(par_ref), True, True)
    put_ends(e_ref, chunk_end((re, im), kp_adj_ref, par_ref, True, True))


def norm_sums(st_ref, stat_ref, vec_ref, bn_ref):
    width = vec_ref.shape[1]
    a, c, b, d = unpack_rows(st_ref[...], 4, width)
    bn_ref[...] = jnp.concatenate((a + b, c + d, jnp.zeros((6, width), F32)), axis=0)
    gain = vec_ref[0:1, :]
    inverse = stat_ref[16:24, :]
    return by_micro(a * gain, b * gain) * inverse, by_micro(c * gain, d * gain) * inverse


def norm_backward(z_ref, u_ref, stat_ref, vec_ref, c1, c2, valid, i):
    normed = normed_tile(u_ref, stat_ref, i)
    z = folded(z_ref[rows_at(i), :]) * vec_ref[0:1, :][None]
    return jnp.where(valid, stat_ref[8:16, :][None] * (z - c1[None] - normed * c2[None]), 0.0)


def k_adjoint(layer, reverse, parts, extra, *refs):
    carry, refs = take_carry(refs, parts)
    sent_refs, refs = refs[:extra], refs[extra:]
    (sg_ref, s_ref, mix_ref, ml_ref, u_ref, stat_ref, lim_ref, vec_ref, par_ref,
     keep_adj_ref, kp_adj_ref, kd_adj_ref, keep_ref, b_ref, z_ref, gb_ref, lg_ref, st_ref, a_ref) = refs
    vec_ref, par_ref = of_layer(vec_ref, layer), of_layer(par_ref, layer)
    width = par_ref.shape[1]
    tiles = width // LANE
    behind = 0 if reverse else SUB
    start = enter(*carry, kd_adj_ref, kp_adj_ref, par_ref, reverse, True)
    scale = [jnp.broadcast_to(par_ref[6:7, j * LANE : (j + 1) * LANE], (SUB, LANE)) for j in range(tiles)]

    def visit(t, unused, adjoint, sums):
        at = pl.ds(pl.multiple_of(t * SUB, SUB), SUB)
        before = pl.ds(pl.multiple_of(t * SUB + behind, SUB), SUB)
        keep = keep_ref[at, :]
        fresh = []
        for j, (re, im) in enumerate(adjoint):
            a_ref[at, j * LANE : (j + 1) * LANE] = re * scale[j]
            a_ref[at, width + j * LANE : width + (j + 1) * LANE] = im * scale[j]
            pr = s_ref[before, j * LANE : (j + 1) * LANE]
            pi = s_ref[before, width + j * LANE : width + (j + 1) * LANE]
            kr, ki = keep * re, keep * im
            fresh.append((sums[j][0] + (kr * pr + ki * pi), sums[j][1] + (ki * pr - kr * pi)))
        return tuple(fresh)

    zero = jnp.zeros((SUB, LANE), F32)
    unused, unused, sums = scan(sg_ref, keep_adj_ref, par_ref, start, reverse, True, visit,
                                tuple((zero, zero) for j in range(tiles)))
    lg_ref[...] = jnp.zeros(lg_ref.shape, F32)
    pack_rows(lg_ref, [
        jnp.sum(jnp.concatenate([part[k] for part in sums], axis=1), axis=0, keepdims=True) for k in range(2)
    ])
    gb_ref[...] = jnp.zeros(gb_ref.shape, F32)

    def step(i, sums):
        at = rows_at(i)
        drive = a_ref[at, :].astype(BF16)
        gb = dot_tn(ml_ref[at, :], drive)
        rows = gb.shape[0]
        gb_ref[:rows, :] += gb[:, :rows]
        gb_ref[rows:, : rows // 2] += gb[: rows // 2, rows:]
        gb_ref[rows:, rows // 2 :] += gb[rows // 2 :, rows:]
        back = dot_nt(drive, b_ref[layer]) + vec_ref[2:3, :] * mix_ref[at, :].astype(F32)
        z = jnp.where(tile_mask(lim_ref, i), folded(back), 0.0)
        z_ref[at, :] = flat(z)
        return (sums[0] + jnp.sum(z, axis=0), sums[1] + jnp.sum(z * normed_tile(u_ref, stat_ref, i), axis=0))

    zero = jnp.zeros(lim_ref.shape, F32)
    sums = lax.fori_loop(0, u_ref.shape[0] // TILE, step, (zero, zero))
    a, b = per_micro(sums[0])
    c, d = per_micro(sums[1])
    pack_rows(st_ref, (a, c, b, d))
    at = 16
    if extra:
        for ref in sent_refs + (lg_ref,):
            st_ref[at : at + ref.shape[0], :] = ref[...]
            at += ref.shape[0]


def k_output(st_ref, z_ref, grad_ref, u_ref, stat_ref, vec_ref, lim_ref, par_ref, stat1_ref, bn1_ref,
             run_mean_ref, run_var_ref,
             out_ref, gain_ref, shift_ref, skip_ref, bias_ref, rate_ref, rotation_ref, mean_ref, var_ref,
             bn_ref, lines_ref):
    vec0_ref = of_layer(vec_ref, 0)
    c1, c2 = norm_sums(st_ref, stat_ref, vec0_ref, bn_ref)

    def step(i, unused):
        extra = norm_backward(z_ref, u_ref, stat_ref, vec0_ref, c1, c2, tile_mask(lim_ref, i), i)
        put_lines(lines_ref, i, grad_ref[rows_at(i), :] + flat(extra))
        return unused

    lax.fori_loop(0, u_ref.shape[0] // TILE, step, 0)
    spread_out(lines_ref, out_ref)
    width, states = gain_ref.shape[1], rate_ref.shape[1]
    per, per_state = width // LANE, states // LANE

    def line(at, count):
        return jnp.concatenate([st_ref[at + j : at + j + 1, :] for j in range(count)], axis=1)

    for layer, (stats_ref, norms_ref) in enumerate(((stat_ref, bn_ref), (stat1_ref, bn1_ref))):
        row = slice(layer, layer + 1)
        at = 40 - 24 * layer
        bias_ref[row, :] = line(at, per)
        skip_ref[row, :] = line(at + per, per)
        product = line(at + 2 * per, per_state)
        grad_re, grad_im = line(at + 16, per_state), line(at + 16 + per_state, per_state)
        par = of_layer(par_ref, layer)
        lam_re, lam_im, norm_in, decay = par[0:1, :], par[1:2, :], par[6:7, :], par[7:8, :]
        rotation_ref[row, :] = lam_re * grad_im - lam_im * grad_re
        rate_ref[row, :] = decay * (
            product * jnp.exp(-2.0 * decay) / (norm_in * norm_in) - (lam_re * grad_re + lam_im * grad_im)
        )
        shift_ref[row, :] = norms_ref[0:1, :]
        gain_ref[row, :] = norms_ref[1:2, :]
        mean, var = run_mean_ref[row, :], run_var_ref[row, :]
        for micro in range(2):
            mean = (1.0 - momentum) * mean + momentum * stats_ref[24 + micro : 25 + micro, :]
            var = (1.0 - momentum) * var + momentum * stats_ref[26 + micro : 27 + micro, :]
        mean_ref[row, :] = mean
        var_ref[row, :] = var


def k_split(side, x_ref, give_ref):
    half = give_ref.shape[0]
    give_ref[...] = x_ref[pl.ds(pl.multiple_of((1 - side()) * half, SUB), half), :]


def k_fold(before, side, kept_ref, got_ref, give_ref, keep_ref):
    half = give_ref.shape[0]
    base = 0 if before is None else before() * got_ref.shape[0]
    mine = side()
    for ref, at in ((give_ref, (1 - mine) * half), (keep_ref, mine * half)):
        here = kept_ref[pl.ds(pl.multiple_of(base + at, SUB), half), :]
        ref[...] = here + got_ref[pl.ds(pl.multiple_of(at, SUB), half), :]


def k_join(side, own_ref, got_ref, out_ref):
    half = own_ref.shape[0]
    mine = side()
    out_ref[pl.ds(pl.multiple_of(mine * half, SUB), half), :] = own_ref[...]
    out_ref[pl.ds(pl.multiple_of((1 - mine) * half, SUB), half), :] = got_ref[...]


def k_maps(side, wc1_ref, own_ref, got_ref, w_ref, c_ref, wc_ref):
    k_join(side, own_ref, got_ref, wc_ref)
    width = w_ref.shape[1]
    for layer, ref in enumerate((wc_ref, wc1_ref)):
        w_ref[layer] = ref[:width, :]
        c_ref[layer] = ref[width:, :]


def k_drives(side, b1_ref, own_ref, got_ref, out_ref, b_ref):
    k_join(side, own_ref, got_ref, b_ref)
    width = out_ref.shape[1]
    for layer, ref in enumerate((b_ref, b1_ref)):
        out_ref[layer, :, :width] = ref[:width, :]
        out_ref[layer, : width // 2, width:] = ref[width:, : width // 2]
        out_ref[layer, width // 2 :, width:] = ref[width:, width // 2 :]


BOTH = ("batch", "tm")

TAIL = "s D A s C D B s D C A s D B s leave C D A D B C D A C D B C D A C B".replace("leave", "L")


def outer_bits():
    nb, nt = lax.axis_size("batch"), lax.axis_size("tm")
    return [("batch", 1 << k, nt << k) for k in range(nb.bit_length() - 1)]


def line_bits():
    return [("tm", 1 << k, 1 << k) for k in range(1, lax.axis_size("tm").bit_length() - 1)]


def swap(block, distance):
    total = lax.axis_size("batch") * lax.axis_size("tm")
    return lax.ppermute(block, BOTH, [(i, i ^ distance) for i in range(total)])


def swap_by_core(block, even, odd):
    total = lax.axis_size("batch") * lax.axis_size("tm")
    return lax.ppermute(block, BOTH, [(i, i ^ (odd if i & 1 else even)) for i in range(total)])


def sum_over(block, bits):
    if len(bits) == 2:
        near, far = bits[0][2], bits[1][2]
        others = [swap(block, distance | 1) for distance in (near, far, near | far)]
        return (block + others[0]) + (others[1] + others[2])
    for unused, unused, distance in bits:
        block = block + swap(block, distance | 1)
    return block


def sums_of_all(block, order=None, between=()):
    stages = [lambda block: block + swap(block, 1), lambda block: sum_over(block, outer_bits()),
              lambda block: sum_over(block, line_bits())]
    for k, stage in enumerate(stages):
        if order is not None:
            block, = order(block)
        block = stage(block)
        if k < len(between):
            between[k]()
    if order is not None:
        order.token = block
    return block


def carries(e, kd, par, layer, reverse, conj):
    other = swap(e, 1)
    block, = call("combine", functools.partial(k_combine, layer, reverse, conj), [shaped(e.shape)], [e, other, kd, par])
    bits = line_bits()
    if len(bits) == 2:
        near, far = bits[0][2], bits[1][2]
        return [block] + [swap(block, distance | 1) for distance in (near, far, near | far)] + [e, other]
    for unused, unused, distance in bits:
        block = jnp.concatenate((block, swap(block, distance | 1)), axis=0)
    return [block, e, other]


def bit_of(axis, bit):
    return lax.div(lax.axis_index(axis), bit) % 2


def plan(rows):
    outer, line = outer_bits(), line_bits()
    is_odd = functools.partial(bit_of, "tm", 1)
    steps = [(is_odd, lambda block: swap(block, 1))]
    for even, odd in zip(outer, outer[::-1]):
        def side(even=even, odd=odd):
            return jnp.where(is_odd() == 1, bit_of(odd[0], odd[1]), bit_of(even[0], even[1]))

        steps.append((side, functools.partial(swap_by_core, even=even[2], odd=odd[2])))
    for axis, bit, distance in line:
        steps.append((functools.partial(bit_of, axis, bit), functools.partial(swap, distance=distance)))
    cuts = 0
    while cuts < len(steps) and rows % (SUB << (cuts + 1)) == 0 and cuts < 4:
        cuts += 1
    return steps[:cuts], [exchange for unused, exchange in steps[cuts:]]


class Order:
    def __init__(self):
        self.token = None

    def __call__(self, *values):
        if self.token is None:
            return values
        tied = lax.optimization_barrier(tuple(values) + (self.token,))
        return tied[:-1]


class Large:
    def __init__(self, order, block):
        self.order = order
        self.rows, self.width = block.shape
        self.cuts, self.whole = plan(self.rows)
        self.block = block
        self.at = 0
        self.got = None

    def half(self):
        return shaped((self.rows >> (self.at + 1), self.width))

    def send(self):
        cuts, at = self.cuts, self.at
        count = len(cuts)
        if at == 0:
            self.block, = self.order(self.block)
        else:
            self.block, self.got = self.order(self.block, self.got)
        if at < count:
            side, exchange = cuts[at]
            if at == 0:
                give, = call("split", functools.partial(k_split, side), [self.half()], [self.block])
            else:
                before = cuts[0][0] if at == 1 else None
                give, self.block = call(
                    "fold", functools.partial(k_fold, before, side), [self.half()] * 2, [self.block, self.got]
                )
        elif at <= count + len(self.whole):
            give = self.block = self.block + self.got
            exchange = (self.whole + [step[1] for step in cuts[::-1]])[at - count]
        else:
            back = at - count - len(self.whole)
            give = self.block = self.joined()
            exchange = cuts[count - 1 - back][1]
        self.order.token = give
        self.got = exchange(give)
        self.at += 1

    def joined(self):
        rows, width = self.block.shape
        side = self.cuts[len(self.cuts) - 1 - (self.at - 1 - len(self.cuts) - len(self.whole))][0]
        out, = call("join", functools.partial(k_join, side), [shaped((2 * rows, width))], [self.block, self.got])
        return out

    def result(self):
        self.block, self.got = self.order(self.block, self.got)
        self.block = self.joined()
        self.order.token = self.block
        return self.block

    def left(self):
        return 2 * len(self.cuts) + len(self.whole) - self.at


def sum_slowly(order, block):
    for distance in [1] + [bit[2] | 1 for bit in outer_bits() + line_bits()]:
        block, = order(block)
        got = swap(block, distance)
        yield None
        block, got = order(block, got)
        block = block + got
        order.token = block
    yield block


def local(tokens, starts, lengths, cotangent, norm_gain, norm_shift, b_proj, log_rate, rotation, c_proj, skip_gain,
          w_gate, gate_bias, run_mean, run_var):
    rows, length, width = tokens.shape
    states = log_rate.shape[1]
    count = rows * length
    n = lax.axis_size("tm")
    chips = n // 2
    parts = 4 if chips == 4 else 1

    big = lambda w, dtype=F32: shaped((count, w), dtype)
    ends = shaped((SUB, 2 * states))
    kept = shaped((count + SUB, 2 * states))
    small = shaped((16, LANE))
    lines = pltpu.VMEM((width // LANE, count, LANE), F32)
    everyone = pltpu.VMEM((chips, SUB, 2 * states), F32)
    keeps = shaped((count, LANE))
    vector, state_vector = shaped((2, width)), shaped((2, states))

    u0, st, lim = call("enter", k_input, [big(width), shaped((24, LANE)), shaped((SUB, width), jnp.int32)],
                       [lengths, tokens], scratch=[lines], scalars=1)
    keep_f, keep_r, kp_f, kp_r, kd_f, kd_r, par, vec = call(
        "prepare", k_prepare,
        [keeps, keeps, shaped((SUB, LANE)), shaped((SUB, LANE)), shaped((n, SUB, LANE)), shaped((n, SUB, LANE)),
         shaped((2 * SUB, states)), shaped((2 * SUB, width))],
        [starts, log_rate, rotation, norm_gain, norm_shift, skip_gain, gate_bias], scalars=1,
    )
    st = sums_of_all(st)
    d0, ml0, stat0, e = call(
        "drive0", functools.partial(k_drive_first, 0, False),
        [big(2 * states), big(width, BF16), shaped((32, width)), ends],
        [st, u0, lim, vec, par, b_proj, keep_f, kp_f],
    )
    s0, al0, sig0, q0, slope0, u1, st = call(
        "finish0", functools.partial(k_finish_first, 0, parts),
        [kept, big(width, BF16), big(width), big(width), big(width), big(width), small],
        carries(e, kd_f, par, 0, False, False)
        + [d0, u0, stat0, lim, vec, par, keep_f, kp_f, kd_f, c_proj, w_gate],
        scratch=[everyone],
    )
    st = sums_of_all(st)
    d1, ml1, stat1, e = call(
        "drive1", functools.partial(k_drive, 1, True),
        [big(2 * states), big(width, BF16), shaped((32, width)), ends],
        [st, stat0, u1, lim, vec, par, b_proj, keep_r, kp_r],
    )
    grads = [shaped((width + 2 * states, width)), small, ends]
    output, s1, cot32, mix1, sg1, wc1, sums1, e = call(
        "middle", functools.partial(k_middle, 1, parts),
        [shaped(tokens.shape, BF16), kept, big(width), big(width, BF16), big(2 * states)] + grads,
        carries(e, kd_r, par, 1, True, False)
        + [d1, u1, stat1, lim, vec, par, keep_r, kp_r, kd_r, keep_f, kp_f, c_proj, w_gate, cotangent],
        scratch=[lines, everyone], results=1,
    )
    order = Order()
    wc1 = Large(order, wc1)
    wc1.send()
    got = carries(e, kd_f, par, 1, False, True)
    wc1.send()
    adjoint = [big(width), shaped((2 * states, width)), shaped((8, LANE))]
    z1, gb1, lg1, st = call(
        "adjoint1", functools.partial(k_adjoint, 1, False, parts, 0), adjoint + [small],
        list(order(*got)) + [sg1, s1, mix1, ml1, u1, stat1, lim, vec, par, keep_f, kp_f, kd_f, keep_r, b_proj],
        scratch=[pltpu.VMEM((count, 2 * states), F32), everyone],
    )
    order.token = st
    b1 = Large(order, gb1)
    st = sums_of_all(st, order, [b1.send, wc1.send, b1.send])
    g0, mix0, sg0, wc0, sums0, e, bn1 = call(
        "lower", functools.partial(k_lower, 0),
        [big(width), big(width, BF16), big(2 * states)] + grads + [shaped((8, width))],
        list(order(st)) + [z1, cot32, u1, stat1, lim, s0, al0, sig0, q0, slope0, u0, stat0, vec, par,
                           c_proj, w_gate, keep_r, kp_r],
    )
    order.token = e
    wc0 = Large(order, wc0)
    wc1.send()
    wc0.send()
    got = carries(e, kd_r, par, 0, True, True)
    b1.send()
    wc0.send()
    z0, gb0, lg0, st = call(
        "adjoint0", functools.partial(k_adjoint, 0, True, parts, 3), adjoint + [shaped((64, LANE))],
        list(order(*got)) + [sums1, lg1, sums0]
        + [sg0, s0, mix0, ml0, u0, stat0, lim, vec, par, keep_r, kp_r, kd_r, keep_f, b_proj],
        scratch=[pltpu.VMEM((count, 2 * states), F32), everyone],
    )
    order.token = st
    b0 = Large(order, gb0)
    small_sum = sum_slowly(order, st)
    queue = TAIL.split()
    returned = {}
    for item in queue:
        if item == "s":
            st = next(small_sum)
        elif item == "L":
            for unused in small_sum:
                st = unused if unused is not None else st
            (tokens_grad, grad_gain, grad_shift, grad_skip, grad_bias, grad_rate, grad_rotation, new_mean, new_var,
             bn0) = call(
                "leave", k_output,
                [shaped(tokens.shape), vector, vector, vector, vector, state_vector, state_vector, vector, vector,
                 shaped((SUB, width))],
                list(order(st)) + [z0, g0, u0, stat0, vec, lim, par, stat1, bn1, run_mean, run_var],
                scratch=[lines], results=9,
            )
            order.token = bn0
        else:
            large = {"A": wc1, "B": b1, "C": wc0, "D": b0}[item]
            if large.left():
                large.send()
            elif item in "AB":
                returned[item] = large.result()
    for large in (wc1, b1, wc0, b0):
        while large.left():
            large.send()
    wc1 = returned["A"] if "A" in returned else wc1.result()
    b1 = returned["B"] if "B" in returned else b1.result()
    last = wc0.cuts[0][0]
    wc0.block, wc0.got = order(wc0.block, wc0.got)
    grad_w, grad_c, unused = call(
        "maps", functools.partial(k_maps, last),
        [shaped((2, width, width)), shaped((2, 2 * states, width)), shaped((width + 2 * states, width))],
        [wc1, wc0.block, wc0.got], results=2,
    )
    order.token = unused
    b0.block, b0.got = order(b0.block, b0.got)
    grad_b, unused = call(
        "drives", functools.partial(k_drives, last),
        [shaped((2, width, 2 * states)), shaped((2 * states, width))],
        [b1, b0.block, b0.got], results=1,
    )
    return (output, tokens_grad, grad_gain, grad_shift, grad_b, grad_rate, grad_rotation, grad_c, grad_skip, grad_w,
            grad_bias, new_mean, new_var)


def solution(mesh):
    tokens_spec = P("batch", "tm", None)
    return jax.shard_map(
        local,
        mesh=mesh,
        in_specs=(tokens_spec, P("batch", None), P("batch"), tokens_spec) + (P(),) * 11,
        out_specs=(tokens_spec, tokens_spec) + (P(),) * 11,
        check_vma=False,
    )
```

time: 347 us -> 246 us (0.71)
  Pallas kernels: 91 us -> 52.6 us
  local copies, waits for them, and re-layouts: 43.1 us -> 8.1 us
  other arithmetic: 25.4 us -> 0.23 us
    all_to_all x8 -> x0, waiting for transfers between devices: 43.4 us -> none  [the longest x4 24.4 us: blocks_of_row(): lax.all_to_all(jnp.broadcast_to(block[None], (n,) + block.shape), 'tm', 0...]
    pallas_call x9 -> x46, Pallas kernels: 91 us -> 52.6 us  [call(): pl.pallas_call(body, name=name, out_shape=outs, in_specs=specs, out_specs...]
    ppermute x28 -> x62, waiting for transfers between devices: 34.4 us -> 70.9 us  [swap(): return lax.ppermute(block, BOTH, [(i, i ^ distance) for i in range(total)])]
    ppermute x28 -> x62, starting transfers between devices: 23.2 us -> 57.1 us  [swap(): return lax.ppermute(block, BOTH, [(i, i ^ distance) for i in range(total)])]
    all_to_all x8 -> x0, starting transfers between devices: 32.8 us -> none  [the longest x4 18.6 us: sums_of_all(): return lax.all_to_all(spread, BOTH, 0, 0, axis_index_groups=groups)]
    broadcast_in_dim x22 -> x0, local copies, waits for them, and re-layouts: 13.7 us -> none  [the longest x10 5.07 us: over_lanes(): return jnp.broadcast_to(values[..., None], values.shape + (LANE,))]
    add x27 -> x22, other arithmetic: 10.8 us -> 0.23 us  [the longest x8 0.16 us: send(): give = self.block = self.block + self.got]
    ppermute x16, waiting for transfers between devices: 30.9 us -> 38.8 us  [swap_by_core(): lax.ppermute(block, BOTH, [(i, i ^ (odd if i & 1 else even)) for i in ran...]
  transfers between devices with their start and end apart: 52 -> 78, of which waited for: 31 -> 43; matrix products, arithmetic and copies ran while one was open for 14% -> 0% of each run, Pallas kernels for 9% -> 8%
where the time goes in v2:
time: 246 us
  waiting for transfers between devices  110 us (45%)
  starting transfers between devices  74.1 us (30%)
  Pallas kernels  52.6 us (21%)
  local copies, waits for them, and re-layouts  8.1 us (3%)
    ppermute x62, waiting for transfers between devices, swap(): return lax.ppermute(block, BOTH, [(i, i ^ distance) for i in range(total)])  70.9 us
    ppermute x62, starting transfers between devices, swap(): return lax.ppermute(block, BOTH, [(i, i ^ distance) for i in range(total)])  57.1 us
    pallas_call x46, Pallas kernels, call(): pl.pallas_call(body, name=name, out_shape=outs, in_specs=specs, out_specs...  52.6 us
    ppermute x16, waiting for transfers between devices, swap_by_core(): lax.ppermute(block, BOTH, [(i, i ^ (odd if i & 1 else even)) for i in ran...  38.8 us
    ppermute x16, starting transfers between devices, swap_by_core(): lax.ppermute(block, BOTH, [(i, i ^ (odd if i & 1 else even)) for i in ran...  17 us
    unnamed x32, local copies, waits for them, and re-layouts  8.1 us
  transfers between devices with their start and end apart: 78, of which 43 were waited for; matrix products, arithmetic and copies ran while one was open for 0% of the time, Pallas kernels for 8%

profile of v2, /device:TPU:0, one launch (start us, length us, event | category | flops | bytes accessed | tf_op | source)
XLA Modules:
  0.0 245.9 jit_solution(13886004902806483145)
XLA Ops:
  2.5 1.9 enter.1
  5.8 3.6 %collective-permute-start.3 = (f32[24,128]{1,0:T(8,128)S(1)}, f32[24,128]{1,0:T(8,128)S(1)}, u32[]{:S(2)}, u32[]{:S(2)}) collective-permute-start(f32[24,128]{1,0:T(8,128)S(1)} %add.102), channel_id=1, source_target_pairs={{0,25},{1,24},{2,27},{3,26},{4,29},{5,28},{6,31},{7,30},{8,17},{9,... | collective-permute-start | bytes 36872 | tf_op jit(solution)/shard_map/ppermute | solution.py:760
  10.8 1.7 collective-permute-done.2
  12.9 3.4 %collective-permute-start.6 = (f32[24,128]{1,0:T(8,128)S(1)}, f32[24,128]{1,0:T(8,128)S(1)}, u32[]{:S(2)}, u32[]{:S(2)}) collective-permute-start(f32[24,128]{1,0:T(8,128)S(1)} %add_add_fusion.1), channel_id=1, source_target_pairs={{0,7},{1,6},{2,5},{3,4},{4,3},{5,2},{6,1},{7,0},{8,15},{9,14},{10,... | collective-permute-start | bytes 36872 | tf_op jit(solution)/shard_map/ppermute | solution.py:760
  21.7 3.2 %prepare.1 = (f32[1024,128]{1,0:T(8,128)S(1)}, f32[1024,128]{1,0:T(8,128)S(1)}, f32[8,128]{1,0:T(8,128)S(1)}, f32[8,128]{1,0:T(8,128)S(1)}, f32[8,8,128]{2,1,0:T...) custom-call(s32[4,16]{1,0:T(4,128)S(1)} %copy-done.14, ...), custom_call_target="tpu_custom_call" | custom-call | tf_op jit(solution)/shard_map/prepare/pallas_call | solution.py:28
  24.9 1.4 copy-done
  26.3 2.4 drive0.1
  30.0 3.5 %collective-permute-start.10 = (f32[8,768]{1,0:T(8,128)S(1)}, f32[8,768]{1,0:T(8,128)S(1)}, u32[]{:S(2)}, u32[]{:S(2)}) collective-permute-start(f32[8,768]{1,0:T(8,128)S(1)} %combine.4.refs_0_), channel_id=1, source_target_pairs={{0,7},{1,6},{2,5},{3,4},{4,3},{5,2},{6,1},{7,0},{8,15},{9,14},{10,... | collective-permute-start | bytes 73736 | tf_op jit(solution)/shard_map/ppermute | solution.py:760
  35.1 2.6 %collective-permute-done.9.refs_2_ = f32[8,768]{1,0:T(8,128)S(1)} collective-permute-done((f32[8,768]{1,0:T(8,128)S(1)}, f32[8,768]{1,0:T(8,128)S(1)}, u32[]{:S(2)}, u32[]{:S(2)}) %collective-permute-start.9) | collective-permute-done | bytes 24608 | tf_op jit(solution)/shard_map/ppermute | solution.py:760
  37.7 4.8 %finish0.1 = (f32[1032,768]{1,0:T(8,128)S(1)}, bf16[1024,512]{1,0:T(8,128)(2,1)S(1)}, f32[1024,512]{1,0:T(8,128)S(1)}, f32[1024,512]{1,0:T(8,128)S(1)}, f32[1024...) custom-call(f32[8,768]{1,0:T(8,128)S(1)} %combine.4.refs_0_, ...), custom_call_target="tpu_custom_call" | custom-call | tf_op jit(solution)/shard_map/finish0/pallas_call | solution.py:28
  43.7 1.3 collective-permute-start.14
  45.4 1.3 collective-permute-start.12
  48.5 1.6 collective-permute-start.17
  50.3 2.1 collective-permute-start.15
  54.1 2.4 drive1.1
  57.8 2.0 collective-permute-start.21
  60.6 1.3 collective-permute-start.19
  63.0 1.3 collective-permute-done.20.refs_2_
  64.3 11.9 %middle.1 = (bf16[4,256,512]{2,1,0:T(8,128)(2,1)}, f32[1032,768]{1,0:T(8,128)S(1)}, f32[1024,512]{1,0:T(8,128)S(1)}, bf16[1024,512]{1,0:T(8,128)(2,1)S(1)}, f32[...) custom-call(f32[8,768]{1,0:T(8,128)S(1)} %combine.5.refs_0_, ...), custom_call_target="tpu_custom_call" | custom-call | tf_op jit(solution)/shard_map/middle/pallas_call | solution.py:28
  76.6 2.9 %collective-permute-done.26.got_ref = f32[640,512]{1,0:T(8,128)S(1)} collective-permute-done((f32[640,512]{1,0:T(8,128)S(1)}, f32[640,512]{1,0:T(8,128)S(1)}, u32[]{:S(2)}, u32[]{:S(2)}) %collective-permute-start.26) | collective-permute-done | bytes 1310752 | tf_op jit(solution)/shard_map/ppermute | solution.py:760
  79.6 1.6 collective-permute-start.31
  82.4 1.9 collective-permute-start.25
  84.6 1.7 collective-permute-start.23
  88.6 4.5 %adjoint1.1 = (f32[1024,512]{1,0:T(8,128)S(1)}, f32[768,512]{1,0:T(8,128)S(1)}, f32[8,128]{1,0:T(8,128)S(1)}, f32[16,128]{1,0:T(8,128)S(1)}) custom-call(f32[8,768]{1,0:T(8,128)S(1)} %combine.6.refs_0_, f32[8,768]{1,0:T(8,128)S(1)} %collective-permute-done.23.refs_1_, f32[8,768]{1,0:T(8,128)S(1)} %collective-permute-done.24.refs_2_, ...), custom_call_target="tpu_custom_call" | custom-call | tf_op jit(solution)/shard_map/adjoint1/pallas_call | solution.py:28
  94.4 1.2 collective-permute-start.30
  95.6 1.4 collective-permute-start.29
  97.4 1.6 collective-permute-start.39
  100.1 1.8 collective-permute-start.34
  102.4 1.6 collective-permute-start.32
  105.9 6.2 %lower.1 = (f32[1024,512]{1,0:T(8,128)S(1)}, bf16[1024,512]{1,0:T(8,128)(2,1)S(1)}, f32[1024,768]{1,0:T(8,128)S(1)}, f32[1280,512]{1,0:T(8,128)S(1)}, f32[16,128...) custom-call(f32[16,128]{1,0:T(8,128)S(1)} %add_add_fusion.2.st_ref, ...), custom_call_target="tpu_custom_call" | custom-call | tf_op jit(solution)/shard_map/lower/pallas_call | solution.py:28
  112.9 3.6 %collective-permute-done.41.got_ref = f32[384,512]{1,0:T(8,128)S(1)} collective-permute-done((f32[384,512]{1,0:T(8,128)S(1)}, f32[384,512]{1,0:T(8,128)S(1)}, u32[]{:S(2)}, u32[]{:S(2)}) %collective-permute-start.41) | collective-permute-done | bytes 786464 | tf_op jit(solution)/shard_map/ppermute | solution.py:760
  118.7 1.5 collective-permute-start.38
  121.1 1.5 collective-permute-start.36
  122.6 1.8 collective-permute-done.42.got_ref
  125.0 4.4 %adjoint0.1 = (f32[1024,512]{1,0:T(8,128)S(1)}, f32[768,512]{1,0:T(8,128)S(1)}, f32[8,128]{1,0:T(8,128)}, f32[64,128]{1,0:T(8,128)S(1)}) custom-call(f32[8,768]{1,0:T(8,128)S(1)} %combine.7.refs_0_, f32[8,768]{1,0:T(8,128)S(1)} %collective-permute-done.36.refs_1_, f32[8,768]{1,0:T(8,128)S(1)} %collective-permute-done.37.refs_2_, ...), custom_call_target="tpu_custom_call" | custom-call | tf_op jit(solution)/shard_map/adjoint0/pallas_call | solution.py:28
  129.6 1.4 collective-permute-start.48
  132.2 5.2 %collective-permute-done.44 = f32[80,512]{1,0:T(8,128)S(1)} collective-permute-done((f32[80,512]{1,0:T(8,128)S(1)}, f32[80,512]{1,0:T(8,128)S(1)}, u32[]{:S(2)}, u32[]{:S(2)}) %collective-permute-start.44) | collective-permute-done | bytes 163872 | tf_op jit(solution)/shard_map/ppermute | solution.py:760
  137.5 2.7 %collective-permute-done.48.got_ref = f32[320,512]{1,0:T(8,128)S(1)} collective-permute-done((f32[320,512]{1,0:T(8,128)S(1)}, f32[320,512]{1,0:T(8,128)S(1)}, u32[]{:S(2)}, u32[]{:S(2)}) %collective-permute-start.48) | collective-permute-done | bytes 655392 | tf_op jit(solution)/shard_map/ppermute | solution.py:765
  140.4 1.5 collective-permute-start.52
  142.6 1.4 collective-permute-start.51
  144.0 1.4 collective-permute-start.50
  145.3 3.6 %collective-permute-done.46.got_ref = f32[96,512]{1,0:T(8,128)S(1)} collective-permute-done((f32[96,512]{1,0:T(8,128)S(1)}, f32[96,512]{1,0:T(8,128)S(1)}, u32[]{:S(2)}, u32[]{:S(2)}) %collective-permute-start.46) | collective-permute-done | bytes 196640 | tf_op jit(solution)/shard_map/ppermute | solution.py:765
  149.0 5.5 %collective-permute-done.45 = f32[64,128]{1,0:T(8,128)S(1)} collective-permute-done((f32[64,128]{1,0:T(8,128)S(1)}, f32[64,128]{1,0:T(8,128)S(1)}, u32[]{:S(2)}, u32[]{:S(2)}) %collective-permute-start.45) | collective-permute-done | bytes 32800 | tf_op jit(solution)/shard_map/ppermute | solution.py:760
  157.3 3.6 %collective-permute-done.49 = f32[64,128]{1,0:T(8,128)S(1)} collective-permute-done((f32[64,128]{1,0:T(8,128)S(1)}, f32[64,128]{1,0:T(8,128)S(1)}, u32[]{:S(2)}, u32[]{:S(2)}) %collective-permute-start.49) | collective-permute-done | bytes 32800 | tf_op jit(solution)/shard_map/ppermute | solution.py:760
  160.9 1.2 collective-permute-start.58
  163.0 1.6 collective-permute-start.64
  164.6 4.7 %collective-permute-done.58 = f32[48,512]{1,0:T(8,128)S(1)} collective-permute-done((f32[48,512]{1,0:T(8,128)S(1)}, f32[48,512]{1,0:T(8,128)S(1)}, u32[]{:S(2)}, u32[]{:S(2)}) %collective-permute-start.58) | collective-permute-done | bytes 98336 | tf_op jit(solution)/shard_map/ppermute | solution.py:760
  169.4 1.9 collective-permute-start.67
  171.4 3.0 %collective-permute-start.57 = (f32[48,512]{1,0:T(8,128)S(1)}, f32[48,512]{1,0:T(8,128)S(1)}, u32[]{:S(2)}, u32[]{:S(2)}) collective-permute-start(f32[48,512]{1,0:T(8,128)S(1)} %add.128), channel_id=1, source_target_pairs={{0,4},{1,5},{2,6},{3,7},{4,0},{5,1},{6,2},{7,3},{8,12},{9,13},{10,... | collective-permute-start | bytes 294920 | tf_op jit(solution)/shard_map/ppermute | solution.py:760
  174.4 6.0 %collective-permute-done.60 = f32[48,512]{1,0:T(8,128)S(1)} collective-permute-done((f32[48,512]{1,0:T(8,128)S(1)}, f32[48,512]{1,0:T(8,128)S(1)}, u32[]{:S(2)}, u32[]{:S(2)}) %collective-permute-start.60) | collective-permute-done | bytes 98336 | tf_op jit(solution)/shard_map/ppermute | solution.py:760
  180.4 1.3 collective-permute-done.57
  181.9 2.0 collective-permute-start.63
  183.9 5.6 %collective-permute-done.63.got_ref = f32[48,512]{1,0:T(8,128)S(1)} collective-permute-done((f32[48,512]{1,0:T(8,128)S(1)}, f32[48,512]{1,0:T(8,128)S(1)}, u32[]{:S(2)}, u32[]{:S(2)}) %collective-permute-start.63) | collective-permute-done | bytes 98336 | tf_op jit(solution)/shard_map/ppermute | solution.py:760
  189.7 1.3 collective-permute-start.69
  192.1 12.4 %collective-permute-done.65.got_ref = f32[96,512]{1,0:T(8,128)S(1)} collective-permute-done((f32[96,512]{1,0:T(8,128)S(1)}, f32[96,512]{1,0:T(8,128)S(1)}, u32[]{:S(2)}, u32[]{:S(2)}) %collective-permute-start.65) | collective-permute-done | bytes 196640 | tf_op jit(solution)/shard_map/ppermute | solution.py:765
  204.8 2.0 collective-permute-start.72
  206.8 1.3 collective-permute-start.68
  208.1 11.5 %collective-permute-done.72.got_ref = f32[192,512]{1,0:T(8,128)S(1)} collective-permute-done((f32[192,512]{1,0:T(8,128)S(1)}, f32[192,512]{1,0:T(8,128)S(1)}, u32[]{:S(2)}, u32[]{:S(2)}) %collective-permute-start.72) | collective-permute-done | bytes 393248 | tf_op jit(solution)/shard_map/ppermute | solution.py:765
  221.7 6.7 %collective-permute-done.73.got_ref = f32[192,512]{1,0:T(8,128)S(1)} collective-permute-done((f32[192,512]{1,0:T(8,128)S(1)}, f32[192,512]{1,0:T(8,128)S(1)}, u32[]{:S(2)}, u32[]{:S(2)}) %collective-permute-start.73) | collective-permute-done | bytes 393248 | tf_op jit(solution)/shard_map/ppermute | solution.py:765
  228.7 3.3 %collective-permute-done.53 = f32[64,128]{1,0:T(8,128)S(1)} collective-permute-done((f32[64,128]{1,0:T(8,128)S(1)}, f32[64,128]{1,0:T(8,128)S(1)}, u32[]{:S(2)}, u32[]{:S(2)}) %collective-permute-start.53) | collective-permute-done | bytes 32800 | tf_op jit(solution)/shard_map/ppermute | solution.py:760
  232.9 4.1 %collective-permute-done.56 = f32[64,128]{1,0:T(8,128)S(1)} collective-permute-done((f32[64,128]{1,0:T(8,128)S(1)}, f32[64,128]{1,0:T(8,128)S(1)}, u32[]{:S(2)}, u32[]{:S(2)}) %collective-permute-start.56) | collective-permute-done | bytes 32800 | tf_op jit(solution)/shard_map/ppermute | solution.py:760
  237.0 2.7 %leave.1 = (f32[4,256,512]{2,1,0:T(8,128)}, f32[2,512]{1,0:T(2,128)}, f32[2,512]{1,0:T(2,128)}, f32[2,512]{1,0:T(2,128)}, f32[2,512]{1,0:T(2,128)}, /*index=5*/f...) custom-call(f32[64,128]{1,0:T(8,128)S(1)} %add.130.st_ref, ...), custom_call_target="tpu_custom_call" | custom-call | tf_op jit(solution)/shard_map/leave/pallas_call | solution.py:28
  240.0 2.3 drives.1
  242.3 3.6 %maps.1 = (f32[2,512,512]{2,1,0:T(8,128)}, f32[2,768,512]{2,1,0:T(8,128)}, f32[1280,512]{1,0:T(8,128)}) custom-call(f32[1280,512]{1,0:T(8,128)S(1)} %join.26.wc1_ref, f32[640,512]{1,0:T(8,128)S(1)} %join.23.own_ref, f32[640,512]{1,0:T(8,128)S(1)} %collective-permute-done.77.got_ref), custom_call_target="tpu_custom_call" | custom-call | tf_op jit(solution)/shard_map/maps/pallas_call | solution.py:28
  (192 shorter events, 47.0 us)
Async XLA Ops:
  5.8 5.0 %collective-permute-start.3 = (f32[24,128]{1,0:T(8,128)S(1)}, f32[24,128]{1,0:T(8,128)S(1)}, u32[]{:S(2)}, u32[]{:S(2)}) collective-permute-start(f32[24,128]{1,0:T(8,128)S(1)} %add.102), channel_id=1, source_target_pairs={{0,25},{1,24},{2,27},{3,26},{4,29},{5,28},{6,31},{7,30},{8,17},{9,... | collective-permute-start | bytes 36872 | tf_op jit(solution)/shard_map/ppermute | solution.py:760
  12.9 11.9 %collective-permute-start.6 = (f32[24,128]{1,0:T(8,128)S(1)}, f32[24,128]{1,0:T(8,128)S(1)}, u32[]{:S(2)}, u32[]{:S(2)}) collective-permute-start(f32[24,128]{1,0:T(8,128)S(1)} %add_add_fusion.1), channel_id=1, source_target_pairs={{0,7},{1,6},{2,5},{3,4},{4,3},{5,2},{6,1},{7,0},{8,15},{9,14},{10,... | collective-permute-start | bytes 36872 | tf_op jit(solution)/shard_map/ppermute | solution.py:760
  16.3 8.5 %collective-permute-start.5 = (f32[24,128]{1,0:T(8,128)S(1)}, f32[24,128]{1,0:T(8,128)S(1)}, u32[]{:S(2)}, u32[]{:S(2)}) collective-permute-start(f32[24,128]{1,0:T(8,128)S(1)} %add_add_fusion.1), channel_id=1, source_target_pairs={{0,5},{1,4},{2,7},{3,6},{4,1},{5,0},{6,3},{7,2},{8,13},{9,12},{10,... | collective-permute-start | bytes 36872 | tf_op jit(solution)/shard_map/ppermute | solution.py:760
  16.3 8.5 %collective-permute-start.4 = (f32[24,128]{1,0:T(8,128)S(1)}, f32[24,128]{1,0:T(8,128)S(1)}, u32[]{:S(2)}, u32[]{:S(2)}) collective-permute-start(f32[24,128]{1,0:T(8,128)S(1)} %add_add_fusion.1), channel_id=1, source_target_pairs={{0,3},{1,2},{2,1},{3,0},{4,7},{5,6},{6,5},{7,4},{8,11},{9,10},{10,... | collective-permute-start | bytes 36872 | tf_op jit(solution)/shard_map/ppermute | solution.py:760
  30.0 5.1 %collective-permute-start.10 = (f32[8,768]{1,0:T(8,128)S(1)}, f32[8,768]{1,0:T(8,128)S(1)}, u32[]{:S(2)}, u32[]{:S(2)}) collective-permute-start(f32[8,768]{1,0:T(8,128)S(1)} %combine.4.refs_0_), channel_id=1, source_target_pairs={{0,7},{1,6},{2,5},{3,4},{4,3},{5,2},{6,1},{7,0},{8,15},{9,14},{10,... | collective-permute-start | bytes 73736 | tf_op jit(solution)/shard_map/ppermute | solution.py:760
  33.5 4.2 %collective-permute-start.9 = (f32[8,768]{1,0:T(8,128)S(1)}, f32[8,768]{1,0:T(8,128)S(1)}, u32[]{:S(2)}, u32[]{:S(2)}) collective-permute-start(f32[8,768]{1,0:T(8,128)S(1)} %combine.4.refs_0_), channel_id=1, source_target_pairs={{0,5},{1,4},{2,7},{3,6},{4,1},{5,0},{6,3},{7,2},{8,13},{9,12},{10,... | collective-permute-start | bytes 73736 | tf_op jit(solution)/shard_map/ppermute | solution.py:760
  33.5 4.2 %collective-permute-start.8 = (f32[8,768]{1,0:T(8,128)S(1)}, f32[8,768]{1,0:T(8,128)S(1)}, u32[]{:S(2)}, u32[]{:S(2)}) collective-permute-start(f32[8,768]{1,0:T(8,128)S(1)} %combine.4.refs_0_), channel_id=1, source_target_pairs={{0,3},{1,2},{2,1},{3,0},{4,7},{5,6},{6,5},{7,4},{8,11},{9,10},{10,... | collective-permute-start | bytes 73736 | tf_op jit(solution)/shard_map/ppermute | solution.py:760
  43.7 4.0 %collective-permute-start.14 = (f32[16,128]{1,0:T(8,128)S(1)}, f32[16,128]{1,0:T(8,128)S(1)}, u32[]{:S(2)}, u32[]{:S(2)}) collective-permute-start(f32[16,128]{1,0:T(8,128)S(1)} %add.109), channel_id=1, source_target_pairs={{0,25},{1,24},{2,27},{3,26},{4,29},{5,28},{6,31},{7,30},{8,17},{9,... | collective-permute-start | bytes 24584 | tf_op jit(solution)/shard_map/ppermute | solution.py:760
  48.5 4.9 %collective-permute-start.17 = (f32[16,128]{1,0:T(8,128)S(1)}, f32[16,128]{1,0:T(8,128)S(1)}, u32[]{:S(2)}, u32[]{:S(2)}) collective-permute-start(f32[16,128]{1,0:T(8,128)S(1)} %add_add_fusion.5), channel_id=1, source_target_pairs={{0,7},{1,6},{2,5},{3,4},{4,3},{5,2},{6,1},{7,0},{8,15},{9,14},{10,... | collective-permute-start | bytes 24584 | tf_op jit(solution)/shard_map/ppermute | solution.py:760
  50.1 4.0 %collective-permute-start.16 = (f32[16,128]{1,0:T(8,128)S(1)}, f32[16,128]{1,0:T(8,128)S(1)}, u32[]{:S(2)}, u32[]{:S(2)}) collective-permute-start(f32[16,128]{1,0:T(8,128)S(1)} %add_add_fusion.5), channel_id=1, source_target_pairs={{0,5},{1,4},{2,7},{3,6},{4,1},{5,0},{6,3},{7,2},{8,13},{9,12},{10,... | collective-permute-start | bytes 24584 | tf_op jit(solution)/shard_map/ppermute | solution.py:760
  50.3 3.8 %collective-permute-start.15 = (f32[16,128]{1,0:T(8,128)S(1)}, f32[16,128]{1,0:T(8,128)S(1)}, u32[]{:S(2)}, u32[]{:S(2)}) collective-permute-start(f32[16,128]{1,0:T(8,128)S(1)} %add_add_fusion.5), channel_id=1, source_target_pairs={{0,3},{1,2},{2,1},{3,0},{4,7},{5,6},{6,5},{7,4},{8,11},{9,10},{10,... | collective-permute-start | bytes 24584 | tf_op jit(solution)/shard_map/ppermute | solution.py:760
  57.8 5.1 %collective-permute-start.21 = (f32[8,768]{1,0:T(8,128)S(1)}, f32[8,768]{1,0:T(8,128)S(1)}, u32[]{:S(2)}, u32[]{:S(2)}) collective-permute-start(f32[8,768]{1,0:T(8,128)S(1)} %combine.5.refs_0_), channel_id=1, source_target_pairs={{0,7},{1,6},{2,5},{3,4},{4,3},{5,2},{6,1},{7,0},{8,15},{9,14},{10,... | collective-permute-start | bytes 73736 | tf_op jit(solution)/shard_map/ppermute | solution.py:760
  59.8 4.5 %collective-permute-start.20 = (f32[8,768]{1,0:T(8,128)S(1)}, f32[8,768]{1,0:T(8,128)S(1)}, u32[]{:S(2)}, u32[]{:S(2)}) collective-permute-start(f32[8,768]{1,0:T(8,128)S(1)} %combine.5.refs_0_), channel_id=1, source_target_pairs={{0,5},{1,4},{2,7},{3,6},{4,1},{5,0},{6,3},{7,2},{8,13},{9,12},{10,... | collective-permute-start | bytes 73736 | tf_op jit(solution)/shard_map/ppermute | solution.py:760
  60.6 3.7 %collective-permute-start.19 = (f32[8,768]{1,0:T(8,128)S(1)}, f32[8,768]{1,0:T(8,128)S(1)}, u32[]{:S(2)}, u32[]{:S(2)}) collective-permute-start(f32[8,768]{1,0:T(8,128)S(1)} %combine.5.refs_0_), channel_id=1, source_target_pairs={{0,3},{1,2},{2,1},{3,0},{4,7},{5,6},{6,5},{7,4},{8,11},{9,10},{10,... | collective-permute-start | bytes 73736 | tf_op jit(solution)/shard_map/ppermute | solution.py:760
  79.6 17.8 %collective-permute-start.31 = (f32[320,512]{1,0:T(8,128)S(1)}, f32[320,512]{1,0:T(8,128)S(1)}, u32[]{:S(2)}, u32[]{:S(2)}) collective-permute-start(f32[320,512]{1,0:T(8,128)S(1)} %get-tuple-element.226), channel_id=1, source_target_pairs={{0,8},{1,17},{2,10},{3,19},{4,12},{5,21},{6,14},{7,23},{8,0},{9,25... | collective-permute-start | bytes 1966088 | tf_op jit(solution)/shard_map/ppermute | solution.py:765
  82.4 5.1 %collective-permute-start.25 = (f32[8,768]{1,0:T(8,128)S(1)}, f32[8,768]{1,0:T(8,128)S(1)}, u32[]{:S(2)}, u32[]{:S(2)}) collective-permute-start(f32[8,768]{1,0:T(8,128)S(1)} %combine.6.refs_0_), channel_id=1, source_target_pairs={{0,7},{1,6},{2,5},{3,4},{4,3},{5,2},{6,1},{7,0},{8,15},{9,14},{10,... | collective-permute-start | bytes 73736 | tf_op jit(solution)/shard_map/ppermute | solution.py:760
  84.3 4.3 %collective-permute-start.24 = (f32[8,768]{1,0:T(8,128)S(1)}, f32[8,768]{1,0:T(8,128)S(1)}, u32[]{:S(2)}, u32[]{:S(2)}) collective-permute-start(f32[8,768]{1,0:T(8,128)S(1)} %combine.6.refs_0_), channel_id=1, source_target_pairs={{0,5},{1,4},{2,7},{3,6},{4,1},{5,0},{6,3},{7,2},{8,13},{9,12},{10,... | collective-permute-start | bytes 73736 | tf_op jit(solution)/shard_map/ppermute | solution.py:760
  84.6 4.0 %collective-permute-start.23 = (f32[8,768]{1,0:T(8,128)S(1)}, f32[8,768]{1,0:T(8,128)S(1)}, u32[]{:S(2)}, u32[]{:S(2)}) collective-permute-start(f32[8,768]{1,0:T(8,128)S(1)} %combine.6.refs_0_), channel_id=1, source_target_pairs={{0,3},{1,2},{2,1},{3,0},{4,7},{5,6},{6,5},{7,4},{8,11},{9,10},{10,... | collective-permute-start | bytes 73736 | tf_op jit(solution)/shard_map/ppermute | solution.py:760
  94.4 4.6 %collective-permute-start.30 = (f32[16,128]{1,0:T(8,128)S(1)}, f32[16,128]{1,0:T(8,128)S(1)}, u32[]{:S(2)}, u32[]{:S(2)}) collective-permute-start(f32[16,128]{1,0:T(8,128)S(1)} %add.116), channel_id=1, source_target_pairs={{0,25},{1,24},{2,27},{3,26},{4,29},{5,28},{6,31},{7,30},{8,17},{9,... | collective-permute-start | bytes 24584 | tf_op jit(solution)/shard_map/ppermute | solution.py:760
  97.4 14.7 %collective-permute-start.39 = (f32[160,512]{1,0:T(8,128)S(1)}, f32[160,512]{1,0:T(8,128)S(1)}, u32[]{:S(2)}, u32[]{:S(2)}) collective-permute-start(f32[160,512]{1,0:T(8,128)S(1)} %get-tuple-element.245), channel_id=1, source_target_pairs={{0,16},{1,9},{2,18},{3,11},{4,20},{5,13},{6,22},{7,15},{8,24},{9,1... | collective-permute-start | bytes 983048 | tf_op jit(solution)/shard_map/ppermute | solution.py:765
  100.1 4.9 %collective-permute-start.34 = (f32[16,128]{1,0:T(8,128)S(1)}, f32[16,128]{1,0:T(8,128)S(1)}, u32[]{:S(2)}, u32[]{:S(2)}) collective-permute-start(f32[16,128]{1,0:T(8,128)S(1)} %add_add_fusion.3), channel_id=1, source_target_pairs={{0,7},{1,6},{2,5},{3,4},{4,3},{5,2},{6,1},{7,0},{8,15},{9,14},{10,... | collective-permute-start | bytes 24584 | tf_op jit(solution)/shard_map/ppermute | solution.py:760
  101.9 4.0 %collective-permute-start.33 = (f32[16,128]{1,0:T(8,128)S(1)}, f32[16,128]{1,0:T(8,128)S(1)}, u32[]{:S(2)}, u32[]{:S(2)}) collective-permute-start(f32[16,128]{1,0:T(8,128)S(1)} %add_add_fusion.3), channel_id=1, source_target_pairs={{0,5},{1,4},{2,7},{3,6},{4,1},{5,0},{6,3},{7,2},{8,13},{9,12},{10,... | collective-permute-start | bytes 24584 | tf_op jit(solution)/shard_map/ppermute | solution.py:760
  102.4 3.5 %collective-permute-start.32 = (f32[16,128]{1,0:T(8,128)S(1)}, f32[16,128]{1,0:T(8,128)S(1)}, u32[]{:S(2)}, u32[]{:S(2)}) collective-permute-start(f32[16,128]{1,0:T(8,128)S(1)} %add_add_fusion.3), channel_id=1, source_target_pairs={{0,3},{1,2},{2,1},{3,0},{4,7},{5,6},{6,5},{7,4},{8,11},{9,10},{10,... | collective-permute-start | bytes 24584 | tf_op jit(solution)/shard_map/ppermute | solution.py:760
  112.3 12.2 %collective-permute-start.40 = (f32[640,512]{1,0:T(8,128)S(1)}, f32[640,512]{1,0:T(8,128)S(1)}, u32[]{:S(2)}, u32[]{:S(2)}) collective-permute-start(f32[640,512]{1,0:T(8,128)S(1)} %split.6), channel_id=1, source_target_pairs={{0,1},{1,0},{2,3},{3,2},{4,5},{5,4},{6,7},{7,6},{8,9},{9,8},{10,11... | collective-permute-start | bytes 3932168 | tf_op jit(solution)/shard_map/ppermute | solution.py:760
  112.7 3.8 %collective-permute-start.41 = (f32[384,512]{1,0:T(8,128)S(1)}, f32[384,512]{1,0:T(8,128)S(1)}, u32[]{:S(2)}, u32[]{:S(2)}) collective-permute-start(f32[384,512]{1,0:T(8,128)S(1)} %split.5), channel_id=1, source_target_pairs={{0,1},{1,0},{2,3},{3,2},{4,5},{5,4},{6,7},{7,6},{8,9},{9,8},{10,11... | collective-permute-start | bytes 2359304 | tf_op jit(solution)/shard_map/ppermute | solution.py:760
  116.6 7.8 %collective-permute-start.42 = (f32[192,512]{1,0:T(8,128)S(1)}, f32[192,512]{1,0:T(8,128)S(1)}, u32[]{:S(2)}, u32[]{:S(2)}) collective-permute-start(f32[192,512]{1,0:T(8,128)S(1)} %get-tuple-element.264), channel_id=1, source_target_pairs={{0,8},{1,17},{2,10},{3,19},{4,12},{5,21},{6,14},{7,23},{8,0},{9,25... | collective-permute-start | bytes 1179656 | tf_op jit(solution)/shard_map/ppermute | solution.py:765
  118.7 6.0 %collective-permute-start.38 = (f32[8,768]{1,0:T(8,128)S(1)}, f32[8,768]{1,0:T(8,128)S(1)}, u32[]{:S(2)}, u32[]{:S(2)}) collective-permute-start(f32[8,768]{1,0:T(8,128)S(1)} %combine.7.refs_0_), channel_id=1, source_target_pairs={{0,7},{1,6},{2,5},{3,4},{4,3},{5,2},{6,1},{7,0},{8,15},{9,14},{10,... | collective-permute-start | bytes 73736 | tf_op jit(solution)/shard_map/ppermute | solution.py:760
  120.2 4.5 %collective-permute-start.37 = (f32[8,768]{1,0:T(8,128)S(1)}, f32[8,768]{1,0:T(8,128)S(1)}, u32[]{:S(2)}, u32[]{:S(2)}) collective-permute-start(f32[8,768]{1,0:T(8,128)S(1)} %combine.7.refs_0_), channel_id=1, source_target_pairs={{0,5},{1,4},{2,7},{3,6},{4,1},{5,0},{6,3},{7,2},{8,13},{9,12},{10,... | collective-permute-start | bytes 73736 | tf_op jit(solution)/shard_map/ppermute | solution.py:760
  121.1 3.9 %collective-permute-start.36 = (f32[8,768]{1,0:T(8,128)S(1)}, f32[8,768]{1,0:T(8,128)S(1)}, u32[]{:S(2)}, u32[]{:S(2)}) collective-permute-start(f32[8,768]{1,0:T(8,128)S(1)} %combine.7.refs_0_), channel_id=1, source_target_pairs={{0,3},{1,2},{2,1},{3,0},{4,7},{5,6},{6,5},{7,4},{8,11},{9,10},{10,... | collective-permute-start | bytes 73736 | tf_op jit(solution)/shard_map/ppermute | solution.py:760
  129.5 10.8 %collective-permute-start.47 = (f32[384,512]{1,0:T(8,128)S(1)}, f32[384,512]{1,0:T(8,128)S(1)}, u32[]{:S(2)}, u32[]{:S(2)}) collective-permute-start(f32[384,512]{1,0:T(8,128)S(1)} %split.7), channel_id=1, source_target_pairs={{0,1},{1,0},{2,3},{3,2},{4,5},{5,4},{6,7},{7,6},{8,9},{9,8},{10,11... | collective-permute-start | bytes 2359304 | tf_op jit(solution)/shard_map/ppermute | solution.py:760
  129.6 10.6 %collective-permute-start.48 = (f32[320,512]{1,0:T(8,128)S(1)}, f32[320,512]{1,0:T(8,128)S(1)}, u32[]{:S(2)}, u32[]{:S(2)}) collective-permute-start(f32[320,512]{1,0:T(8,128)S(1)} %get-tuple-element.270), channel_id=1, source_target_pairs={{0,8},{1,17},{2,10},{3,19},{4,12},{5,21},{6,14},{7,23},{8,0},{9,25... | collective-permute-start | bytes 1966088 | tf_op jit(solution)/shard_map/ppermute | solution.py:765
  131.1 6.3 %collective-permute-start.44 = (f32[80,512]{1,0:T(8,128)S(1)}, f32[80,512]{1,0:T(8,128)S(1)}, u32[]{:S(2)}, u32[]{:S(2)}) collective-permute-start(f32[80,512]{1,0:T(8,128)S(1)} %get-tuple-element.259), channel_id=1, source_target_pairs={{0,2},{1,3},{2,0},{3,1},{4,6},{5,7},{6,4},{7,5},{8,10},{9,11},{10,... | collective-permute-start | bytes 491528 | tf_op jit(solution)/shard_map/ppermute | solution.py:760
  132.2 5.3 %collective-permute-start.43 = (f32[64,128]{1,0:T(8,128)S(1)}, f32[64,128]{1,0:T(8,128)S(1)}, u32[]{:S(2)}, u32[]{:S(2)}) collective-permute-start(f32[64,128]{1,0:T(8,128)S(1)} %get-tuple-element.290), channel_id=1, source_target_pairs={{0,1},{1,0},{2,3},{3,2},{4,5},{5,4},{6,7},{7,6},{8,9},{9,8},{10,11... | collective-permute-start | bytes 98312 | tf_op jit(solution)/shard_map/ppermute | solution.py:760
  140.4 14.0 %collective-permute-start.52 = (f32[192,512]{1,0:T(8,128)S(1)}, f32[192,512]{1,0:T(8,128)S(1)}, u32[]{:S(2)}, u32[]{:S(2)}) collective-permute-start(f32[192,512]{1,0:T(8,128)S(1)} %get-tuple-element.300), channel_id=1, source_target_pairs={{0,8},{1,17},{2,10},{3,19},{4,12},{5,21},{6,14},{7,23},{8,0},{9,25... | collective-permute-start | bytes 1179656 | tf_op jit(solution)/shard_map/ppermute | solution.py:765
  141.9 7.0 %collective-permute-start.46 = (f32[96,512]{1,0:T(8,128)S(1)}, f32[96,512]{1,0:T(8,128)S(1)}, u32[]{:S(2)}, u32[]{:S(2)}) collective-permute-start(f32[96,512]{1,0:T(8,128)S(1)} %get-tuple-element.267), channel_id=1, source_target_pairs={{0,16},{1,9},{2,18},{3,11},{4,20},{5,13},{6,22},{7,15},{8,24},{9,1... | collective-permute-start | bytes 589832 | tf_op jit(solution)/shard_map/ppermute | solution.py:765
  142.6 12.5 %collective-permute-start.51 = (f32[160,512]{1,0:T(8,128)S(1)}, f32[160,512]{1,0:T(8,128)S(1)}, u32[]{:S(2)}, u32[]{:S(2)}) collective-permute-start(f32[160,512]{1,0:T(8,128)S(1)} %get-tuple-element.297), channel_id=1, source_target_pairs={{0,16},{1,9},{2,18},{3,11},{4,20},{5,13},{6,22},{7,15},{8,24},{9,1... | collective-permute-start | bytes 983048 | tf_op jit(solution)/shard_map/ppermute | solution.py:765
  144.0 10.5 %collective-permute-start.45 = (f32[64,128]{1,0:T(8,128)S(1)}, f32[64,128]{1,0:T(8,128)S(1)}, u32[]{:S(2)}, u32[]{:S(2)}) collective-permute-start(f32[64,128]{1,0:T(8,128)S(1)} %add.124), channel_id=1, source_target_pairs={{0,9},{1,8},{2,11},{3,10},{4,13},{5,12},{6,15},{7,14},{8,1},{9,0},... | collective-permute-start | bytes 98312 | tf_op jit(solution)/shard_map/ppermute | solution.py:760
  144.0 12.3 %collective-permute-start.50 = (f32[80,512]{1,0:T(8,128)S(1)}, f32[80,512]{1,0:T(8,128)S(1)}, u32[]{:S(2)}, u32[]{:S(2)}) collective-permute-start(f32[80,512]{1,0:T(8,128)S(1)} %add.123), channel_id=1, source_target_pairs={{0,4},{1,5},{2,6},{3,7},{4,0},{5,1},{6,2},{7,3},{8,12},{9,13},{10,... | collective-permute-start | bytes 491528 | tf_op jit(solution)/shard_map/ppermute | solution.py:760
  154.5 6.3 %collective-permute-start.55 = (f32[96,512]{1,0:T(8,128)S(1)}, f32[96,512]{1,0:T(8,128)S(1)}, u32[]{:S(2)}, u32[]{:S(2)}) collective-permute-start(f32[96,512]{1,0:T(8,128)S(1)} %get-tuple-element.311), channel_id=1, source_target_pairs={{0,16},{1,9},{2,18},{3,11},{4,20},{5,13},{6,22},{7,15},{8,24},{9,1... | collective-permute-start | bytes 589832 | tf_op jit(solution)/shard_map/ppermute | solution.py:765
  155.1 7.9 %collective-permute-start.59 = (f32[80,512]{1,0:T(8,128)S(1)}, f32[80,512]{1,0:T(8,128)S(1)}, u32[]{:S(2)}, u32[]{:S(2)}) collective-permute-start(f32[80,512]{1,0:T(8,128)S(1)} %get-tuple-element.314), channel_id=1, source_target_pairs={{0,2},{1,3},{2,0},{3,1},{4,6},{5,7},{6,4},{7,5},{8,10},{9,11},{10,... | collective-permute-start | bytes 491528 | tf_op jit(solution)/shard_map/ppermute | solution.py:760
  156.3 13.1 %collective-permute-start.61 = (f32[80,512]{1,0:T(8,128)S(1)}, f32[80,512]{1,0:T(8,128)S(1)}, u32[]{:S(2)}, u32[]{:S(2)}) collective-permute-start(f32[80,512]{1,0:T(8,128)S(1)} %add.126.own_ref), channel_id=1, source_target_pairs={{0,2},{1,3},{2,0},{3,1},{4,6},{5,7},{6,4},{7,5},{8,10},{9,11},{10,... | collective-permute-start | bytes 491528 | tf_op jit(solution)/shard_map/ppermute | solution.py:760
  157.3 3.6 %collective-permute-start.49 = (f32[64,128]{1,0:T(8,128)S(1)}, f32[64,128]{1,0:T(8,128)S(1)}, u32[]{:S(2)}, u32[]{:S(2)}) collective-permute-start(f32[64,128]{1,0:T(8,128)S(1)} %add.125), channel_id=1, source_target_pairs={{0,17},{1,16},{2,19},{3,18},{4,21},{5,20},{6,23},{7,22},{8,25},{9,... | collective-permute-start | bytes 98312 | tf_op jit(solution)/shard_map/ppermute | solution.py:760
  160.9 8.5 %collective-permute-start.58 = (f32[48,512]{1,0:T(8,128)S(1)}, f32[48,512]{1,0:T(8,128)S(1)}, u32[]{:S(2)}, u32[]{:S(2)}) collective-permute-start(f32[48,512]{1,0:T(8,128)S(1)} %get-tuple-element.324), channel_id=1, source_target_pairs={{0,2},{1,3},{2,0},{3,1},{4,6},{5,7},{6,4},{7,5},{8,10},{9,11},{10,... | collective-permute-start | bytes 294920 | tf_op jit(solution)/shard_map/ppermute | solution.py:760
  162.2 9.2 %collective-permute-start.54 = (f32[48,512]{1,0:T(8,128)S(1)}, f32[48,512]{1,0:T(8,128)S(1)}, u32[]{:S(2)}, u32[]{:S(2)}) collective-permute-start(f32[48,512]{1,0:T(8,128)S(1)} %get-tuple-element.303), channel_id=1, source_target_pairs={{0,2},{1,3},{2,0},{3,1},{4,6},{5,7},{6,4},{7,5},{8,10},{9,11},{10,... | collective-permute-start | bytes 294920 | tf_op jit(solution)/shard_map/ppermute | solution.py:760
  163.0 18.8 %collective-permute-start.64 = (f32[80,512]{1,0:T(8,128)S(1)}, f32[80,512]{1,0:T(8,128)S(1)}, u32[]{:S(2)}, u32[]{:S(2)}) collective-permute-start(f32[80,512]{1,0:T(8,128)S(1)} %add.131), channel_id=1, source_target_pairs={{0,4},{1,5},{2,6},{3,7},{4,0},{5,1},{6,2},{7,3},{8,12},{9,13},{10,... | collective-permute-start | bytes 491528 | tf_op jit(solution)/shard_map/ppermute | solution.py:760
  169.4 20.1 %collective-permute-start.67 = (f32[160,512]{1,0:T(8,128)S(1)}, f32[160,512]{1,0:T(8,128)S(1)}, u32[]{:S(2)}, u32[]{:S(2)}) collective-permute-start(f32[160,512]{1,0:T(8,128)S(1)} %join.14.own_ref), channel_id=1, source_target_pairs={{0,16},{1,9},{2,18},{3,11},{4,20},{5,13},{6,22},{7,15},{8,24},{9,1... | collective-permute-start | bytes 983048 | tf_op jit(solution)/shard_map/ppermute | solution.py:765
  171.3 9.1 %collective-permute-start.60 = (f32[48,512]{1,0:T(8,128)S(1)}, f32[48,512]{1,0:T(8,128)S(1)}, u32[]{:S(2)}, u32[]{:S(2)}) collective-permute-start(f32[48,512]{1,0:T(8,128)S(1)} %add.132), channel_id=1, source_target_pairs={{0,4},{1,5},{2,6},{3,7},{4,0},{5,1},{6,2},{7,3},{8,12},{9,13},{10,... | collective-permute-start | bytes 294920 | tf_op jit(solution)/shard_map/ppermute | solution.py:760
  171.4 10.4 %collective-permute-start.57 = (f32[48,512]{1,0:T(8,128)S(1)}, f32[48,512]{1,0:T(8,128)S(1)}, u32[]{:S(2)}, u32[]{:S(2)}) collective-permute-start(f32[48,512]{1,0:T(8,128)S(1)} %add.128), channel_id=1, source_target_pairs={{0,4},{1,5},{2,6},{3,7},{4,0},{5,1},{6,2},{7,3},{8,12},{9,13},{10,... | collective-permute-start | bytes 294920 | tf_op jit(solution)/shard_map/ppermute | solution.py:760
  181.8 7.8 %collective-permute-start.66 = (f32[80,512]{1,0:T(8,128)S(1)}, f32[80,512]{1,0:T(8,128)S(1)}, u32[]{:S(2)}, u32[]{:S(2)}) collective-permute-start(f32[80,512]{1,0:T(8,128)S(1)} %add.135.own_ref), channel_id=1, source_target_pairs={{0,2},{1,3},{2,0},{3,1},{4,6},{5,7},{6,4},{7,5},{8,10},{9,11},{10,... | collective-permute-start | bytes 491528 | tf_op jit(solution)/shard_map/ppermute | solution.py:760
  181.9 7.6 %collective-permute-start.63 = (f32[48,512]{1,0:T(8,128)S(1)}, f32[48,512]{1,0:T(8,128)S(1)}, u32[]{:S(2)}, u32[]{:S(2)}) collective-permute-start(f32[48,512]{1,0:T(8,128)S(1)} %add.133.own_ref), channel_id=1, source_target_pairs={{0,2},{1,3},{2,0},{3,1},{4,6},{5,7},{6,4},{7,5},{8,10},{9,11},{10,... | collective-permute-start | bytes 294920 | tf_op jit(solution)/shard_map/ppermute | solution.py:760
  189.7 14.9 %collective-permute-start.69 = (f32[160,512]{1,0:T(8,128)S(1)}, f32[160,512]{1,0:T(8,128)S(1)}, u32[]{:S(2)}, u32[]{:S(2)}) collective-permute-start(f32[160,512]{1,0:T(8,128)S(1)} %join.17.own_ref), channel_id=1, source_target_pairs={{0,16},{1,9},{2,18},{3,11},{4,20},{5,13},{6,22},{7,15},{8,24},{9,1... | collective-permute-start | bytes 983048 | tf_op jit(solution)/shard_map/ppermute | solution.py:765
  191.0 13.5 %collective-permute-start.65 = (f32[96,512]{1,0:T(8,128)S(1)}, f32[96,512]{1,0:T(8,128)S(1)}, u32[]{:S(2)}, u32[]{:S(2)}) collective-permute-start(f32[96,512]{1,0:T(8,128)S(1)} %join.15.own_ref), channel_id=1, source_target_pairs={{0,16},{1,9},{2,18},{3,11},{4,20},{5,13},{6,22},{7,15},{8,24},{9,1... | collective-permute-start | bytes 589832 | tf_op jit(solution)/shard_map/ppermute | solution.py:765
  191.8 12.8 %collective-permute-start.62 = (f32[48,512]{1,0:T(8,128)S(1)}, f32[48,512]{1,0:T(8,128)S(1)}, u32[]{:S(2)}, u32[]{:S(2)}) collective-permute-start(f32[48,512]{1,0:T(8,128)S(1)} %add.134.own_ref), channel_id=1, source_target_pairs={{0,2},{1,3},{2,0},{3,1},{4,6},{5,7},{6,4},{7,5},{8,10},{9,11},{10,... | collective-permute-start | bytes 294920 | tf_op jit(solution)/shard_map/ppermute | solution.py:760
  192.0 27.6 %collective-permute-start.71 = (f32[320,512]{1,0:T(8,128)S(1)}, f32[320,512]{1,0:T(8,128)S(1)}, u32[]{:S(2)}, u32[]{:S(2)}) collective-permute-start(f32[320,512]{1,0:T(8,128)S(1)} %join.16.own_ref), channel_id=1, source_target_pairs={{0,8},{1,17},{2,10},{3,19},{4,12},{5,21},{6,14},{7,23},{8,0},{9,25... | collective-permute-start | bytes 1966088 | tf_op jit(solution)/shard_map/ppermute | solution.py:765
  204.7 15.2 %collective-permute-start.70 = (f32[320,512]{1,0:T(8,128)S(1)}, f32[320,512]{1,0:T(8,128)S(1)}, u32[]{:S(2)}, u32[]{:S(2)}) collective-permute-start(f32[320,512]{1,0:T(8,128)S(1)} %join.20.own_ref), channel_id=1, source_target_pairs={{0,8},{1,17},{2,10},{3,19},{4,12},{5,21},{6,14},{7,23},{8,0},{9,25... | collective-permute-start | bytes 1966088 | tf_op jit(solution)/shard_map/ppermute | solution.py:765
  204.8 14.8 %collective-permute-start.72 = (f32[192,512]{1,0:T(8,128)S(1)}, f32[192,512]{1,0:T(8,128)S(1)}, u32[]{:S(2)}, u32[]{:S(2)}) collective-permute-start(f32[192,512]{1,0:T(8,128)S(1)} %join.18.own_ref), channel_id=1, source_target_pairs={{0,8},{1,17},{2,10},{3,19},{4,12},{5,21},{6,14},{7,23},{8,0},{9,25... | collective-permute-start | bytes 1179656 | tf_op jit(solution)/shard_map/ppermute | solution.py:765
  206.8 13.8 %collective-permute-start.68 = (f32[96,512]{1,0:T(8,128)S(1)}, f32[96,512]{1,0:T(8,128)S(1)}, u32[]{:S(2)}, u32[]{:S(2)}) collective-permute-start(f32[96,512]{1,0:T(8,128)S(1)} %join.19.own_ref), channel_id=1, source_target_pairs={{0,16},{1,9},{2,18},{3,11},{4,20},{5,13},{6,22},{7,15},{8,24},{9,1... | collective-permute-start | bytes 589832 | tf_op jit(solution)/shard_map/ppermute | solution.py:765
  219.8 19.9 %collective-permute-start.75 = (f32[640,512]{1,0:T(8,128)S(1)}, f32[640,512]{1,0:T(8,128)S(1)}, u32[]{:S(2)}, u32[]{:S(2)}) collective-permute-start(f32[640,512]{1,0:T(8,128)S(1)} %join.22.own_ref), channel_id=1, source_target_pairs={{0,1},{1,0},{2,3},{3,2},{4,5},{5,4},{6,7},{7,6},{8,9},{9,8},{10,11... | collective-permute-start | bytes 3932168 | tf_op jit(solution)/shard_map/ppermute | solution.py:760
  220.0 22.3 %collective-permute-start.77 = (f32[640,512]{1,0:T(8,128)S(1)}, f32[640,512]{1,0:T(8,128)S(1)}, u32[]{:S(2)}, u32[]{:S(2)}) collective-permute-start(f32[640,512]{1,0:T(8,128)S(1)} %join.23.own_ref), channel_id=1, source_target_pairs={{0,1},{1,0},{2,3},{3,2},{4,5},{5,4},{6,7},{7,6},{8,9},{9,8},{10,11... | collective-permute-start | bytes 3932168 | tf_op jit(solution)/shard_map/ppermute | solution.py:760
  220.6 7.8 %collective-permute-start.73 = (f32[192,512]{1,0:T(8,128)S(1)}, f32[192,512]{1,0:T(8,128)S(1)}, u32[]{:S(2)}, u32[]{:S(2)}) collective-permute-start(f32[192,512]{1,0:T(8,128)S(1)} %join.24.own_ref), channel_id=1, source_target_pairs={{0,8},{1,17},{2,10},{3,19},{4,12},{5,21},{6,14},{7,23},{8,0},{9,25... | collective-permute-start | bytes 1179656 | tf_op jit(solution)/shard_map/ppermute | solution.py:765
  220.7 19.0 %collective-permute-start.76 = (f32[384,512]{1,0:T(8,128)S(1)}, f32[384,512]{1,0:T(8,128)S(1)}, u32[]{:S(2)}, u32[]{:S(2)}) collective-permute-start(f32[384,512]{1,0:T(8,128)S(1)} %join.21.own_ref), channel_id=1, source_target_pairs={{0,1},{1,0},{2,3},{3,2},{4,5},{5,4},{6,7},{7,6},{8,9},{9,8},{10,11... | collective-permute-start | bytes 2359304 | tf_op jit(solution)/shard_map/ppermute | solution.py:760
  228.5 11.4 %collective-permute-start.74 = (f32[384,512]{1,0:T(8,128)S(1)}, f32[384,512]{1,0:T(8,128)S(1)}, u32[]{:S(2)}, u32[]{:S(2)}) collective-permute-start(f32[384,512]{1,0:T(8,128)S(1)} %join.25.own_ref), channel_id=1, source_target_pairs={{0,1},{1,0},{2,3},{3,2},{4,5},{5,4},{6,7},{7,6},{8,9},{9,8},{10,11... | collective-permute-start | bytes 2359304 | tf_op jit(solution)/shard_map/ppermute | solution.py:760
  228.6 3.4 %collective-permute-start.53 = (f32[64,128]{1,0:T(8,128)S(1)}, f32[64,128]{1,0:T(8,128)S(1)}, u32[]{:S(2)}, u32[]{:S(2)}) collective-permute-start(f32[64,128]{1,0:T(8,128)S(1)} %add.127), channel_id=1, source_target_pairs={{0,3},{1,2},{2,1},{3,0},{4,7},{5,6},{6,5},{7,4},{8,11},{9,10},{10,... | collective-permute-start | bytes 98312 | tf_op jit(solution)/shard_map/ppermute | solution.py:760
  232.0 5.0 %collective-permute-start.56 = (f32[64,128]{1,0:T(8,128)S(1)}, f32[64,128]{1,0:T(8,128)S(1)}, u32[]{:S(2)}, u32[]{:S(2)}) collective-permute-start(f32[64,128]{1,0:T(8,128)S(1)} %add.129), channel_id=1, source_target_pairs={{0,5},{1,4},{2,7},{3,6},{4,1},{5,0},{6,3},{7,2},{8,13},{9,12},{10,... | collective-permute-start | bytes 98312 | tf_op jit(solution)/shard_map/ppermute | solution.py:760
  (30 other events, 122.7 us)

commit v3 on v2

--- a/solution.py
+++ b/solution.py
@@ -16,24 +16,47 @@
 SUB = 8
 LANE = 128
 TILE = 256
+WORK = 5 * 10**9
 
 
 def in_vmem(count):
     return [pl.BlockSpec(memory_space=pltpu.VMEM)] * count
 
 
-def call(name, body, outs, args, scratch=(), scalars=0, results=0):
-    room = 6 * 1024 * 1024 + sum(4 * math.prod(item.shape) for item in list(scratch) + list(outs[:results]))
+class Order:
+    def __init__(self):
+        self.token = None
+
+
+def call(name, body, outs, args, scratch=(), scalars=0, results=0, order=None, token=0, far=(), alias=None, out_far=0, work=WORK):
+    room = 6 * 1024 * 1024 + sum(4 * math.prod(item.shape) for item in list(scratch) + list(outs[:results]) if hasattr(item, "shape"))
     specs = [pl.BlockSpec(memory_space=pltpu.SMEM)] * scalars + in_vmem(len(args) - scalars)
-    return pl.pallas_call(
-        body,
+    for k in far:
+        specs[k] = pl.BlockSpec(memory_space=pltpu.HBM)
+    count = len(args)
+    args = list(args)
+    run = body
+    if order is not None and order.token is not None:
+        args.append(order.token)
+        specs.append(pl.BlockSpec(memory_space=pl.ANY))
+        run = lambda *refs: body(*refs[:count], *refs[count + 1 :])
+    out_specs = in_vmem(len(outs))
+    for k in range(out_far):
+        out_specs[k] = pl.BlockSpec(memory_space=pltpu.HBM)
+    done = pl.pallas_call(
+        run,
         name=name,
         out_shape=outs,
         in_specs=specs,
-        out_specs=in_vmem(len(outs)),
+        out_specs=out_specs,
         scratch_shapes=list(scratch),
+        input_output_aliases=alias or {},
         compiler_params=pltpu.CompilerParams(vmem_limit_bytes=room),
+        cost_estimate=pl.CostEstimate(flops=work, bytes_accessed=1, transcendentals=0),
     )(*args)
+    if order is not None:
+        order.token = done[token]
+    return done
 
 
 def shaped(shape, dtype=F32):
@@ -297,12 +320,8 @@
     return jnp.where(x < 0.5, x * series, 1.0 - jnp.exp(-x))
 
 
-def k_prepare(starts_ref, rate_ref, rotation_ref, gain_ref, shift_ref, skip_ref, bias_ref,
-              keep_f_ref, keep_r_ref, kp_f_ref, kp_r_ref, kd_f_ref, kd_r_ref, par_ref, vec_ref):
+def all_starts(starts_ref):
     rows, segments = starts_ref.shape
-    steps = keep_f_ref.shape[0] // SUB
-    n = kd_f_ref.shape[0]
-    length = 2 * steps
     sub = lax.broadcasted_iota(jnp.int32, (SUB, LANE), 0)
     starts = []
     for k in range(segments):
@@ -310,41 +329,46 @@
         for r in range(rows):
             start = jnp.where(sub // 2 == r, starts_ref[r, k], start)
         starts.append(start)
-    base = lax.axis_index("tm") * length + (sub % 2) * steps
+    return starts
+
+
+def k_keep(reverse, starts_ref, keep_ref, kp_ref, kd_ref):
+    steps = keep_ref.shape[0] // SUB
+    n = kd_ref.shape[0]
+    length = 2 * steps
+    starts = all_starts(starts_ref)
+    sub = lax.broadcasted_iota(jnp.int32, (SUB, LANE), 0)
+    base = lax.axis_index("tm") * length + (sub % 2) * steps + (1 if reverse else 0)
     block = 8
 
     def fill(i, least):
-        t = lax.broadcasted_iota(jnp.int32, (block, SUB, LANE), 0) + i * block
-        place = t + base[None]
-        here = starts[0][None] == place
-        following = starts[0][None] == place + 1
+        place = lax.broadcasted_iota(jnp.int32, (block, SUB, LANE), 0) + i * block + base[None]
+        hit = starts[0][None] == place
         for start in starts[1:]:
-            here = here | (start[None] == place)
-            following = following | (start[None] == place + 1)
-        following = following | (place == n * length - 1)
-        here = jnp.where(here, 0.0, 1.0)
-        following = jnp.where(following, 0.0, 1.0)
-        at = pl.ds(pl.multiple_of(i * block * SUB, SUB), block * SUB)
-        keep_f_ref[at, :] = flat(here)
-        keep_r_ref[at, :] = flat(following)
-        return (jnp.minimum(least[0], jnp.min(here, axis=0)), jnp.minimum(least[1], jnp.min(following, axis=0)))
-
-    ones = jnp.ones((SUB, LANE), F32)
-    least = lax.fori_loop(0, steps // block, fill, (ones, ones))
-    kp_f_ref[...], kp_r_ref[...] = least
+            hit = hit | (start[None] == place)
+        if reverse:
+            hit = hit | (place == n * length)
+        keep = jnp.where(hit, 0.0, 1.0)
+        keep_ref[pl.ds(pl.multiple_of(i * block * SUB, SUB), block * SUB), :] = flat(keep)
+        return jnp.minimum(least, jnp.min(keep, axis=0))
+
+    kp_ref[...] = lax.fori_loop(0, steps // block, fill, jnp.ones((SUB, LANE), F32))
 
     def fill_devices(j, unused):
-        first = j * length
-        forward = jnp.zeros((SUB, LANE), jnp.bool_)
-        backward = jnp.zeros((SUB, LANE), jnp.bool_)
+        first = j * length + (1 if reverse else 0)
+        hit = jnp.zeros((SUB, LANE), jnp.bool_)
         for start in starts:
-            forward = forward | ((start >= first) & (start < first + length))
-            backward = backward | ((start > first) & (start <= first + length))
-        kd_f_ref[j] = jnp.where(forward, 0.0, 1.0)
-        kd_r_ref[j] = jnp.where(backward, 0.0, 1.0)
+            hit = hit | ((start >= first) & (start < first + length))
+        kd_ref[j] = jnp.where(hit, 0.0, 1.0)
         return unused
 
     lax.fori_loop(0, n, fill_devices, 0)
+
+
+def k_prepare(starts_ref, rate_ref, rotation_ref, gain_ref, shift_ref, skip_ref, bias_ref,
+              keep_ref, kp_ref, kd_ref, par_ref, vec_ref):
+    k_keep(False, starts_ref, keep_ref, kp_ref, kd_ref)
+    doublings = (keep_ref.shape[0] // SUB).bit_length() - 1
     for layer in range(2):
         decay = jnp.exp(rate_ref[layer : layer + 1, :])
         magnitude = jnp.exp(-decay)
@@ -354,7 +378,7 @@
         norm_in = jnp.sqrt(one_minus_exp(2.0 * decay))
         par_ref[at : at + 1, :] = re
         par_ref[at + 1 : at + 2, :] = im
-        for unused in range(steps.bit_length() - 1):
+        for unused in range(doublings):
             re, im = times(re, im, re, im)
         par_ref[at + 2 : at + 3, :] = re
         par_ref[at + 3 : at + 4, :] = im
@@ -421,7 +445,7 @@
         d_ref[rows_at(i), :] = dot(low, b_ref[layer]) * both
         return unused
 
-    lax.fori_loop(0, u_ref.shape[0] // TILE, step, 0)
+    lax.fori_loop(0, u_ref.shape[0] // TILE, step, 0, unroll=True)
     re, im, unused = scan(d_ref, keep_ref, par_ref, zeros_state(par_ref), reverse, False)
     put_ends(e_ref, chunk_end((re, im), kp_ref, par_ref, reverse, False))
 
@@ -449,9 +473,22 @@
     return first
 
 
+def sigmoid(x):
+    return 0.5 + 0.5 * jnp.tanh(0.5 * x)
+
+
 def gelu_parts(x):
-    cdf = 0.5 * (1.0 + lax.erf(x * 0.7071067811865476))
-    return x * cdf, cdf + x * jnp.exp(-0.5 * x * x) * 0.3989422804014327
+    bell = jnp.exp(-0.5 * x * x)
+    base = 1.0 + (0.3275911 * 0.7071067811865476) * jnp.abs(x)
+    near = pl.reciprocal(base, approx=True)
+    near = near * (2.0 - base * near)
+    tail = near * (0.5 * 1.061405429) + (0.5 * -1.453152027)
+    tail = tail * near + (0.5 * 1.421413741)
+    tail = tail * near + (0.5 * -0.284496736)
+    tail = tail * near + (0.5 * 0.254829592)
+    tail = tail * near * bell
+    cdf = jnp.where(x < 0.0, tail, 1.0 - tail)
+    return x * cdf, cdf + (0.3989422804014327 * x) * bell
 
 
 def states_low(s_ref, first, i):
@@ -476,7 +513,7 @@
         mixed = dot(states_low(s_ref, first, i), c_ref[layer]) + vec_ref[2:3, :] * flat(masked)
         active, slope = gelu_parts(mixed)
         low = active.astype(BF16)
-        sig = jax.nn.sigmoid(dot(low, w_ref[layer]) + vec_ref[3:4, :])
+        sig = sigmoid(dot(low, w_ref[layer]) + vec_ref[3:4, :])
         gated = active * sig
         al_ref[at, :] = low
         sig_ref[at, :] = sig
@@ -488,20 +525,20 @@
         return (sums[0] + jnp.sum(x, axis=0), sums[1] + jnp.sum(x * x, axis=0))
 
     zero = jnp.zeros(lim_ref.shape, F32)
-    sums, squares = lax.fori_loop(0, u_ref.shape[0] // TILE, step, (zero, zero))
+    sums, squares = lax.fori_loop(0, u_ref.shape[0] // TILE, step, (zero, zero), unroll=True)
     a, b = per_micro(sums)
     c, d = per_micro(squares)
     pack_rows(st_ref, (a, c, b, d))
 
 
-def gate_backward(layer, upstream, q, sig, slope, low, masked, s_low, state, c_ref, w_ref, mix_ref, sg_ref, wc_ref, i):
+def gate_backward(layer, upstream, q, sig, slope, low, masked, s_low, state, c_ref, w_ref, mix_ref, sg_ref, gw_ref, gc_ref, i):
     at = rows_at(i)
     gate = (upstream * q).astype(BF16)
-    wc_ref[: gate.shape[1], :] += dot_tn(low, gate)
+    gw_ref[...] += dot_tn(low, gate)
     act = upstream * sig + dot_nt(gate, w_ref[layer])
     mix = (act * slope).astype(BF16)
     mix_ref[at, :] = mix
-    wc_ref[gate.shape[1] :, :] += dot_tn(s_low, mix)
+    gc_ref[...] += dot_tn(s_low, mix)
     sg = dot_nt(mix, c_ref[layer])
     sg_ref[at, :] = sg
     wide_sum = jnp.sum(folded(sg * state), axis=0)
@@ -525,12 +562,12 @@
 def k_middle(layer, parts, *refs):
     carry, refs = take_carry(refs, parts)
     (d_ref, u_ref, stat_ref, lim_ref, vec_ref, par_ref, keep_ref, kp_ref, kd_ref,
-     keep_adj_ref, kp_adj_ref, c_ref, w_ref, cot_ref,
-     out_ref, s_ref, cot32_ref, mix_ref, sg_ref, wc_ref, sums_ref, e_ref, lines_ref) = refs
+     keep_adj_ref, kp_adj_ref, c_ref, w_ref, cot32_ref,
+     lines_ref, s_ref, mix_ref, sg_ref, wc_ref, sums_ref, e_ref) = refs
     vec_ref, par_ref = of_layer(vec_ref, layer), of_layer(par_ref, layer)
-    spread_in(cot_ref, cot32_ref, lines_ref)
     first = run_states(carry, d_ref, keep_ref, kp_ref, kd_ref, par_ref, s_ref, True)
     wc_ref[...] = jnp.zeros(wc_ref.shape, F32)
+    gw_ref, gc_ref = wc_ref.at[: u_ref.shape[1]], wc_ref.at[u_ref.shape[1] :]
 
     def step(i, sums):
         at = rows_at(i)
@@ -541,17 +578,16 @@
         mixed = dot(s_low, c_ref[layer]) + vec_ref[2:3, :] * masked
         active, slope = gelu_parts(mixed)
         low = active.astype(BF16)
-        sig = jax.nn.sigmoid(dot(low, w_ref[layer]) + vec_ref[3:4, :])
+        sig = sigmoid(dot(low, w_ref[layer]) + vec_ref[3:4, :])
         gated = active * sig
         put_lines(lines_ref, i, flat(folded(u_ref[at, :]) + jnp.where(valid, folded(gated), 0.0)))
         upstream = flat(jnp.where(valid, folded(cot32_ref[at, :]), 0.0))
         more = gate_backward(layer, upstream, gated * (1.0 - sig), sig, slope, low, masked, s_low, state,
-                             c_ref, w_ref, mix_ref, sg_ref, wc_ref, i)
+                             c_ref, w_ref, mix_ref, sg_ref, gw_ref, gc_ref, i)
         return tuple(x + y for x, y in zip(sums, more))
 
-    sums = lax.fori_loop(0, u_ref.shape[0] // TILE, step, zero_sums(u_ref.shape[1], par_ref.shape[1]))
+    sums = lax.fori_loop(0, u_ref.shape[0] // TILE, step, zero_sums(u_ref.shape[1], par_ref.shape[1]), unroll=True)
     put_sums(sums_ref, sums)
-    spread_out(lines_ref, out_ref)
     re, im, unused = scan(sg_ref, keep_adj_ref, par_ref, zeros_state(par_ref), False, True)
     put_ends(e_ref, chunk_end((re, im), kp_adj_ref, par_ref, False, True))
 
@@ -559,12 +595,13 @@
 def k_lower(layer, st_ref, z_ref, cot32_ref, u1_ref, stat1_ref, lim_ref,
             s_ref, al_ref, sig_ref, q_ref, slope_ref, u_ref, stat_ref, vec_ref, par_ref, c_ref, w_ref,
             keep_adj_ref, kp_adj_ref,
-            grad_ref, mix_ref, sg_ref, wc_ref, sums_ref, e_ref, bn_ref):
+            grad_ref, mix_ref, sg_ref, gw_ref, gc_ref, sums_ref, e_ref, bn_ref):
     vec1_ref = of_layer(vec_ref, layer + 1)
     vec_ref, par_ref = of_layer(vec_ref, layer), of_layer(par_ref, layer)
     first = SUB
     c1, c2 = norm_sums(st_ref, stat1_ref, vec1_ref, bn_ref)
-    wc_ref[...] = jnp.zeros(wc_ref.shape, F32)
+    gw_ref[...] = jnp.zeros(gw_ref.shape, F32)
+    gc_ref[...] = jnp.zeros(gc_ref.shape, F32)
 
     def step(i, sums):
         at = rows_at(i)
@@ -576,10 +613,10 @@
         masked = flat(masked_tile(u_ref, stat_ref, vec_ref, lim_ref, i))
         state = s_ref[pl.ds(pl.multiple_of(i * TILE + first, SUB), TILE), :]
         more = gate_backward(layer, upstream, q_ref[at, :], sig_ref[at, :], slope_ref[at, :], al_ref[at, :], masked,
-                             state.astype(BF16), state, c_ref, w_ref, mix_ref, sg_ref, wc_ref, i)
+                             state.astype(BF16), state, c_ref, w_ref, mix_ref, sg_ref, gw_ref, gc_ref, i)
         return tuple(x + y for x, y in zip(sums, more))
 
-    sums = lax.fori_loop(0, u_ref.shape[0] // TILE, step, zero_sums(u_ref.shape[1], par_ref.shape[1]))
+    sums = lax.fori_loop(0, u_ref.shape[0] // TILE, step, zero_sums(u_ref.shape[1], par_ref.shape[1]), unroll=True)
     put_sums(sums_ref, sums)
     re, im, unused = scan(sg_ref, keep_adj_ref, par_ref, zeros_state(par_ref), True, True)
     put_ends(e_ref, chunk_end((re, im), kp_adj_ref, par_ref, True, True))
@@ -649,7 +686,7 @@
         return (sums[0] + jnp.sum(z, axis=0), sums[1] + jnp.sum(z * normed_tile(u_ref, stat_ref, i), axis=0))
 
     zero = jnp.zeros(lim_ref.shape, F32)
-    sums = lax.fori_loop(0, u_ref.shape[0] // TILE, step, (zero, zero))
+    sums = lax.fori_loop(0, u_ref.shape[0] // TILE, step, (zero, zero), unroll=True)
     a, b = per_micro(sums[0])
     c, d = per_micro(sums[1])
     pack_rows(st_ref, (a, c, b, d))
@@ -672,7 +709,7 @@
         put_lines(lines_ref, i, grad_ref[rows_at(i), :] + flat(extra))
         return unused
 
-    lax.fori_loop(0, u_ref.shape[0] // TILE, step, 0)
+    lax.fori_loop(0, u_ref.shape[0] // TILE, step, 0, unroll=True)
     spread_out(lines_ref, out_ref)
     width, states = gain_ref.shape[1], rate_ref.shape[1]
     per, per_state = width // LANE, states // LANE
@@ -717,6 +754,17 @@
         ref[...] = here + got_ref[pl.ds(pl.multiple_of(at, SUB), half), :]
 
 
+def k_copy(src_ref, dst_ref):
+    dst_ref[...] = src_ref[...]
+
+
+def k_add(*refs):
+    total = refs[1][...]
+    for ref in refs[2:-1]:
+        total = total + ref[...]
+    refs[-1][...] = refs[0][...] + total
+
+
 def k_join(side, own_ref, got_ref, out_ref):
     half = own_ref.shape[0]
     mine = side()
@@ -724,26 +772,80 @@
     out_ref[pl.ds(pl.multiple_of((1 - mine) * half, SUB), half), :] = got_ref[...]
 
 
-def k_maps(side, wc1_ref, own_ref, got_ref, w_ref, c_ref, wc_ref):
-    k_join(side, own_ref, got_ref, wc_ref)
-    width = w_ref.shape[1]
-    for layer, ref in enumerate((wc_ref, wc1_ref)):
-        w_ref[layer] = ref[:width, :]
-        c_ref[layer] = ref[width:, :]
-
-
-def k_drives(side, b1_ref, own_ref, got_ref, out_ref, b_ref):
-    k_join(side, own_ref, got_ref, b_ref)
-    width = out_ref.shape[1]
-    for layer, ref in enumerate((b_ref, b1_ref)):
-        out_ref[layer, :, :width] = ref[:width, :]
-        out_ref[layer, : width // 2, width:] = ref[width:, : width // 2]
-        out_ref[layer, width // 2 :, width:] = ref[width:, width // 2 :]
+def copy_all(pairs, sem_ref):
+    copies = [pltpu.make_async_copy(src, dst, sem_ref.at[k]) for k, (src, dst) in enumerate(pairs)]
+    for copy in copies:
+        copy.start()
+    for copy in copies:
+        copy.wait()
+
+
+def cut_to(layer, first, src_ref, outs):
+    pairs = []
+    for begin, end, place in outs:
+        low, high = max(begin, first), min(end, first + src_ref.shape[0])
+        if low < high:
+            pairs.extend(place(src_ref, low - first, low - begin, high - low))
+    return pairs
+
+
+def rows_to(layer, ref):
+    return lambda src, at, row, size: [(src.at[pl.ds(at, size), :], ref.at[layer, pl.ds(row, size), :])]
+
+
+def map_places(layer, *refs):
+    places, first = [], 0
+    for ref in refs:
+        places.append((first, first + ref.shape[1], rows_to(layer, ref)))
+        first += ref.shape[1]
+    return places
+
+
+def drive_places(layer, b_ref):
+    width = b_ref.shape[1]
+
+    def left(src, at, row, size):
+        return [(src.at[pl.ds(at, size), :], b_ref.at[layer, pl.ds(row, size), pl.ds(0, width)])]
+
+    def right(src, at, row, size):
+        part = width // 2
+        return [
+            (src.at[pl.ds(at, size), pl.ds(k * part, part)],
+             b_ref.at[layer, pl.ds(k * part + row, size), pl.ds(width, part)])
+            for k in range(2)
+        ]
+
+    return [(0, width, left), (width, width + width // 2, right)]
+
+
+def k_place(side, places, layer, count, own_ref, got_ref, *refs):
+    token_ref, sem_ref = refs[-2:]
+    outs = refs[-2 - count : -2]
+    token_ref[...] = jnp.zeros(token_ref.shape, F32)
+    half = own_ref.shape[0]
+    for mine in range(2):
+        @pl.when(side() == mine)
+        def _():
+            where = places(layer, *outs)
+            copy_all(
+                cut_to(layer, mine * half, own_ref, where) + cut_to(layer, (1 - mine) * half, got_ref, where), sem_ref
+            )
+
+
+def place(large, places, layer, shapes, into=None):
+    count = len(shapes)
+    args = [large.block, large.got] + list(into or [])
+    alias = {2 + k: k for k in range(count)} if into else {}
+    return list(call(
+        "place", functools.partial(k_place, large.side(), places, layer, count), shapes + [shaped((SUB, LANE))], args,
+        scratch=[pltpu.SemaphoreType.DMA((8,))], order=large.order, token=count, far=range(2, len(args)), alias=alias,
+        out_far=count,
+    ))[:count]
 
 
 BOTH = ("batch", "tm")
 
-TAIL = "s D A s C D B s D C A s D B s leave C D A D B C D A C D B C D A C B".replace("leave", "L")
+TAIL = ("DABSDECBSA", "DCBEADCSBD", "EASCBDECDB", "SCEDALBCAE", "CDBED")
 
 
 def outer_bits():
@@ -765,37 +867,52 @@
     return lax.ppermute(block, BOTH, [(i, i ^ (odd if i & 1 else even)) for i in range(total)])
 
 
+def sum_four(block, others, order=None):
+    block, = call("add", k_add, [shaped(block.shape)], [block, others[0]], order=order, work=1)
+    return call("add", k_add, [shaped(block.shape)], [block] + others[1:], order=order, work=1)[0]
+
+
 def sum_over(block, bits):
     if len(bits) == 2:
         near, far = bits[0][2], bits[1][2]
-        others = [swap(block, distance | 1) for distance in (near, far, near | far)]
-        return (block + others[0]) + (others[1] + others[2])
+        return sum_four(block, [swap(block, distance | 1) for distance in (near | far, far, near)])
     for unused, unused, distance in bits:
         block = block + swap(block, distance | 1)
     return block
 
 
-def sums_of_all(block, order=None, between=()):
-    stages = [lambda block: block + swap(block, 1), lambda block: sum_over(block, outer_bits()),
-              lambda block: sum_over(block, line_bits())]
-    for k, stage in enumerate(stages):
-        if order is not None:
-            block, = order(block)
-        block = stage(block)
-        if k < len(between):
-            between[k]()
-    if order is not None:
-        order.token = block
+def sums_of_all(block):
+    block = block + swap(block, 1)
+    return sum_over(sum_over(block, outer_bits()), line_bits())
+
+
+def sums_in_order(block, order, between):
+    for bits, start in zip(([("tm", 1, 0)], outer_bits(), line_bits()), between):
+        if len(bits) == 2:
+            near, far = bits[0][2], bits[1][2]
+            got = [swap(block, distance | 1) for distance in (near | far, far, near)]
+            start()
+            block = sum_four(block, got, order)
+        else:
+            for k, bit in enumerate(bits):
+                got = swap(block, bit[2] | 1)
+                if k == 0:
+                    start()
+                block, = call("add", k_add, [shaped(block.shape)], [block, got], order=order)
     return block
 
 
-def carries(e, kd, par, layer, reverse, conj):
+def carries(e, kd, par, layer, reverse, conj, order=None):
     other = swap(e, 1)
-    block, = call("combine", functools.partial(k_combine, layer, reverse, conj), [shaped(e.shape)], [e, other, kd, par])
+    block, = call("combine", functools.partial(k_combine, layer, reverse, conj), [shaped(e.shape)], [e, other, kd, par],
+                  order=order)
     bits = line_bits()
     if len(bits) == 2:
         near, far = bits[0][2], bits[1][2]
-        return [block] + [swap(block, distance | 1) for distance in (near, far, near | far)] + [e, other]
+        last = swap(block, near | far | 1)
+        others = [swap(block, distance | 1) for distance in (near, far)]
+        last, = call("copy", k_copy, [shaped(block.shape)], [last], work=1)
+        return [block] + others + [last, e, other]
     for unused, unused, distance in bits:
         block = jnp.concatenate((block, swap(block, distance | 1)), axis=0)
     return [block, e, other]
@@ -805,97 +922,74 @@
     return lax.div(lax.axis_index(axis), bit) % 2
 
 
-def plan(rows):
+def plan(rows, line_first):
     outer, line = outer_bits(), line_bits()
     is_odd = functools.partial(bit_of, "tm", 1)
-    steps = [(is_odd, lambda block: swap(block, 1))]
+    steps = []
     for even, odd in zip(outer, outer[::-1]):
         def side(even=even, odd=odd):
             return jnp.where(is_odd() == 1, bit_of(odd[0], odd[1]), bit_of(even[0], even[1]))
 
         steps.append((side, functools.partial(swap_by_core, even=even[2], odd=odd[2])))
-    for axis, bit, distance in line:
-        steps.append((functools.partial(bit_of, axis, bit), functools.partial(swap, distance=distance)))
+    along = [(functools.partial(bit_of, axis, bit), functools.partial(swap, distance=distance))
+             for axis, bit, distance in line]
+    steps = [(is_odd, lambda block: swap(block, 1))] + (along + steps if line_first else steps + along)
+    most = 3 if line_first else 4
     cuts = 0
-    while cuts < len(steps) and rows % (SUB << (cuts + 1)) == 0 and cuts < 4:
+    while cuts < len(steps) and rows % (SUB << (cuts + 1)) == 0 and cuts < most:
         cuts += 1
     return steps[:cuts], [exchange for unused, exchange in steps[cuts:]]
 
 
-class Order:
-    def __init__(self):
-        self.token = None
-
-    def __call__(self, *values):
-        if self.token is None:
-            return values
-        tied = lax.optimization_barrier(tuple(values) + (self.token,))
-        return tied[:-1]
-
-
 class Large:
-    def __init__(self, order, block):
+    def __init__(self, order, block, line_first=False):
         self.order = order
         self.rows, self.width = block.shape
-        self.cuts, self.whole = plan(self.rows)
+        self.cuts, self.whole = plan(self.rows, line_first)
         self.block = block
         self.at = 0
         self.got = None
 
-    def half(self):
-        return shaped((self.rows >> (self.at + 1), self.width))
+    def call(self, name, body, outs):
+        args = [self.block] if self.got is None else [self.block, self.got]
+        return call(name, body, outs, args, order=self.order)
 
     def send(self):
         cuts, at = self.cuts, self.at
         count = len(cuts)
-        if at == 0:
-            self.block, = self.order(self.block)
-        else:
-            self.block, self.got = self.order(self.block, self.got)
         if at < count:
             side, exchange = cuts[at]
+            half = shaped((self.rows >> (at + 1), self.width))
             if at == 0:
-                give, = call("split", functools.partial(k_split, side), [self.half()], [self.block])
+                give, = self.call("split", functools.partial(k_split, side), [half])
             else:
                 before = cuts[0][0] if at == 1 else None
-                give, self.block = call(
-                    "fold", functools.partial(k_fold, before, side), [self.half()] * 2, [self.block, self.got]
-                )
-        elif at <= count + len(self.whole):
-            give = self.block = self.block + self.got
+                give, self.block = self.call("fold", functools.partial(k_fold, before, side), [half, half])
+        else:
+            if at <= count + len(self.whole):
+                give, = self.call("add", k_add, [shaped(self.got.shape)])
+            else:
+                give, = self.call("join", functools.partial(k_join, self.side()), [self.doubled()])
+            self.block = give
             exchange = (self.whole + [step[1] for step in cuts[::-1]])[at - count]
-        else:
-            back = at - count - len(self.whole)
-            give = self.block = self.joined()
-            exchange = cuts[count - 1 - back][1]
-        self.order.token = give
         self.got = exchange(give)
         self.at += 1
 
-    def joined(self):
-        rows, width = self.block.shape
-        side = self.cuts[len(self.cuts) - 1 - (self.at - 1 - len(self.cuts) - len(self.whole))][0]
-        out, = call("join", functools.partial(k_join, side), [shaped((2 * rows, width))], [self.block, self.got])
-        return out
-
-    def result(self):
-        self.block, self.got = self.order(self.block, self.got)
-        self.block = self.joined()
-        self.order.token = self.block
-        return self.block
+    def side(self):
+        return self.cuts[2 * len(self.cuts) + len(self.whole) - self.at][0]
+
+    def doubled(self):
+        return shaped((2 * self.block.shape[0], self.width))
 
     def left(self):
         return 2 * len(self.cuts) + len(self.whole) - self.at
 
 
-def sum_slowly(order, block):
+def small_sum(order, block):
     for distance in [1] + [bit[2] | 1 for bit in outer_bits() + line_bits()]:
-        block, = order(block)
         got = swap(block, distance)
         yield None
-        block, got = order(block, got)
-        block = block + got
-        order.token = block
+        block, = call("add", k_add, [shaped(block.shape)], [block, got], order=order)
     yield block
 
 
@@ -919,10 +1013,9 @@
 
     u0, st, lim = call("enter", k_input, [big(width), shaped((24, LANE)), shaped((SUB, width), jnp.int32)],
                        [lengths, tokens], scratch=[lines], scalars=1)
-    keep_f, keep_r, kp_f, kp_r, kd_f, kd_r, par, vec = call(
-        "prepare", k_prepare,
-        [keeps, keeps, shaped((SUB, LANE)), shaped((SUB, LANE)), shaped((n, SUB, LANE)), shaped((n, SUB, LANE)),
-         shaped((2 * SUB, states)), shaped((2 * SUB, width))],
+    keep_shapes = [keeps, shaped((SUB, LANE)), shaped((n, SUB, LANE))]
+    keep_f, kp_f, kd_f, par, vec = call(
+        "prepare", k_prepare, keep_shapes + [shaped((2 * SUB, states)), shaped((2 * SUB, width))],
         [starts, log_rate, rotation, norm_gain, norm_shift, skip_gain, gate_bias], scalars=1,
     )
     st = sums_of_all(st)
@@ -930,6 +1023,11 @@
         "drive0", functools.partial(k_drive_first, 0, False),
         [big(2 * states), big(width, BF16), shaped((32, width)), ends],
         [st, u0, lim, vec, par, b_proj, keep_f, kp_f],
+    )
+    side = Order()
+    side.token = e
+    keep_r, kp_r, kd_r = call(
+        "keep", functools.partial(k_keep, True), keep_shapes, [starts], scalars=1, order=side,
     )
     s0, al0, sig0, q0, slope0, u1, st = call(
         "finish0", functools.partial(k_finish_first, 0, parts),
@@ -945,91 +1043,103 @@
         [st, stat0, u1, lim, vec, par, b_proj, keep_r, kp_r],
     )
     grads = [shaped((width + 2 * states, width)), small, ends]
-    output, s1, cot32, mix1, sg1, wc1, sums1, e = call(
+    side.token = u1
+    cot32, = call("cotangent", spread_in, [big(width)], [cotangent], scratch=[lines], order=side)
+    out32, s1, mix1, sg1, wc1, sums1, e = call(
         "middle", functools.partial(k_middle, 1, parts),
-        [shaped(tokens.shape, BF16), kept, big(width), big(width, BF16), big(2 * states)] + grads,
+        [shaped((width // LANE, count, LANE)), kept, big(width, BF16), big(2 * states)] + grads,
         carries(e, kd_r, par, 1, True, False)
-        + [d1, u1, stat1, lim, vec, par, keep_r, kp_r, kd_r, keep_f, kp_f, c_proj, w_gate, cotangent],
-        scratch=[lines, everyone], results=1,
+        + [d1, u1, stat1, lim, vec, par, keep_r, kp_r, kd_r, keep_f, kp_f, c_proj, w_gate, cot32],
+        scratch=[everyone],
     )
     order = Order()
+    order.token = e
     wc1 = Large(order, wc1)
+    got = carries(e, kd_f, par, 1, False, True, order)
     wc1.send()
-    got = carries(e, kd_f, par, 1, False, True)
     wc1.send()
     adjoint = [big(width), shaped((2 * states, width)), shaped((8, LANE))]
     z1, gb1, lg1, st = call(
         "adjoint1", functools.partial(k_adjoint, 1, False, parts, 0), adjoint + [small],
-        list(order(*got)) + [sg1, s1, mix1, ml1, u1, stat1, lim, vec, par, keep_f, kp_f, kd_f, keep_r, b_proj],
-        scratch=[pltpu.VMEM((count, 2 * states), F32), everyone],
-    )
-    order.token = st
+        got + [sg1, s1, mix1, ml1, u1, stat1, lim, vec, par, keep_f, kp_f, kd_f, keep_r, b_proj],
+        scratch=[pltpu.VMEM((count, 2 * states), F32), everyone], order=order, token=3,
+    )
     b1 = Large(order, gb1)
-    st = sums_of_all(st, order, [b1.send, wc1.send, b1.send])
-    g0, mix0, sg0, wc0, sums0, e, bn1 = call(
+    emitted = []
+
+    def emit():
+        emitted.extend(call("emit", spread_out, [shaped(tokens.shape, BF16)], [out32], results=1, order=order))
+
+    st = sums_in_order(st, order, [b1.send, wc1.send, emit])
+    b1.send()
+    wc1.send()
+    output, = emitted
+    g0, mix0, sg0, gw0, gc0, sums0, e, bn1 = call(
         "lower", functools.partial(k_lower, 0),
-        [big(width), big(width, BF16), big(2 * states)] + grads + [shaped((8, width))],
-        list(order(st)) + [z1, cot32, u1, stat1, lim, s0, al0, sig0, q0, slope0, u0, stat0, vec, par,
-                           c_proj, w_gate, keep_r, kp_r],
-    )
-    order.token = e
-    wc0 = Large(order, wc0)
-    wc1.send()
-    wc0.send()
-    got = carries(e, kd_r, par, 0, True, True)
-    b1.send()
-    wc0.send()
+        [big(width), big(width, BF16), big(2 * states), shaped((width, width)), shaped((2 * states, width)), small, ends,
+         shaped((SUB, width))],
+        [st, z1, cot32, u1, stat1, lim, s0, al0, sig0, q0, slope0, u0, stat0, vec, par,
+         c_proj, w_gate, keep_r, kp_r],
+        order=order, token=6,
+    )
+    w0, c0 = Large(order, gw0, True), Large(order, gc0)
+    got = carries(e, kd_r, par, 0, True, True, order)
+    c0.send()
+    w0.send()
+    c0.send()
+    w0.send()
     z0, gb0, lg0, st = call(
         "adjoint0", functools.partial(k_adjoint, 0, True, parts, 3), adjoint + [shaped((64, LANE))],
-        list(order(*got)) + [sums1, lg1, sums0]
+        got + [sums1, lg1, sums0]
         + [sg0, s0, mix0, ml0, u0, stat0, lim, vec, par, keep_r, kp_r, kd_r, keep_f, b_proj],
-        scratch=[pltpu.VMEM((count, 2 * states), F32), everyone],
-    )
-    order.token = st
+        scratch=[pltpu.VMEM((count, 2 * states), F32), everyone], order=order, token=3,
+    )
     b0 = Large(order, gb0)
-    small_sum = sum_slowly(order, st)
-    queue = TAIL.split()
-    returned = {}
-    for item in queue:
-        if item == "s":
-            st = next(small_sum)
-        elif item == "L":
-            for unused in small_sum:
-                st = unused if unused is not None else st
-            (tokens_grad, grad_gain, grad_shift, grad_skip, grad_bias, grad_rate, grad_rotation, new_mean, new_var,
-             bn0) = call(
-                "leave", k_output,
-                [shaped(tokens.shape), vector, vector, vector, vector, state_vector, state_vector, vector, vector,
-                 shaped((SUB, width))],
-                list(order(st)) + [z0, g0, u0, stat0, vec, lim, par, stat1, bn1, run_mean, run_var],
-                scratch=[lines], results=9,
-            )
-            order.token = bn0
-        else:
-            large = {"A": wc1, "B": b1, "C": wc0, "D": b0}[item]
-            if large.left():
-                large.send()
-            elif item in "AB":
-                returned[item] = large.result()
-    for large in (wc1, b1, wc0, b0):
-        while large.left():
+    steps = small_sum(order, st)
+    w_shape, c_shape = shaped((2, width, width)), shaped((2, 2 * states, width))
+    drive_shapes = [shaped((2, width, 2 * states))]
+    larges = {"A": wc1, "B": b1, "C": c0, "E": w0, "D": b0}
+    into = {}
+
+    def step(item):
+        if item == "S":
+            return next(steps, None)
+        large = larges[item]
+        if large.left():
             large.send()
-    wc1 = returned["A"] if "A" in returned else wc1.result()
-    b1 = returned["B"] if "B" in returned else b1.result()
-    last = wc0.cuts[0][0]
-    wc0.block, wc0.got = order(wc0.block, wc0.got)
-    grad_w, grad_c, unused = call(
-        "maps", functools.partial(k_maps, last),
-        [shaped((2, width, width)), shaped((2, 2 * states, width)), shaped((width + 2 * states, width))],
-        [wc1, wc0.block, wc0.got], results=2,
-    )
-    order.token = unused
-    b0.block, b0.got = order(b0.block, b0.got)
-    grad_b, unused = call(
-        "drives", functools.partial(k_drives, last),
-        [shaped((2, width, 2 * states)), shaped((2 * states, width))],
-        [b1, b0.block, b0.got], results=1,
-    )
+        elif item == "A":
+            into["E"], into["C"] = ([made] for made in place(large, map_places, 1, [w_shape, c_shape]))
+        elif item == "B":
+            into["D"] = place(large, drive_places, 1, drive_shapes)
+        elif item in "CDE" and item not in into:
+            step("B" if item == "D" else "A")
+            step(item)
+        elif item in "CE":
+            if len(into[item]) == 1:
+                into[item] = place(large, map_places, 0, [c_shape if item == "C" else w_shape], into[item]) + [None]
+        elif len(into["D"]) == 1:
+            into["D"] = place(large, drive_places, 0, drive_shapes, into["D"]) + [None]
+        return None
+
+    for item in "".join(TAIL):
+        if item != "L":
+            sent = step(item)
+            st = st if sent is None else sent
+            continue
+        for sent in steps:
+            st = st if sent is None else sent
+        (tokens_grad, grad_gain, grad_shift, grad_skip, grad_bias, grad_rate, grad_rotation, new_mean, new_var,
+         unused) = call(
+            "leave", k_output,
+            [shaped(tokens.shape), vector, vector, vector, vector, state_vector, state_vector, vector, vector,
+             shaped((SUB, width))],
+            [st, z0, g0, u0, stat0, vec, lim, par, stat1, bn1, run_mean, run_var],
+            scratch=[lines], results=9, order=order, token=9,
+        )
+    for item in "CED":
+        while len(into.get(item, ())) < 2:
+            step(item)
+    (grad_w, unused), (grad_c, unused), (grad_b, unused) = into["E"], into["C"], into["D"]
     return (output, tokens_grad, grad_gain, grad_shift, grad_b, grad_rate, grad_rotation, grad_c, grad_skip, grad_w,
             grad_bias, new_mean, new_var)
 

time: 246 us -> 191 us (0.78)
  waiting for transfers between devices: 110 us -> 57.6 us
  local copies, waits for them, and re-layouts: 8.1 us -> 3.55 us
    ppermute x62 -> x68, waiting for transfers between devices: 70.9 us -> 40.1 us  [swap(): return lax.ppermute(block, BOTH, [(i, i ^ distance) for i in range(total)])]
    ppermute x16 -> x18, waiting for transfers between devices: 38.8 us -> 17.5 us  [swap_by_core(): lax.ppermute(block, BOTH, [(i, i ^ (odd if i & 1 else even)) for i in ran...]
    unnamed x32 -> x40, local copies, waits for them, and re-layouts: 8.1 us -> 3.55 us
    ppermute x62 -> x68, starting transfers between devices: 57.1 us -> 60.8 us  [swap(): return lax.ppermute(block, BOTH, [(i, i ^ distance) for i in range(total)])]
    ppermute x16 -> x18, starting transfers between devices: 17 us -> 14.7 us  [swap_by_core(): lax.ppermute(block, BOTH, [(i, i ^ (odd if i & 1 else even)) for i in ran...]
    pallas_call x46 -> x88, Pallas kernels: 52.6 us -> 52.7 us  [call(): pl.pallas_call(run, name=name, out_shape=outs, in_specs=specs, out_specs=...]
  transfers between devices with their start and end apart: 78 -> 86, of which waited for: 43 -> 45; matrix products, arithmetic and copies ran while one was open for 0% -> 0% of each run, Pallas kernels for 8% -> 13%
where the time goes in v3:
time: 191 us
  starting transfers between devices  75.5 us (40%)
  waiting for transfers between devices  57.6 us (30%)
  Pallas kernels  52.7 us (28%)
  local copies, waits for them, and re-layouts  3.55 us (2%)
    ppermute x68, starting transfers between devices, swap(): return lax.ppermute(block, BOTH, [(i, i ^ distance) for i in range(total)])  60.8 us
    pallas_call x88, Pallas kernels, call(): pl.pallas_call(run, name=name, out_shape=outs, in_specs=specs, out_specs=...  52.7 us
    ppermute x68, waiting for transfers between devices, swap(): return lax.ppermute(block, BOTH, [(i, i ^ distance) for i in range(total)])  40.1 us
    ppermute x18, waiting for transfers between devices, swap_by_core(): lax.ppermute(block, BOTH, [(i, i ^ (odd if i & 1 else even)) for i in ran...  17.5 us
    ppermute x18, starting transfers between devices, swap_by_core(): lax.ppermute(block, BOTH, [(i, i ^ (odd if i & 1 else even)) for i in ran...  14.7 us
  transfers between devices with their start and end apart: 86, of which 45 were waited for; matrix products, arithmetic and copies ran while one was open for 0% of the time, Pallas kernels for 13%

profile of v3, /device:TPU:0, one launch (start us, length us, event | category | flops | bytes accessed | tf_op | source)
XLA Modules:
  0.0 191.0 jit_solution(13671251954160333701)
XLA Ops:
  0.7 1.2 copy-done.8
  2.6 1.9 %enter.1 = (f32[1024,512]{1,0:T(8,128)S(1)}, f32[24,128]{1,0:T(8,128)S(1)}, s32[8,512]{1,0:T(8,128)S(1)}) custom-call(s32[4]{0:T(128)S(1)} %copy-done.19, bf16[4,256,512]{2,1,0:T(8,128)(2,1)S(1)} %copy-done.8), custom_call_target="tpu_custom_call" | custom-call | flops 5000000000 | bytes 1 | tf_op jit(solution)/shard_map/enter/pallas_call | solution.py:46
  5.8 3.6 %collective-permute-start.1 = (f32[24,128]{1,0:T(8,128)S(1)}, f32[24,128]{1,0:T(8,128)S(1)}, u32[]{:S(2)}, u32[]{:S(2)}) collective-permute-start(f32[24,128]{1,0:T(8,128)S(1)} %add.35.refs_0_), channel_id=1, source_target_pairs={{0,25},{1,24},{2,27},{3,26},{4,29},{5,28},{6,31},{7,30},{8,17},{9,... | collective-permute-start | bytes 36872 | tf_op jit(solution)/shard_map/ppermute | solution.py:862
  10.8 1.7 collective-permute-done.2.refs_1_
  13.0 3.4 %collective-permute-start.4 = (f32[24,128]{1,0:T(8,128)S(1)}, f32[24,128]{1,0:T(8,128)S(1)}, u32[]{:S(2)}, u32[]{:S(2)}) collective-permute-start(f32[24,128]{1,0:T(8,128)S(1)} %add.38.refs_0_), channel_id=1, source_target_pairs={{0,7},{1,6},{2,5},{3,4},{4,3},{5,2},{6,1},{7,0},{8,15},{9,14},{10,... | collective-permute-start | bytes 36872 | tf_op jit(solution)/shard_map/ppermute | solution.py:862
  17.0 1.9 %prepare.1 = (f32[1024,128]{1,0:T(8,128)S(1)}, f32[8,128]{1,0:T(8,128)S(1)}, f32[8,8,128]{2,1,0:T(8,128)S(1)}, f32[16,384]{1,0:T(8,128)S(1)}, f32[16,512]{1,0:T(8,128)S(1)}) custom-call(s32[4,16]{1,0:T(4,128)S(1)} %copy-done.18, f32[2,384]{1,0:T(2,128)S(1)} %copy-done.16, f32[2,384]{1,0:T(2,128)S(1)} %copy-done.17, f32[2,512]{1,0:T(2,128)S(1)} %copy-done.10, ...), custom_call_target="tpu_custom_call" | custom-call | flops 5000000000 | bytes 1 | tf_op jit(solution)/shard_map/prepare/pallas_call | solution.py:46
  19.0 1.4 collective-permute-done.5.refs_1_
  20.4 1.9 drive0.1
  23.6 2.1 %collective-permute-start.10 = (f32[8,768]{1,0:T(8,128)S(1)}, f32[8,768]{1,0:T(8,128)S(1)}, u32[]{:S(2)}, u32[]{:S(2)}) collective-permute-start(f32[8,768]{1,0:T(8,128)S(1)} %combine.4.refs_0_), channel_id=1, source_target_pairs={{0,7},{1,6},{2,5},{3,4},{4,3},{5,2},{6,1},{7,0},{8,15},{9,14},{10,... | collective-permute-start | bytes 73736 | tf_op jit(solution)/shard_map/ppermute | solution.py:862
  25.9 1.8 collective-permute-start.9
  30.0 5.4 %finish0.1 = (f32[1032,768]{1,0:T(8,128)S(1)}, bf16[1024,512]{1,0:T(8,128)(2,1)S(1)}, f32[1024,512]{1,0:T(8,128)S(1)}, f32[1024,512]{1,0:T(8,128)S(1)}, f32[1024...) custom-call(f32[8,768]{1,0:T(8,128)S(1)} %combine.4.refs_0_, ...), custom_call_target="tpu_custom_call" | custom-call | flops 5000000000 | bytes 1 | tf_op jit(solution)/shard_map/finish0/pallas_call | solution.py:46
  36.6 1.3 collective-permute-start.12
  38.4 1.3 collective-permute-start.14
  41.5 1.4 collective-permute-start.15
  42.9 1.4 collective-permute-start.16
  45.4 2.0 %keep.1 = (f32[1024,128]{1,0:T(8,128)S(1)}, f32[8,128]{1,0:T(8,128)S(1)}, f32[8,8,128]{2,1,0:T(8,128)S(1)}) custom-call(s32[4,16]{1,0:T(4,128)S(1)} %copy-done.18, f32[8,768]{1,0:T(8,128)S(1)} %get-tuple-element.116.e_ref.refs_4_.refs_1_), custom_call_target="tpu_custom_call" | custom-call | flops 5000000000 | bytes 1 | tf_op jit(solution)/shard_map/keep/pallas_call | solution.py:46
  47.5 1.8 drive1.1
  50.6 1.6 collective-permute-start.21
  52.3 2.3 %collective-permute-start.20 = (f32[8,768]{1,0:T(8,128)S(1)}, f32[8,768]{1,0:T(8,128)S(1)}, u32[]{:S(2)}, u32[]{:S(2)}) collective-permute-start(f32[8,768]{1,0:T(8,128)S(1)} %combine.5.refs_0_), channel_id=1, source_target_pairs={{0,5},{1,4},{2,7},{3,6},{4,1},{5,0},{6,3},{7,2},{8,13},{9,12},{10,... | collective-permute-start | bytes 73736 | tf_op jit(solution)/shard_map/ppermute | solution.py:862
  56.6 9.9 %middle.1 = (f32[4,1024,128]{2,1,0:T(8,128)S(1)}, f32[1032,768]{1,0:T(8,128)S(1)}, bf16[1024,512]{1,0:T(8,128)(2,1)S(1)}, f32[1024,768]{1,0:T(8,128)S(1)}, f32[1...) custom-call(f32[8,768]{1,0:T(8,128)S(1)} %combine.5.refs_0_, ...), custom_call_target="tpu_custom_call" | custom-call | flops 5000000000 | bytes 1 | tf_op jit(solution)/shard_map/middle/pallas_call | solution.py:46
  68.1 2.0 %collective-permute-start.25 = (f32[8,768]{1,0:T(8,128)S(1)}, f32[8,768]{1,0:T(8,128)S(1)}, u32[]{:S(2)}, u32[]{:S(2)}) collective-permute-start(f32[8,768]{1,0:T(8,128)S(1)} %combine.6.refs_1_.refs_0_), channel_id=1, source_target_pairs={{0,7},{1,6},{2,5},{3,4},{4,3},{5,2},{6,1},{7,0},{8,15},{9,14},{10,... | collective-permute-start | bytes 73736 | tf_op jit(solution)/shard_map/ppermute | solution.py:862
  70.9 1.3 collective-permute-start.24
  73.5 1.5 collective-permute-start.29
  75.0 3.7 %adjoint1.1 = (f32[1024,512]{1,0:T(8,128)S(1)}, f32[768,512]{1,0:T(8,128)S(1)}, f32[8,128]{1,0:T(8,128)S(1)}, f32[16,128]{1,0:T(8,128)S(1)}) custom-call(f32[8,768]{1,0:T(8,128)S(1)} %combine.6.refs_1_.refs_0_, f32[8,768]{1,0:T(8,128)S(1)} %collective-permute-done.23.refs_1_, f32[8,768]{1,0:T(8,128)S(1)} %collective-permute-done.24.refs_2_, ...), custom_call_target="tpu_custom_call" | custom-call | flops 5000000000 | bytes 1 | tf_op jit(solution)/shard_map/adjoint1/pallas_call | solution.py:46
  80.2 2.3 %collective-permute-start.28 = (f32[16,128]{1,0:T(8,128)S(1)}, f32[16,128]{1,0:T(8,128)S(1)}, u32[]{:S(2)}, u32[]{:S(2)}) collective-permute-start(f32[16,128]{1,0:T(8,128)S(1)} %add.45.refs_2_.refs_0_), channel_id=1, source_target_pairs={{0,25},{1,24},{2,27},{3,26},{4,29},{5,28},{6,31},{7,30},{8,17},{9,... | collective-permute-start | bytes 24584 | tf_op jit(solution)/shard_map/ppermute | solution.py:862
  84.3 1.2 collective-permute-done.30.refs_1_
  85.9 1.7 collective-permute-start.32
  88.1 1.8 collective-permute-start.34
  89.9 1.5 collective-permute-start.35
  91.4 1.5 emit.1.refs_2_
  92.9 1.2 copy-done.2
  94.3 2.7 %collective-permute-done.35.refs_1_ = f32[160,512]{1,0:T(8,128)S(1)} collective-permute-done((f32[160,512]{1,0:T(8,128)S(1)}, f32[160,512]{1,0:T(8,128)S(1)}, u32[]{:S(2)}, u32[]{:S(2)}) %collective-permute-start.35) | collective-permute-done | bytes 327712 | tf_op jit(solution)/shard_map/ppermute | solution.py:867
  97.0 5.1 %lower.1 = (f32[1024,512]{1,0:T(8,128)S(1)}, bf16[1024,512]{1,0:T(8,128)(2,1)S(1)}, f32[1024,768]{1,0:T(8,128)S(1)}, f32[512,512]{1,0:T(8,128)S(1)}, f32[768,512...) custom-call(f32[16,128]{1,0:T(8,128)S(1)} %add.49.refs_2_.refs_0_, ...), custom_call_target="tpu_custom_call" | custom-call | flops 5000000000 | bytes 1 | tf_op jit(solution)/shard_map/lower/pallas_call | solution.py:46
  102.3 1.2 collective-permute-done.37.refs_1_.refs_5_
  104.2 1.5 collective-permute-start.40
  106.5 2.8 %collective-permute-done.40.src_ref = f32[8,768]{1,0:T(8,128)S(1)} collective-permute-done((f32[8,768]{1,0:T(8,128)S(1)}, f32[8,768]{1,0:T(8,128)S(1)}, u32[]{:S(2)}, u32[]{:S(2)}) %collective-permute-start.40) | collective-permute-done | bytes 24608 | tf_op jit(solution)/shard_map/ppermute | solution.py:862
  109.3 2.0 %collective-permute-start.39 = (f32[8,768]{1,0:T(8,128)S(1)}, f32[8,768]{1,0:T(8,128)S(1)}, u32[]{:S(2)}, u32[]{:S(2)}) collective-permute-start(f32[8,768]{1,0:T(8,128)S(1)} %combine.7.refs_1_.refs_0_), channel_id=1, source_target_pairs={{0,5},{1,4},{2,7},{3,6},{4,1},{5,0},{6,3},{7,2},{8,13},{9,12},{10,... | collective-permute-start | bytes 73736 | tf_op jit(solution)/shard_map/ppermute | solution.py:862
  112.3 1.9 collective-permute-done.38.refs_1_
  114.2 4.4 %adjoint0.1 = (f32[1024,512]{1,0:T(8,128)S(1)}, f32[768,512]{1,0:T(8,128)S(1)}, f32[8,128]{1,0:T(8,128)}, f32[64,128]{1,0:T(8,128)S(1)}) custom-call(f32[8,768]{1,0:T(8,128)S(1)} %combine.7.refs_1_.refs_0_, f32[8,768]{1,0:T(8,128)S(1)} %collective-permute-done.38.refs_1_, f32[8,768]{1,0:T(8,128)S(1)} %collective-permute-done.39.refs_2_, ...), custom_call_target="tpu_custom_call" | custom-call | flops 5000000000 | bytes 1 | tf_op jit(solution)/shard_map/adjoint0/pallas_call | solution.py:46
  119.3 2.9 %collective-permute-start.53 = (f32[80,512]{1,0:T(8,128)S(1)}, f32[80,512]{1,0:T(8,128)S(1)}, u32[]{:S(2)}, u32[]{:S(2)}) collective-permute-start(f32[80,512]{1,0:T(8,128)S(1)} %add.50.refs_2_.refs_0_), channel_id=1, source_target_pairs={{0,4},{1,5},{2,6},{3,7},{4,0},{5,1},{6,2},{7,3},{8,12},{9,13},{10,... | collective-permute-start | bytes 491528 | tf_op jit(solution)/shard_map/ppermute | solution.py:862
  123.4 1.8 collective-permute-start.57
  125.2 4.9 %collective-permute-done.46.refs_1_ = f32[96,512]{1,0:T(8,128)S(1)} collective-permute-done((f32[96,512]{1,0:T(8,128)S(1)}, f32[96,512]{1,0:T(8,128)S(1)}, u32[]{:S(2)}, u32[]{:S(2)}) %collective-permute-start.46) | collective-permute-done | bytes 196640 | tf_op jit(solution)/shard_map/ppermute | solution.py:867
  130.4 1.4 collective-permute-start.58
  131.8 2.0 %collective-permute-done.53.refs_1_ = f32[80,512]{1,0:T(8,128)S(1)} collective-permute-done((f32[80,512]{1,0:T(8,128)S(1)}, f32[80,512]{1,0:T(8,128)S(1)}, u32[]{:S(2)}, u32[]{:S(2)}) %collective-permute-start.53) | collective-permute-done | bytes 163872 | tf_op jit(solution)/shard_map/ppermute | solution.py:862
  134.0 1.9 collective-permute-done.51.refs_1_
  136.0 1.2 collective-permute-done.58.refs_1_
  137.5 3.4 %collective-permute-start.63 = (f32[48,512]{1,0:T(8,128)S(1)}, f32[48,512]{1,0:T(8,128)S(1)}, u32[]{:S(2)}, u32[]{:S(2)}) collective-permute-start(f32[48,512]{1,0:T(8,128)S(1)} %add.53.refs_2_.refs_0_), channel_id=1, source_target_pairs={{0,4},{1,5},{2,6},{3,7},{4,0},{5,1},{6,2},{7,3},{8,12},{9,13},{10,... | collective-permute-start | bytes 294920 | tf_op jit(solution)/shard_map/ppermute | solution.py:862
  141.8 2.6 %collective-permute-done.54.refs_1_ = f32[48,512]{1,0:T(8,128)S(1)} collective-permute-done((f32[48,512]{1,0:T(8,128)S(1)}, f32[48,512]{1,0:T(8,128)S(1)}, u32[]{:S(2)}, u32[]{:S(2)}) %collective-permute-start.54) | collective-permute-done | bytes 98336 | tf_op jit(solution)/shard_map/ppermute | solution.py:862
  144.4 3.2 %collective-permute-start.66 = (f32[48,512]{1,0:T(8,128)S(1)}, f32[48,512]{1,0:T(8,128)S(1)}, u32[]{:S(2)}, u32[]{:S(2)}) collective-permute-start(f32[48,512]{1,0:T(8,128)S(1)} %add.55.refs_2_.refs_0_), channel_id=1, source_target_pairs={{0,4},{1,5},{2,6},{3,7},{4,0},{5,1},{6,2},{7,3},{8,12},{9,13},{10,... | collective-permute-start | bytes 294920 | tf_op jit(solution)/shard_map/ppermute | solution.py:862
  147.8 2.8 %collective-permute-done.62.refs_1_ = f32[48,512]{1,0:T(8,128)S(1)} collective-permute-done((f32[48,512]{1,0:T(8,128)S(1)}, f32[48,512]{1,0:T(8,128)S(1)}, u32[]{:S(2)}, u32[]{:S(2)}) %collective-permute-start.62) | collective-permute-done | bytes 98336 | tf_op jit(solution)/shard_map/ppermute | solution.py:862
  150.7 2.5 %collective-permute-start.68 = (f32[48,512]{1,0:T(8,128)S(1)}, f32[48,512]{1,0:T(8,128)S(1)}, u32[]{:S(2)}, u32[]{:S(2)}) collective-permute-start(f32[48,512]{1,0:T(8,128)S(1)} %add.58.refs_2_.refs_0_), channel_id=1, source_target_pairs={{0,4},{1,5},{2,6},{3,7},{4,0},{5,1},{6,2},{7,3},{8,12},{9,13},{10,... | collective-permute-start | bytes 294920 | tf_op jit(solution)/shard_map/ppermute | solution.py:862
  155.9 2.0 %collective-permute-done.68.refs_1_ = f32[48,512]{1,0:T(8,128)S(1)} collective-permute-done((f32[48,512]{1,0:T(8,128)S(1)}, f32[48,512]{1,0:T(8,128)S(1)}, u32[]{:S(2)}, u32[]{:S(2)}) %collective-permute-start.68) | collective-permute-done | bytes 98336 | tf_op jit(solution)/shard_map/ppermute | solution.py:862
  160.6 1.8 collective-permute-start.75
  162.4 3.0 %collective-permute-done.69.refs_1_ = f32[48,512]{1,0:T(8,128)S(1)} collective-permute-done((f32[48,512]{1,0:T(8,128)S(1)}, f32[48,512]{1,0:T(8,128)S(1)}, u32[]{:S(2)}, u32[]{:S(2)}) %collective-permute-start.69) | collective-permute-done | bytes 98336 | tf_op jit(solution)/shard_map/ppermute | solution.py:862
  165.6 1.9 collective-permute-start.74
  167.6 1.3 collective-permute-start.79
  168.9 4.3 %collective-permute-done.76.refs_1_ = f32[96,512]{1,0:T(8,128)S(1)} collective-permute-done((f32[96,512]{1,0:T(8,128)S(1)}, f32[96,512]{1,0:T(8,128)S(1)}, u32[]{:S(2)}, u32[]{:S(2)}) %collective-permute-start.76) | collective-permute-done | bytes 196640 | tf_op jit(solution)/shard_map/ppermute | solution.py:867
  173.2 1.3 collective-permute-start.78
  174.6 1.4 collective-permute-done.74.refs_1_
  178.4 3.1 %leave.1 = (f32[4,256,512]{2,1,0:T(8,128)}, f32[2,512]{1,0:T(2,128)}, f32[2,512]{1,0:T(2,128)}, f32[2,512]{1,0:T(2,128)}, f32[2,512]{1,0:T(2,128)}, /*index=5*/f...) custom-call(f32[64,128]{1,0:T(8,128)S(1)} %add.65.refs_0_.refs_12_, ...), custom_call_target="tpu_custom_call" | custom-call | flops 5000000000 | bytes 1 | tf_op jit(solution)/shard_map/leave/pallas_call | solution.py:46
  182.3 1.6 place.5
  185.1 1.2 place.6
  186.7 1.2 place.7
  189.0 1.8 place.9
  (238 shorter events, 42.1 us)
Async XLA Ops:
  5.8 5.0 %collective-permute-start.1 = (f32[24,128]{1,0:T(8,128)S(1)}, f32[24,128]{1,0:T(8,128)S(1)}, u32[]{:S(2)}, u32[]{:S(2)}) collective-permute-start(f32[24,128]{1,0:T(8,128)S(1)} %add.35.refs_0_), channel_id=1, source_target_pairs={{0,25},{1,24},{2,27},{3,26},{4,29},{5,28},{6,31},{7,30},{8,17},{9,... | collective-permute-start | bytes 36872 | tf_op jit(solution)/shard_map/ppermute | solution.py:862
  13.0 6.0 %collective-permute-start.4 = (f32[24,128]{1,0:T(8,128)S(1)}, f32[24,128]{1,0:T(8,128)S(1)}, u32[]{:S(2)}, u32[]{:S(2)}) collective-permute-start(f32[24,128]{1,0:T(8,128)S(1)} %add.38.refs_0_), channel_id=1, source_target_pairs={{0,7},{1,6},{2,5},{3,4},{4,3},{5,2},{6,1},{7,0},{8,15},{9,14},{10,... | collective-permute-start | bytes 36872 | tf_op jit(solution)/shard_map/ppermute | solution.py:862
  16.4 4.0 %collective-permute-start.5 = (f32[24,128]{1,0:T(8,128)S(1)}, f32[24,128]{1,0:T(8,128)S(1)}, u32[]{:S(2)}, u32[]{:S(2)}) collective-permute-start(f32[24,128]{1,0:T(8,128)S(1)} %add.38.refs_0_), channel_id=1, source_target_pairs={{0,5},{1,4},{2,7},{3,6},{4,1},{5,0},{6,3},{7,2},{8,13},{9,12},{10,... | collective-permute-start | bytes 36872 | tf_op jit(solution)/shard_map/ppermute | solution.py:862
  23.6 5.1 %collective-permute-start.10 = (f32[8,768]{1,0:T(8,128)S(1)}, f32[8,768]{1,0:T(8,128)S(1)}, u32[]{:S(2)}, u32[]{:S(2)}) collective-permute-start(f32[8,768]{1,0:T(8,128)S(1)} %combine.4.refs_0_), channel_id=1, source_target_pairs={{0,7},{1,6},{2,5},{3,4},{4,3},{5,2},{6,1},{7,0},{8,15},{9,14},{10,... | collective-permute-start | bytes 73736 | tf_op jit(solution)/shard_map/ppermute | solution.py:862
  25.9 4.2 %collective-permute-start.9 = (f32[8,768]{1,0:T(8,128)S(1)}, f32[8,768]{1,0:T(8,128)S(1)}, u32[]{:S(2)}, u32[]{:S(2)}) collective-permute-start(f32[8,768]{1,0:T(8,128)S(1)} %combine.4.refs_0_), channel_id=1, source_target_pairs={{0,5},{1,4},{2,7},{3,6},{4,1},{5,0},{6,3},{7,2},{8,13},{9,12},{10,... | collective-permute-start | bytes 73736 | tf_op jit(solution)/shard_map/ppermute | solution.py:862
  41.5 5.9 %collective-permute-start.15 = (f32[16,128]{1,0:T(8,128)S(1)}, f32[16,128]{1,0:T(8,128)S(1)}, u32[]{:S(2)}, u32[]{:S(2)}) collective-permute-start(f32[16,128]{1,0:T(8,128)S(1)} %add.42.refs_0_), channel_id=1, source_target_pairs={{0,7},{1,6},{2,5},{3,4},{4,3},{5,2},{6,1},{7,0},{8,15},{9,14},{10,... | collective-permute-start | bytes 24584 | tf_op jit(solution)/shard_map/ppermute | solution.py:862
  42.9 4.5 %collective-permute-start.16 = (f32[16,128]{1,0:T(8,128)S(1)}, f32[16,128]{1,0:T(8,128)S(1)}, u32[]{:S(2)}, u32[]{:S(2)}) collective-permute-start(f32[16,128]{1,0:T(8,128)S(1)} %add.42.refs_0_), channel_id=1, source_target_pairs={{0,5},{1,4},{2,7},{3,6},{4,1},{5,0},{6,3},{7,2},{8,13},{9,12},{10,... | collective-permute-start | bytes 24584 | tf_op jit(solution)/shard_map/ppermute | solution.py:862
  50.6 5.2 %collective-permute-start.21 = (f32[8,768]{1,0:T(8,128)S(1)}, f32[8,768]{1,0:T(8,128)S(1)}, u32[]{:S(2)}, u32[]{:S(2)}) collective-permute-start(f32[8,768]{1,0:T(8,128)S(1)} %combine.5.refs_0_), channel_id=1, source_target_pairs={{0,7},{1,6},{2,5},{3,4},{4,3},{5,2},{6,1},{7,0},{8,15},{9,14},{10,... | collective-permute-start | bytes 73736 | tf_op jit(solution)/shard_map/ppermute | solution.py:862
  52.3 4.2 %collective-permute-start.20 = (f32[8,768]{1,0:T(8,128)S(1)}, f32[8,768]{1,0:T(8,128)S(1)}, u32[]{:S(2)}, u32[]{:S(2)}) collective-permute-start(f32[8,768]{1,0:T(8,128)S(1)} %combine.5.refs_0_), channel_id=1, source_target_pairs={{0,5},{1,4},{2,7},{3,6},{4,1},{5,0},{6,3},{7,2},{8,13},{9,12},{10,... | collective-permute-start | bytes 73736 | tf_op jit(solution)/shard_map/ppermute | solution.py:862
  67.9 5.4 %collective-permute-start.26 = (f32[640,512]{1,0:T(8,128)S(1)}, f32[640,512]{1,0:T(8,128)S(1)}, u32[]{:S(2)}, u32[]{:S(2)}) collective-permute-start(f32[640,512]{1,0:T(8,128)S(1)} %split.5.refs_2_), channel_id=1, source_target_pairs={{0,1},{1,0},{2,3},{3,2},{4,5},{5,4},{6,7},{7,6},{8,9},{9,8},{10,11... | collective-permute-start | bytes 3932168 | tf_op jit(solution)/shard_map/ppermute | solution.py:862
  68.1 5.2 %collective-permute-start.25 = (f32[8,768]{1,0:T(8,128)S(1)}, f32[8,768]{1,0:T(8,128)S(1)}, u32[]{:S(2)}, u32[]{:S(2)}) collective-permute-start(f32[8,768]{1,0:T(8,128)S(1)} %combine.6.refs_1_.refs_0_), channel_id=1, source_target_pairs={{0,7},{1,6},{2,5},{3,4},{4,3},{5,2},{6,1},{7,0},{8,15},{9,14},{10,... | collective-permute-start | bytes 73736 | tf_op jit(solution)/shard_map/ppermute | solution.py:862
  70.1 4.8 %collective-permute-start.23 = (f32[8,768]{1,0:T(8,128)S(1)}, f32[8,768]{1,0:T(8,128)S(1)}, u32[]{:S(2)}, u32[]{:S(2)}) collective-permute-start(f32[8,768]{1,0:T(8,128)S(1)} %combine.6.refs_1_.refs_0_), channel_id=1, source_target_pairs={{0,3},{1,2},{2,1},{3,0},{4,7},{5,6},{6,5},{7,4},{8,11},{9,10},{10,... | collective-permute-start | bytes 73736 | tf_op jit(solution)/shard_map/ppermute | solution.py:862
  70.9 4.2 %collective-permute-start.24 = (f32[8,768]{1,0:T(8,128)S(1)}, f32[8,768]{1,0:T(8,128)S(1)}, u32[]{:S(2)}, u32[]{:S(2)}) collective-permute-start(f32[8,768]{1,0:T(8,128)S(1)} %combine.6.refs_1_.refs_0_), channel_id=1, source_target_pairs={{0,5},{1,4},{2,7},{3,6},{4,1},{5,0},{6,3},{7,2},{8,13},{9,12},{10,... | collective-permute-start | bytes 73736 | tf_op jit(solution)/shard_map/ppermute | solution.py:862
  73.5 10.7 %collective-permute-start.29 = (f32[320,512]{1,0:T(8,128)S(1)}, f32[320,512]{1,0:T(8,128)S(1)}, u32[]{:S(2)}, u32[]{:S(2)}) collective-permute-start(f32[320,512]{1,0:T(8,128)S(1)} %get-tuple-element.135.refs_20_), channel_id=1, source_target_pairs={{0,8},{1,17},{2,10},{3,19},{4,12},{5,21},{6,14},{7,23},{8,0},{9,25... | collective-permute-start | bytes 1966088 | tf_op jit(solution)/shard_map/ppermute | solution.py:867
  79.4 14.7 %collective-permute-start.36 = (f32[384,512]{1,0:T(8,128)S(1)}, f32[384,512]{1,0:T(8,128)S(1)}, u32[]{:S(2)}, u32[]{:S(2)}) collective-permute-start(f32[384,512]{1,0:T(8,128)S(1)} %split.6.refs_2_), channel_id=1, source_target_pairs={{0,1},{1,0},{2,3},{3,2},{4,5},{5,4},{6,7},{7,6},{8,9},{9,8},{10,11... | collective-permute-start | bytes 2359304 | tf_op jit(solution)/shard_map/ppermute | solution.py:862
  80.2 4.1 %collective-permute-start.28 = (f32[16,128]{1,0:T(8,128)S(1)}, f32[16,128]{1,0:T(8,128)S(1)}, u32[]{:S(2)}, u32[]{:S(2)}) collective-permute-start(f32[16,128]{1,0:T(8,128)S(1)} %add.45.refs_2_.refs_0_), channel_id=1, source_target_pairs={{0,25},{1,24},{2,27},{3,26},{4,29},{5,28},{6,31},{7,30},{8,17},{9,... | collective-permute-start | bytes 24584 | tf_op jit(solution)/shard_map/ppermute | solution.py:862
  85.9 7.0 %collective-permute-start.32 = (f32[16,128]{1,0:T(8,128)S(1)}, f32[16,128]{1,0:T(8,128)S(1)}, u32[]{:S(2)}, u32[]{:S(2)}) collective-permute-start(f32[16,128]{1,0:T(8,128)S(1)} %add.47.refs_1_.refs_0_), channel_id=1, source_target_pairs={{0,7},{1,6},{2,5},{3,4},{4,3},{5,2},{6,1},{7,0},{8,15},{9,14},{10,... | collective-permute-start | bytes 24584 | tf_op jit(solution)/shard_map/ppermute | solution.py:862
  87.5 6.6 %collective-permute-start.33 = (f32[16,128]{1,0:T(8,128)S(1)}, f32[16,128]{1,0:T(8,128)S(1)}, u32[]{:S(2)}, u32[]{:S(2)}) collective-permute-start(f32[16,128]{1,0:T(8,128)S(1)} %add.47.refs_1_.refs_0_), channel_id=1, source_target_pairs={{0,5},{1,4},{2,7},{3,6},{4,1},{5,0},{6,3},{7,2},{8,13},{9,12},{10,... | collective-permute-start | bytes 24584 | tf_op jit(solution)/shard_map/ppermute | solution.py:862
  88.1 6.0 %collective-permute-start.34 = (f32[16,128]{1,0:T(8,128)S(1)}, f32[16,128]{1,0:T(8,128)S(1)}, u32[]{:S(2)}, u32[]{:S(2)}) collective-permute-start(f32[16,128]{1,0:T(8,128)S(1)} %add.47.refs_1_.refs_0_), channel_id=1, source_target_pairs={{0,3},{1,2},{2,1},{3,0},{4,7},{5,6},{6,5},{7,4},{8,11},{9,10},{10,... | collective-permute-start | bytes 24584 | tf_op jit(solution)/shard_map/ppermute | solution.py:862
  89.9 7.1 %collective-permute-start.35 = (f32[160,512]{1,0:T(8,128)S(1)}, f32[160,512]{1,0:T(8,128)S(1)}, u32[]{:S(2)}, u32[]{:S(2)}) collective-permute-start(f32[160,512]{1,0:T(8,128)S(1)} %get-tuple-element.139.refs_2_), channel_id=1, source_target_pairs={{0,16},{1,9},{2,18},{3,11},{4,20},{5,13},{6,22},{7,15},{8,24},{9,1... | collective-permute-start | bytes 983048 | tf_op jit(solution)/shard_map/ppermute | solution.py:867
  103.5 5.7 %collective-permute-start.42 = (f32[384,512]{1,0:T(8,128)S(1)}, f32[384,512]{1,0:T(8,128)S(1)}, u32[]{:S(2)}, u32[]{:S(2)}) collective-permute-start(f32[384,512]{1,0:T(8,128)S(1)} %split.7.refs_1_), channel_id=1, source_target_pairs={{0,1},{1,0},{2,3},{3,2},{4,5},{5,4},{6,7},{7,6},{8,9},{9,8},{10,11... | collective-permute-start | bytes 2359304 | tf_op jit(solution)/shard_map/ppermute | solution.py:862
  103.8 7.6 %collective-permute-start.41 = (f32[256,512]{1,0:T(8,128)S(1)}, f32[256,512]{1,0:T(8,128)S(1)}, u32[]{:S(2)}, u32[]{:S(2)}) collective-permute-start(f32[256,512]{1,0:T(8,128)S(1)} %split.8.refs_2_), channel_id=1, source_target_pairs={{0,1},{1,0},{2,3},{3,2},{4,5},{5,4},{6,7},{7,6},{8,9},{9,8},{10,11... | collective-permute-start | bytes 1572872 | tf_op jit(solution)/shard_map/ppermute | solution.py:862
  104.2 5.0 %collective-permute-start.40 = (f32[8,768]{1,0:T(8,128)S(1)}, f32[8,768]{1,0:T(8,128)S(1)}, u32[]{:S(2)}, u32[]{:S(2)}) collective-permute-start(f32[8,768]{1,0:T(8,128)S(1)} %combine.7.refs_1_.refs_0_), channel_id=1, source_target_pairs={{0,7},{1,6},{2,5},{3,4},{4,3},{5,2},{6,1},{7,0},{8,15},{9,14},{10,... | collective-permute-start | bytes 73736 | tf_op jit(solution)/shard_map/ppermute | solution.py:862
  105.7 13.6 %collective-permute-start.44 = (f32[192,512]{1,0:T(8,128)S(1)}, f32[192,512]{1,0:T(8,128)S(1)}, u32[]{:S(2)}, u32[]{:S(2)}) collective-permute-start(f32[192,512]{1,0:T(8,128)S(1)} %get-tuple-element.147.refs_2_), channel_id=1, source_target_pairs={{0,8},{1,17},{2,10},{3,19},{4,12},{5,21},{6,14},{7,23},{8,0},{9,25... | collective-permute-start | bytes 1179656 | tf_op jit(solution)/shard_map/ppermute | solution.py:867
  106.5 12.3 %collective-permute-start.45 = (f32[80,512]{1,0:T(8,128)S(1)}, f32[80,512]{1,0:T(8,128)S(1)}, u32[]{:S(2)}, u32[]{:S(2)}) collective-permute-start(f32[80,512]{1,0:T(8,128)S(1)} %get-tuple-element.148.refs_19_), channel_id=1, source_target_pairs={{0,2},{1,3},{2,0},{3,1},{4,6},{5,7},{6,4},{7,5},{8,10},{9,11},{10,... | collective-permute-start | bytes 491528 | tf_op jit(solution)/shard_map/ppermute | solution.py:862
  109.3 5.0 %collective-permute-start.38 = (f32[8,768]{1,0:T(8,128)S(1)}, f32[8,768]{1,0:T(8,128)S(1)}, u32[]{:S(2)}, u32[]{:S(2)}) collective-permute-start(f32[8,768]{1,0:T(8,128)S(1)} %combine.7.refs_1_.refs_0_), channel_id=1, source_target_pairs={{0,3},{1,2},{2,1},{3,0},{4,7},{5,6},{6,5},{7,4},{8,11},{9,10},{10,... | collective-permute-start | bytes 73736 | tf_op jit(solution)/shard_map/ppermute | solution.py:862
  109.3 4.9 %collective-permute-start.39 = (f32[8,768]{1,0:T(8,128)S(1)}, f32[8,768]{1,0:T(8,128)S(1)}, u32[]{:S(2)}, u32[]{:S(2)}) collective-permute-start(f32[8,768]{1,0:T(8,128)S(1)} %combine.7.refs_1_.refs_0_), channel_id=1, source_target_pairs={{0,5},{1,4},{2,7},{3,6},{4,1},{5,0},{6,3},{7,2},{8,13},{9,12},{10,... | collective-permute-start | bytes 73736 | tf_op jit(solution)/shard_map/ppermute | solution.py:862
  111.4 12.0 %collective-permute-start.47 = (f32[192,512]{1,0:T(8,128)S(1)}, f32[192,512]{1,0:T(8,128)S(1)}, u32[]{:S(2)}, u32[]{:S(2)}) collective-permute-start(f32[192,512]{1,0:T(8,128)S(1)} %get-tuple-element.158.refs_2_), channel_id=1, source_target_pairs={{0,8},{1,17},{2,10},{3,19},{4,12},{5,21},{6,14},{7,23},{8,0},{9,25... | collective-permute-start | bytes 1179656 | tf_op jit(solution)/shard_map/ppermute | solution.py:867
  114.2 8.4 %collective-permute-start.48 = (f32[128,512]{1,0:T(8,128)S(1)}, f32[128,512]{1,0:T(8,128)S(1)}, u32[]{:S(2)}, u32[]{:S(2)}) collective-permute-start(f32[128,512]{1,0:T(8,128)S(1)} %get-tuple-element.159.refs_23_), channel_id=1, source_target_pairs={{0,2},{1,3},{2,0},{3,1},{4,6},{5,7},{6,4},{7,5},{8,10},{9,11},{10,... | collective-permute-start | bytes 786440 | tf_op jit(solution)/shard_map/ppermute | solution.py:862
  118.7 11.7 %collective-permute-start.43 = (f32[64,128]{1,0:T(8,128)S(1)}, f32[64,128]{1,0:T(8,128)S(1)}, u32[]{:S(2)}, u32[]{:S(2)}) collective-permute-start(f32[64,128]{1,0:T(8,128)S(1)} %get-tuple-element.160.refs_1_.refs_0_), channel_id=1, source_target_pairs={{0,1},{1,0},{2,3},{3,2},{4,5},{5,4},{6,7},{7,6},{8,9},{9,8},{10,11... | collective-permute-start | bytes 98312 | tf_op jit(solution)/shard_map/ppermute | solution.py:862
  119.3 14.4 %collective-permute-start.53 = (f32[80,512]{1,0:T(8,128)S(1)}, f32[80,512]{1,0:T(8,128)S(1)}, u32[]{:S(2)}, u32[]{:S(2)}) collective-permute-start(f32[80,512]{1,0:T(8,128)S(1)} %add.50.refs_2_.refs_0_), channel_id=1, source_target_pairs={{0,4},{1,5},{2,6},{3,7},{4,0},{5,1},{6,2},{7,3},{8,12},{9,13},{10,... | collective-permute-start | bytes 491528 | tf_op jit(solution)/shard_map/ppermute | solution.py:862
  122.3 7.8 %collective-permute-start.46 = (f32[96,512]{1,0:T(8,128)S(1)}, f32[96,512]{1,0:T(8,128)S(1)}, u32[]{:S(2)}, u32[]{:S(2)}) collective-permute-start(f32[96,512]{1,0:T(8,128)S(1)} %get-tuple-element.165.refs_2_), channel_id=1, source_target_pairs={{0,16},{1,9},{2,18},{3,11},{4,20},{5,13},{6,22},{7,15},{8,24},{9,1... | collective-permute-start | bytes 589832 | tf_op jit(solution)/shard_map/ppermute | solution.py:867
  122.7 11.1 %collective-permute-start.52 = (f32[192,512]{1,0:T(8,128)S(1)}, f32[192,512]{1,0:T(8,128)S(1)}, u32[]{:S(2)}, u32[]{:S(2)}) collective-permute-start(f32[192,512]{1,0:T(8,128)S(1)} %get-tuple-element.168.refs_2_), channel_id=1, source_target_pairs={{0,8},{1,17},{2,10},{3,19},{4,12},{5,21},{6,14},{7,23},{8,0},{9,25... | collective-permute-start | bytes 1179656 | tf_op jit(solution)/shard_map/ppermute | solution.py:867
  123.4 14.1 %collective-permute-start.57 = (f32[64,512]{1,0:T(8,128)S(1)}, f32[64,512]{1,0:T(8,128)S(1)}, u32[]{:S(2)}, u32[]{:S(2)}) collective-permute-start(f32[64,512]{1,0:T(8,128)S(1)} %get-tuple-element.169.refs_2_), channel_id=1, source_target_pairs={{0,4},{1,5},{2,6},{3,7},{4,0},{5,1},{6,2},{7,3},{8,12},{9,13},{10,... | collective-permute-start | bytes 393224 | tf_op jit(solution)/shard_map/ppermute | solution.py:862
  130.1 5.7 %collective-permute-start.51 = (f32[96,512]{1,0:T(8,128)S(1)}, f32[96,512]{1,0:T(8,128)S(1)}, u32[]{:S(2)}, u32[]{:S(2)}) collective-permute-start(f32[96,512]{1,0:T(8,128)S(1)} %get-tuple-element.170.refs_2_), channel_id=1, source_target_pairs={{0,16},{1,9},{2,18},{3,11},{4,20},{5,13},{6,22},{7,15},{8,24},{9,1... | collective-permute-start | bytes 589832 | tf_op jit(solution)/shard_map/ppermute | solution.py:867
  130.4 6.9 %collective-permute-start.58 = (f32[48,512]{1,0:T(8,128)S(1)}, f32[48,512]{1,0:T(8,128)S(1)}, u32[]{:S(2)}, u32[]{:S(2)}) collective-permute-start(f32[48,512]{1,0:T(8,128)S(1)} %get-tuple-element.171.refs_2_), channel_id=1, source_target_pairs={{0,2},{1,3},{2,0},{3,1},{4,6},{5,7},{6,4},{7,5},{8,10},{9,11},{10,... | collective-permute-start | bytes 294920 | tf_op jit(solution)/shard_map/ppermute | solution.py:862
  133.8 10.7 %collective-permute-start.50 = (f32[64,128]{1,0:T(8,128)S(1)}, f32[64,128]{1,0:T(8,128)S(1)}, u32[]{:S(2)}, u32[]{:S(2)}) collective-permute-start(f32[64,128]{1,0:T(8,128)S(1)} %add.51.refs_2_.refs_0_), channel_id=1, source_target_pairs={{0,9},{1,8},{2,11},{3,10},{4,13},{5,12},{6,15},{7,14},{8,1},{9,0},... | collective-permute-start | bytes 98312 | tf_op jit(solution)/shard_map/ppermute | solution.py:862
  133.8 7.1 %collective-permute-start.56 = (f32[80,512]{1,0:T(8,128)S(1)}, f32[80,512]{1,0:T(8,128)S(1)}, u32[]{:S(2)}, u32[]{:S(2)}) collective-permute-start(f32[80,512]{1,0:T(8,128)S(1)} %add.52.refs_2_.refs_0_), channel_id=1, source_target_pairs={{0,2},{1,3},{2,0},{3,1},{4,6},{5,7},{6,4},{7,5},{8,10},{9,11},{10,... | collective-permute-start | bytes 491528 | tf_op jit(solution)/shard_map/ppermute | solution.py:862
  135.8 5.7 %collective-permute-start.55 = (f32[96,512]{1,0:T(8,128)S(1)}, f32[96,512]{1,0:T(8,128)S(1)}, u32[]{:S(2)}, u32[]{:S(2)}) collective-permute-start(f32[96,512]{1,0:T(8,128)S(1)} %get-tuple-element.174.refs_2_), channel_id=1, source_target_pairs={{0,16},{1,9},{2,18},{3,11},{4,20},{5,13},{6,22},{7,15},{8,24},{9,1... | collective-permute-start | bytes 589832 | tf_op jit(solution)/shard_map/ppermute | solution.py:867
  137.2 7.2 %collective-permute-start.54 = (f32[48,512]{1,0:T(8,128)S(1)}, f32[48,512]{1,0:T(8,128)S(1)}, u32[]{:S(2)}, u32[]{:S(2)}) collective-permute-start(f32[48,512]{1,0:T(8,128)S(1)} %get-tuple-element.176.refs_2_), channel_id=1, source_target_pairs={{0,2},{1,3},{2,0},{3,1},{4,6},{5,7},{6,4},{7,5},{8,10},{9,11},{10,... | collective-permute-start | bytes 294920 | tf_op jit(solution)/shard_map/ppermute | solution.py:862
  137.5 10.2 %collective-permute-start.63 = (f32[48,512]{1,0:T(8,128)S(1)}, f32[48,512]{1,0:T(8,128)S(1)}, u32[]{:S(2)}, u32[]{:S(2)}) collective-permute-start(f32[48,512]{1,0:T(8,128)S(1)} %add.53.refs_2_.refs_0_), channel_id=1, source_target_pairs={{0,4},{1,5},{2,6},{3,7},{4,0},{5,1},{6,2},{7,3},{8,12},{9,13},{10,... | collective-permute-start | bytes 294920 | tf_op jit(solution)/shard_map/ppermute | solution.py:862
  140.9 9.7 %collective-permute-start.61 = (f32[64,512]{1,0:T(8,128)S(1)}, f32[64,512]{1,0:T(8,128)S(1)}, u32[]{:S(2)}, u32[]{:S(2)}) collective-permute-start(f32[64,512]{1,0:T(8,128)S(1)} %add.54.refs_2_.refs_0_), channel_id=1, source_target_pairs={{0,8},{1,17},{2,10},{3,19},{4,12},{5,21},{6,14},{7,23},{8,0},{9,25... | collective-permute-start | bytes 393224 | tf_op jit(solution)/shard_map/ppermute | solution.py:867
  141.5 11.7 %collective-permute-start.60 = (f32[160,512]{1,0:T(8,128)S(1)}, f32[160,512]{1,0:T(8,128)S(1)}, u32[]{:S(2)}, u32[]{:S(2)}) collective-permute-start(f32[160,512]{1,0:T(8,128)S(1)} %join.14.refs_2_.refs_0_), channel_id=1, source_target_pairs={{0,16},{1,9},{2,18},{3,11},{4,20},{5,13},{6,22},{7,15},{8,24},{9,1... | collective-permute-start | bytes 983048 | tf_op jit(solution)/shard_map/ppermute | solution.py:867
  144.4 6.2 %collective-permute-start.62 = (f32[48,512]{1,0:T(8,128)S(1)}, f32[48,512]{1,0:T(8,128)S(1)}, u32[]{:S(2)}, u32[]{:S(2)}) collective-permute-start(f32[48,512]{1,0:T(8,128)S(1)} %get-tuple-element.180.refs_2_), channel_id=1, source_target_pairs={{0,2},{1,3},{2,0},{3,1},{4,6},{5,7},{6,4},{7,5},{8,10},{9,11},{10,... | collective-permute-start | bytes 294920 | tf_op jit(solution)/shard_map/ppermute | solution.py:862
  144.4 10.6 %collective-permute-start.66 = (f32[48,512]{1,0:T(8,128)S(1)}, f32[48,512]{1,0:T(8,128)S(1)}, u32[]{:S(2)}, u32[]{:S(2)}) collective-permute-start(f32[48,512]{1,0:T(8,128)S(1)} %add.55.refs_2_.refs_0_), channel_id=1, source_target_pairs={{0,4},{1,5},{2,6},{3,7},{4,0},{5,1},{6,2},{7,3},{8,12},{9,13},{10,... | collective-permute-start | bytes 294920 | tf_op jit(solution)/shard_map/ppermute | solution.py:862
  147.7 6.2 %collective-permute-start.59 = (f32[64,128]{1,0:T(8,128)S(1)}, f32[64,128]{1,0:T(8,128)S(1)}, u32[]{:S(2)}, u32[]{:S(2)}) collective-permute-start(f32[64,128]{1,0:T(8,128)S(1)} %add.56.refs_2_.refs_0_), channel_id=1, source_target_pairs={{0,17},{1,16},{2,19},{3,18},{4,21},{5,20},{6,23},{7,22},{8,25},{9,... | collective-permute-start | bytes 98312 | tf_op jit(solution)/shard_map/ppermute | solution.py:862
  150.6 5.2 %collective-permute-start.65 = (f32[48,512]{1,0:T(8,128)S(1)}, f32[48,512]{1,0:T(8,128)S(1)}, u32[]{:S(2)}, u32[]{:S(2)}) collective-permute-start(f32[48,512]{1,0:T(8,128)S(1)} %add.57.refs_2_.refs_0_), channel_id=1, source_target_pairs={{0,2},{1,3},{2,0},{3,1},{4,6},{5,7},{6,4},{7,5},{8,10},{9,11},{10,... | collective-permute-start | bytes 294920 | tf_op jit(solution)/shard_map/ppermute | solution.py:862
  150.7 7.3 %collective-permute-start.68 = (f32[48,512]{1,0:T(8,128)S(1)}, f32[48,512]{1,0:T(8,128)S(1)}, u32[]{:S(2)}, u32[]{:S(2)}) collective-permute-start(f32[48,512]{1,0:T(8,128)S(1)} %add.58.refs_2_.refs_0_), channel_id=1, source_target_pairs={{0,4},{1,5},{2,6},{3,7},{4,0},{5,1},{6,2},{7,3},{8,12},{9,13},{10,... | collective-permute-start | bytes 294920 | tf_op jit(solution)/shard_map/ppermute | solution.py:862
  153.2 6.5 %collective-permute-start.71 = (f32[64,512]{1,0:T(8,128)S(1)}, f32[64,512]{1,0:T(8,128)S(1)}, u32[]{:S(2)}, u32[]{:S(2)}) collective-permute-start(f32[64,512]{1,0:T(8,128)S(1)} %add.59.refs_2_.refs_0_), channel_id=1, source_target_pairs={{0,16},{1,9},{2,18},{3,11},{4,20},{5,13},{6,22},{7,15},{8,24},{9,1... | collective-permute-start | bytes 393224 | tf_op jit(solution)/shard_map/ppermute | solution.py:867
  153.9 22.4 %collective-permute-start.73 = (f32[320,512]{1,0:T(8,128)S(1)}, f32[320,512]{1,0:T(8,128)S(1)}, u32[]{:S(2)}, u32[]{:S(2)}) collective-permute-start(f32[320,512]{1,0:T(8,128)S(1)} %join.15.refs_2_.refs_0_), channel_id=1, source_target_pairs={{0,8},{1,17},{2,10},{3,19},{4,12},{5,21},{6,14},{7,23},{8,0},{9,25... | collective-permute-start | bytes 1966088 | tf_op jit(solution)/shard_map/ppermute | solution.py:867
  155.0 12.5 %collective-permute-start.64 = (f32[64,128]{1,0:T(8,128)S(1)}, f32[64,128]{1,0:T(8,128)S(1)}, u32[]{:S(2)}, u32[]{:S(2)}) collective-permute-start(f32[64,128]{1,0:T(8,128)S(1)} %add.60.refs_2_.refs_0_), channel_id=1, source_target_pairs={{0,3},{1,2},{2,1},{3,0},{4,7},{5,6},{6,5},{7,4},{8,11},{9,10},{10,... | collective-permute-start | bytes 98312 | tf_op jit(solution)/shard_map/ppermute | solution.py:862
  155.9 4.7 %collective-permute-start.70 = (f32[48,512]{1,0:T(8,128)S(1)}, f32[48,512]{1,0:T(8,128)S(1)}, u32[]{:S(2)}, u32[]{:S(2)}) collective-permute-start(f32[48,512]{1,0:T(8,128)S(1)} %add.61.refs_2_.refs_0_), channel_id=1, source_target_pairs={{0,2},{1,3},{2,0},{3,1},{4,6},{5,7},{6,4},{7,5},{8,10},{9,11},{10,... | collective-permute-start | bytes 294920 | tf_op jit(solution)/shard_map/ppermute | solution.py:862
  157.9 7.7 %collective-permute-start.67 = (f32[96,512]{1,0:T(8,128)S(1)}, f32[96,512]{1,0:T(8,128)S(1)}, u32[]{:S(2)}, u32[]{:S(2)}) collective-permute-start(f32[96,512]{1,0:T(8,128)S(1)} %join.16.refs_2_.refs_0_), channel_id=1, source_target_pairs={{0,16},{1,9},{2,18},{3,11},{4,20},{5,13},{6,22},{7,15},{8,24},{9,1... | collective-permute-start | bytes 589832 | tf_op jit(solution)/shard_map/ppermute | solution.py:867
  159.7 5.7 %collective-permute-start.69 = (f32[48,512]{1,0:T(8,128)S(1)}, f32[48,512]{1,0:T(8,128)S(1)}, u32[]{:S(2)}, u32[]{:S(2)}) collective-permute-start(f32[48,512]{1,0:T(8,128)S(1)} %add.62.refs_2_.refs_0_), channel_id=1, source_target_pairs={{0,2},{1,3},{2,0},{3,1},{4,6},{5,7},{6,4},{7,5},{8,10},{9,11},{10,... | collective-permute-start | bytes 294920 | tf_op jit(solution)/shard_map/ppermute | solution.py:862
  160.6 12.7 %collective-permute-start.75 = (f32[64,512]{1,0:T(8,128)S(1)}, f32[64,512]{1,0:T(8,128)S(1)}, u32[]{:S(2)}, u32[]{:S(2)}) collective-permute-start(f32[64,512]{1,0:T(8,128)S(1)} %add.63.refs_2_.refs_0_), channel_id=1, source_target_pairs={{0,4},{1,5},{2,6},{3,7},{4,0},{5,1},{6,2},{7,3},{8,12},{9,13},{10,... | collective-permute-start | bytes 393224 | tf_op jit(solution)/shard_map/ppermute | solution.py:862
  165.4 7.8 %collective-permute-start.76 = (f32[96,512]{1,0:T(8,128)S(1)}, f32[96,512]{1,0:T(8,128)S(1)}, u32[]{:S(2)}, u32[]{:S(2)}) collective-permute-start(f32[96,512]{1,0:T(8,128)S(1)} %join.17.refs_2_.refs_0_), channel_id=1, source_target_pairs={{0,16},{1,9},{2,18},{3,11},{4,20},{5,13},{6,22},{7,15},{8,24},{9,1... | collective-permute-start | bytes 589832 | tf_op jit(solution)/shard_map/ppermute | solution.py:867
  165.6 10.4 %collective-permute-start.74 = (f32[96,512]{1,0:T(8,128)S(1)}, f32[96,512]{1,0:T(8,128)S(1)}, u32[]{:S(2)}, u32[]{:S(2)}) collective-permute-start(f32[96,512]{1,0:T(8,128)S(1)} %join.18.refs_2_.refs_0_), channel_id=1, source_target_pairs={{0,16},{1,9},{2,18},{3,11},{4,20},{5,13},{6,22},{7,15},{8,24},{9,1... | collective-permute-start | bytes 589832 | tf_op jit(solution)/shard_map/ppermute | solution.py:867
  167.6 14.0 %collective-permute-start.79 = (f32[192,512]{1,0:T(8,128)S(1)}, f32[192,512]{1,0:T(8,128)S(1)}, u32[]{:S(2)}, u32[]{:S(2)}) collective-permute-start(f32[192,512]{1,0:T(8,128)S(1)} %join.19.refs_2_.refs_0_), channel_id=1, source_target_pairs={{0,8},{1,17},{2,10},{3,19},{4,12},{5,21},{6,14},{7,23},{8,0},{9,25... | collective-permute-start | bytes 1179656 | tf_op jit(solution)/shard_map/ppermute | solution.py:867
  173.2 4.7 %collective-permute-start.72 = (f32[64,128]{1,0:T(8,128)S(1)}, f32[64,128]{1,0:T(8,128)S(1)}, u32[]{:S(2)}, u32[]{:S(2)}) collective-permute-start(f32[64,128]{1,0:T(8,128)S(1)} %add.64.refs_2_.refs_0_), channel_id=1, source_target_pairs={{0,5},{1,4},{2,7},{3,6},{4,1},{5,0},{6,3},{7,2},{8,13},{9,12},{10,... | collective-permute-start | bytes 98312 | tf_op jit(solution)/shard_map/ppermute | solution.py:862
  173.2 8.7 %collective-permute-start.78 = (f32[192,512]{1,0:T(8,128)S(1)}, f32[192,512]{1,0:T(8,128)S(1)}, u32[]{:S(2)}, u32[]{:S(2)}) collective-permute-start(f32[192,512]{1,0:T(8,128)S(1)} %join.20.refs_2_.refs_0_), channel_id=1, source_target_pairs={{0,8},{1,17},{2,10},{3,19},{4,12},{5,21},{6,14},{7,23},{8,0},{9,25... | collective-permute-start | bytes 1179656 | tf_op jit(solution)/shard_map/ppermute | solution.py:867
  176.0 7.9 %collective-permute-start.82 = (f32[128,512]{1,0:T(8,128)S(1)}, f32[128,512]{1,0:T(8,128)S(1)}, u32[]{:S(2)}, u32[]{:S(2)}) collective-permute-start(f32[128,512]{1,0:T(8,128)S(1)} %join.21.refs_2_.refs_0_), channel_id=1, source_target_pairs={{0,2},{1,3},{2,0},{3,1},{4,6},{5,7},{6,4},{7,5},{8,10},{9,11},{10,... | collective-permute-start | bytes 786440 | tf_op jit(solution)/shard_map/ppermute | solution.py:862
  176.4 9.9 %collective-permute-start.77 = (f32[192,512]{1,0:T(8,128)S(1)}, f32[192,512]{1,0:T(8,128)S(1)}, u32[]{:S(2)}, u32[]{:S(2)}) collective-permute-start(f32[192,512]{1,0:T(8,128)S(1)} %join.22.refs_2_.refs_0_), channel_id=1, source_target_pairs={{0,8},{1,17},{2,10},{3,19},{4,12},{5,21},{6,14},{7,23},{8,0},{9,25... | collective-permute-start | bytes 1179656 | tf_op jit(solution)/shard_map/ppermute | solution.py:867
  177.9 4.5 %collective-permute-start.81 = (f32[640,512]{1,0:T(8,128)S(1)}, f32[640,512]{1,0:T(8,128)S(1)}, u32[]{:S(2)}, u32[]{:S(2)}) collective-permute-start(f32[640,512]{1,0:T(8,128)S(1)} %join.23.refs_2_.refs_0_), channel_id=1, source_target_pairs={{0,1},{1,0},{2,3},{3,2},{4,5},{5,4},{6,7},{7,6},{8,9},{9,8},{10,11... | collective-permute-start | bytes 3932168 | tf_op jit(solution)/shard_map/ppermute | solution.py:862
  181.6 5.1 %collective-permute-start.84 = (f32[384,512]{1,0:T(8,128)S(1)}, f32[384,512]{1,0:T(8,128)S(1)}, u32[]{:S(2)}, u32[]{:S(2)}) collective-permute-start(f32[384,512]{1,0:T(8,128)S(1)} %join.24.refs_2_.refs_0_), channel_id=1, source_target_pairs={{0,1},{1,0},{2,3},{3,2},{4,5},{5,4},{6,7},{7,6},{8,9},{9,8},{10,11... | collective-permute-start | bytes 2359304 | tf_op jit(solution)/shard_map/ppermute | solution.py:862
  (42 other events, 380.7 us)

commit v4 on v3

--- a/solution.py
+++ b/solution.py
@@ -81,43 +81,49 @@
     return (ar * br - ai * bi, ar * bi + ai * br)
 
 
-def scan(d_ref, keep_ref, par_ref, start, reverse, conj, visit=None, extra=(), unroll=8):
-    width = par_ref.shape[1]
-    count = d_ref.shape[0] // SUB
-    tiles = width // LANE
-    lam = []
-    for j in range(tiles):
-        lanes = slice(j * LANE, (j + 1) * LANE)
-        lr = jnp.broadcast_to(par_ref[0:1, lanes], (SUB, LANE))
-        li = jnp.broadcast_to(par_ref[1:2, lanes], (SUB, LANE))
-        lam.append((lr, -li if conj else li))
-    state = tuple(
-        (start[0][:, j * LANE : (j + 1) * LANE], start[1][:, j * LANE : (j + 1) * LANE])
-        for j in range(tiles)
-    )
-
-    def step(i, carry):
-        state, extra = carry
-        t = count - 1 - i if reverse else i
-        at = pl.ds(pl.multiple_of(t * SUB, SUB), SUB)
-        keep = keep_ref[at, :]
-        fresh = []
-        for j in range(tiles):
-            re, im = state[j]
-            a = keep * lam[j][0]
-            b = keep * lam[j][1]
-            dr = d_ref[at, j * LANE : (j + 1) * LANE]
-            di = d_ref[at, width + j * LANE : width + (j + 1) * LANE]
-            fresh.append((a * re - b * im + dr, a * im + b * re + di))
-        fresh = tuple(fresh)
-        if visit is not None:
-            extra = visit(t, keep, fresh, extra)
-        return (fresh, extra)
-
-    state, extra = lax.fori_loop(0, count, step, (state, tuple(extra)), unroll=unroll)
-    re = jnp.concatenate([part[0] for part in state], axis=1)
-    im = jnp.concatenate([part[1] for part in state], axis=1)
-    return re, im, extra
+class Scan:
+    def __init__(self, d_ref, keep_ref, par_ref, start, reverse, conj, visit=None, extra=()):
+        self.d_ref, self.keep_ref, self.reverse = d_ref, keep_ref, reverse
+        self.width = par_ref.shape[1]
+        self.visit, self.extra = visit, extra
+        self.lanes = [slice(j * LANE, (j + 1) * LANE) for j in range(self.width // LANE)]
+        self.lam = []
+        for lanes in self.lanes:
+            re = jnp.broadcast_to(par_ref[0:1, lanes], (SUB, LANE))
+            im = jnp.broadcast_to(par_ref[1:2, lanes], (SUB, LANE))
+            self.lam.append((re, -im if conj else im))
+        self.state = [(start[0][:, lanes], start[1][:, lanes]) for lanes in self.lanes]
+
+    def tiles(self):
+        count = self.d_ref.shape[0] // TILE
+        return range(count - 1, -1, -1) if self.reverse else range(count)
+
+    def ahead(self):
+        order = list(self.tiles())
+        self.run(order[0])
+        for k, i in enumerate(order):
+            if k + 1 < len(order):
+                self.run(order[k + 1])
+            yield i
+
+    def run(self, i):
+        steps = TILE // SUB
+        for k in range(steps):
+            t = i * steps + (steps - 1 - k if self.reverse else k)
+            at = pl.ds(t * SUB, SUB)
+            keep = self.keep_ref[at, :]
+            fresh = []
+            for (re, im), (lam_re, lam_im), lanes in zip(self.state, self.lam, self.lanes):
+                a, b = keep * lam_re, keep * lam_im
+                dr = self.d_ref[at, lanes]
+                di = self.d_ref[at, lanes.start + self.width : lanes.stop + self.width]
+                fresh.append((a * re - b * im + dr, a * im + b * re + di))
+            self.state = fresh
+            if self.visit is not None:
+                self.extra = self.visit(t, fresh, self.extra)
+
+    def ends(self):
+        return tuple(jnp.concatenate([part[k] for part in self.state], axis=1) for k in range(2))
 
 
 def wide(values, width):
@@ -129,7 +135,7 @@
     re, im = ends
     shift = SUB - 1 if reverse else 1
     pr, pi = pltpu.roll(re, shift, 0), pltpu.roll(im, shift, 0)
-    keep = wide(kp_ref[...], width)
+    keep = wide(kp_ref[:SUB, :], width)
     lr = keep * par_ref[2:3, :]
     li = keep * par_ref[3:4, :]
     li = -li if conj else li
@@ -179,7 +185,7 @@
     xi = xi + use * (qi + other_ref[:, width:] - xi)
     near, far = (1, SUB - 1) if reverse else (SUB - 1, 1)
     sr, si = pltpu.roll(xr, near, 0), pltpu.roll(xi, near, 0)
-    keep = wide(kp_ref[...], width)
+    keep = wide(kp_ref[:SUB, :], width)
     hr = keep * par_ref[2:3, :]
     hi = sign * keep * par_ref[3:4, :]
     tr, ti = times(hr, hi, sr, si)
@@ -274,6 +280,11 @@
         for j in range(tiles):
             part = lines_ref[j, pl.ds(s, half, stride=SUB), :]
             dst_ref[s // 2, (s % 2) * half : (s % 2 + 1) * half, j * LANE : (j + 1) * LANE] = part.astype(dst_ref.dtype)
+
+
+def k_emit(lines_ref, out_ref, token_ref):
+    token_ref[...] = jnp.zeros(token_ref.shape, F32)
+    spread_out(lines_ref, out_ref)
 
 
 def put_lines(lines_ref, i, values):
@@ -320,55 +331,42 @@
     return jnp.where(x < 0.5, x * series, 1.0 - jnp.exp(-x))
 
 
-def all_starts(starts_ref):
-    rows, segments = starts_ref.shape
-    sub = lax.broadcasted_iota(jnp.int32, (SUB, LANE), 0)
-    starts = []
-    for k in range(segments):
-        start = jnp.zeros((SUB, LANE), jnp.int32)
-        for r in range(rows):
-            start = jnp.where(sub // 2 == r, starts_ref[r, k], start)
-        starts.append(start)
-    return starts
-
-
 def k_keep(reverse, starts_ref, keep_ref, kp_ref, kd_ref):
-    steps = keep_ref.shape[0] // SUB
-    n = kd_ref.shape[0]
+    count = keep_ref.shape[0] - SUB
+    steps = count // SUB
     length = 2 * steps
-    starts = all_starts(starts_ref)
-    sub = lax.broadcasted_iota(jnp.int32, (SUB, LANE), 0)
-    base = lax.axis_index("tm") * length + (sub % 2) * steps + (1 if reverse else 0)
-    block = 8
-
-    def fill(i, least):
-        place = lax.broadcasted_iota(jnp.int32, (block, SUB, LANE), 0) + i * block + base[None]
-        hit = starts[0][None] == place
-        for start in starts[1:]:
-            hit = hit | (start[None] == place)
-        if reverse:
-            hit = hit | (place == n * length)
-        keep = jnp.where(hit, 0.0, 1.0)
-        keep_ref[pl.ds(pl.multiple_of(i * block * SUB, SUB), block * SUB), :] = flat(keep)
-        return jnp.minimum(least, jnp.min(keep, axis=0))
-
-    kp_ref[...] = lax.fori_loop(0, steps // block, fill, jnp.ones((SUB, LANE), F32))
-
-    def fill_devices(j, unused):
-        first = j * length + (1 if reverse else 0)
-        hit = jnp.zeros((SUB, LANE), jnp.bool_)
-        for start in starts:
-            hit = hit | ((start >= first) & (start < first + length))
-        kd_ref[j] = jnp.where(hit, 0.0, 1.0)
+    n = kd_ref.shape[0] - 1
+    base = lax.axis_index("tm") * length
+    for ref in (keep_ref, kp_ref, kd_ref):
+        ref[...] = jnp.ones(ref.shape, F32)
+    none = jnp.zeros((1, LANE), F32)
+
+    def mark(r, place):
+        local = place - base
+        here = (local >= 0) & (local < length)
+        second = jnp.where(local >= steps, 1, 0)
+        row = (local - second * steps) * SUB + 2 * r + second
+        keep_ref[pl.ds(jnp.where(here, row, count), 1), :] = none
+        kp_ref[pl.ds(jnp.where(here, 2 * r + second, SUB), 1), :] = none
+
+    def each(k, unused):
+        for r in range(starts_ref.shape[0]):
+            place = starts_ref[r, k] - (1 if reverse else 0)
+            mark(r, place)
+            device = jnp.where(place >= 0, lax.div(place, length), n)
+            kd_ref[device, 2 * r : 2 * r + 2, :] = jnp.zeros((2, LANE), F32)
         return unused
 
-    lax.fori_loop(0, n, fill_devices, 0)
+    lax.fori_loop(0, starts_ref.shape[1], each, 0)
+    if reverse:
+        for r in range(starts_ref.shape[0]):
+            mark(r, n * length - 1)
 
 
 def k_prepare(starts_ref, rate_ref, rotation_ref, gain_ref, shift_ref, skip_ref, bias_ref,
               keep_ref, kp_ref, kd_ref, par_ref, vec_ref):
     k_keep(False, starts_ref, keep_ref, kp_ref, kd_ref)
-    doublings = (keep_ref.shape[0] // SUB).bit_length() - 1
+    doublings = ((keep_ref.shape[0] - SUB) // SUB).bit_length() - 1
     for layer in range(2):
         decay = jnp.exp(rate_ref[layer : layer + 1, :])
         magnitude = jnp.exp(-decay)
@@ -413,7 +411,7 @@
 
 
 def k_drive(layer, reverse, st_ref, cnt_ref, u_ref, lim_ref, vec_ref, par_ref, b_ref, keep_ref, kp_ref,
-            d_ref, ml_ref, stat_ref, e_ref):
+            d_ref, ml_ref, m_ref, stat_ref, e_ref):
     vec_ref, par_ref = of_layer(vec_ref, layer), of_layer(par_ref, layer)
     total = st_ref[...]
     a, c, b, d = unpack_rows(total, 4, u_ref.shape[1])
@@ -440,14 +438,18 @@
     both = jnp.concatenate((par_ref[6:7, :], par_ref[6:7, :]), axis=1)
 
     def step(i, unused):
-        low = flat(masked_tile(u_ref, stat_ref, vec_ref, lim_ref, i)).astype(BF16)
+        masked = flat(masked_tile(u_ref, stat_ref, vec_ref, lim_ref, i))
+        m_ref[rows_at(i), :] = masked
+        low = masked.astype(BF16)
         ml_ref[rows_at(i), :] = low
         d_ref[rows_at(i), :] = dot(low, b_ref[layer]) * both
         return unused
 
-    lax.fori_loop(0, u_ref.shape[0] // TILE, step, 0, unroll=True)
-    re, im, unused = scan(d_ref, keep_ref, par_ref, zeros_state(par_ref), reverse, False)
-    put_ends(e_ref, chunk_end((re, im), kp_ref, par_ref, reverse, False))
+    scan = Scan(d_ref, keep_ref, par_ref, zeros_state(par_ref), reverse, False)
+    for i in scan.tiles():
+        step(i, 0)
+        scan.run(i)
+    put_ends(e_ref, chunk_end(scan.ends(), kp_ref, par_ref, reverse, False))
 
 
 def k_drive_first(layer, reverse, st_ref, *refs):
@@ -462,15 +464,14 @@
         jnp.concatenate(start, axis=1)
     )
 
-    def visit(t, keep, states, extra):
-        at = pl.ds(pl.multiple_of(t * SUB + first, SUB), SUB)
+    def visit(t, states, extra):
+        at = pl.ds(t * SUB + first, SUB)
         for j, (re, im) in enumerate(states):
             s_ref[at, j * LANE : (j + 1) * LANE] = re
             s_ref[at, width + j * LANE : width + (j + 1) * LANE] = im
         return extra
 
-    scan(d_ref, keep_ref, par_ref, start, reverse, False, visit)
-    return first
+    return first, Scan(d_ref, keep_ref, par_ref, start, reverse, False, visit)
 
 
 def sigmoid(x):
@@ -478,17 +479,8 @@
 
 
 def gelu_parts(x):
-    bell = jnp.exp(-0.5 * x * x)
-    base = 1.0 + (0.3275911 * 0.7071067811865476) * jnp.abs(x)
-    near = pl.reciprocal(base, approx=True)
-    near = near * (2.0 - base * near)
-    tail = near * (0.5 * 1.061405429) + (0.5 * -1.453152027)
-    tail = tail * near + (0.5 * 1.421413741)
-    tail = tail * near + (0.5 * -0.284496736)
-    tail = tail * near + (0.5 * 0.254829592)
-    tail = tail * near * bell
-    cdf = jnp.where(x < 0.0, tail, 1.0 - tail)
-    return x * cdf, cdf + (0.3989422804014327 * x) * bell
+    cdf = 0.5 * (1.0 + lax.erf(x * 0.7071067811865476))
+    return x * cdf, cdf + x * jnp.exp(-0.5 * x * x) * 0.3989422804014327
 
 
 def states_low(s_ref, first, i):
@@ -501,16 +493,15 @@
 
 def k_finish_first(layer, parts, *refs):
     carry, refs = take_carry(refs, parts)
-    (d_ref, u_ref, stat_ref, lim_ref, vec_ref, par_ref, keep_ref, kp_ref, kd_ref, c_ref, w_ref,
+    (d_ref, u_ref, m_ref, lim_ref, vec_ref, par_ref, keep_ref, kp_ref, kd_ref, c_ref, w_ref,
      s_ref, al_ref, sig_ref, q_ref, slope_ref, next_ref, st_ref) = refs
     vec_ref, par_ref = of_layer(vec_ref, layer), of_layer(par_ref, layer)
-    first = run_states(carry, d_ref, keep_ref, kp_ref, kd_ref, par_ref, s_ref, False)
+    first, scan = run_states(carry, d_ref, keep_ref, kp_ref, kd_ref, par_ref, s_ref, False)
 
     def step(i, sums):
         at = rows_at(i)
         valid = tile_mask(lim_ref, i)
-        masked = masked_tile(u_ref, stat_ref, vec_ref, lim_ref, i)
-        mixed = dot(states_low(s_ref, first, i), c_ref[layer]) + vec_ref[2:3, :] * flat(masked)
+        mixed = dot(states_low(s_ref, first, i), c_ref[layer]) + vec_ref[2:3, :] * m_ref[at, :]
         active, slope = gelu_parts(mixed)
         low = active.astype(BF16)
         sig = sigmoid(dot(low, w_ref[layer]) + vec_ref[3:4, :])
@@ -525,20 +516,22 @@
         return (sums[0] + jnp.sum(x, axis=0), sums[1] + jnp.sum(x * x, axis=0))
 
     zero = jnp.zeros(lim_ref.shape, F32)
-    sums, squares = lax.fori_loop(0, u_ref.shape[0] // TILE, step, (zero, zero), unroll=True)
+    totals = (zero, zero)
+    for i in scan.ahead():
+        totals = step(i, totals)
+    sums, squares = totals
     a, b = per_micro(sums)
     c, d = per_micro(squares)
     pack_rows(st_ref, (a, c, b, d))
 
 
-def gate_backward(layer, upstream, q, sig, slope, low, masked, s_low, state, c_ref, w_ref, mix_ref, sg_ref, gw_ref, gc_ref, i):
+def gate_backward(layer, upstream, q, sig, slope, masked, state, c_ref, w_ref, gate_ref, mix_ref, sg_ref, i):
     at = rows_at(i)
     gate = (upstream * q).astype(BF16)
-    gw_ref[...] += dot_tn(low, gate)
+    gate_ref[at, :] = gate
     act = upstream * sig + dot_nt(gate, w_ref[layer])
     mix = (act * slope).astype(BF16)
     mix_ref[at, :] = mix
-    gc_ref[...] += dot_tn(s_low, mix)
     sg = dot_nt(mix, c_ref[layer])
     sg_ref[at, :] = sg
     wide_sum = jnp.sum(folded(sg * state), axis=0)
@@ -559,20 +552,38 @@
     return (jnp.zeros((SUB, width), F32), jnp.zeros((SUB, width), F32), jnp.zeros((SUB, states), F32))
 
 
+class Ends:
+    def __init__(self, keep_ref, par_ref):
+        self.keep_ref = keep_ref
+        re, im = par_ref[0:1, :], -par_ref[1:2, :]
+        for unused in range((TILE // SUB).bit_length() - 1):
+            re, im = times(re, im, re, im)
+        self.step = tuple(jnp.broadcast_to(part, (SUB, part.shape[1])) for part in (re, im))
+        self.factor = self.total = None
+
+    def put_before(self, i, ends):
+        if self.total is None:
+            self.total = ends
+        else:
+            re, im = times(*self.factor, *ends)
+            self.total = (self.total[0] + re, self.total[1] + im)
+        keep = wide(jnp.min(folded(self.keep_ref[i * TILE : (i + 1) * TILE, :]), axis=0), ends[0].shape[1])
+        here = tuple(keep * part for part in self.step)
+        self.factor = here if self.factor is None else times(*self.factor, *here)
+
+
 def k_middle(layer, parts, *refs):
     carry, refs = take_carry(refs, parts)
-    (d_ref, u_ref, stat_ref, lim_ref, vec_ref, par_ref, keep_ref, kp_ref, kd_ref,
+    (d_ref, u_ref, m_ref, lim_ref, vec_ref, par_ref, keep_ref, kp_ref, kd_ref,
      keep_adj_ref, kp_adj_ref, c_ref, w_ref, cot32_ref,
-     lines_ref, s_ref, mix_ref, sg_ref, wc_ref, sums_ref, e_ref) = refs
+     lines_ref, s_ref, mix_ref, sg_ref, wc_ref, sums_ref, e_ref, al_ref, gate_ref, slow_ref) = refs
     vec_ref, par_ref = of_layer(vec_ref, layer), of_layer(par_ref, layer)
-    first = run_states(carry, d_ref, keep_ref, kp_ref, kd_ref, par_ref, s_ref, True)
-    wc_ref[...] = jnp.zeros(wc_ref.shape, F32)
-    gw_ref, gc_ref = wc_ref.at[: u_ref.shape[1]], wc_ref.at[u_ref.shape[1] :]
+    first, scan = run_states(carry, d_ref, keep_ref, kp_ref, kd_ref, par_ref, s_ref, True)
 
     def step(i, sums):
         at = rows_at(i)
         valid = tile_mask(lim_ref, i)
-        masked = flat(masked_tile(u_ref, stat_ref, vec_ref, lim_ref, i))
+        masked = m_ref[at, :]
         state = s_ref[pl.ds(pl.multiple_of(i * TILE + first, SUB), TILE), :]
         s_low = state.astype(BF16)
         mixed = dot(s_low, c_ref[layer]) + vec_ref[2:3, :] * masked
@@ -582,26 +593,33 @@
         gated = active * sig
         put_lines(lines_ref, i, flat(folded(u_ref[at, :]) + jnp.where(valid, folded(gated), 0.0)))
         upstream = flat(jnp.where(valid, folded(cot32_ref[at, :]), 0.0))
-        more = gate_backward(layer, upstream, gated * (1.0 - sig), sig, slope, low, masked, s_low, state,
-                             c_ref, w_ref, mix_ref, sg_ref, gw_ref, gc_ref, i)
+        al_ref[at, :] = low
+        slow_ref[at, :] = s_low
+        more = gate_backward(layer, upstream, gated * (1.0 - sig), sig, slope, masked, state,
+                             c_ref, w_ref, gate_ref, mix_ref, sg_ref, i)
         return tuple(x + y for x, y in zip(sums, more))
 
-    sums = lax.fori_loop(0, u_ref.shape[0] // TILE, step, zero_sums(u_ref.shape[1], par_ref.shape[1]), unroll=True)
+    sums = zero_sums(u_ref.shape[1], par_ref.shape[1])
+    ends = Ends(keep_adj_ref, par_ref)
+    for i in scan.ahead():
+        sums = step(i, sums)
+        local = Scan(sg_ref, keep_adj_ref, par_ref, zeros_state(par_ref), False, True)
+        local.run(i)
+        ends.put_before(i, local.ends())
+    wc_ref[: u_ref.shape[1], :] = dot_tn(al_ref[...], gate_ref[...])
+    wc_ref[u_ref.shape[1] :, :] = dot_tn(slow_ref[...], mix_ref[...])
     put_sums(sums_ref, sums)
-    re, im, unused = scan(sg_ref, keep_adj_ref, par_ref, zeros_state(par_ref), False, True)
-    put_ends(e_ref, chunk_end((re, im), kp_adj_ref, par_ref, False, True))
+    put_ends(e_ref, chunk_end(ends.total, kp_adj_ref, par_ref, False, True))
 
 
 def k_lower(layer, st_ref, z_ref, cot32_ref, u1_ref, stat1_ref, lim_ref,
-            s_ref, al_ref, sig_ref, q_ref, slope_ref, u_ref, stat_ref, vec_ref, par_ref, c_ref, w_ref,
+            s_ref, al_ref, sig_ref, q_ref, slope_ref, m_ref, vec_ref, par_ref, c_ref, w_ref,
             keep_adj_ref, kp_adj_ref,
-            grad_ref, mix_ref, sg_ref, gw_ref, gc_ref, sums_ref, e_ref, bn_ref):
+            grad_ref, mix_ref, sg_ref, gw_ref, gc_ref, sums_ref, e_ref, bn_ref, gate_ref, slow_ref):
     vec1_ref = of_layer(vec_ref, layer + 1)
     vec_ref, par_ref = of_layer(vec_ref, layer), of_layer(par_ref, layer)
     first = SUB
     c1, c2 = norm_sums(st_ref, stat1_ref, vec1_ref, bn_ref)
-    gw_ref[...] = jnp.zeros(gw_ref.shape, F32)
-    gc_ref[...] = jnp.zeros(gc_ref.shape, F32)
 
     def step(i, sums):
         at = rows_at(i)
@@ -610,16 +628,22 @@
         grad = folded(cot32_ref[at, :]) + extra
         grad_ref[at, :] = flat(grad)
         upstream = flat(jnp.where(valid, grad, 0.0))
-        masked = flat(masked_tile(u_ref, stat_ref, vec_ref, lim_ref, i))
+        masked = m_ref[at, :]
         state = s_ref[pl.ds(pl.multiple_of(i * TILE + first, SUB), TILE), :]
-        more = gate_backward(layer, upstream, q_ref[at, :], sig_ref[at, :], slope_ref[at, :], al_ref[at, :], masked,
-                             state.astype(BF16), state, c_ref, w_ref, mix_ref, sg_ref, gw_ref, gc_ref, i)
+        slow_ref[at, :] = state.astype(BF16)
+        more = gate_backward(layer, upstream, q_ref[at, :], sig_ref[at, :], slope_ref[at, :], masked,
+                             state, c_ref, w_ref, gate_ref, mix_ref, sg_ref, i)
         return tuple(x + y for x, y in zip(sums, more))
 
-    sums = lax.fori_loop(0, u_ref.shape[0] // TILE, step, zero_sums(u_ref.shape[1], par_ref.shape[1]), unroll=True)
+    sums = zero_sums(m_ref.shape[1], par_ref.shape[1])
+    scan = Scan(sg_ref, keep_adj_ref, par_ref, zeros_state(par_ref), True, True)
+    for i in scan.tiles():
+        sums = step(i, sums)
+        scan.run(i)
+    gw_ref[...] = dot_tn(al_ref[...], gate_ref[...])
+    gc_ref[...] = dot_tn(slow_ref[...], mix_ref[...])
     put_sums(sums_ref, sums)
-    re, im, unused = scan(sg_ref, keep_adj_ref, par_ref, zeros_state(par_ref), True, True)
-    put_ends(e_ref, chunk_end((re, im), kp_adj_ref, par_ref, True, True))
+    put_ends(e_ref, chunk_end(scan.ends(), kp_adj_ref, par_ref, True, True))
 
 
 def norm_sums(st_ref, stat_ref, vec_ref, bn_ref):
@@ -637,21 +661,16 @@
     return jnp.where(valid, stat_ref[8:16, :][None] * (z - c1[None] - normed * c2[None]), 0.0)
 
 
-def k_adjoint(layer, reverse, parts, extra, *refs):
-    carry, refs = take_carry(refs, parts)
-    sent_refs, refs = refs[:extra], refs[extra:]
-    (sg_ref, s_ref, mix_ref, ml_ref, u_ref, stat_ref, lim_ref, vec_ref, par_ref,
-     keep_adj_ref, kp_adj_ref, kd_adj_ref, keep_ref, b_ref, z_ref, gb_ref, lg_ref, st_ref, a_ref) = refs
-    vec_ref, par_ref = of_layer(vec_ref, layer), of_layer(par_ref, layer)
+def adjoint_scan(reverse, carry, sg_ref, s_ref, par_ref, keep_adj_ref, kp_adj_ref, kd_adj_ref, keep_ref, a_ref):
     width = par_ref.shape[1]
     tiles = width // LANE
     behind = 0 if reverse else SUB
     start = enter(*carry, kd_adj_ref, kp_adj_ref, par_ref, reverse, True)
     scale = [jnp.broadcast_to(par_ref[6:7, j * LANE : (j + 1) * LANE], (SUB, LANE)) for j in range(tiles)]
 
-    def visit(t, unused, adjoint, sums):
-        at = pl.ds(pl.multiple_of(t * SUB, SUB), SUB)
-        before = pl.ds(pl.multiple_of(t * SUB + behind, SUB), SUB)
+    def visit(t, adjoint, sums):
+        at = pl.ds(t * SUB, SUB)
+        before = pl.ds(t * SUB + behind, SUB)
         keep = keep_ref[at, :]
         fresh = []
         for j, (re, im) in enumerate(adjoint):
@@ -664,37 +683,81 @@
         return tuple(fresh)
 
     zero = jnp.zeros((SUB, LANE), F32)
-    unused, unused, sums = scan(sg_ref, keep_adj_ref, par_ref, start, reverse, True, visit,
-                                tuple((zero, zero) for j in range(tiles)))
+    return Scan(sg_ref, keep_adj_ref, par_ref, start, reverse, True, visit, tuple((zero, zero) for j in range(tiles)))
+
+
+def put_lam(lg_ref, sums):
     lg_ref[...] = jnp.zeros(lg_ref.shape, F32)
     pack_rows(lg_ref, [
         jnp.sum(jnp.concatenate([part[k] for part in sums], axis=1), axis=0, keepdims=True) for k in range(2)
     ])
-    gb_ref[...] = jnp.zeros(gb_ref.shape, F32)
-
-    def step(i, sums):
-        at = rows_at(i)
-        drive = a_ref[at, :].astype(BF16)
-        gb = dot_tn(ml_ref[at, :], drive)
-        rows = gb.shape[0]
-        gb_ref[:rows, :] += gb[:, :rows]
-        gb_ref[rows:, : rows // 2] += gb[: rows // 2, rows:]
-        gb_ref[rows:, rows // 2 :] += gb[rows // 2 :, rows:]
-        back = dot_nt(drive, b_ref[layer]) + vec_ref[2:3, :] * mix_ref[at, :].astype(F32)
-        z = jnp.where(tile_mask(lim_ref, i), folded(back), 0.0)
-        z_ref[at, :] = flat(z)
-        return (sums[0] + jnp.sum(z, axis=0), sums[1] + jnp.sum(z * normed_tile(u_ref, stat_ref, i), axis=0))
-
-    zero = jnp.zeros(lim_ref.shape, F32)
-    sums = lax.fori_loop(0, u_ref.shape[0] // TILE, step, (zero, zero), unroll=True)
+
+
+def add_drives(gb_ref, low, drive):
+    gb = dot_tn(low, drive)
+    rows = gb.shape[0]
+    gb_ref[:rows, :] += gb[:, :rows]
+    gb_ref[rows:, : rows // 2] += gb[: rows // 2, rows:]
+    gb_ref[rows:, rows // 2 :] += gb[rows // 2 :, rows:]
+
+
+def back_to_norm(layer, i, drive, sums, b_ref, vec_ref, mix_ref, lim_ref, u_ref, stat_ref, z_ref):
+    at = rows_at(i)
+    back = dot_nt(drive, b_ref[layer]) + vec_ref[2:3, :] * mix_ref[at, :].astype(F32)
+    z = jnp.where(tile_mask(lim_ref, i), folded(back), 0.0)
+    z_ref[at, :] = flat(z)
+    return (sums[0] + jnp.sum(z, axis=0), sums[1] + jnp.sum(z * normed_tile(u_ref, stat_ref, i), axis=0))
+
+
+def put_norm_sums(st_ref, sums):
     a, b = per_micro(sums[0])
     c, d = per_micro(sums[1])
     pack_rows(st_ref, (a, c, b, d))
+
+
+def k_adjoint(layer, reverse, parts, *refs):
+    carry, refs = take_carry(refs, parts)
+    (sg_ref, s_ref, mix_ref, ml_ref, u_ref, stat_ref, lim_ref, vec_ref, par_ref,
+     keep_adj_ref, kp_adj_ref, kd_adj_ref, keep_ref, b_ref, z_ref, gb_ref, lg_ref, st_ref, a_ref) = refs
+    vec_ref, par_ref = of_layer(vec_ref, layer), of_layer(par_ref, layer)
+    scan = adjoint_scan(reverse, carry, sg_ref, s_ref, par_ref, keep_adj_ref, kp_adj_ref, kd_adj_ref, keep_ref, a_ref)
+    gb_ref[...] = jnp.zeros(gb_ref.shape, F32)
+    zero = jnp.zeros(lim_ref.shape, F32)
+    sums = (zero, zero)
+    for i in scan.ahead():
+        drive = a_ref[rows_at(i), :].astype(BF16)
+        add_drives(gb_ref, ml_ref[rows_at(i), :], drive)
+        sums = back_to_norm(layer, i, drive, sums, b_ref, vec_ref, mix_ref, lim_ref, u_ref, stat_ref, z_ref)
+    put_lam(lg_ref, scan.extra)
+    put_norm_sums(st_ref, sums)
+
+
+def k_adjoint_last(layer, reverse, parts, *refs):
+    carry, refs = take_carry(refs, parts)
+    (sg_ref, s_ref, ml_ref, par_ref, keep_adj_ref, kp_adj_ref, kd_adj_ref, keep_ref,
+     drive_ref, gb_ref, lg_ref, a_ref) = refs
+    par_ref = of_layer(par_ref, layer)
+    scan = adjoint_scan(reverse, carry, sg_ref, s_ref, par_ref, keep_adj_ref, kp_adj_ref, kd_adj_ref, keep_ref, a_ref)
+    gb_ref[...] = jnp.zeros(gb_ref.shape, F32)
+    for i in scan.ahead():
+        drive = a_ref[rows_at(i), :].astype(BF16)
+        drive_ref[rows_at(i), :] = drive
+        add_drives(gb_ref, ml_ref[rows_at(i), :], drive)
+    put_lam(lg_ref, scan.extra)
+
+
+def k_back(layer, drive_ref, mix_ref, u_ref, stat_ref, lim_ref, vec_ref, b_ref, *refs):
+    z_ref, st_ref = refs[-2:]
+    vec_ref = of_layer(vec_ref, layer)
+    zero = jnp.zeros(lim_ref.shape, F32)
+    sums = (zero, zero)
+    for i in range(u_ref.shape[0] // TILE):
+        sums = back_to_norm(layer, i, drive_ref[rows_at(i), :], sums, b_ref, vec_ref, mix_ref, lim_ref, u_ref, stat_ref, z_ref)
+    put_norm_sums(st_ref, sums)
     at = 16
-    if extra:
-        for ref in sent_refs + (lg_ref,):
-            st_ref[at : at + ref.shape[0], :] = ref[...]
-            at += ref.shape[0]
+    for ref in refs[:-2]:
+        st_ref[at : at + ref.shape[0], :] = ref[...]
+        at += ref.shape[0]
 
 
 def k_output(st_ref, z_ref, grad_ref, u_ref, stat_ref, vec_ref, lim_ref, par_ref, stat1_ref, bn1_ref,
@@ -845,7 +908,12 @@
 
 BOTH = ("batch", "tm")
 
-TAIL = ("DABSDECBSA", "DCBEADCSBD", "EASCBDECDB", "SCEDALBCAE", "CDBED")
+ORDER = (
+    ("AA",),
+    ("B", "A", "e", "BA"),
+    ("CECE",),
+    ("D", "ABSDECBSA", "DCBEADCSBD", "EASCBDECDB", "SCEDALBCAE", "CDBED"),
+)
 
 
 def outer_bits():
@@ -881,8 +949,11 @@
     return block
 
 
-def sums_of_all(block):
-    block = block + swap(block, 1)
+def sums_of_all(block, fill):
+    order = Order()
+    got = swap(block, 1)
+    order.token = fill()
+    block, = call("add", k_add, [shaped(block.shape)], [block, got], order=order)
     return sum_over(sum_over(block, outer_bits()), line_bits())
 
 
@@ -985,6 +1056,46 @@
         return 2 * len(self.cuts) + len(self.whole) - self.at
 
 
+class Steps:
+    def __init__(self, order):
+        self.order = order
+        self.larges, self.other, self.into, self.shapes = {}, {}, {}, {}
+
+    def add(self, name, block, line_first=False):
+        self.larges[name] = Large(self.order, block, line_first)
+
+    def run(self, items):
+        for item in items:
+            if item in self.other:
+                self.other[item]()
+            elif self.larges[item].left():
+                self.larges[item].send()
+            else:
+                self.put(item)
+
+    def put(self, item):
+        large = self.larges[item]
+        while large.left():
+            large.send()
+        if item == "A":
+            w_out, c_out = place(large, map_places, 1, self.shapes["A"])
+            self.into.update(E=(w_out, False), C=(c_out, False))
+        elif item == "B":
+            self.into["D"] = (place(large, drive_places, 1, self.shapes["B"])[0], False)
+        else:
+            if item not in self.into:
+                self.put("B" if item == "D" else "A")
+            out, done = self.into[item]
+            if not done:
+                shape = shaped(out.shape)
+                out, = place(large, drive_places if item == "D" else map_places, 0, [shape], [out])
+                self.into[item] = (out, True)
+
+    def placed(self, item):
+        self.put(item)
+        return self.into[item][0]
+
+
 def small_sum(order, block):
     for distance in [1] + [bit[2] | 1 for bit in outer_bits() + line_bits()]:
         got = swap(block, distance)
@@ -1007,139 +1118,136 @@
     kept = shaped((count + SUB, 2 * states))
     small = shaped((16, LANE))
     lines = pltpu.VMEM((width // LANE, count, LANE), F32)
+    rows_low, states_low_rows = pltpu.VMEM((count, width), BF16), pltpu.VMEM((count, 2 * states), BF16)
     everyone = pltpu.VMEM((chips, SUB, 2 * states), F32)
-    keeps = shaped((count, LANE))
+    keeps = shaped((count + SUB, LANE))
     vector, state_vector = shaped((2, width)), shaped((2, states))
 
     u0, st, lim = call("enter", k_input, [big(width), shaped((24, LANE)), shaped((SUB, width), jnp.int32)],
                        [lengths, tokens], scratch=[lines], scalars=1)
-    keep_shapes = [keeps, shaped((SUB, LANE)), shaped((n, SUB, LANE))]
-    keep_f, kp_f, kd_f, par, vec = call(
-        "prepare", k_prepare, keep_shapes + [shaped((2 * SUB, states)), shaped((2 * SUB, width))],
-        [starts, log_rate, rotation, norm_gain, norm_shift, skip_gain, gate_bias], scalars=1,
-    )
-    st = sums_of_all(st)
-    d0, ml0, stat0, e = call(
+    keep_shapes = [keeps, shaped((2 * SUB, LANE)), shaped((n + 1, SUB, LANE))]
+    made = []
+
+    def prepare():
+        made.extend(call(
+            "prepare", k_prepare, keep_shapes + [shaped((2 * SUB, states)), shaped((2 * SUB, width))],
+            [starts, log_rate, rotation, norm_gain, norm_shift, skip_gain, gate_bias], scalars=1,
+        ))
+        return made[1]
+
+    st = sums_of_all(st, prepare)
+    keep_f, kp_f, kd_f, par, vec = made
+    d0, ml0, m0, stat0, e = call(
         "drive0", functools.partial(k_drive_first, 0, False),
-        [big(2 * states), big(width, BF16), shaped((32, width)), ends],
+        [big(2 * states), big(width, BF16), big(width), shaped((32, width)), ends],
         [st, u0, lim, vec, par, b_proj, keep_f, kp_f],
-    )
-    side = Order()
-    side.token = e
-    keep_r, kp_r, kd_r = call(
-        "keep", functools.partial(k_keep, True), keep_shapes, [starts], scalars=1, order=side,
     )
     s0, al0, sig0, q0, slope0, u1, st = call(
         "finish0", functools.partial(k_finish_first, 0, parts),
         [kept, big(width, BF16), big(width), big(width), big(width), big(width), small],
         carries(e, kd_f, par, 0, False, False)
-        + [d0, u0, stat0, lim, vec, par, keep_f, kp_f, kd_f, c_proj, w_gate],
+        + [d0, u0, m0, lim, vec, par, keep_f, kp_f, kd_f, c_proj, w_gate],
         scratch=[everyone],
     )
-    st = sums_of_all(st)
-    d1, ml1, stat1, e = call(
+    after_first = Order()
+    after_first.token = st
+    backward = []
+
+    def keep():
+        backward.extend(call(
+            "keep", functools.partial(k_keep, True), keep_shapes, [starts], scalars=1, order=after_first, token=1,
+        ))
+        return backward[1]
+
+    st = sums_of_all(st, keep)
+    keep_r, kp_r, kd_r = backward
+    d1, ml1, m1, stat1, e = call(
         "drive1", functools.partial(k_drive, 1, True),
-        [big(2 * states), big(width, BF16), shaped((32, width)), ends],
+        [big(2 * states), big(width, BF16), big(width), shaped((32, width)), ends],
         [st, stat0, u1, lim, vec, par, b_proj, keep_r, kp_r],
     )
     grads = [shaped((width + 2 * states, width)), small, ends]
-    side.token = u1
-    cot32, = call("cotangent", spread_in, [big(width)], [cotangent], scratch=[lines], order=side)
+    after_second = Order()
+    after_second.token = e
+    cot32, = call("cotangent", spread_in, [big(width)], [cotangent], scratch=[lines], order=after_second)
     out32, s1, mix1, sg1, wc1, sums1, e = call(
         "middle", functools.partial(k_middle, 1, parts),
         [shaped((width // LANE, count, LANE)), kept, big(width, BF16), big(2 * states)] + grads,
-        carries(e, kd_r, par, 1, True, False)
-        + [d1, u1, stat1, lim, vec, par, keep_r, kp_r, kd_r, keep_f, kp_f, c_proj, w_gate, cot32],
-        scratch=[everyone],
+        carries(e, kd_r, par, 1, True, False, after_second)
+        + [d1, u1, m1, lim, vec, par, keep_r, kp_r, kd_r, keep_f, kp_f, c_proj, w_gate, cot32],
+        scratch=[rows_low, rows_low, states_low_rows, everyone],
     )
     order = Order()
     order.token = e
-    wc1 = Large(order, wc1)
+    steps = Steps(order)
+    steps.add("A", wc1)
     got = carries(e, kd_f, par, 1, False, True, order)
-    wc1.send()
-    wc1.send()
+    steps.run(ORDER[0][0])
     adjoint = [big(width), shaped((2 * states, width)), shaped((8, LANE))]
     z1, gb1, lg1, st = call(
-        "adjoint1", functools.partial(k_adjoint, 1, False, parts, 0), adjoint + [small],
+        "adjoint1", functools.partial(k_adjoint, 1, False, parts), adjoint + [small],
         got + [sg1, s1, mix1, ml1, u1, stat1, lim, vec, par, keep_f, kp_f, kd_f, keep_r, b_proj],
         scratch=[pltpu.VMEM((count, 2 * states), F32), everyone], order=order, token=3,
     )
-    b1 = Large(order, gb1)
+    steps.add("B", gb1)
     emitted = []
 
     def emit():
-        emitted.extend(call("emit", spread_out, [shaped(tokens.shape, BF16)], [out32], results=1, order=order))
-
-    st = sums_in_order(st, order, [b1.send, wc1.send, emit])
-    b1.send()
-    wc1.send()
-    output, = emitted
+        emitted.extend(
+            call("emit", k_emit, [shaped(tokens.shape, BF16), shaped((SUB, LANE))], [out32], results=1, order=order, token=1)
+        )
+
+    steps.other["e"] = emit
+    st = sums_in_order(st, order, [functools.partial(steps.run, items) for items in ORDER[1][:3]])
+    steps.run(ORDER[1][3])
     g0, mix0, sg0, gw0, gc0, sums0, e, bn1 = call(
         "lower", functools.partial(k_lower, 0),
         [big(width), big(width, BF16), big(2 * states), shaped((width, width)), shaped((2 * states, width)), small, ends,
          shaped((SUB, width))],
-        [st, z1, cot32, u1, stat1, lim, s0, al0, sig0, q0, slope0, u0, stat0, vec, par,
+        [st, z1, cot32, u1, stat1, lim, s0, al0, sig0, q0, slope0, m0, vec, par,
          c_proj, w_gate, keep_r, kp_r],
-        order=order, token=6,
+        scratch=[rows_low, states_low_rows], order=order, token=6,
     )
-    w0, c0 = Large(order, gw0, True), Large(order, gc0)
+    steps.add("E", gw0, True)
+    steps.add("C", gc0)
     got = carries(e, kd_r, par, 0, True, True, order)
-    c0.send()
-    w0.send()
-    c0.send()
-    w0.send()
-    z0, gb0, lg0, st = call(
-        "adjoint0", functools.partial(k_adjoint, 0, True, parts, 3), adjoint + [shaped((64, LANE))],
-        got + [sums1, lg1, sums0]
-        + [sg0, s0, mix0, ml0, u0, stat0, lim, vec, par, keep_r, kp_r, kd_r, keep_f, b_proj],
-        scratch=[pltpu.VMEM((count, 2 * states), F32), everyone], order=order, token=3,
+    steps.run(ORDER[2][0])
+    drive0, gb0, lg0 = call(
+        "adjoint0", functools.partial(k_adjoint_last, 0, True, parts), [big(2 * states, BF16)] + adjoint[1:],
+        got + [sg0, s0, ml0, par, keep_r, kp_r, kd_r, keep_f],
+        scratch=[pltpu.VMEM((count, 2 * states), F32), everyone], order=order, token=2,
     )
-    b0 = Large(order, gb0)
-    steps = small_sum(order, st)
-    w_shape, c_shape = shaped((2, width, width)), shaped((2, 2 * states, width))
-    drive_shapes = [shaped((2, width, 2 * states))]
-    larges = {"A": wc1, "B": b1, "C": c0, "E": w0, "D": b0}
-    into = {}
-
-    def step(item):
-        if item == "S":
-            return next(steps, None)
-        large = larges[item]
-        if large.left():
-            large.send()
-        elif item == "A":
-            into["E"], into["C"] = ([made] for made in place(large, map_places, 1, [w_shape, c_shape]))
-        elif item == "B":
-            into["D"] = place(large, drive_places, 1, drive_shapes)
-        elif item in "CDE" and item not in into:
-            step("B" if item == "D" else "A")
-            step(item)
-        elif item in "CE":
-            if len(into[item]) == 1:
-                into[item] = place(large, map_places, 0, [c_shape if item == "C" else w_shape], into[item]) + [None]
-        elif len(into["D"]) == 1:
-            into["D"] = place(large, drive_places, 0, drive_shapes, into["D"]) + [None]
-        return None
-
-    for item in "".join(TAIL):
-        if item != "L":
-            sent = step(item)
-            st = st if sent is None else sent
-            continue
-        for sent in steps:
-            st = st if sent is None else sent
-        (tokens_grad, grad_gain, grad_shift, grad_skip, grad_bias, grad_rate, grad_rotation, new_mean, new_var,
-         unused) = call(
+    steps.add("D", gb0)
+    steps.shapes = {
+        "A": [shaped((2, width, width)), shaped((2, 2 * states, width))],
+        "B": [shaped((2, width, 2 * states))],
+    }
+    steps.run(ORDER[3][0])
+    z0, st = call(
+        "back", functools.partial(k_back, 0), [big(width), shaped((64, LANE))],
+        [drive0, mix0, u0, stat0, lim, vec, b_proj, sums1, lg1, sums0, lg0], order=order, token=1,
+    )
+    small_steps = small_sum(order, st)
+    last = []
+
+    def small():
+        last.extend(item for item in [next(small_steps, None)] if item is not None)
+
+    def leave():
+        while not last:
+            small()
+        last.extend(call(
             "leave", k_output,
             [shaped(tokens.shape), vector, vector, vector, vector, state_vector, state_vector, vector, vector,
              shaped((SUB, width))],
-            [st, z0, g0, u0, stat0, vec, lim, par, stat1, bn1, run_mean, run_var],
+            [last[0], z0, g0, u0, stat0, vec, lim, par, stat1, bn1, run_mean, run_var],
             scratch=[lines], results=9, order=order, token=9,
-        )
-    for item in "CED":
-        while len(into.get(item, ())) < 2:
-            step(item)
-    (grad_w, unused), (grad_c, unused), (grad_b, unused) = into["E"], into["C"], into["D"]
+        ))
+
+    steps.other.update({"S": small, "L": leave})
+    steps.run("".join(ORDER[3][1:]))
+    (tokens_grad, grad_gain, grad_shift, grad_skip, grad_bias, grad_rate, grad_rotation, new_mean, new_var) = last[1:10]
+    output, grad_w, grad_c, grad_b = emitted[0], steps.placed("E"), steps.placed("C"), steps.placed("D")
     return (output, tokens_grad, grad_gain, grad_shift, grad_b, grad_rate, grad_rotation, grad_c, grad_skip, grad_w,
             grad_bias, new_mean, new_var)
 

time: 191 us -> 185 us (0.969)
  Pallas kernels: 52.7 us -> 43.6 us
  waiting for transfers between devices: 57.6 us -> 60 us
    pallas_call x88 -> x91, Pallas kernels: 52.7 us -> 43.6 us  [call(): pl.pallas_call(run, name=name, out_shape=outs, in_specs=specs, out_specs=...]
    ppermute x18, starting transfers between devices: 14.7 us -> 20.2 us  [swap_by_core(): lax.ppermute(block, BOTH, [(i, i ^ (odd if i & 1 else even)) for i in ran...]
    ppermute x68, starting transfers between devices: 60.8 us -> 57.2 us  [swap(): return lax.ppermute(block, BOTH, [(i, i ^ distance) for i in range(total)])]
  transfers between devices with their start and end apart: 86 -> 86, of which waited for: 45 -> 45; matrix products, arithmetic and copies ran while one was open for 0% -> 0% of each run, Pallas kernels for 13% -> 12%
where the time goes in v4:
time: 185 us
  starting transfers between devices  77.4 us (42%)
  waiting for transfers between devices  60 us (32%)
  Pallas kernels  43.6 us (24%)
  local copies, waits for them, and re-layouts  2.67 us (1%)
    ppermute x68, starting transfers between devices, swap(): return lax.ppermute(block, BOTH, [(i, i ^ distance) for i in range(total)])  57.2 us
    pallas_call x91, Pallas kernels, call(): pl.pallas_call(run, name=name, out_shape=outs, in_specs=specs, out_specs=...  43.6 us
    ppermute x68, waiting for transfers between devices, swap(): return lax.ppermute(block, BOTH, [(i, i ^ distance) for i in range(total)])  41.6 us
    ppermute x18, starting transfers between devices, swap_by_core(): lax.ppermute(block, BOTH, [(i, i ^ (odd if i & 1 else even)) for i in ran...  20.2 us
    ppermute x18, waiting for transfers between devices, swap_by_core(): lax.ppermute(block, BOTH, [(i, i ^ (odd if i & 1 else even)) for i in ran...  18.3 us
  transfers between devices with their start and end apart: 86, of which 45 were waited for; matrix products, arithmetic and copies ran while one was open for 0% of the time, Pallas kernels for 12%

profile of v4, /device:TPU:0, one launch (start us, length us, event | category | flops | bytes accessed | tf_op | source)
XLA Modules:
  0.0 185.3 jit_solution(11447592590390771726)
XLA Ops:
  0.7 1.2 copy-done.3
  2.6 1.9 %enter.1 = (f32[1024,512]{1,0:T(8,128)S(1)}, f32[24,128]{1,0:T(8,128)S(1)}, s32[8,512]{1,0:T(8,128)S(1)}) custom-call(s32[4]{0:T(128)S(1)} %copy-done.14, bf16[4,256,512]{2,1,0:T(8,128)(2,1)S(1)} %copy-done.3), custom_call_target="tpu_custom_call" | custom-call | flops 5000000000 | bytes 1 | tf_op jit(solution)/shard_map/enter/pallas_call | solution.py:46
  5.0 1.2 prepare.1
  6.3 3.6 %collective-permute-start.1 = (f32[24,128]{1,0:T(8,128)S(1)}, f32[24,128]{1,0:T(8,128)S(1)}, u32[]{:S(2)}, u32[]{:S(2)}) collective-permute-start(f32[24,128]{1,0:T(8,128)S(1)} %add.31.refs_0_), channel_id=1, source_target_pairs={{0,25},{1,24},{2,27},{3,26},{4,29},{5,28},{6,31},{7,30},{8,17},{9,... | collective-permute-start | bytes 36872 | tf_op jit(solution)/shard_map/ppermute | solution.py:930
  11.3 1.7 collective-permute-done.3.refs_2_
  13.2 3.7 %collective-permute-start.4 = (f32[24,128]{1,0:T(8,128)S(1)}, f32[24,128]{1,0:T(8,128)S(1)}, u32[]{:S(2)}, u32[]{:S(2)}) collective-permute-start(f32[24,128]{1,0:T(8,128)S(1)} %add.33.refs_0_), channel_id=1, source_target_pairs={{0,7},{1,6},{2,5},{3,4},{4,3},{5,2},{6,1},{7,0},{8,15},{9,14},{10,... | collective-permute-start | bytes 36872 | tf_op jit(solution)/shard_map/ppermute | solution.py:930
  18.3 1.7 collective-permute-done.6.refs_2_
  21.0 1.5 drive0.1
  23.7 1.6 collective-permute-start.10
  25.3 1.5 collective-permute-start.9
  27.7 1.3 collective-permute-done.10.src_ref
  29.0 1.4 collective-permute-done.9.refs_2_
  30.6 3.7 %finish0.1 = (f32[1032,768]{1,0:T(8,128)S(1)}, bf16[1024,512]{1,0:T(8,128)(2,1)S(1)}, f32[1024,512]{1,0:T(8,128)S(1)}, f32[1024,512]{1,0:T(8,128)S(1)}, f32[1024...) custom-call(f32[8,768]{1,0:T(8,128)S(1)} %combine.4.refs_0_, ...), custom_call_target="tpu_custom_call" | custom-call | flops 5000000000 | bytes 1 | tf_op jit(solution)/shard_map/finish0/pallas_call | solution.py:46
  34.5 1.4 keep.1
  35.9 1.6 collective-permute-start.12
  37.7 1.5 collective-permute-start.13
  40.8 1.4 collective-permute-start.15
  42.2 2.6 %collective-permute-start.16 = (f32[16,128]{1,0:T(8,128)S(1)}, f32[16,128]{1,0:T(8,128)S(1)}, u32[]{:S(2)}, u32[]{:S(2)}) collective-permute-start(f32[16,128]{1,0:T(8,128)S(1)} %add.38.refs_0_), channel_id=1, source_target_pairs={{0,5},{1,4},{2,7},{3,6},{4,1},{5,0},{6,3},{7,2},{8,13},{9,12},{10,... | collective-permute-start | bytes 24584 | tf_op jit(solution)/shard_map/ppermute | solution.py:930
  46.3 1.6 drive1.1
  49.2 2.1 %collective-permute-start.21 = (f32[8,768]{1,0:T(8,128)S(1)}, f32[8,768]{1,0:T(8,128)S(1)}, u32[]{:S(2)}, u32[]{:S(2)}) collective-permute-start(f32[8,768]{1,0:T(8,128)S(1)} %combine.5.refs_0_), channel_id=1, source_target_pairs={{0,7},{1,6},{2,5},{3,4},{4,3},{5,2},{6,1},{7,0},{8,15},{9,14},{10,... | collective-permute-start | bytes 73736 | tf_op jit(solution)/shard_map/ppermute | solution.py:930
  55.8 7.0 %middle.1 = (f32[4,1024,128]{2,1,0:T(8,128)S(1)}, f32[1032,768]{1,0:T(8,128)S(1)}, bf16[1024,512]{1,0:T(8,128)(2,1)S(1)}, f32[1024,768]{1,0:T(8,128)S(1)}, f32[1...) custom-call(f32[8,768]{1,0:T(8,128)S(1)} %combine.5.refs_0_, ...), custom_call_target="tpu_custom_call" | custom-call | flops 5000000000 | bytes 1 | tf_op jit(solution)/shard_map/middle/pallas_call | solution.py:46
  64.8 1.8 collective-permute-start.25
  66.6 2.1 %collective-permute-start.23 = (f32[8,768]{1,0:T(8,128)S(1)}, f32[8,768]{1,0:T(8,128)S(1)}, u32[]{:S(2)}, u32[]{:S(2)}) collective-permute-start(f32[8,768]{1,0:T(8,128)S(1)} %combine.6.refs_1_.refs_0_), channel_id=1, source_target_pairs={{0,3},{1,2},{2,1},{3,0},{4,7},{5,6},{6,5},{7,4},{8,11},{9,10},{10,... | collective-permute-start | bytes 73736 | tf_op jit(solution)/shard_map/ppermute | solution.py:930
  70.0 1.6 collective-permute-start.29
  71.7 3.1 %adjoint1.1 = (f32[1024,512]{1,0:T(8,128)S(1)}, f32[768,512]{1,0:T(8,128)S(1)}, f32[8,128]{1,0:T(8,128)S(1)}, f32[16,128]{1,0:T(8,128)S(1)}) custom-call(f32[8,768]{1,0:T(8,128)S(1)} %combine.6.refs_1_.refs_0_, f32[8,768]{1,0:T(8,128)S(1)} %collective-permute-done.23.refs_1_, f32[8,768]{1,0:T(8,128)S(1)} %collective-permute-done.24.refs_2_, ...), custom_call_target="tpu_custom_call" | custom-call | flops 5000000000 | bytes 1 | tf_op jit(solution)/shard_map/adjoint1/pallas_call | solution.py:46
  76.0 1.2 collective-permute-start.31
  79.0 1.8 collective-permute-done.29.refs_1_
  80.9 1.2 collective-permute-done.28.refs_1_
  83.0 1.5 collective-permute-start.33
  84.6 1.5 collective-permute-start.32
  87.1 1.5 emit.1
  89.6 3.5 %collective-permute-done.35.refs_1_ = f32[160,512]{1,0:T(8,128)S(1)} collective-permute-done((f32[160,512]{1,0:T(8,128)S(1)}, f32[160,512]{1,0:T(8,128)S(1)}, u32[]{:S(2)}, u32[]{:S(2)}) %collective-permute-start.35) | collective-permute-done | bytes 327712 | tf_op jit(solution)/shard_map/ppermute | solution.py:935
  93.2 4.2 %lower.1 = (f32[1024,512]{1,0:T(8,128)S(1)}, bf16[1024,512]{1,0:T(8,128)(2,1)S(1)}, f32[1024,768]{1,0:T(8,128)S(1)}, f32[512,512]{1,0:T(8,128)S(1)}, f32[768,512...) custom-call(f32[16,128]{1,0:T(8,128)S(1)} %add.45.refs_2_.refs_0_, ...), custom_call_target="tpu_custom_call" | custom-call | flops 5000000000 | bytes 1 | tf_op jit(solution)/shard_map/lower/pallas_call | solution.py:46
  99.5 1.9 %collective-permute-start.40 = (f32[8,768]{1,0:T(8,128)S(1)}, f32[8,768]{1,0:T(8,128)S(1)}, u32[]{:S(2)}, u32[]{:S(2)}) collective-permute-start(f32[8,768]{1,0:T(8,128)S(1)} %combine.7.refs_1_.refs_0_), channel_id=1, source_target_pairs={{0,7},{1,6},{2,5},{3,4},{4,3},{5,2},{6,1},{7,0},{8,15},{9,14},{10,... | collective-permute-start | bytes 73736 | tf_op jit(solution)/shard_map/ppermute | solution.py:930
  102.3 2.2 %collective-permute-done.40.src_ref = f32[8,768]{1,0:T(8,128)S(1)} collective-permute-done((f32[8,768]{1,0:T(8,128)S(1)}, f32[8,768]{1,0:T(8,128)S(1)}, u32[]{:S(2)}, u32[]{:S(2)}) %collective-permute-start.40) | collective-permute-done | bytes 24608 | tf_op jit(solution)/shard_map/ppermute | solution.py:930
  104.5 2.4 %collective-permute-start.38 = (f32[8,768]{1,0:T(8,128)S(1)}, f32[8,768]{1,0:T(8,128)S(1)}, u32[]{:S(2)}, u32[]{:S(2)}) collective-permute-start(f32[8,768]{1,0:T(8,128)S(1)} %combine.7.refs_1_.refs_0_), channel_id=1, source_target_pairs={{0,3},{1,2},{2,1},{3,0},{4,7},{5,6},{6,5},{7,4},{8,11},{9,10},{10,... | collective-permute-start | bytes 73736 | tf_op jit(solution)/shard_map/ppermute | solution.py:930
  109.2 2.0 %adjoint0.1 = (bf16[1024,768]{1,0:T(8,128)(2,1)S(1)}, f32[768,512]{1,0:T(8,128)S(1)}, f32[8,128]{1,0:T(8,128)S(1)}) custom-call(f32[8,768]{1,0:T(8,128)S(1)} %combine.7.refs_1_.refs_0_, f32[8,768]{1,0:T(8,128)S(1)} %collective-permute-done.38.refs_1_, f32[8,768]{1,0:T(8,128)S(1)} %collective-permute-done.39.refs_2_, f32[8,768]{1,0:T(8,128)S(1)} %copy.41.refs_3_, ...), custom_call_target="tpu_custom_call" | custom-call | flops 5000000000 | bytes 1 | tf_op jit(solution)/shard_map/adjoint0/pallas_call | solution.py:46
  111.4 1.2 back.1
  113.2 2.4 %collective-permute-start.53 = (f32[80,512]{1,0:T(8,128)S(1)}, f32[80,512]{1,0:T(8,128)S(1)}, u32[]{:S(2)}, u32[]{:S(2)}) collective-permute-start(f32[80,512]{1,0:T(8,128)S(1)} %add.46.refs_2_.refs_0_), channel_id=1, source_target_pairs={{0,4},{1,5},{2,6},{3,7},{4,0},{5,1},{6,2},{7,3},{8,12},{9,13},{10,... | collective-permute-start | bytes 491528 | tf_op jit(solution)/shard_map/ppermute | solution.py:930
  116.6 1.8 collective-permute-done.48.refs_1_
  118.4 1.3 collective-permute-start.52
  119.9 3.3 %collective-permute-done.46.refs_1_ = f32[96,512]{1,0:T(8,128)S(1)} collective-permute-done((f32[96,512]{1,0:T(8,128)S(1)}, f32[96,512]{1,0:T(8,128)S(1)}, u32[]{:S(2)}, u32[]{:S(2)}) %collective-permute-start.46) | collective-permute-done | bytes 196640 | tf_op jit(solution)/shard_map/ppermute | solution.py:935
  124.0 1.3 collective-permute-start.58
  125.3 2.2 %collective-permute-done.53.refs_1_ = f32[80,512]{1,0:T(8,128)S(1)} collective-permute-done((f32[80,512]{1,0:T(8,128)S(1)}, f32[80,512]{1,0:T(8,128)S(1)}, u32[]{:S(2)}, u32[]{:S(2)}) %collective-permute-start.53) | collective-permute-done | bytes 163872 | tf_op jit(solution)/shard_map/ppermute | solution.py:930
  130.6 1.3 collective-permute-start.54
  132.0 1.4 collective-permute-start.63
  133.4 3.0 %collective-permute-done.56.refs_1_ = f32[80,512]{1,0:T(8,128)S(1)} collective-permute-done((f32[80,512]{1,0:T(8,128)S(1)}, f32[80,512]{1,0:T(8,128)S(1)}, u32[]{:S(2)}, u32[]{:S(2)}) %collective-permute-start.56) | collective-permute-done | bytes 163872 | tf_op jit(solution)/shard_map/ppermute | solution.py:930
  136.4 2.4 %collective-permute-start.61 = (f32[64,512]{1,0:T(8,128)S(1)}, f32[64,512]{1,0:T(8,128)S(1)}, u32[]{:S(2)}, u32[]{:S(2)}) collective-permute-start(f32[64,512]{1,0:T(8,128)S(1)} %add.50.refs_2_.refs_0_), channel_id=1, source_target_pairs={{0,8},{1,17},{2,10},{3,19},{4,12},{5,21},{6,14},{7,23},{8,0},{9,25... | collective-permute-start | bytes 393224 | tf_op jit(solution)/shard_map/ppermute | solution.py:935
  139.1 2.5 %collective-permute-start.66 = (f32[48,512]{1,0:T(8,128)S(1)}, f32[48,512]{1,0:T(8,128)S(1)}, u32[]{:S(2)}, u32[]{:S(2)}) collective-permute-start(f32[48,512]{1,0:T(8,128)S(1)} %add.51.refs_2_.refs_0_), channel_id=1, source_target_pairs={{0,4},{1,5},{2,6},{3,7},{4,0},{5,1},{6,2},{7,3},{8,12},{9,13},{10,... | collective-permute-start | bytes 294920 | tf_op jit(solution)/shard_map/ppermute | solution.py:930
  141.7 2.2 %collective-permute-done.62.refs_1_ = f32[48,512]{1,0:T(8,128)S(1)} collective-permute-done((f32[48,512]{1,0:T(8,128)S(1)}, f32[48,512]{1,0:T(8,128)S(1)}, u32[]{:S(2)}, u32[]{:S(2)}) %collective-permute-start.62) | collective-permute-done | bytes 98336 | tf_op jit(solution)/shard_map/ppermute | solution.py:930
  144.2 2.8 %collective-permute-start.68 = (f32[48,512]{1,0:T(8,128)S(1)}, f32[48,512]{1,0:T(8,128)S(1)}, u32[]{:S(2)}, u32[]{:S(2)}) collective-permute-start(f32[48,512]{1,0:T(8,128)S(1)} %add.54.refs_2_.refs_0_), channel_id=1, source_target_pairs={{0,4},{1,5},{2,6},{3,7},{4,0},{5,1},{6,2},{7,3},{8,12},{9,13},{10,... | collective-permute-start | bytes 294920 | tf_op jit(solution)/shard_map/ppermute | solution.py:930
  147.0 1.3 collective-permute-start.71
  150.3 1.5 collective-permute-done.68.refs_1_
  151.8 1.4 collective-permute-start.67
  153.6 1.6 collective-permute-done.70.refs_1_
  156.0 2.1 %collective-permute-done.69.refs_1_ = f32[48,512]{1,0:T(8,128)S(1)} collective-permute-done((f32[48,512]{1,0:T(8,128)S(1)}, f32[48,512]{1,0:T(8,128)S(1)}, u32[]{:S(2)}, u32[]{:S(2)}) %collective-permute-start.69) | collective-permute-done | bytes 98336 | tf_op jit(solution)/shard_map/ppermute | solution.py:930
  158.1 2.8 %collective-permute-start.76 = (f32[96,512]{1,0:T(8,128)S(1)}, f32[96,512]{1,0:T(8,128)S(1)}, u32[]{:S(2)}, u32[]{:S(2)}) collective-permute-start(f32[96,512]{1,0:T(8,128)S(1)} %join.17.refs_2_.refs_0_), channel_id=1, source_target_pairs={{0,16},{1,9},{2,18},{3,11},{4,20},{5,13},{6,22},{7,15},{8,24},{9,1... | collective-permute-start | bytes 589832 | tf_op jit(solution)/shard_map/ppermute | solution.py:935
  161.9 4.8 %collective-permute-done.76.refs_1_ = f32[96,512]{1,0:T(8,128)S(1)} collective-permute-done((f32[96,512]{1,0:T(8,128)S(1)}, f32[96,512]{1,0:T(8,128)S(1)}, u32[]{:S(2)}, u32[]{:S(2)}) %collective-permute-start.76) | collective-permute-done | bytes 196640 | tf_op jit(solution)/shard_map/ppermute | solution.py:935
  167.5 3.4 %collective-permute-done.74.refs_1_ = f32[96,512]{1,0:T(8,128)S(1)} collective-permute-done((f32[96,512]{1,0:T(8,128)S(1)}, f32[96,512]{1,0:T(8,128)S(1)}, u32[]{:S(2)}, u32[]{:S(2)}) %collective-permute-start.74) | collective-permute-done | bytes 196640 | tf_op jit(solution)/shard_map/ppermute | solution.py:935
  172.7 3.1 %leave.1 = (f32[4,256,512]{2,1,0:T(8,128)}, f32[2,512]{1,0:T(2,128)}, f32[2,512]{1,0:T(2,128)}, f32[2,512]{1,0:T(2,128)}, f32[2,512]{1,0:T(2,128)}, /*index=5*/f...) custom-call(f32[64,128]{1,0:T(8,128)S(1)} %add.61.refs_0_.refs_12_, ...), custom_call_target="tpu_custom_call" | custom-call | flops 5000000000 | bytes 1 | tf_op jit(solution)/shard_map/leave/pallas_call | solution.py:46
  176.7 1.6 place.5
  179.5 1.2 place.6
  181.0 1.2 place.7
  183.3 1.8 place.9
  (233 shorter events, 47.8 us)
Async XLA Ops:
  6.3 5.0 %collective-permute-start.1 = (f32[24,128]{1,0:T(8,128)S(1)}, f32[24,128]{1,0:T(8,128)S(1)}, u32[]{:S(2)}, u32[]{:S(2)}) collective-permute-start(f32[24,128]{1,0:T(8,128)S(1)} %add.31.refs_0_), channel_id=1, source_target_pairs={{0,25},{1,24},{2,27},{3,26},{4,29},{5,28},{6,31},{7,30},{8,17},{9,... | collective-permute-start | bytes 36872 | tf_op jit(solution)/shard_map/ppermute | solution.py:930
  13.2 5.1 %collective-permute-start.4 = (f32[24,128]{1,0:T(8,128)S(1)}, f32[24,128]{1,0:T(8,128)S(1)}, u32[]{:S(2)}, u32[]{:S(2)}) collective-permute-start(f32[24,128]{1,0:T(8,128)S(1)} %add.33.refs_0_), channel_id=1, source_target_pairs={{0,7},{1,6},{2,5},{3,4},{4,3},{5,2},{6,1},{7,0},{8,15},{9,14},{10,... | collective-permute-start | bytes 36872 | tf_op jit(solution)/shard_map/ppermute | solution.py:930
  23.7 5.2 %collective-permute-start.10 = (f32[8,768]{1,0:T(8,128)S(1)}, f32[8,768]{1,0:T(8,128)S(1)}, u32[]{:S(2)}, u32[]{:S(2)}) collective-permute-start(f32[8,768]{1,0:T(8,128)S(1)} %combine.4.refs_0_), channel_id=1, source_target_pairs={{0,7},{1,6},{2,5},{3,4},{4,3},{5,2},{6,1},{7,0},{8,15},{9,14},{10,... | collective-permute-start | bytes 73736 | tf_op jit(solution)/shard_map/ppermute | solution.py:930
  25.3 5.1 %collective-permute-start.9 = (f32[8,768]{1,0:T(8,128)S(1)}, f32[8,768]{1,0:T(8,128)S(1)}, u32[]{:S(2)}, u32[]{:S(2)}) collective-permute-start(f32[8,768]{1,0:T(8,128)S(1)} %combine.4.refs_0_), channel_id=1, source_target_pairs={{0,5},{1,4},{2,7},{3,6},{4,1},{5,0},{6,3},{7,2},{8,13},{9,12},{10,... | collective-permute-start | bytes 73736 | tf_op jit(solution)/shard_map/ppermute | solution.py:930
  40.8 4.9 %collective-permute-start.15 = (f32[16,128]{1,0:T(8,128)S(1)}, f32[16,128]{1,0:T(8,128)S(1)}, u32[]{:S(2)}, u32[]{:S(2)}) collective-permute-start(f32[16,128]{1,0:T(8,128)S(1)} %add.38.refs_0_), channel_id=1, source_target_pairs={{0,7},{1,6},{2,5},{3,4},{4,3},{5,2},{6,1},{7,0},{8,15},{9,14},{10,... | collective-permute-start | bytes 24584 | tf_op jit(solution)/shard_map/ppermute | solution.py:930
  49.2 5.2 %collective-permute-start.21 = (f32[8,768]{1,0:T(8,128)S(1)}, f32[8,768]{1,0:T(8,128)S(1)}, u32[]{:S(2)}, u32[]{:S(2)}) collective-permute-start(f32[8,768]{1,0:T(8,128)S(1)} %combine.5.refs_0_), channel_id=1, source_target_pairs={{0,7},{1,6},{2,5},{3,4},{4,3},{5,2},{6,1},{7,0},{8,15},{9,14},{10,... | collective-permute-start | bytes 73736 | tf_op jit(solution)/shard_map/ppermute | solution.py:930
  51.4 4.2 %collective-permute-start.20 = (f32[8,768]{1,0:T(8,128)S(1)}, f32[8,768]{1,0:T(8,128)S(1)}, u32[]{:S(2)}, u32[]{:S(2)}) collective-permute-start(f32[8,768]{1,0:T(8,128)S(1)} %combine.5.refs_0_), channel_id=1, source_target_pairs={{0,5},{1,4},{2,7},{3,6},{4,1},{5,0},{6,3},{7,2},{8,13},{9,12},{10,... | collective-permute-start | bytes 73736 | tf_op jit(solution)/shard_map/ppermute | solution.py:930
  64.4 5.5 %collective-permute-start.26 = (f32[640,512]{1,0:T(8,128)S(1)}, f32[640,512]{1,0:T(8,128)S(1)}, u32[]{:S(2)}, u32[]{:S(2)}) collective-permute-start(f32[640,512]{1,0:T(8,128)S(1)} %split.5.refs_2_), channel_id=1, source_target_pairs={{0,1},{1,0},{2,3},{3,2},{4,5},{5,4},{6,7},{7,6},{8,9},{9,8},{10,11... | collective-permute-start | bytes 3932168 | tf_op jit(solution)/shard_map/ppermute | solution.py:930
  64.8 5.0 %collective-permute-start.25 = (f32[8,768]{1,0:T(8,128)S(1)}, f32[8,768]{1,0:T(8,128)S(1)}, u32[]{:S(2)}, u32[]{:S(2)}) collective-permute-start(f32[8,768]{1,0:T(8,128)S(1)} %combine.6.refs_1_.refs_0_), channel_id=1, source_target_pairs={{0,7},{1,6},{2,5},{3,4},{4,3},{5,2},{6,1},{7,0},{8,15},{9,14},{10,... | collective-permute-start | bytes 73736 | tf_op jit(solution)/shard_map/ppermute | solution.py:930
  66.6 5.1 %collective-permute-start.24 = (f32[8,768]{1,0:T(8,128)S(1)}, f32[8,768]{1,0:T(8,128)S(1)}, u32[]{:S(2)}, u32[]{:S(2)}) collective-permute-start(f32[8,768]{1,0:T(8,128)S(1)} %combine.6.refs_1_.refs_0_), channel_id=1, source_target_pairs={{0,5},{1,4},{2,7},{3,6},{4,1},{5,0},{6,3},{7,2},{8,13},{9,12},{10,... | collective-permute-start | bytes 73736 | tf_op jit(solution)/shard_map/ppermute | solution.py:930
  66.6 5.1 %collective-permute-start.23 = (f32[8,768]{1,0:T(8,128)S(1)}, f32[8,768]{1,0:T(8,128)S(1)}, u32[]{:S(2)}, u32[]{:S(2)}) collective-permute-start(f32[8,768]{1,0:T(8,128)S(1)} %combine.6.refs_1_.refs_0_), channel_id=1, source_target_pairs={{0,3},{1,2},{2,1},{3,0},{4,7},{5,6},{6,5},{7,4},{8,11},{9,10},{10,... | collective-permute-start | bytes 73736 | tf_op jit(solution)/shard_map/ppermute | solution.py:930
  70.0 10.7 %collective-permute-start.29 = (f32[320,512]{1,0:T(8,128)S(1)}, f32[320,512]{1,0:T(8,128)S(1)}, u32[]{:S(2)}, u32[]{:S(2)}) collective-permute-start(f32[320,512]{1,0:T(8,128)S(1)} %get-tuple-element.143.refs_20_), channel_id=1, source_target_pairs={{0,8},{1,17},{2,10},{3,19},{4,12},{5,21},{6,14},{7,23},{8,0},{9,25... | collective-permute-start | bytes 1966088 | tf_op jit(solution)/shard_map/ppermute | solution.py:935
  75.0 14.5 %collective-permute-start.36 = (f32[384,512]{1,0:T(8,128)S(1)}, f32[384,512]{1,0:T(8,128)S(1)}, u32[]{:S(2)}, u32[]{:S(2)}) collective-permute-start(f32[384,512]{1,0:T(8,128)S(1)} %split.6.refs_2_), channel_id=1, source_target_pairs={{0,1},{1,0},{2,3},{3,2},{4,5},{5,4},{6,7},{7,6},{8,9},{9,8},{10,11... | collective-permute-start | bytes 2359304 | tf_op jit(solution)/shard_map/ppermute | solution.py:930
  76.0 6.1 %collective-permute-start.31 = (f32[16,128]{1,0:T(8,128)S(1)}, f32[16,128]{1,0:T(8,128)S(1)}, u32[]{:S(2)}, u32[]{:S(2)}) collective-permute-start(f32[16,128]{1,0:T(8,128)S(1)} %add.41.refs_2_.refs_0_), channel_id=1, source_target_pairs={{0,9},{1,8},{2,11},{3,10},{4,13},{5,12},{6,15},{7,14},{8,1},{9,0},... | collective-permute-start | bytes 24584 | tf_op jit(solution)/shard_map/ppermute | solution.py:930
  77.2 4.9 %collective-permute-start.30 = (f32[16,128]{1,0:T(8,128)S(1)}, f32[16,128]{1,0:T(8,128)S(1)}, u32[]{:S(2)}, u32[]{:S(2)}) collective-permute-start(f32[16,128]{1,0:T(8,128)S(1)} %add.41.refs_2_.refs_0_), channel_id=1, source_target_pairs={{0,17},{1,16},{2,19},{3,18},{4,21},{5,20},{6,23},{7,22},{8,25},{9,... | collective-permute-start | bytes 24584 | tf_op jit(solution)/shard_map/ppermute | solution.py:930
  82.1 7.3 %collective-permute-start.34 = (f32[16,128]{1,0:T(8,128)S(1)}, f32[16,128]{1,0:T(8,128)S(1)}, u32[]{:S(2)}, u32[]{:S(2)}) collective-permute-start(f32[16,128]{1,0:T(8,128)S(1)} %add.43.refs_1_.refs_0_), channel_id=1, source_target_pairs={{0,3},{1,2},{2,1},{3,0},{4,7},{5,6},{6,5},{7,4},{8,11},{9,10},{10,... | collective-permute-start | bytes 24584 | tf_op jit(solution)/shard_map/ppermute | solution.py:930
  83.0 6.4 %collective-permute-start.33 = (f32[16,128]{1,0:T(8,128)S(1)}, f32[16,128]{1,0:T(8,128)S(1)}, u32[]{:S(2)}, u32[]{:S(2)}) collective-permute-start(f32[16,128]{1,0:T(8,128)S(1)} %add.43.refs_1_.refs_0_), channel_id=1, source_target_pairs={{0,5},{1,4},{2,7},{3,6},{4,1},{5,0},{6,3},{7,2},{8,13},{9,12},{10,... | collective-permute-start | bytes 24584 | tf_op jit(solution)/shard_map/ppermute | solution.py:930
  84.6 4.9 %collective-permute-start.32 = (f32[16,128]{1,0:T(8,128)S(1)}, f32[16,128]{1,0:T(8,128)S(1)}, u32[]{:S(2)}, u32[]{:S(2)}) collective-permute-start(f32[16,128]{1,0:T(8,128)S(1)} %add.43.refs_1_.refs_0_), channel_id=1, source_target_pairs={{0,7},{1,6},{2,5},{3,4},{4,3},{5,2},{6,1},{7,0},{8,15},{9,14},{10,... | collective-permute-start | bytes 24584 | tf_op jit(solution)/shard_map/ppermute | solution.py:930
  86.1 7.1 %collective-permute-start.35 = (f32[160,512]{1,0:T(8,128)S(1)}, f32[160,512]{1,0:T(8,128)S(1)}, u32[]{:S(2)}, u32[]{:S(2)}) collective-permute-start(f32[160,512]{1,0:T(8,128)S(1)} %get-tuple-element.147.refs_2_), channel_id=1, source_target_pairs={{0,16},{1,9},{2,18},{3,11},{4,20},{5,13},{6,22},{7,15},{8,24},{9,1... | collective-permute-start | bytes 983048 | tf_op jit(solution)/shard_map/ppermute | solution.py:935
  98.8 5.7 %collective-permute-start.42 = (f32[384,512]{1,0:T(8,128)S(1)}, f32[384,512]{1,0:T(8,128)S(1)}, u32[]{:S(2)}, u32[]{:S(2)}) collective-permute-start(f32[384,512]{1,0:T(8,128)S(1)} %split.7.refs_1_), channel_id=1, source_target_pairs={{0,1},{1,0},{2,3},{3,2},{4,5},{5,4},{6,7},{7,6},{8,9},{9,8},{10,11... | collective-permute-start | bytes 2359304 | tf_op jit(solution)/shard_map/ppermute | solution.py:930
  99.1 7.9 %collective-permute-start.41 = (f32[256,512]{1,0:T(8,128)S(1)}, f32[256,512]{1,0:T(8,128)S(1)}, u32[]{:S(2)}, u32[]{:S(2)}) collective-permute-start(f32[256,512]{1,0:T(8,128)S(1)} %split.8.refs_2_), channel_id=1, source_target_pairs={{0,1},{1,0},{2,3},{3,2},{4,5},{5,4},{6,7},{7,6},{8,9},{9,8},{10,11... | collective-permute-start | bytes 1572872 | tf_op jit(solution)/shard_map/ppermute | solution.py:930
  99.5 5.0 %collective-permute-start.40 = (f32[8,768]{1,0:T(8,128)S(1)}, f32[8,768]{1,0:T(8,128)S(1)}, u32[]{:S(2)}, u32[]{:S(2)}) collective-permute-start(f32[8,768]{1,0:T(8,128)S(1)} %combine.7.refs_1_.refs_0_), channel_id=1, source_target_pairs={{0,7},{1,6},{2,5},{3,4},{4,3},{5,2},{6,1},{7,0},{8,15},{9,14},{10,... | collective-permute-start | bytes 73736 | tf_op jit(solution)/shard_map/ppermute | solution.py:930
  101.3 11.8 %collective-permute-start.44 = (f32[192,512]{1,0:T(8,128)S(1)}, f32[192,512]{1,0:T(8,128)S(1)}, u32[]{:S(2)}, u32[]{:S(2)}) collective-permute-start(f32[192,512]{1,0:T(8,128)S(1)} %get-tuple-element.157.refs_2_), channel_id=1, source_target_pairs={{0,8},{1,17},{2,10},{3,19},{4,12},{5,21},{6,14},{7,23},{8,0},{9,25... | collective-permute-start | bytes 1179656 | tf_op jit(solution)/shard_map/ppermute | solution.py:935
  102.3 10.4 %collective-permute-start.45 = (f32[80,512]{1,0:T(8,128)S(1)}, f32[80,512]{1,0:T(8,128)S(1)}, u32[]{:S(2)}, u32[]{:S(2)}) collective-permute-start(f32[80,512]{1,0:T(8,128)S(1)} %get-tuple-element.158.refs_18_), channel_id=1, source_target_pairs={{0,2},{1,3},{2,0},{3,1},{4,6},{5,7},{6,4},{7,5},{8,10},{9,11},{10,... | collective-permute-start | bytes 491528 | tf_op jit(solution)/shard_map/ppermute | solution.py:930
  104.5 4.3 %collective-permute-start.39 = (f32[8,768]{1,0:T(8,128)S(1)}, f32[8,768]{1,0:T(8,128)S(1)}, u32[]{:S(2)}, u32[]{:S(2)}) collective-permute-start(f32[8,768]{1,0:T(8,128)S(1)} %combine.7.refs_1_.refs_0_), channel_id=1, source_target_pairs={{0,5},{1,4},{2,7},{3,6},{4,1},{5,0},{6,3},{7,2},{8,13},{9,12},{10,... | collective-permute-start | bytes 73736 | tf_op jit(solution)/shard_map/ppermute | solution.py:930
  104.5 4.6 %collective-permute-start.38 = (f32[8,768]{1,0:T(8,128)S(1)}, f32[8,768]{1,0:T(8,128)S(1)}, u32[]{:S(2)}, u32[]{:S(2)}) collective-permute-start(f32[8,768]{1,0:T(8,128)S(1)} %combine.7.refs_1_.refs_0_), channel_id=1, source_target_pairs={{0,3},{1,2},{2,1},{3,0},{4,7},{5,6},{6,5},{7,4},{8,11},{9,10},{10,... | collective-permute-start | bytes 73736 | tf_op jit(solution)/shard_map/ppermute | solution.py:930
  107.0 12.8 %collective-permute-start.47 = (f32[192,512]{1,0:T(8,128)S(1)}, f32[192,512]{1,0:T(8,128)S(1)}, u32[]{:S(2)}, u32[]{:S(2)}) collective-permute-start(f32[192,512]{1,0:T(8,128)S(1)} %get-tuple-element.164.refs_2_), channel_id=1, source_target_pairs={{0,8},{1,17},{2,10},{3,19},{4,12},{5,21},{6,14},{7,23},{8,0},{9,25... | collective-permute-start | bytes 1179656 | tf_op jit(solution)/shard_map/ppermute | solution.py:935
  108.8 9.6 %collective-permute-start.48 = (f32[128,512]{1,0:T(8,128)S(1)}, f32[128,512]{1,0:T(8,128)S(1)}, u32[]{:S(2)}, u32[]{:S(2)}) collective-permute-start(f32[128,512]{1,0:T(8,128)S(1)} %get-tuple-element.165.refs_14_), channel_id=1, source_target_pairs={{0,2},{1,3},{2,0},{3,1},{4,6},{5,7},{6,4},{7,5},{8,10},{9,11},{10,... | collective-permute-start | bytes 786440 | tf_op jit(solution)/shard_map/ppermute | solution.py:930
  111.2 4.3 %collective-permute-start.49 = (f32[384,512]{1,0:T(8,128)S(1)}, f32[384,512]{1,0:T(8,128)S(1)}, u32[]{:S(2)}, u32[]{:S(2)}) collective-permute-start(f32[384,512]{1,0:T(8,128)S(1)} %split.9.refs_11_), channel_id=1, source_target_pairs={{0,1},{1,0},{2,3},{3,2},{4,5},{5,4},{6,7},{7,6},{8,9},{9,8},{10,11... | collective-permute-start | bytes 2359304 | tf_op jit(solution)/shard_map/ppermute | solution.py:930
  112.7 11.3 %collective-permute-start.43 = (f32[64,128]{1,0:T(8,128)S(1)}, f32[64,128]{1,0:T(8,128)S(1)}, u32[]{:S(2)}, u32[]{:S(2)}) collective-permute-start(f32[64,128]{1,0:T(8,128)S(1)} %get-tuple-element.173.refs_2_.refs_0_), channel_id=1, source_target_pairs={{0,1},{1,0},{2,3},{3,2},{4,5},{5,4},{6,7},{7,6},{8,9},{9,8},{10,11... | collective-permute-start | bytes 98312 | tf_op jit(solution)/shard_map/ppermute | solution.py:930
  113.2 14.4 %collective-permute-start.53 = (f32[80,512]{1,0:T(8,128)S(1)}, f32[80,512]{1,0:T(8,128)S(1)}, u32[]{:S(2)}, u32[]{:S(2)}) collective-permute-start(f32[80,512]{1,0:T(8,128)S(1)} %add.46.refs_2_.refs_0_), channel_id=1, source_target_pairs={{0,4},{1,5},{2,6},{3,7},{4,0},{5,1},{6,2},{7,3},{8,12},{9,13},{10,... | collective-permute-start | bytes 491528 | tf_op jit(solution)/shard_map/ppermute | solution.py:930
  115.6 7.6 %collective-permute-start.46 = (f32[96,512]{1,0:T(8,128)S(1)}, f32[96,512]{1,0:T(8,128)S(1)}, u32[]{:S(2)}, u32[]{:S(2)}) collective-permute-start(f32[96,512]{1,0:T(8,128)S(1)} %get-tuple-element.177.refs_2_), channel_id=1, source_target_pairs={{0,16},{1,9},{2,18},{3,11},{4,20},{5,13},{6,22},{7,15},{8,24},{9,1... | collective-permute-start | bytes 589832 | tf_op jit(solution)/shard_map/ppermute | solution.py:935
  118.4 9.9 %collective-permute-start.52 = (f32[192,512]{1,0:T(8,128)S(1)}, f32[192,512]{1,0:T(8,128)S(1)}, u32[]{:S(2)}, u32[]{:S(2)}) collective-permute-start(f32[192,512]{1,0:T(8,128)S(1)} %get-tuple-element.180.refs_2_), channel_id=1, source_target_pairs={{0,8},{1,17},{2,10},{3,19},{4,12},{5,21},{6,14},{7,23},{8,0},{9,25... | collective-permute-start | bytes 1179656 | tf_op jit(solution)/shard_map/ppermute | solution.py:935
  119.8 12.2 %collective-permute-start.57 = (f32[64,512]{1,0:T(8,128)S(1)}, f32[64,512]{1,0:T(8,128)S(1)}, u32[]{:S(2)}, u32[]{:S(2)}) collective-permute-start(f32[64,512]{1,0:T(8,128)S(1)} %get-tuple-element.181.refs_2_), channel_id=1, source_target_pairs={{0,4},{1,5},{2,6},{3,7},{4,0},{5,1},{6,2},{7,3},{8,12},{9,13},{10,... | collective-permute-start | bytes 393224 | tf_op jit(solution)/shard_map/ppermute | solution.py:930
  123.2 5.7 %collective-permute-start.51 = (f32[96,512]{1,0:T(8,128)S(1)}, f32[96,512]{1,0:T(8,128)S(1)}, u32[]{:S(2)}, u32[]{:S(2)}) collective-permute-start(f32[96,512]{1,0:T(8,128)S(1)} %get-tuple-element.182.refs_2_), channel_id=1, source_target_pairs={{0,16},{1,9},{2,18},{3,11},{4,20},{5,13},{6,22},{7,15},{8,24},{9,1... | collective-permute-start | bytes 589832 | tf_op jit(solution)/shard_map/ppermute | solution.py:935
  124.0 6.6 %collective-permute-start.58 = (f32[48,512]{1,0:T(8,128)S(1)}, f32[48,512]{1,0:T(8,128)S(1)}, u32[]{:S(2)}, u32[]{:S(2)}) collective-permute-start(f32[48,512]{1,0:T(8,128)S(1)} %get-tuple-element.183.refs_2_), channel_id=1, source_target_pairs={{0,2},{1,3},{2,0},{3,1},{4,6},{5,7},{6,4},{7,5},{8,10},{9,11},{10,... | collective-permute-start | bytes 294920 | tf_op jit(solution)/shard_map/ppermute | solution.py:930
  127.6 11.5 %collective-permute-start.50 = (f32[64,128]{1,0:T(8,128)S(1)}, f32[64,128]{1,0:T(8,128)S(1)}, u32[]{:S(2)}, u32[]{:S(2)}) collective-permute-start(f32[64,128]{1,0:T(8,128)S(1)} %add.47.refs_2_.refs_0_), channel_id=1, source_target_pairs={{0,9},{1,8},{2,11},{3,10},{4,13},{5,12},{6,15},{7,14},{8,1},{9,0},... | collective-permute-start | bytes 98312 | tf_op jit(solution)/shard_map/ppermute | solution.py:930
  128.3 8.1 %collective-permute-start.56 = (f32[80,512]{1,0:T(8,128)S(1)}, f32[80,512]{1,0:T(8,128)S(1)}, u32[]{:S(2)}, u32[]{:S(2)}) collective-permute-start(f32[80,512]{1,0:T(8,128)S(1)} %add.48.refs_2_.refs_0_), channel_id=1, source_target_pairs={{0,2},{1,3},{2,0},{3,1},{4,6},{5,7},{6,4},{7,5},{8,10},{9,11},{10,... | collective-permute-start | bytes 491528 | tf_op jit(solution)/shard_map/ppermute | solution.py:930
  128.9 9.9 %collective-permute-start.55 = (f32[96,512]{1,0:T(8,128)S(1)}, f32[96,512]{1,0:T(8,128)S(1)}, u32[]{:S(2)}, u32[]{:S(2)}) collective-permute-start(f32[96,512]{1,0:T(8,128)S(1)} %get-tuple-element.186.refs_2_), channel_id=1, source_target_pairs={{0,16},{1,9},{2,18},{3,11},{4,20},{5,13},{6,22},{7,15},{8,24},{9,1... | collective-permute-start | bytes 589832 | tf_op jit(solution)/shard_map/ppermute | solution.py:935
  130.6 8.4 %collective-permute-start.54 = (f32[48,512]{1,0:T(8,128)S(1)}, f32[48,512]{1,0:T(8,128)S(1)}, u32[]{:S(2)}, u32[]{:S(2)}) collective-permute-start(f32[48,512]{1,0:T(8,128)S(1)} %get-tuple-element.188.refs_2_), channel_id=1, source_target_pairs={{0,2},{1,3},{2,0},{3,1},{4,6},{5,7},{6,4},{7,5},{8,10},{9,11},{10,... | collective-permute-start | bytes 294920 | tf_op jit(solution)/shard_map/ppermute | solution.py:930
  132.0 9.6 %collective-permute-start.63 = (f32[48,512]{1,0:T(8,128)S(1)}, f32[48,512]{1,0:T(8,128)S(1)}, u32[]{:S(2)}, u32[]{:S(2)}) collective-permute-start(f32[48,512]{1,0:T(8,128)S(1)} %add.49.refs_2_.refs_0_), channel_id=1, source_target_pairs={{0,4},{1,5},{2,6},{3,7},{4,0},{5,1},{6,2},{7,3},{8,12},{9,13},{10,... | collective-permute-start | bytes 294920 | tf_op jit(solution)/shard_map/ppermute | solution.py:930
  136.4 7.8 %collective-permute-start.61 = (f32[64,512]{1,0:T(8,128)S(1)}, f32[64,512]{1,0:T(8,128)S(1)}, u32[]{:S(2)}, u32[]{:S(2)}) collective-permute-start(f32[64,512]{1,0:T(8,128)S(1)} %add.50.refs_2_.refs_0_), channel_id=1, source_target_pairs={{0,8},{1,17},{2,10},{3,19},{4,12},{5,21},{6,14},{7,23},{8,0},{9,25... | collective-permute-start | bytes 393224 | tf_op jit(solution)/shard_map/ppermute | solution.py:935
  138.8 8.2 %collective-permute-start.60 = (f32[160,512]{1,0:T(8,128)S(1)}, f32[160,512]{1,0:T(8,128)S(1)}, u32[]{:S(2)}, u32[]{:S(2)}) collective-permute-start(f32[160,512]{1,0:T(8,128)S(1)} %join.14.refs_2_.refs_0_), channel_id=1, source_target_pairs={{0,16},{1,9},{2,18},{3,11},{4,20},{5,13},{6,22},{7,15},{8,24},{9,1... | collective-permute-start | bytes 983048 | tf_op jit(solution)/shard_map/ppermute | solution.py:935
  139.0 4.9 %collective-permute-start.62 = (f32[48,512]{1,0:T(8,128)S(1)}, f32[48,512]{1,0:T(8,128)S(1)}, u32[]{:S(2)}, u32[]{:S(2)}) collective-permute-start(f32[48,512]{1,0:T(8,128)S(1)} %get-tuple-element.192.refs_2_), channel_id=1, source_target_pairs={{0,2},{1,3},{2,0},{3,1},{4,6},{5,7},{6,4},{7,5},{8,10},{9,11},{10,... | collective-permute-start | bytes 294920 | tf_op jit(solution)/shard_map/ppermute | solution.py:930
  139.1 10.5 %collective-permute-start.66 = (f32[48,512]{1,0:T(8,128)S(1)}, f32[48,512]{1,0:T(8,128)S(1)}, u32[]{:S(2)}, u32[]{:S(2)}) collective-permute-start(f32[48,512]{1,0:T(8,128)S(1)} %add.51.refs_2_.refs_0_), channel_id=1, source_target_pairs={{0,4},{1,5},{2,6},{3,7},{4,0},{5,1},{6,2},{7,3},{8,12},{9,13},{10,... | collective-permute-start | bytes 294920 | tf_op jit(solution)/shard_map/ppermute | solution.py:930
  141.6 6.8 %collective-permute-start.59 = (f32[64,128]{1,0:T(8,128)S(1)}, f32[64,128]{1,0:T(8,128)S(1)}, u32[]{:S(2)}, u32[]{:S(2)}) collective-permute-start(f32[64,128]{1,0:T(8,128)S(1)} %add.52.refs_2_.refs_0_), channel_id=1, source_target_pairs={{0,17},{1,16},{2,19},{3,18},{4,21},{5,20},{6,23},{7,22},{8,25},{9,... | collective-permute-start | bytes 98312 | tf_op jit(solution)/shard_map/ppermute | solution.py:930
  143.9 6.1 %collective-permute-start.65 = (f32[48,512]{1,0:T(8,128)S(1)}, f32[48,512]{1,0:T(8,128)S(1)}, u32[]{:S(2)}, u32[]{:S(2)}) collective-permute-start(f32[48,512]{1,0:T(8,128)S(1)} %add.53.refs_2_.refs_0_), channel_id=1, source_target_pairs={{0,2},{1,3},{2,0},{3,1},{4,6},{5,7},{6,4},{7,5},{8,10},{9,11},{10,... | collective-permute-start | bytes 294920 | tf_op jit(solution)/shard_map/ppermute | solution.py:930
  144.2 7.6 %collective-permute-start.68 = (f32[48,512]{1,0:T(8,128)S(1)}, f32[48,512]{1,0:T(8,128)S(1)}, u32[]{:S(2)}, u32[]{:S(2)}) collective-permute-start(f32[48,512]{1,0:T(8,128)S(1)} %add.54.refs_2_.refs_0_), channel_id=1, source_target_pairs={{0,4},{1,5},{2,6},{3,7},{4,0},{5,1},{6,2},{7,3},{8,12},{9,13},{10,... | collective-permute-start | bytes 294920 | tf_op jit(solution)/shard_map/ppermute | solution.py:930
  147.0 6.5 %collective-permute-start.71 = (f32[64,512]{1,0:T(8,128)S(1)}, f32[64,512]{1,0:T(8,128)S(1)}, u32[]{:S(2)}, u32[]{:S(2)}) collective-permute-start(f32[64,512]{1,0:T(8,128)S(1)} %add.55.refs_2_.refs_0_), channel_id=1, source_target_pairs={{0,16},{1,9},{2,18},{3,11},{4,20},{5,13},{6,22},{7,15},{8,24},{9,1... | collective-permute-start | bytes 393224 | tf_op jit(solution)/shard_map/ppermute | solution.py:935
  148.5 22.5 %collective-permute-start.73 = (f32[320,512]{1,0:T(8,128)S(1)}, f32[320,512]{1,0:T(8,128)S(1)}, u32[]{:S(2)}, u32[]{:S(2)}) collective-permute-start(f32[320,512]{1,0:T(8,128)S(1)} %join.15.refs_2_.refs_0_), channel_id=1, source_target_pairs={{0,8},{1,17},{2,10},{3,19},{4,12},{5,21},{6,14},{7,23},{8,0},{9,25... | collective-permute-start | bytes 1966088 | tf_op jit(solution)/shard_map/ppermute | solution.py:935
  149.6 11.5 %collective-permute-start.64 = (f32[64,128]{1,0:T(8,128)S(1)}, f32[64,128]{1,0:T(8,128)S(1)}, u32[]{:S(2)}, u32[]{:S(2)}) collective-permute-start(f32[64,128]{1,0:T(8,128)S(1)} %add.56.refs_2_.refs_0_), channel_id=1, source_target_pairs={{0,3},{1,2},{2,1},{3,0},{4,7},{5,6},{6,5},{7,4},{8,11},{9,10},{10,... | collective-permute-start | bytes 98312 | tf_op jit(solution)/shard_map/ppermute | solution.py:930
  150.0 5.1 %collective-permute-start.70 = (f32[48,512]{1,0:T(8,128)S(1)}, f32[48,512]{1,0:T(8,128)S(1)}, u32[]{:S(2)}, u32[]{:S(2)}) collective-permute-start(f32[48,512]{1,0:T(8,128)S(1)} %add.57.refs_2_.refs_0_), channel_id=1, source_target_pairs={{0,2},{1,3},{2,0},{3,1},{4,6},{5,7},{6,4},{7,5},{8,10},{9,11},{10,... | collective-permute-start | bytes 294920 | tf_op jit(solution)/shard_map/ppermute | solution.py:930
  151.8 9.2 %collective-permute-start.67 = (f32[96,512]{1,0:T(8,128)S(1)}, f32[96,512]{1,0:T(8,128)S(1)}, u32[]{:S(2)}, u32[]{:S(2)}) collective-permute-start(f32[96,512]{1,0:T(8,128)S(1)} %join.16.refs_2_.refs_0_), channel_id=1, source_target_pairs={{0,16},{1,9},{2,18},{3,11},{4,20},{5,13},{6,22},{7,15},{8,24},{9,1... | collective-permute-start | bytes 589832 | tf_op jit(solution)/shard_map/ppermute | solution.py:935
  153.5 4.6 %collective-permute-start.69 = (f32[48,512]{1,0:T(8,128)S(1)}, f32[48,512]{1,0:T(8,128)S(1)}, u32[]{:S(2)}, u32[]{:S(2)}) collective-permute-start(f32[48,512]{1,0:T(8,128)S(1)} %add.58.refs_2_.refs_0_), channel_id=1, source_target_pairs={{0,2},{1,3},{2,0},{3,1},{4,6},{5,7},{6,4},{7,5},{8,10},{9,11},{10,... | collective-permute-start | bytes 294920 | tf_op jit(solution)/shard_map/ppermute | solution.py:930
  155.1 11.6 %collective-permute-start.75 = (f32[64,512]{1,0:T(8,128)S(1)}, f32[64,512]{1,0:T(8,128)S(1)}, u32[]{:S(2)}, u32[]{:S(2)}) collective-permute-start(f32[64,512]{1,0:T(8,128)S(1)} %add.59.refs_2_.refs_0_), channel_id=1, source_target_pairs={{0,4},{1,5},{2,6},{3,7},{4,0},{5,1},{6,2},{7,3},{8,12},{9,13},{10,... | collective-permute-start | bytes 393224 | tf_op jit(solution)/shard_map/ppermute | solution.py:930
  158.1 8.5 %collective-permute-start.76 = (f32[96,512]{1,0:T(8,128)S(1)}, f32[96,512]{1,0:T(8,128)S(1)}, u32[]{:S(2)}, u32[]{:S(2)}) collective-permute-start(f32[96,512]{1,0:T(8,128)S(1)} %join.17.refs_2_.refs_0_), channel_id=1, source_target_pairs={{0,16},{1,9},{2,18},{3,11},{4,20},{5,13},{6,22},{7,15},{8,24},{9,1... | collective-permute-start | bytes 589832 | tf_op jit(solution)/shard_map/ppermute | solution.py:935
  161.0 9.9 %collective-permute-start.74 = (f32[96,512]{1,0:T(8,128)S(1)}, f32[96,512]{1,0:T(8,128)S(1)}, u32[]{:S(2)}, u32[]{:S(2)}) collective-permute-start(f32[96,512]{1,0:T(8,128)S(1)} %join.18.refs_2_.refs_0_), channel_id=1, source_target_pairs={{0,16},{1,9},{2,18},{3,11},{4,20},{5,13},{6,22},{7,15},{8,24},{9,1... | collective-permute-start | bytes 589832 | tf_op jit(solution)/shard_map/ppermute | solution.py:935
  161.1 14.8 %collective-permute-start.79 = (f32[192,512]{1,0:T(8,128)S(1)}, f32[192,512]{1,0:T(8,128)S(1)}, u32[]{:S(2)}, u32[]{:S(2)}) collective-permute-start(f32[192,512]{1,0:T(8,128)S(1)} %join.19.refs_2_.refs_0_), channel_id=1, source_target_pairs={{0,8},{1,17},{2,10},{3,19},{4,12},{5,21},{6,14},{7,23},{8,0},{9,25... | collective-permute-start | bytes 1179656 | tf_op jit(solution)/shard_map/ppermute | solution.py:935
  166.7 5.2 %collective-permute-start.72 = (f32[64,128]{1,0:T(8,128)S(1)}, f32[64,128]{1,0:T(8,128)S(1)}, u32[]{:S(2)}, u32[]{:S(2)}) collective-permute-start(f32[64,128]{1,0:T(8,128)S(1)} %add.60.refs_2_.refs_0_), channel_id=1, source_target_pairs={{0,5},{1,4},{2,7},{3,6},{4,1},{5,0},{6,3},{7,2},{8,13},{9,12},{10,... | collective-permute-start | bytes 98312 | tf_op jit(solution)/shard_map/ppermute | solution.py:930
  166.8 9.3 %collective-permute-start.78 = (f32[192,512]{1,0:T(8,128)S(1)}, f32[192,512]{1,0:T(8,128)S(1)}, u32[]{:S(2)}, u32[]{:S(2)}) collective-permute-start(f32[192,512]{1,0:T(8,128)S(1)} %join.20.refs_2_.refs_0_), channel_id=1, source_target_pairs={{0,8},{1,17},{2,10},{3,19},{4,12},{5,21},{6,14},{7,23},{8,0},{9,25... | collective-permute-start | bytes 1179656 | tf_op jit(solution)/shard_map/ppermute | solution.py:935
  170.9 7.4 %collective-permute-start.82 = (f32[128,512]{1,0:T(8,128)S(1)}, f32[128,512]{1,0:T(8,128)S(1)}, u32[]{:S(2)}, u32[]{:S(2)}) collective-permute-start(f32[128,512]{1,0:T(8,128)S(1)} %join.21.refs_2_.refs_0_), channel_id=1, source_target_pairs={{0,2},{1,3},{2,0},{3,1},{4,6},{5,7},{6,4},{7,5},{8,10},{9,11},{10,... | collective-permute-start | bytes 786440 | tf_op jit(solution)/shard_map/ppermute | solution.py:930
  171.0 9.7 %collective-permute-start.77 = (f32[192,512]{1,0:T(8,128)S(1)}, f32[192,512]{1,0:T(8,128)S(1)}, u32[]{:S(2)}, u32[]{:S(2)}) collective-permute-start(f32[192,512]{1,0:T(8,128)S(1)} %join.22.refs_2_.refs_0_), channel_id=1, source_target_pairs={{0,8},{1,17},{2,10},{3,19},{4,12},{5,21},{6,14},{7,23},{8,0},{9,25... | collective-permute-start | bytes 1179656 | tf_op jit(solution)/shard_map/ppermute | solution.py:935
  171.9 4.8 %collective-permute-start.81 = (f32[640,512]{1,0:T(8,128)S(1)}, f32[640,512]{1,0:T(8,128)S(1)}, u32[]{:S(2)}, u32[]{:S(2)}) collective-permute-start(f32[640,512]{1,0:T(8,128)S(1)} %join.23.refs_2_.refs_0_), channel_id=1, source_target_pairs={{0,1},{1,0},{2,3},{3,2},{4,5},{5,4},{6,7},{7,6},{8,9},{9,8},{10,11... | collective-permute-start | bytes 3932168 | tf_op jit(solution)/shard_map/ppermute | solution.py:930
  176.0 5.0 %collective-permute-start.84 = (f32[384,512]{1,0:T(8,128)S(1)}, f32[384,512]{1,0:T(8,128)S(1)}, u32[]{:S(2)}, u32[]{:S(2)}) collective-permute-start(f32[384,512]{1,0:T(8,128)S(1)} %join.24.refs_2_.refs_0_), channel_id=1, source_target_pairs={{0,1},{1,0},{2,3},{3,2},{4,5},{5,4},{6,7},{7,6},{8,9},{9,8},{10,11... | collective-permute-start | bytes 2359304 | tf_op jit(solution)/shard_map/ppermute | solution.py:930
  (39 other events, 202.7 us)

commit v5 on v4

--- a/solution.py
+++ b/solution.py
@@ -881,29 +881,31 @@
     return [(0, width, left), (width, width + width // 2, right)]
 
 
-def k_place(side, places, layer, count, own_ref, got_ref, *refs):
+def k_place(side, layer, groups, *refs):
     token_ref, sem_ref = refs[-2:]
-    outs = refs[-2 - count : -2]
+    outs = refs[-2 - sum(count for unused, count in groups) : -2]
     token_ref[...] = jnp.zeros(token_ref.shape, F32)
-    half = own_ref.shape[0]
     for mine in range(2):
         @pl.when(side() == mine)
         def _():
-            where = places(layer, *outs)
-            copy_all(
-                cut_to(layer, mine * half, own_ref, where) + cut_to(layer, (1 - mine) * half, got_ref, where), sem_ref
-            )
-
-
-def place(large, places, layer, shapes, into=None):
-    count = len(shapes)
-    args = [large.block, large.got] + list(into or [])
-    alias = {2 + k: k for k in range(count)} if into else {}
+            pairs, first = [], 0
+            for k, (places, count) in enumerate(groups):
+                where = places(layer, *outs[first : first + count])
+                first += count
+                for ref, at in zip(refs[2 * k : 2 * k + 2], (mine, 1 - mine)):
+                    pairs.extend(cut_to(layer, at * ref.shape[0], ref, where))
+            copy_all(pairs, sem_ref)
+
+
+def place(order, layer, items, into=()):
+    args = [array for large, unused, unused in items for array in (large.block, large.got)]
+    shapes = [shape for unused, unused, more in items for shape in more]
+    alias = {len(args) + k: k for k in range(len(into))}
     return list(call(
-        "place", functools.partial(k_place, large.side(), places, layer, count), shapes + [shaped((SUB, LANE))], args,
-        scratch=[pltpu.SemaphoreType.DMA((8,))], order=large.order, token=count, far=range(2, len(args)), alias=alias,
-        out_far=count,
-    ))[:count]
+        "place", functools.partial(k_place, items[0][0].side(), layer, [(places, len(more)) for unused, places, more in items]),
+        shapes + [shaped((SUB, LANE))], args + list(into), scratch=[pltpu.SemaphoreType.DMA((16,))], order=order,
+        token=len(shapes), far=range(len(args), len(args) + len(into)), alias=alias, out_far=len(shapes),
+    ))[: len(shapes)]
 
 
 BOTH = ("batch", "tm")
@@ -912,7 +914,7 @@
     ("AA",),
     ("B", "A", "e", "BA"),
     ("CECE",),
-    ("D", "ABSDECBSA", "DCBEADCSBD", "EASCBDECDB", "SCEDALBCAE", "CDBED"),
+    ("D", "ABSDECBSAD", "CSBEADCSBD", "EASCBDECDB", "LCEDABCAEC", "DBED"),
 )
 
 
@@ -1059,7 +1061,7 @@
 class Steps:
     def __init__(self, order):
         self.order = order
-        self.larges, self.other, self.into, self.shapes = {}, {}, {}, {}
+        self.larges, self.other, self.out, self.shapes, self.come = {}, {}, {}, {}, set()
 
     def add(self, name, block, line_first=False):
         self.larges[name] = Large(self.order, block, line_first)
@@ -1074,26 +1076,32 @@
                 self.put(item)
 
     def put(self, item):
-        large = self.larges[item]
-        while large.left():
-            large.send()
-        if item == "A":
-            w_out, c_out = place(large, map_places, 1, self.shapes["A"])
-            self.into.update(E=(w_out, False), C=(c_out, False))
-        elif item == "B":
-            self.into["D"] = (place(large, drive_places, 1, self.shapes["B"])[0], False)
-        else:
-            if item not in self.into:
-                self.put("B" if item == "D" else "A")
-            out, done = self.into[item]
-            if not done:
-                shape = shaped(out.shape)
-                out, = place(large, drive_places if item == "D" else map_places, 0, [shape], [out])
-                self.into[item] = (out, True)
+        group = [names for names in ("AB", "CE", "D") if item in names][0]
+        self.come.add(item)
+        if group in self.out or not self.come.issuperset(group):
+            return
+        for name in group:
+            while self.larges[name].left():
+                self.larges[name].send()
+        if group == "AB":
+            self.out[group] = place(self.order, 1, [
+                (self.larges["A"], map_places, self.shapes["A"]), (self.larges["B"], drive_places, self.shapes["B"]),
+            ])
+            return
+        if "AB" not in self.out:
+            self.put("A")
+            self.put("B")
+        w_out, c_out, b_out = self.out["AB"]
+        into = [b_out] if group == "D" else [c_out, w_out]
+        self.out[group] = place(self.order, 0, [
+            (self.larges[name], drive_places if name == "D" else map_places, [shaped(out.shape)])
+            for name, out in zip(group, into)
+        ], into)
 
     def placed(self, item):
-        self.put(item)
-        return self.into[item][0]
+        for name in "CED":
+            self.put(name)
+        return {"C": self.out["CE"][0], "E": self.out["CE"][1], "D": self.out["D"][0]}[item]
 
 
 def small_sum(order, block):

time: 185 us -> 185 us (level)
  waiting for transfers between devices: 60 us -> 62.6 us
    ppermute x18, starting transfers between devices: 20.2 us -> 18.2 us  [swap_by_core(): lax.ppermute(block, BOTH, [(i, i ^ (odd if i & 1 else even)) for i in ran...]
    pallas_call x91 -> x89, Pallas kernels: 43.6 us -> 42.7 us  [call(): pl.pallas_call(run, name=name, out_shape=outs, in_specs=specs, out_specs=...]
  transfers between devices with their start and end apart: 86 -> 86, of which waited for: 45 -> 48; matrix products, arithmetic and copies ran while one was open for 0% -> 0% of each run, Pallas kernels for 12% -> 11%
where the time goes in v5:
time: 185 us; the launch traced here: 184 us
  starting transfers between devices  75.6 us (41%)
  waiting for transfers between devices  62.6 us (34%)
  Pallas kernels  42.7 us (23%)
  local copies, waits for them, and re-layouts  1.94 us (1%)
    ppermute x68, starting transfers between devices, swap(): return lax.ppermute(block, BOTH, [(i, i ^ distance) for i in range(total)])  57.3 us
    ppermute x68, waiting for transfers between devices, swap(): return lax.ppermute(block, BOTH, [(i, i ^ distance) for i in range(total)])  43.3 us
    pallas_call x89, Pallas kernels, call(): pl.pallas_call(run, name=name, out_shape=outs, in_specs=specs, out_specs=...  42.7 us
    ppermute x18, waiting for transfers between devices, swap_by_core(): lax.ppermute(block, BOTH, [(i, i ^ (odd if i & 1 else even)) for i in ran...  19.3 us
    ppermute x18, starting transfers between devices, swap_by_core(): lax.ppermute(block, BOTH, [(i, i ^ (odd if i & 1 else even)) for i in ran...  18.2 us
  transfers between devices with their start and end apart: 86, of which 48 were waited for; matrix products, arithmetic and copies ran while one was open for 0% of the time, Pallas kernels for 11%

profile of v5, /device:TPU:0, one launch (start us, length us, event | category | flops | bytes accessed | tf_op | source)
XLA Modules:
  0.0 184.4 jit_solution(14683139765804807015)
XLA Ops:
  0.7 1.2 copy-done.3
  2.6 1.9 %enter.1 = (f32[1024,512]{1,0:T(8,128)S(1)}, f32[24,128]{1,0:T(8,128)S(1)}, s32[8,512]{1,0:T(8,128)S(1)}) custom-call(s32[4]{0:T(128)S(1)} %copy-done.14, bf16[4,256,512]{2,1,0:T(8,128)(2,1)S(1)} %copy-done.3), custom_call_target="tpu_custom_call" | custom-call | flops 5000000000 | bytes 1 | tf_op jit(solution)/shard_map/enter/pallas_call | solution.py:46
  5.0 1.2 prepare.1
  6.3 3.6 %collective-permute-start.1 = (f32[24,128]{1,0:T(8,128)S(1)}, f32[24,128]{1,0:T(8,128)S(1)}, u32[]{:S(2)}, u32[]{:S(2)}) collective-permute-start(f32[24,128]{1,0:T(8,128)S(1)} %add.31.refs_0_), channel_id=1, source_target_pairs={{0,25},{1,24},{2,27},{3,26},{4,29},{5,28},{6,31},{7,30},{8,17},{9,... | collective-permute-start | bytes 36872 | tf_op jit(solution)/shard_map/ppermute | solution.py:932
  11.3 1.7 collective-permute-done.3.refs_2_
  13.2 3.7 %collective-permute-start.4 = (f32[24,128]{1,0:T(8,128)S(1)}, f32[24,128]{1,0:T(8,128)S(1)}, u32[]{:S(2)}, u32[]{:S(2)}) collective-permute-start(f32[24,128]{1,0:T(8,128)S(1)} %add.33.refs_0_), channel_id=1, source_target_pairs={{0,7},{1,6},{2,5},{3,4},{4,3},{5,2},{6,1},{7,0},{8,15},{9,14},{10,... | collective-permute-start | bytes 36872 | tf_op jit(solution)/shard_map/ppermute | solution.py:932
  18.3 1.7 collective-permute-done.6.refs_2_
  21.0 1.5 drive0.1
  23.7 1.6 collective-permute-start.10
  25.3 1.5 collective-permute-start.9
  27.7 1.3 collective-permute-done.10.src_ref
  29.0 1.4 collective-permute-done.9.refs_2_
  30.6 3.7 %finish0.1 = (f32[1032,768]{1,0:T(8,128)S(1)}, bf16[1024,512]{1,0:T(8,128)(2,1)S(1)}, f32[1024,512]{1,0:T(8,128)S(1)}, f32[1024,512]{1,0:T(8,128)S(1)}, f32[1024...) custom-call(f32[8,768]{1,0:T(8,128)S(1)} %combine.4.refs_0_, ...), custom_call_target="tpu_custom_call" | custom-call | flops 5000000000 | bytes 1 | tf_op jit(solution)/shard_map/finish0/pallas_call | solution.py:46
  34.5 1.4 keep.1
  35.9 1.6 collective-permute-start.12
  37.7 1.5 collective-permute-start.13
  40.8 1.4 collective-permute-start.15
  42.2 2.6 %collective-permute-start.16 = (f32[16,128]{1,0:T(8,128)S(1)}, f32[16,128]{1,0:T(8,128)S(1)}, u32[]{:S(2)}, u32[]{:S(2)}) collective-permute-start(f32[16,128]{1,0:T(8,128)S(1)} %add.38.refs_0_), channel_id=1, source_target_pairs={{0,5},{1,4},{2,7},{3,6},{4,1},{5,0},{6,3},{7,2},{8,13},{9,12},{10,... | collective-permute-start | bytes 24584 | tf_op jit(solution)/shard_map/ppermute | solution.py:932
  46.3 1.6 drive1.1
  49.2 2.1 %collective-permute-start.21 = (f32[8,768]{1,0:T(8,128)S(1)}, f32[8,768]{1,0:T(8,128)S(1)}, u32[]{:S(2)}, u32[]{:S(2)}) collective-permute-start(f32[8,768]{1,0:T(8,128)S(1)} %combine.5.refs_0_), channel_id=1, source_target_pairs={{0,7},{1,6},{2,5},{3,4},{4,3},{5,2},{6,1},{7,0},{8,15},{9,14},{10,... | collective-permute-start | bytes 73736 | tf_op jit(solution)/shard_map/ppermute | solution.py:932
  55.8 7.0 %middle.1 = (f32[4,1024,128]{2,1,0:T(8,128)S(1)}, f32[1032,768]{1,0:T(8,128)S(1)}, bf16[1024,512]{1,0:T(8,128)(2,1)S(1)}, f32[1024,768]{1,0:T(8,128)S(1)}, f32[1...) custom-call(f32[8,768]{1,0:T(8,128)S(1)} %combine.5.refs_0_, ...), custom_call_target="tpu_custom_call" | custom-call | flops 5000000000 | bytes 1 | tf_op jit(solution)/shard_map/middle/pallas_call | solution.py:46
  64.8 1.8 collective-permute-start.25
  66.6 2.1 %collective-permute-start.23 = (f32[8,768]{1,0:T(8,128)S(1)}, f32[8,768]{1,0:T(8,128)S(1)}, u32[]{:S(2)}, u32[]{:S(2)}) collective-permute-start(f32[8,768]{1,0:T(8,128)S(1)} %combine.6.refs_1_.refs_0_), channel_id=1, source_target_pairs={{0,3},{1,2},{2,1},{3,0},{4,7},{5,6},{6,5},{7,4},{8,11},{9,10},{10,... | collective-permute-start | bytes 73736 | tf_op jit(solution)/shard_map/ppermute | solution.py:932
  70.0 1.6 collective-permute-start.29
  71.7 3.1 %adjoint1.1 = (f32[1024,512]{1,0:T(8,128)S(1)}, f32[768,512]{1,0:T(8,128)S(1)}, f32[8,128]{1,0:T(8,128)S(1)}, f32[16,128]{1,0:T(8,128)S(1)}) custom-call(f32[8,768]{1,0:T(8,128)S(1)} %combine.6.refs_1_.refs_0_, f32[8,768]{1,0:T(8,128)S(1)} %collective-permute-done.23.refs_1_, f32[8,768]{1,0:T(8,128)S(1)} %collective-permute-done.24.refs_2_, ...), custom_call_target="tpu_custom_call" | custom-call | flops 5000000000 | bytes 1 | tf_op jit(solution)/shard_map/adjoint1/pallas_call | solution.py:46
  76.0 1.2 collective-permute-start.31
  79.0 1.8 collective-permute-done.29.refs_1_
  80.9 1.2 collective-permute-done.28.refs_1_
  83.0 1.5 collective-permute-start.33
  84.6 1.5 collective-permute-start.32
  87.1 1.5 emit.1
  89.6 3.5 %collective-permute-done.35.refs_1_ = f32[160,512]{1,0:T(8,128)S(1)} collective-permute-done((f32[160,512]{1,0:T(8,128)S(1)}, f32[160,512]{1,0:T(8,128)S(1)}, u32[]{:S(2)}, u32[]{:S(2)}) %collective-permute-start.35) | collective-permute-done | bytes 327712 | tf_op jit(solution)/shard_map/ppermute | solution.py:937
  93.2 4.2 %lower.1 = (f32[1024,512]{1,0:T(8,128)S(1)}, bf16[1024,512]{1,0:T(8,128)(2,1)S(1)}, f32[1024,768]{1,0:T(8,128)S(1)}, f32[512,512]{1,0:T(8,128)S(1)}, f32[768,512...) custom-call(f32[16,128]{1,0:T(8,128)S(1)} %add.45.refs_2_.refs_0_, ...), custom_call_target="tpu_custom_call" | custom-call | flops 5000000000 | bytes 1 | tf_op jit(solution)/shard_map/lower/pallas_call | solution.py:46
  97.5 1.2 collective-permute-done.37.refs_1_.refs_5_
  99.5 1.9 %collective-permute-start.40 = (f32[8,768]{1,0:T(8,128)S(1)}, f32[8,768]{1,0:T(8,128)S(1)}, u32[]{:S(2)}, u32[]{:S(2)}) collective-permute-start(f32[8,768]{1,0:T(8,128)S(1)} %combine.7.refs_1_.refs_0_), channel_id=1, source_target_pairs={{0,7},{1,6},{2,5},{3,4},{4,3},{5,2},{6,1},{7,0},{8,15},{9,14},{10,... | collective-permute-start | bytes 73736 | tf_op jit(solution)/shard_map/ppermute | solution.py:932
  102.3 2.2 %collective-permute-done.40.src_ref = f32[8,768]{1,0:T(8,128)S(1)} collective-permute-done((f32[8,768]{1,0:T(8,128)S(1)}, f32[8,768]{1,0:T(8,128)S(1)}, u32[]{:S(2)}, u32[]{:S(2)}) %collective-permute-start.40) | collective-permute-done | bytes 24608 | tf_op jit(solution)/shard_map/ppermute | solution.py:932
  104.5 2.4 %collective-permute-start.38 = (f32[8,768]{1,0:T(8,128)S(1)}, f32[8,768]{1,0:T(8,128)S(1)}, u32[]{:S(2)}, u32[]{:S(2)}) collective-permute-start(f32[8,768]{1,0:T(8,128)S(1)} %combine.7.refs_1_.refs_0_), channel_id=1, source_target_pairs={{0,3},{1,2},{2,1},{3,0},{4,7},{5,6},{6,5},{7,4},{8,11},{9,10},{10,... | collective-permute-start | bytes 73736 | tf_op jit(solution)/shard_map/ppermute | solution.py:932
  109.2 2.0 %adjoint0.1 = (bf16[1024,768]{1,0:T(8,128)(2,1)S(1)}, f32[768,512]{1,0:T(8,128)S(1)}, f32[8,128]{1,0:T(8,128)S(1)}) custom-call(f32[8,768]{1,0:T(8,128)S(1)} %combine.7.refs_1_.refs_0_, f32[8,768]{1,0:T(8,128)S(1)} %collective-permute-done.38.refs_1_, f32[8,768]{1,0:T(8,128)S(1)} %collective-permute-done.39.refs_2_, f32[8,768]{1,0:T(8,128)S(1)} %copy.41.refs_3_, ...), custom_call_target="tpu_custom_call" | custom-call | flops 5000000000 | bytes 1 | tf_op jit(solution)/shard_map/adjoint0/pallas_call | solution.py:46
  111.4 1.2 back.1
  113.2 2.4 %collective-permute-start.53 = (f32[80,512]{1,0:T(8,128)S(1)}, f32[80,512]{1,0:T(8,128)S(1)}, u32[]{:S(2)}, u32[]{:S(2)}) collective-permute-start(f32[80,512]{1,0:T(8,128)S(1)} %add.46.refs_2_.refs_0_), channel_id=1, source_target_pairs={{0,4},{1,5},{2,6},{3,7},{4,0},{5,1},{6,2},{7,3},{8,12},{9,13},{10,... | collective-permute-start | bytes 491528 | tf_op jit(solution)/shard_map/ppermute | solution.py:932
  116.6 1.8 collective-permute-done.48.refs_1_
  118.4 1.3 collective-permute-start.52
  119.9 3.3 %collective-permute-done.46.refs_1_ = f32[96,512]{1,0:T(8,128)S(1)} collective-permute-done((f32[96,512]{1,0:T(8,128)S(1)}, f32[96,512]{1,0:T(8,128)S(1)}, u32[]{:S(2)}, u32[]{:S(2)}) %collective-permute-start.46) | collective-permute-done | bytes 196640 | tf_op jit(solution)/shard_map/ppermute | solution.py:937
  124.0 1.3 collective-permute-start.59
  125.3 2.2 %collective-permute-done.53.refs_1_ = f32[80,512]{1,0:T(8,128)S(1)} collective-permute-done((f32[80,512]{1,0:T(8,128)S(1)}, f32[80,512]{1,0:T(8,128)S(1)}, u32[]{:S(2)}, u32[]{:S(2)}) %collective-permute-start.53) | collective-permute-done | bytes 163872 | tf_op jit(solution)/shard_map/ppermute | solution.py:932
  132.1 1.6 collective-permute-start.64
  133.7 1.6 collective-permute-done.57.refs_1_
  135.3 1.4 collective-permute-start.62
  138.0 2.2 %collective-permute-start.67 = (f32[48,512]{1,0:T(8,128)S(1)}, f32[48,512]{1,0:T(8,128)S(1)}, u32[]{:S(2)}, u32[]{:S(2)}) collective-permute-start(f32[48,512]{1,0:T(8,128)S(1)} %add.52.refs_2_.refs_0_), channel_id=1, source_target_pairs={{0,4},{1,5},{2,6},{3,7},{4,0},{5,1},{6,2},{7,3},{8,12},{9,13},{10,... | collective-permute-start | bytes 294920 | tf_op jit(solution)/shard_map/ppermute | solution.py:932
  140.8 3.9 %collective-permute-done.63.refs_1_ = f32[48,512]{1,0:T(8,128)S(1)} collective-permute-done((f32[48,512]{1,0:T(8,128)S(1)}, f32[48,512]{1,0:T(8,128)S(1)}, u32[]{:S(2)}, u32[]{:S(2)}) %collective-permute-start.63) | collective-permute-done | bytes 98336 | tf_op jit(solution)/shard_map/ppermute | solution.py:932
  144.7 2.2 %collective-permute-start.69 = (f32[48,512]{1,0:T(8,128)S(1)}, f32[48,512]{1,0:T(8,128)S(1)}, u32[]{:S(2)}, u32[]{:S(2)}) collective-permute-start(f32[48,512]{1,0:T(8,128)S(1)} %add.55.refs_2_.refs_0_), channel_id=1, source_target_pairs={{0,4},{1,5},{2,6},{3,7},{4,0},{5,1},{6,2},{7,3},{8,12},{9,13},{10,... | collective-permute-start | bytes 294920 | tf_op jit(solution)/shard_map/ppermute | solution.py:932
  148.4 1.6 collective-permute-start.80
  150.6 1.9 %collective-permute-done.69.refs_1_ = f32[48,512]{1,0:T(8,128)S(1)} collective-permute-done((f32[48,512]{1,0:T(8,128)S(1)}, f32[48,512]{1,0:T(8,128)S(1)}, u32[]{:S(2)}, u32[]{:S(2)}) %collective-permute-start.69) | collective-permute-done | bytes 98336 | tf_op jit(solution)/shard_map/ppermute | solution.py:932
  153.6 2.4 %collective-permute-done.71.refs_1_ = f32[48,512]{1,0:T(8,128)S(1)} collective-permute-done((f32[48,512]{1,0:T(8,128)S(1)}, f32[48,512]{1,0:T(8,128)S(1)}, u32[]{:S(2)}, u32[]{:S(2)}) %collective-permute-start.71) | collective-permute-done | bytes 98336 | tf_op jit(solution)/shard_map/ppermute | solution.py:932
  156.5 1.6 collective-permute-done.70.refs_1_
  160.4 1.3 collective-permute-start.79
  161.7 3.1 %leave.1 = (f32[4,256,512]{2,1,0:T(8,128)}, f32[2,512]{1,0:T(2,128)}, f32[2,512]{1,0:T(2,128)}, f32[2,512]{1,0:T(2,128)}, f32[2,512]{1,0:T(2,128)}, /*index=5*/f...) custom-call(f32[64,128]{1,0:T(8,128)S(1)} %add.61.refs_0_.refs_12_, ...), custom_call_target="tpu_custom_call" | custom-call | flops 5000000000 | bytes 1 | tf_op jit(solution)/shard_map/leave/pallas_call | solution.py:46
  166.8 1.9 %collective-permute-done.73.refs_1_ = f32[96,512]{1,0:T(8,128)S(1)} collective-permute-done((f32[96,512]{1,0:T(8,128)S(1)}, f32[96,512]{1,0:T(8,128)S(1)}, u32[]{:S(2)}, u32[]{:S(2)}) %collective-permute-start.73) | collective-permute-done | bytes 196640 | tf_op jit(solution)/shard_map/ppermute | solution.py:937
  168.8 1.3 collective-permute-start.76
  171.0 2.9 %collective-permute-done.78.refs_1_ = f32[192,512]{1,0:T(8,128)S(1)} collective-permute-done((f32[192,512]{1,0:T(8,128)S(1)}, f32[192,512]{1,0:T(8,128)S(1)}, u32[]{:S(2)}, u32[]{:S(2)}) %collective-permute-start.78) | collective-permute-done | bytes 393248 | tf_op jit(solution)/shard_map/ppermute | solution.py:937
  174.7 3.3 %collective-permute-done.76.refs_1_ = f32[192,512]{1,0:T(8,128)S(1)} collective-permute-done((f32[192,512]{1,0:T(8,128)S(1)}, f32[192,512]{1,0:T(8,128)S(1)}, u32[]{:S(2)}, u32[]{:S(2)}) %collective-permute-start.76) | collective-permute-done | bytes 393248 | tf_op jit(solution)/shard_map/ppermute | solution.py:937
  178.5 2.1 %place.3 = (f32[2,512,512]{2,1,0:T(8,128)}, f32[2,768,512]{2,1,0:T(8,128)}, f32[2,512,768]{2,1,0:T(8,128)}, f32[8,128]{1,0:T(8,128)S(1)}) custom-call(f32[640,512]{1,0:T(8,128)S(1)} %join.23.refs_2_.refs_0_, f32[640,512]{1,0:T(8,128)S(1)} %collective-permute-done.82.refs_1_, f32[384,512]{1,0:T(8,128)S(1)} %join.24.refs_2_, ...), custom_call_target="tpu_custom_call" | custom-call | flops 5000000000 | bytes 1 | tf_op jit(solution)/shard_map/place/pallas_call | solution.py:46
  180.7 1.6 place.4
  182.3 1.9 %place.5 = (f32[2,512,768]{2,1,0:T(8,128)}, f32[8,128]{1,0:T(8,128)}) custom-call(f32[384,512]{1,0:T(8,128)S(1)} %join.27.refs_4_.refs_0_, f32[384,512]{1,0:T(8,128)S(1)} %collective-permute-done.81.refs_1_, f32[2,512,768]{2,1,0:T(8,128)} %get-tuple-element.199.refs_2_, f32[8,128]{1,0:T(8,128)S(1)} %get-tuple-element.203.refs_3_), custom_call_target="tpu_custom_call", output_to_operand_aliasing={{0}: (2, {})} | custom-call | flops 5000000000 | bytes 1 | tf_op jit(solution)/shard_map/place/pallas_call | solution.py:46
  (231 shorter events, 49.4 us)
Async XLA Ops:
  6.3 5.0 %collective-permute-start.1 = (f32[24,128]{1,0:T(8,128)S(1)}, f32[24,128]{1,0:T(8,128)S(1)}, u32[]{:S(2)}, u32[]{:S(2)}) collective-permute-start(f32[24,128]{1,0:T(8,128)S(1)} %add.31.refs_0_), channel_id=1, source_target_pairs={{0,25},{1,24},{2,27},{3,26},{4,29},{5,28},{6,31},{7,30},{8,17},{9,... | collective-permute-start | bytes 36872 | tf_op jit(solution)/shard_map/ppermute | solution.py:932
  13.2 5.1 %collective-permute-start.4 = (f32[24,128]{1,0:T(8,128)S(1)}, f32[24,128]{1,0:T(8,128)S(1)}, u32[]{:S(2)}, u32[]{:S(2)}) collective-permute-start(f32[24,128]{1,0:T(8,128)S(1)} %add.33.refs_0_), channel_id=1, source_target_pairs={{0,7},{1,6},{2,5},{3,4},{4,3},{5,2},{6,1},{7,0},{8,15},{9,14},{10,... | collective-permute-start | bytes 36872 | tf_op jit(solution)/shard_map/ppermute | solution.py:932
  23.7 5.2 %collective-permute-start.10 = (f32[8,768]{1,0:T(8,128)S(1)}, f32[8,768]{1,0:T(8,128)S(1)}, u32[]{:S(2)}, u32[]{:S(2)}) collective-permute-start(f32[8,768]{1,0:T(8,128)S(1)} %combine.4.refs_0_), channel_id=1, source_target_pairs={{0,7},{1,6},{2,5},{3,4},{4,3},{5,2},{6,1},{7,0},{8,15},{9,14},{10,... | collective-permute-start | bytes 73736 | tf_op jit(solution)/shard_map/ppermute | solution.py:932
  25.3 5.1 %collective-permute-start.9 = (f32[8,768]{1,0:T(8,128)S(1)}, f32[8,768]{1,0:T(8,128)S(1)}, u32[]{:S(2)}, u32[]{:S(2)}) collective-permute-start(f32[8,768]{1,0:T(8,128)S(1)} %combine.4.refs_0_), channel_id=1, source_target_pairs={{0,5},{1,4},{2,7},{3,6},{4,1},{5,0},{6,3},{7,2},{8,13},{9,12},{10,... | collective-permute-start | bytes 73736 | tf_op jit(solution)/shard_map/ppermute | solution.py:932
  40.8 4.9 %collective-permute-start.15 = (f32[16,128]{1,0:T(8,128)S(1)}, f32[16,128]{1,0:T(8,128)S(1)}, u32[]{:S(2)}, u32[]{:S(2)}) collective-permute-start(f32[16,128]{1,0:T(8,128)S(1)} %add.38.refs_0_), channel_id=1, source_target_pairs={{0,7},{1,6},{2,5},{3,4},{4,3},{5,2},{6,1},{7,0},{8,15},{9,14},{10,... | collective-permute-start | bytes 24584 | tf_op jit(solution)/shard_map/ppermute | solution.py:932
  49.2 5.2 %collective-permute-start.21 = (f32[8,768]{1,0:T(8,128)S(1)}, f32[8,768]{1,0:T(8,128)S(1)}, u32[]{:S(2)}, u32[]{:S(2)}) collective-permute-start(f32[8,768]{1,0:T(8,128)S(1)} %combine.5.refs_0_), channel_id=1, source_target_pairs={{0,7},{1,6},{2,5},{3,4},{4,3},{5,2},{6,1},{7,0},{8,15},{9,14},{10,... | collective-permute-start | bytes 73736 | tf_op jit(solution)/shard_map/ppermute | solution.py:932
  64.4 5.5 %collective-permute-start.26 = (f32[640,512]{1,0:T(8,128)S(1)}, f32[640,512]{1,0:T(8,128)S(1)}, u32[]{:S(2)}, u32[]{:S(2)}) collective-permute-start(f32[640,512]{1,0:T(8,128)S(1)} %split.5.refs_2_), channel_id=1, source_target_pairs={{0,1},{1,0},{2,3},{3,2},{4,5},{5,4},{6,7},{7,6},{8,9},{9,8},{10,11... | collective-permute-start | bytes 3932168 | tf_op jit(solution)/shard_map/ppermute | solution.py:932
  64.8 5.0 %collective-permute-start.25 = (f32[8,768]{1,0:T(8,128)S(1)}, f32[8,768]{1,0:T(8,128)S(1)}, u32[]{:S(2)}, u32[]{:S(2)}) collective-permute-start(f32[8,768]{1,0:T(8,128)S(1)} %combine.6.refs_1_.refs_0_), channel_id=1, source_target_pairs={{0,7},{1,6},{2,5},{3,4},{4,3},{5,2},{6,1},{7,0},{8,15},{9,14},{10,... | collective-permute-start | bytes 73736 | tf_op jit(solution)/shard_map/ppermute | solution.py:932
  66.6 5.1 %collective-permute-start.24 = (f32[8,768]{1,0:T(8,128)S(1)}, f32[8,768]{1,0:T(8,128)S(1)}, u32[]{:S(2)}, u32[]{:S(2)}) collective-permute-start(f32[8,768]{1,0:T(8,128)S(1)} %combine.6.refs_1_.refs_0_), channel_id=1, source_target_pairs={{0,5},{1,4},{2,7},{3,6},{4,1},{5,0},{6,3},{7,2},{8,13},{9,12},{10,... | collective-permute-start | bytes 73736 | tf_op jit(solution)/shard_map/ppermute | solution.py:932
  66.6 5.1 %collective-permute-start.23 = (f32[8,768]{1,0:T(8,128)S(1)}, f32[8,768]{1,0:T(8,128)S(1)}, u32[]{:S(2)}, u32[]{:S(2)}) collective-permute-start(f32[8,768]{1,0:T(8,128)S(1)} %combine.6.refs_1_.refs_0_), channel_id=1, source_target_pairs={{0,3},{1,2},{2,1},{3,0},{4,7},{5,6},{6,5},{7,4},{8,11},{9,10},{10,... | collective-permute-start | bytes 73736 | tf_op jit(solution)/shard_map/ppermute | solution.py:932
  70.0 10.7 %collective-permute-start.29 = (f32[320,512]{1,0:T(8,128)S(1)}, f32[320,512]{1,0:T(8,128)S(1)}, u32[]{:S(2)}, u32[]{:S(2)}) collective-permute-start(f32[320,512]{1,0:T(8,128)S(1)} %get-tuple-element.141.refs_20_), channel_id=1, source_target_pairs={{0,8},{1,17},{2,10},{3,19},{4,12},{5,21},{6,14},{7,23},{8,0},{9,25... | collective-permute-start | bytes 1966088 | tf_op jit(solution)/shard_map/ppermute | solution.py:937
  75.0 14.5 %collective-permute-start.36 = (f32[384,512]{1,0:T(8,128)S(1)}, f32[384,512]{1,0:T(8,128)S(1)}, u32[]{:S(2)}, u32[]{:S(2)}) collective-permute-start(f32[384,512]{1,0:T(8,128)S(1)} %split.6.refs_2_), channel_id=1, source_target_pairs={{0,1},{1,0},{2,3},{3,2},{4,5},{5,4},{6,7},{7,6},{8,9},{9,8},{10,11... | collective-permute-start | bytes 2359304 | tf_op jit(solution)/shard_map/ppermute | solution.py:932
  76.0 6.1 %collective-permute-start.31 = (f32[16,128]{1,0:T(8,128)S(1)}, f32[16,128]{1,0:T(8,128)S(1)}, u32[]{:S(2)}, u32[]{:S(2)}) collective-permute-start(f32[16,128]{1,0:T(8,128)S(1)} %add.41.refs_2_.refs_0_), channel_id=1, source_target_pairs={{0,9},{1,8},{2,11},{3,10},{4,13},{5,12},{6,15},{7,14},{8,1},{9,0},... | collective-permute-start | bytes 24584 | tf_op jit(solution)/shard_map/ppermute | solution.py:932
  77.2 4.9 %collective-permute-start.30 = (f32[16,128]{1,0:T(8,128)S(1)}, f32[16,128]{1,0:T(8,128)S(1)}, u32[]{:S(2)}, u32[]{:S(2)}) collective-permute-start(f32[16,128]{1,0:T(8,128)S(1)} %add.41.refs_2_.refs_0_), channel_id=1, source_target_pairs={{0,17},{1,16},{2,19},{3,18},{4,21},{5,20},{6,23},{7,22},{8,25},{9,... | collective-permute-start | bytes 24584 | tf_op jit(solution)/shard_map/ppermute | solution.py:932
  82.1 7.3 %collective-permute-start.34 = (f32[16,128]{1,0:T(8,128)S(1)}, f32[16,128]{1,0:T(8,128)S(1)}, u32[]{:S(2)}, u32[]{:S(2)}) collective-permute-start(f32[16,128]{1,0:T(8,128)S(1)} %add.43.refs_1_.refs_0_), channel_id=1, source_target_pairs={{0,3},{1,2},{2,1},{3,0},{4,7},{5,6},{6,5},{7,4},{8,11},{9,10},{10,... | collective-permute-start | bytes 24584 | tf_op jit(solution)/shard_map/ppermute | solution.py:932
  83.0 6.4 %collective-permute-start.33 = (f32[16,128]{1,0:T(8,128)S(1)}, f32[16,128]{1,0:T(8,128)S(1)}, u32[]{:S(2)}, u32[]{:S(2)}) collective-permute-start(f32[16,128]{1,0:T(8,128)S(1)} %add.43.refs_1_.refs_0_), channel_id=1, source_target_pairs={{0,5},{1,4},{2,7},{3,6},{4,1},{5,0},{6,3},{7,2},{8,13},{9,12},{10,... | collective-permute-start | bytes 24584 | tf_op jit(solution)/shard_map/ppermute | solution.py:932
  84.6 4.9 %collective-permute-start.32 = (f32[16,128]{1,0:T(8,128)S(1)}, f32[16,128]{1,0:T(8,128)S(1)}, u32[]{:S(2)}, u32[]{:S(2)}) collective-permute-start(f32[16,128]{1,0:T(8,128)S(1)} %add.43.refs_1_.refs_0_), channel_id=1, source_target_pairs={{0,7},{1,6},{2,5},{3,4},{4,3},{5,2},{6,1},{7,0},{8,15},{9,14},{10,... | collective-permute-start | bytes 24584 | tf_op jit(solution)/shard_map/ppermute | solution.py:932
  86.1 7.1 %collective-permute-start.35 = (f32[160,512]{1,0:T(8,128)S(1)}, f32[160,512]{1,0:T(8,128)S(1)}, u32[]{:S(2)}, u32[]{:S(2)}) collective-permute-start(f32[160,512]{1,0:T(8,128)S(1)} %get-tuple-element.145.refs_2_), channel_id=1, source_target_pairs={{0,16},{1,9},{2,18},{3,11},{4,20},{5,13},{6,22},{7,15},{8,24},{9,1... | collective-permute-start | bytes 983048 | tf_op jit(solution)/shard_map/ppermute | solution.py:937
  98.8 5.7 %collective-permute-start.42 = (f32[384,512]{1,0:T(8,128)S(1)}, f32[384,512]{1,0:T(8,128)S(1)}, u32[]{:S(2)}, u32[]{:S(2)}) collective-permute-start(f32[384,512]{1,0:T(8,128)S(1)} %split.7.refs_1_), channel_id=1, source_target_pairs={{0,1},{1,0},{2,3},{3,2},{4,5},{5,4},{6,7},{7,6},{8,9},{9,8},{10,11... | collective-permute-start | bytes 2359304 | tf_op jit(solution)/shard_map/ppermute | solution.py:932
  99.1 7.9 %collective-permute-start.41 = (f32[256,512]{1,0:T(8,128)S(1)}, f32[256,512]{1,0:T(8,128)S(1)}, u32[]{:S(2)}, u32[]{:S(2)}) collective-permute-start(f32[256,512]{1,0:T(8,128)S(1)} %split.8.refs_2_), channel_id=1, source_target_pairs={{0,1},{1,0},{2,3},{3,2},{4,5},{5,4},{6,7},{7,6},{8,9},{9,8},{10,11... | collective-permute-start | bytes 1572872 | tf_op jit(solution)/shard_map/ppermute | solution.py:932
  99.5 5.0 %collective-permute-start.40 = (f32[8,768]{1,0:T(8,128)S(1)}, f32[8,768]{1,0:T(8,128)S(1)}, u32[]{:S(2)}, u32[]{:S(2)}) collective-permute-start(f32[8,768]{1,0:T(8,128)S(1)} %combine.7.refs_1_.refs_0_), channel_id=1, source_target_pairs={{0,7},{1,6},{2,5},{3,4},{4,3},{5,2},{6,1},{7,0},{8,15},{9,14},{10,... | collective-permute-start | bytes 73736 | tf_op jit(solution)/shard_map/ppermute | solution.py:932
  101.3 11.8 %collective-permute-start.44 = (f32[192,512]{1,0:T(8,128)S(1)}, f32[192,512]{1,0:T(8,128)S(1)}, u32[]{:S(2)}, u32[]{:S(2)}) collective-permute-start(f32[192,512]{1,0:T(8,128)S(1)} %get-tuple-element.155.refs_2_), channel_id=1, source_target_pairs={{0,8},{1,17},{2,10},{3,19},{4,12},{5,21},{6,14},{7,23},{8,0},{9,25... | collective-permute-start | bytes 1179656 | tf_op jit(solution)/shard_map/ppermute | solution.py:937
  102.3 10.4 %collective-permute-start.45 = (f32[80,512]{1,0:T(8,128)S(1)}, f32[80,512]{1,0:T(8,128)S(1)}, u32[]{:S(2)}, u32[]{:S(2)}) collective-permute-start(f32[80,512]{1,0:T(8,128)S(1)} %get-tuple-element.156.refs_18_), channel_id=1, source_target_pairs={{0,2},{1,3},{2,0},{3,1},{4,6},{5,7},{6,4},{7,5},{8,10},{9,11},{10,... | collective-permute-start | bytes 491528 | tf_op jit(solution)/shard_map/ppermute | solution.py:932
  104.5 4.3 %collective-permute-start.39 = (f32[8,768]{1,0:T(8,128)S(1)}, f32[8,768]{1,0:T(8,128)S(1)}, u32[]{:S(2)}, u32[]{:S(2)}) collective-permute-start(f32[8,768]{1,0:T(8,128)S(1)} %combine.7.refs_1_.refs_0_), channel_id=1, source_target_pairs={{0,5},{1,4},{2,7},{3,6},{4,1},{5,0},{6,3},{7,2},{8,13},{9,12},{10,... | collective-permute-start | bytes 73736 | tf_op jit(solution)/shard_map/ppermute | solution.py:932
  104.5 4.6 %collective-permute-start.38 = (f32[8,768]{1,0:T(8,128)S(1)}, f32[8,768]{1,0:T(8,128)S(1)}, u32[]{:S(2)}, u32[]{:S(2)}) collective-permute-start(f32[8,768]{1,0:T(8,128)S(1)} %combine.7.refs_1_.refs_0_), channel_id=1, source_target_pairs={{0,3},{1,2},{2,1},{3,0},{4,7},{5,6},{6,5},{7,4},{8,11},{9,10},{10,... | collective-permute-start | bytes 73736 | tf_op jit(solution)/shard_map/ppermute | solution.py:932
  107.0 12.8 %collective-permute-start.47 = (f32[192,512]{1,0:T(8,128)S(1)}, f32[192,512]{1,0:T(8,128)S(1)}, u32[]{:S(2)}, u32[]{:S(2)}) collective-permute-start(f32[192,512]{1,0:T(8,128)S(1)} %get-tuple-element.162.refs_2_), channel_id=1, source_target_pairs={{0,8},{1,17},{2,10},{3,19},{4,12},{5,21},{6,14},{7,23},{8,0},{9,25... | collective-permute-start | bytes 1179656 | tf_op jit(solution)/shard_map/ppermute | solution.py:937
  108.8 9.6 %collective-permute-start.48 = (f32[128,512]{1,0:T(8,128)S(1)}, f32[128,512]{1,0:T(8,128)S(1)}, u32[]{:S(2)}, u32[]{:S(2)}) collective-permute-start(f32[128,512]{1,0:T(8,128)S(1)} %get-tuple-element.163.refs_14_), channel_id=1, source_target_pairs={{0,2},{1,3},{2,0},{3,1},{4,6},{5,7},{6,4},{7,5},{8,10},{9,11},{10,... | collective-permute-start | bytes 786440 | tf_op jit(solution)/shard_map/ppermute | solution.py:932
  111.2 4.3 %collective-permute-start.49 = (f32[384,512]{1,0:T(8,128)S(1)}, f32[384,512]{1,0:T(8,128)S(1)}, u32[]{:S(2)}, u32[]{:S(2)}) collective-permute-start(f32[384,512]{1,0:T(8,128)S(1)} %split.9.refs_11_), channel_id=1, source_target_pairs={{0,1},{1,0},{2,3},{3,2},{4,5},{5,4},{6,7},{7,6},{8,9},{9,8},{10,11... | collective-permute-start | bytes 2359304 | tf_op jit(solution)/shard_map/ppermute | solution.py:932
  112.7 11.3 %collective-permute-start.43 = (f32[64,128]{1,0:T(8,128)S(1)}, f32[64,128]{1,0:T(8,128)S(1)}, u32[]{:S(2)}, u32[]{:S(2)}) collective-permute-start(f32[64,128]{1,0:T(8,128)S(1)} %get-tuple-element.171.refs_2_.refs_0_), channel_id=1, source_target_pairs={{0,1},{1,0},{2,3},{3,2},{4,5},{5,4},{6,7},{7,6},{8,9},{9,8},{10,11... | collective-permute-start | bytes 98312 | tf_op jit(solution)/shard_map/ppermute | solution.py:932
  113.2 14.4 %collective-permute-start.53 = (f32[80,512]{1,0:T(8,128)S(1)}, f32[80,512]{1,0:T(8,128)S(1)}, u32[]{:S(2)}, u32[]{:S(2)}) collective-permute-start(f32[80,512]{1,0:T(8,128)S(1)} %add.46.refs_2_.refs_0_), channel_id=1, source_target_pairs={{0,4},{1,5},{2,6},{3,7},{4,0},{5,1},{6,2},{7,3},{8,12},{9,13},{10,... | collective-permute-start | bytes 491528 | tf_op jit(solution)/shard_map/ppermute | solution.py:932
  115.6 7.6 %collective-permute-start.46 = (f32[96,512]{1,0:T(8,128)S(1)}, f32[96,512]{1,0:T(8,128)S(1)}, u32[]{:S(2)}, u32[]{:S(2)}) collective-permute-start(f32[96,512]{1,0:T(8,128)S(1)} %get-tuple-element.175.refs_2_), channel_id=1, source_target_pairs={{0,16},{1,9},{2,18},{3,11},{4,20},{5,13},{6,22},{7,15},{8,24},{9,1... | collective-permute-start | bytes 589832 | tf_op jit(solution)/shard_map/ppermute | solution.py:937
  118.4 9.9 %collective-permute-start.52 = (f32[192,512]{1,0:T(8,128)S(1)}, f32[192,512]{1,0:T(8,128)S(1)}, u32[]{:S(2)}, u32[]{:S(2)}) collective-permute-start(f32[192,512]{1,0:T(8,128)S(1)} %get-tuple-element.178.refs_2_), channel_id=1, source_target_pairs={{0,8},{1,17},{2,10},{3,19},{4,12},{5,21},{6,14},{7,23},{8,0},{9,25... | collective-permute-start | bytes 1179656 | tf_op jit(solution)/shard_map/ppermute | solution.py:937
  119.8 12.3 %collective-permute-start.58 = (f32[64,512]{1,0:T(8,128)S(1)}, f32[64,512]{1,0:T(8,128)S(1)}, u32[]{:S(2)}, u32[]{:S(2)}) collective-permute-start(f32[64,512]{1,0:T(8,128)S(1)} %get-tuple-element.179.refs_2_), channel_id=1, source_target_pairs={{0,4},{1,5},{2,6},{3,7},{4,0},{5,1},{6,2},{7,3},{8,12},{9,13},{10,... | collective-permute-start | bytes 393224 | tf_op jit(solution)/shard_map/ppermute | solution.py:932
  123.2 5.7 %collective-permute-start.51 = (f32[96,512]{1,0:T(8,128)S(1)}, f32[96,512]{1,0:T(8,128)S(1)}, u32[]{:S(2)}, u32[]{:S(2)}) collective-permute-start(f32[96,512]{1,0:T(8,128)S(1)} %get-tuple-element.180.refs_2_), channel_id=1, source_target_pairs={{0,16},{1,9},{2,18},{3,11},{4,20},{5,13},{6,22},{7,15},{8,24},{9,1... | collective-permute-start | bytes 589832 | tf_op jit(solution)/shard_map/ppermute | solution.py:937
  124.0 7.9 %collective-permute-start.59 = (f32[48,512]{1,0:T(8,128)S(1)}, f32[48,512]{1,0:T(8,128)S(1)}, u32[]{:S(2)}, u32[]{:S(2)}) collective-permute-start(f32[48,512]{1,0:T(8,128)S(1)} %get-tuple-element.181.refs_2_), channel_id=1, source_target_pairs={{0,2},{1,3},{2,0},{3,1},{4,6},{5,7},{6,4},{7,5},{8,10},{9,11},{10,... | collective-permute-start | bytes 294920 | tf_op jit(solution)/shard_map/ppermute | solution.py:932
  128.3 7.0 %collective-permute-start.57 = (f32[80,512]{1,0:T(8,128)S(1)}, f32[80,512]{1,0:T(8,128)S(1)}, u32[]{:S(2)}, u32[]{:S(2)}) collective-permute-start(f32[80,512]{1,0:T(8,128)S(1)} %add.48.refs_2_.refs_0_), channel_id=1, source_target_pairs={{0,2},{1,3},{2,0},{3,1},{4,6},{5,7},{6,4},{7,5},{8,10},{9,11},{10,... | collective-permute-start | bytes 491528 | tf_op jit(solution)/shard_map/ppermute | solution.py:932
  128.9 7.8 %collective-permute-start.56 = (f32[96,512]{1,0:T(8,128)S(1)}, f32[96,512]{1,0:T(8,128)S(1)}, u32[]{:S(2)}, u32[]{:S(2)}) collective-permute-start(f32[96,512]{1,0:T(8,128)S(1)} %get-tuple-element.184.refs_2_), channel_id=1, source_target_pairs={{0,16},{1,9},{2,18},{3,11},{4,20},{5,13},{6,22},{7,15},{8,24},{9,1... | collective-permute-start | bytes 589832 | tf_op jit(solution)/shard_map/ppermute | solution.py:937
  130.9 6.7 %collective-permute-start.55 = (f32[48,512]{1,0:T(8,128)S(1)}, f32[48,512]{1,0:T(8,128)S(1)}, u32[]{:S(2)}, u32[]{:S(2)}) collective-permute-start(f32[48,512]{1,0:T(8,128)S(1)} %get-tuple-element.185.refs_2_), channel_id=1, source_target_pairs={{0,2},{1,3},{2,0},{3,1},{4,6},{5,7},{6,4},{7,5},{8,10},{9,11},{10,... | collective-permute-start | bytes 294920 | tf_op jit(solution)/shard_map/ppermute | solution.py:932
  131.9 6.0 %collective-permute-start.54 = (f32[64,128]{1,0:T(8,128)S(1)}, f32[64,128]{1,0:T(8,128)S(1)}, u32[]{:S(2)}, u32[]{:S(2)}) collective-permute-start(f32[64,128]{1,0:T(8,128)S(1)} %add.49.refs_2_.refs_0_), channel_id=1, source_target_pairs={{0,17},{1,16},{2,19},{3,18},{4,21},{5,20},{6,23},{7,22},{8,25},{9,... | collective-permute-start | bytes 98312 | tf_op jit(solution)/shard_map/ppermute | solution.py:932
  132.1 8.7 %collective-permute-start.64 = (f32[48,512]{1,0:T(8,128)S(1)}, f32[48,512]{1,0:T(8,128)S(1)}, u32[]{:S(2)}, u32[]{:S(2)}) collective-permute-start(f32[48,512]{1,0:T(8,128)S(1)} %add.50.refs_2_.refs_0_), channel_id=1, source_target_pairs={{0,4},{1,5},{2,6},{3,7},{4,0},{5,1},{6,2},{7,3},{8,12},{9,13},{10,... | collective-permute-start | bytes 294920 | tf_op jit(solution)/shard_map/ppermute | solution.py:932
  135.3 9.4 %collective-permute-start.62 = (f32[64,512]{1,0:T(8,128)S(1)}, f32[64,512]{1,0:T(8,128)S(1)}, u32[]{:S(2)}, u32[]{:S(2)}) collective-permute-start(f32[64,512]{1,0:T(8,128)S(1)} %add.51.refs_2_.refs_0_), channel_id=1, source_target_pairs={{0,8},{1,17},{2,10},{3,19},{4,12},{5,21},{6,14},{7,23},{8,0},{9,25... | collective-permute-start | bytes 393224 | tf_op jit(solution)/shard_map/ppermute | solution.py:937
  136.7 10.2 %collective-permute-start.61 = (f32[160,512]{1,0:T(8,128)S(1)}, f32[160,512]{1,0:T(8,128)S(1)}, u32[]{:S(2)}, u32[]{:S(2)}) collective-permute-start(f32[160,512]{1,0:T(8,128)S(1)} %join.14.refs_2_.refs_0_), channel_id=1, source_target_pairs={{0,16},{1,9},{2,18},{3,11},{4,20},{5,13},{6,22},{7,15},{8,24},{9,1... | collective-permute-start | bytes 983048 | tf_op jit(solution)/shard_map/ppermute | solution.py:937
  137.6 7.1 %collective-permute-start.63 = (f32[48,512]{1,0:T(8,128)S(1)}, f32[48,512]{1,0:T(8,128)S(1)}, u32[]{:S(2)}, u32[]{:S(2)}) collective-permute-start(f32[48,512]{1,0:T(8,128)S(1)} %get-tuple-element.190.refs_2_), channel_id=1, source_target_pairs={{0,2},{1,3},{2,0},{3,1},{4,6},{5,7},{6,4},{7,5},{8,10},{9,11},{10,... | collective-permute-start | bytes 294920 | tf_op jit(solution)/shard_map/ppermute | solution.py:932
  138.0 12.1 %collective-permute-start.67 = (f32[48,512]{1,0:T(8,128)S(1)}, f32[48,512]{1,0:T(8,128)S(1)}, u32[]{:S(2)}, u32[]{:S(2)}) collective-permute-start(f32[48,512]{1,0:T(8,128)S(1)} %add.52.refs_2_.refs_0_), channel_id=1, source_target_pairs={{0,4},{1,5},{2,6},{3,7},{4,0},{5,1},{6,2},{7,3},{8,12},{9,13},{10,... | collective-permute-start | bytes 294920 | tf_op jit(solution)/shard_map/ppermute | solution.py:932
  140.8 7.7 %collective-permute-start.60 = (f32[64,128]{1,0:T(8,128)S(1)}, f32[64,128]{1,0:T(8,128)S(1)}, u32[]{:S(2)}, u32[]{:S(2)}) collective-permute-start(f32[64,128]{1,0:T(8,128)S(1)} %add.53.refs_2_.refs_0_), channel_id=1, source_target_pairs={{0,3},{1,2},{2,1},{3,0},{4,7},{5,6},{6,5},{7,4},{8,11},{9,10},{10,... | collective-permute-start | bytes 98312 | tf_op jit(solution)/shard_map/ppermute | solution.py:932
  144.7 5.9 %collective-permute-start.66 = (f32[48,512]{1,0:T(8,128)S(1)}, f32[48,512]{1,0:T(8,128)S(1)}, u32[]{:S(2)}, u32[]{:S(2)}) collective-permute-start(f32[48,512]{1,0:T(8,128)S(1)} %add.54.refs_2_.refs_0_), channel_id=1, source_target_pairs={{0,2},{1,3},{2,0},{3,1},{4,6},{5,7},{6,4},{7,5},{8,10},{9,11},{10,... | collective-permute-start | bytes 294920 | tf_op jit(solution)/shard_map/ppermute | solution.py:932
  144.7 7.7 %collective-permute-start.69 = (f32[48,512]{1,0:T(8,128)S(1)}, f32[48,512]{1,0:T(8,128)S(1)}, u32[]{:S(2)}, u32[]{:S(2)}) collective-permute-start(f32[48,512]{1,0:T(8,128)S(1)} %add.55.refs_2_.refs_0_), channel_id=1, source_target_pairs={{0,4},{1,5},{2,6},{3,7},{4,0},{5,1},{6,2},{7,3},{8,12},{9,13},{10,... | collective-permute-start | bytes 294920 | tf_op jit(solution)/shard_map/ppermute | solution.py:932
  147.0 6.5 %collective-permute-start.72 = (f32[64,512]{1,0:T(8,128)S(1)}, f32[64,512]{1,0:T(8,128)S(1)}, u32[]{:S(2)}, u32[]{:S(2)}) collective-permute-start(f32[64,512]{1,0:T(8,128)S(1)} %add.56.refs_2_.refs_0_), channel_id=1, source_target_pairs={{0,16},{1,9},{2,18},{3,11},{4,20},{5,13},{6,22},{7,15},{8,24},{9,1... | collective-permute-start | bytes 393224 | tf_op jit(solution)/shard_map/ppermute | solution.py:937
  148.4 21.7 %collective-permute-start.80 = (f32[320,512]{1,0:T(8,128)S(1)}, f32[320,512]{1,0:T(8,128)S(1)}, u32[]{:S(2)}, u32[]{:S(2)}) collective-permute-start(f32[320,512]{1,0:T(8,128)S(1)} %join.15.refs_2_.refs_0_), channel_id=1, source_target_pairs={{0,8},{1,17},{2,10},{3,19},{4,12},{5,21},{6,14},{7,23},{8,0},{9,25... | collective-permute-start | bytes 1966088 | tf_op jit(solution)/shard_map/ppermute | solution.py:937
  150.0 10.3 %collective-permute-start.65 = (f32[64,128]{1,0:T(8,128)S(1)}, f32[64,128]{1,0:T(8,128)S(1)}, u32[]{:S(2)}, u32[]{:S(2)}) collective-permute-start(f32[64,128]{1,0:T(8,128)S(1)} %add.57.refs_2_.refs_0_), channel_id=1, source_target_pairs={{0,5},{1,4},{2,7},{3,6},{4,1},{5,0},{6,3},{7,2},{8,13},{9,12},{10,... | collective-permute-start | bytes 98312 | tf_op jit(solution)/shard_map/ppermute | solution.py:932
  150.5 5.4 %collective-permute-start.71 = (f32[48,512]{1,0:T(8,128)S(1)}, f32[48,512]{1,0:T(8,128)S(1)}, u32[]{:S(2)}, u32[]{:S(2)}) collective-permute-start(f32[48,512]{1,0:T(8,128)S(1)} %add.58.refs_2_.refs_0_), channel_id=1, source_target_pairs={{0,2},{1,3},{2,0},{3,1},{4,6},{5,7},{6,4},{7,5},{8,10},{9,11},{10,... | collective-permute-start | bytes 294920 | tf_op jit(solution)/shard_map/ppermute | solution.py:932
  152.4 7.1 %collective-permute-start.68 = (f32[96,512]{1,0:T(8,128)S(1)}, f32[96,512]{1,0:T(8,128)S(1)}, u32[]{:S(2)}, u32[]{:S(2)}) collective-permute-start(f32[96,512]{1,0:T(8,128)S(1)} %join.16.refs_2_.refs_0_), channel_id=1, source_target_pairs={{0,16},{1,9},{2,18},{3,11},{4,20},{5,13},{6,22},{7,15},{8,24},{9,1... | collective-permute-start | bytes 589832 | tf_op jit(solution)/shard_map/ppermute | solution.py:937
  153.5 4.6 %collective-permute-start.70 = (f32[48,512]{1,0:T(8,128)S(1)}, f32[48,512]{1,0:T(8,128)S(1)}, u32[]{:S(2)}, u32[]{:S(2)}) collective-permute-start(f32[48,512]{1,0:T(8,128)S(1)} %add.59.refs_2_.refs_0_), channel_id=1, source_target_pairs={{0,2},{1,3},{2,0},{3,1},{4,6},{5,7},{6,4},{7,5},{8,10},{9,11},{10,... | collective-permute-start | bytes 294920 | tf_op jit(solution)/shard_map/ppermute | solution.py:932
  155.9 10.0 %collective-permute-start.74 = (f32[64,512]{1,0:T(8,128)S(1)}, f32[64,512]{1,0:T(8,128)S(1)}, u32[]{:S(2)}, u32[]{:S(2)}) collective-permute-start(f32[64,512]{1,0:T(8,128)S(1)} %add.60.refs_2_.refs_0_), channel_id=1, source_target_pairs={{0,4},{1,5},{2,6},{3,7},{4,0},{5,1},{6,2},{7,3},{8,12},{9,13},{10,... | collective-permute-start | bytes 393224 | tf_op jit(solution)/shard_map/ppermute | solution.py:932
  158.1 6.8 %collective-permute-start.75 = (f32[96,512]{1,0:T(8,128)S(1)}, f32[96,512]{1,0:T(8,128)S(1)}, u32[]{:S(2)}, u32[]{:S(2)}) collective-permute-start(f32[96,512]{1,0:T(8,128)S(1)} %join.17.refs_2_.refs_0_), channel_id=1, source_target_pairs={{0,16},{1,9},{2,18},{3,11},{4,20},{5,13},{6,22},{7,15},{8,24},{9,1... | collective-permute-start | bytes 589832 | tf_op jit(solution)/shard_map/ppermute | solution.py:937
  159.5 9.2 %collective-permute-start.73 = (f32[96,512]{1,0:T(8,128)S(1)}, f32[96,512]{1,0:T(8,128)S(1)}, u32[]{:S(2)}, u32[]{:S(2)}) collective-permute-start(f32[96,512]{1,0:T(8,128)S(1)} %join.18.refs_2_.refs_0_), channel_id=1, source_target_pairs={{0,16},{1,9},{2,18},{3,11},{4,20},{5,13},{6,22},{7,15},{8,24},{9,1... | collective-permute-start | bytes 589832 | tf_op jit(solution)/shard_map/ppermute | solution.py:937
  160.4 9.9 %collective-permute-start.79 = (f32[192,512]{1,0:T(8,128)S(1)}, f32[192,512]{1,0:T(8,128)S(1)}, u32[]{:S(2)}, u32[]{:S(2)}) collective-permute-start(f32[192,512]{1,0:T(8,128)S(1)} %join.19.refs_2_.refs_0_), channel_id=1, source_target_pairs={{0,8},{1,17},{2,10},{3,19},{4,12},{5,21},{6,14},{7,23},{8,0},{9,25... | collective-permute-start | bytes 1179656 | tf_op jit(solution)/shard_map/ppermute | solution.py:937
  164.9 8.9 %collective-permute-start.78 = (f32[192,512]{1,0:T(8,128)S(1)}, f32[192,512]{1,0:T(8,128)S(1)}, u32[]{:S(2)}, u32[]{:S(2)}) collective-permute-start(f32[192,512]{1,0:T(8,128)S(1)} %join.20.refs_2_.refs_0_), channel_id=1, source_target_pairs={{0,8},{1,17},{2,10},{3,19},{4,12},{5,21},{6,14},{7,23},{8,0},{9,25... | collective-permute-start | bytes 1179656 | tf_op jit(solution)/shard_map/ppermute | solution.py:937
  165.9 8.6 %collective-permute-start.77 = (f32[128,512]{1,0:T(8,128)S(1)}, f32[128,512]{1,0:T(8,128)S(1)}, u32[]{:S(2)}, u32[]{:S(2)}) collective-permute-start(f32[128,512]{1,0:T(8,128)S(1)} %join.21.refs_2_.refs_0_), channel_id=1, source_target_pairs={{0,2},{1,3},{2,0},{3,1},{4,6},{5,7},{6,4},{7,5},{8,10},{9,11},{10,... | collective-permute-start | bytes 786440 | tf_op jit(solution)/shard_map/ppermute | solution.py:932
  168.8 9.3 %collective-permute-start.76 = (f32[192,512]{1,0:T(8,128)S(1)}, f32[192,512]{1,0:T(8,128)S(1)}, u32[]{:S(2)}, u32[]{:S(2)}) collective-permute-start(f32[192,512]{1,0:T(8,128)S(1)} %join.22.refs_2_.refs_0_), channel_id=1, source_target_pairs={{0,8},{1,17},{2,10},{3,19},{4,12},{5,21},{6,14},{7,23},{8,0},{9,25... | collective-permute-start | bytes 1179656 | tf_op jit(solution)/shard_map/ppermute | solution.py:937
  170.2 8.3 %collective-permute-start.82 = (f32[640,512]{1,0:T(8,128)S(1)}, f32[640,512]{1,0:T(8,128)S(1)}, u32[]{:S(2)}, u32[]{:S(2)}) collective-permute-start(f32[640,512]{1,0:T(8,128)S(1)} %join.23.refs_2_.refs_0_), channel_id=1, source_target_pairs={{0,1},{1,0},{2,3},{3,2},{4,5},{5,4},{6,7},{7,6},{8,9},{9,8},{10,11... | collective-permute-start | bytes 3932168 | tf_op jit(solution)/shard_map/ppermute | solution.py:932
  170.4 8.1 %collective-permute-start.83 = (f32[384,512]{1,0:T(8,128)S(1)}, f32[384,512]{1,0:T(8,128)S(1)}, u32[]{:S(2)}, u32[]{:S(2)}) collective-permute-start(f32[384,512]{1,0:T(8,128)S(1)} %join.24.refs_2_), channel_id=1, source_target_pairs={{0,1},{1,0},{2,3},{3,2},{4,5},{5,4},{6,7},{7,6},{8,9},{9,8},{10,11... | collective-permute-start | bytes 2359304 | tf_op jit(solution)/shard_map/ppermute | solution.py:932
  173.9 6.7 %collective-permute-start.84 = (f32[384,512]{1,0:T(8,128)S(1)}, f32[384,512]{1,0:T(8,128)S(1)}, u32[]{:S(2)}, u32[]{:S(2)}) collective-permute-start(f32[384,512]{1,0:T(8,128)S(1)} %join.25.refs_2_.refs_0_), channel_id=1, source_target_pairs={{0,1},{1,0},{2,3},{3,2},{4,5},{5,4},{6,7},{7,6},{8,9},{9,8},{10,11... | collective-permute-start | bytes 2359304 | tf_op jit(solution)/shard_map/ppermute | solution.py:932
  174.6 6.0 %collective-permute-start.85 = (f32[256,512]{1,0:T(8,128)S(1)}, f32[256,512]{1,0:T(8,128)S(1)}, u32[]{:S(2)}, u32[]{:S(2)}) collective-permute-start(f32[256,512]{1,0:T(8,128)S(1)} %join.26.refs_2_), channel_id=1, source_target_pairs={{0,1},{1,0},{2,3},{3,2},{4,5},{5,4},{6,7},{7,6},{8,9},{9,8},{10,11... | collective-permute-start | bytes 1572872 | tf_op jit(solution)/shard_map/ppermute | solution.py:932
  (39 other events, 206.6 us)

commit v6 on v5

--- a/solution.py
+++ b/solution.py
@@ -914,7 +914,7 @@
     ("AA",),
     ("B", "A", "e", "BA"),
     ("CECE",),
-    ("D", "ABSDECBSAD", "CSBEADCSBD", "EASCBDECDB", "LCEDABCAEC", "DBED"),
+    ("DAB", "SDECBSADCS", "BEADCSBDEA", "SCBDECDBLC", "EDABCAECDB", "ED"),
 )
 
 

time: 185 us -> 184 us (level)
  waiting for transfers between devices: 62.6 us -> 58.4 us
  starting transfers between devices: 75.6 us -> 79.1 us
    ppermute x68, waiting for transfers between devices: 43.3 us -> 39 us  [swap(): return lax.ppermute(block, BOTH, [(i, i ^ distance) for i in range(total)])]
    ppermute x18, starting transfers between devices: 18.2 us -> 22.3 us  [swap_by_core(): lax.ppermute(block, BOTH, [(i, i ^ (odd if i & 1 else even)) for i in ran...]
  transfers between devices with their start and end apart: 86 -> 86, of which waited for: 48 -> 40; matrix products, arithmetic and copies ran while one was open for 0% -> 0% of each run, Pallas kernels for 11% -> 11%
where the time goes in v6:
time: 184 us
  starting transfers between devices  79.1 us (43%)
  waiting for transfers between devices  58.4 us (32%)
  Pallas kernels  42.7 us (23%)
  local copies, waits for them, and re-layouts  1.93 us (1%)
    ppermute x68, starting transfers between devices, swap(): return lax.ppermute(block, BOTH, [(i, i ^ distance) for i in range(total)])  56.8 us
    pallas_call x89, Pallas kernels, call(): pl.pallas_call(run, name=name, out_shape=outs, in_specs=specs, out_specs=...  42.7 us
    ppermute x68, waiting for transfers between devices, swap(): return lax.ppermute(block, BOTH, [(i, i ^ distance) for i in range(total)])  39 us
    ppermute x18, starting transfers between devices, swap_by_core(): lax.ppermute(block, BOTH, [(i, i ^ (odd if i & 1 else even)) for i in ran...  22.3 us
    ppermute x18, waiting for transfers between devices, swap_by_core(): lax.ppermute(block, BOTH, [(i, i ^ (odd if i & 1 else even)) for i in ran...  19.4 us
  transfers between devices with their start and end apart: 86, of which 40 were waited for; matrix products, arithmetic and copies ran while one was open for 0% of the time, Pallas kernels for 11%

profile of v6, /device:TPU:0, one launch (start us, length us, event | category | flops | bytes accessed | tf_op | source)
XLA Modules:
  0.0 183.7 jit_solution(10700655137179233061)
XLA Ops:
  2.6 1.9 %enter.1 = (f32[1024,512]{1,0:T(8,128)S(1)}, f32[24,128]{1,0:T(8,128)S(1)}, s32[8,512]{1,0:T(8,128)S(1)}) custom-call(s32[4]{0:T(128)S(1)} %copy-done.14, bf16[4,256,512]{2,1,0:T(8,128)(2,1)S(1)} %copy-done.3), custom_call_target="tpu_custom_call" | custom-call | flops 5000000000 | bytes 1 | tf_op jit(solution)/shard_map/enter/pallas_call | solution.py:46
  6.3 3.6 %collective-permute-start.1 = (f32[24,128]{1,0:T(8,128)S(1)}, f32[24,128]{1,0:T(8,128)S(1)}, u32[]{:S(2)}, u32[]{:S(2)}) collective-permute-start(f32[24,128]{1,0:T(8,128)S(1)} %add.31.refs_0_), channel_id=1, source_target_pairs={{0,25},{1,24},{2,27},{3,26},{4,29},{5,28},{6,31},{7,30},{8,17},{9,... | collective-permute-start | bytes 36872 | tf_op jit(solution)/shard_map/ppermute | solution.py:932
  11.3 1.7 collective-permute-done.3.refs_2_
  13.2 3.7 %collective-permute-start.4 = (f32[24,128]{1,0:T(8,128)S(1)}, f32[24,128]{1,0:T(8,128)S(1)}, u32[]{:S(2)}, u32[]{:S(2)}) collective-permute-start(f32[24,128]{1,0:T(8,128)S(1)} %add.33.refs_0_), channel_id=1, source_target_pairs={{0,7},{1,6},{2,5},{3,4},{4,3},{5,2},{6,1},{7,0},{8,15},{9,14},{10,... | collective-permute-start | bytes 36872 | tf_op jit(solution)/shard_map/ppermute | solution.py:932
  18.3 1.7 collective-permute-done.6.refs_2_
  21.0 1.5 drive0.1
  23.7 1.6 collective-permute-start.10
  25.3 1.5 collective-permute-start.9
  27.7 1.3 collective-permute-done.10.src_ref
  28.9 1.4 collective-permute-done.9.refs_2_
  30.6 3.8 %finish0.1 = (f32[1032,768]{1,0:T(8,128)S(1)}, bf16[1024,512]{1,0:T(8,128)(2,1)S(1)}, f32[1024,512]{1,0:T(8,128)S(1)}, f32[1024,512]{1,0:T(8,128)S(1)}, f32[1024...) custom-call(f32[8,768]{1,0:T(8,128)S(1)} %combine.4.refs_0_, ...), custom_call_target="tpu_custom_call" | custom-call | flops 5000000000 | bytes 1 | tf_op jit(solution)/shard_map/finish0/pallas_call | solution.py:46
  34.5 1.4 keep.1
  35.9 1.5 collective-permute-start.12
  37.7 1.6 collective-permute-start.13
  40.7 1.5 collective-permute-start.15
  42.2 2.7 %collective-permute-start.16 = (f32[16,128]{1,0:T(8,128)S(1)}, f32[16,128]{1,0:T(8,128)S(1)}, u32[]{:S(2)}, u32[]{:S(2)}) collective-permute-start(f32[16,128]{1,0:T(8,128)S(1)} %add.38.refs_0_), channel_id=1, source_target_pairs={{0,5},{1,4},{2,7},{3,6},{4,1},{5,0},{6,3},{7,2},{8,13},{9,12},{10,... | collective-permute-start | bytes 24584 | tf_op jit(solution)/shard_map/ppermute | solution.py:932
  46.3 1.6 drive1.1
  49.2 2.2 %collective-permute-start.21 = (f32[8,768]{1,0:T(8,128)S(1)}, f32[8,768]{1,0:T(8,128)S(1)}, u32[]{:S(2)}, u32[]{:S(2)}) collective-permute-start(f32[8,768]{1,0:T(8,128)S(1)} %combine.5.refs_0_), channel_id=1, source_target_pairs={{0,7},{1,6},{2,5},{3,4},{4,3},{5,2},{6,1},{7,0},{8,15},{9,14},{10,... | collective-permute-start | bytes 73736 | tf_op jit(solution)/shard_map/ppermute | solution.py:932
  55.9 7.0 %middle.1 = (f32[4,1024,128]{2,1,0:T(8,128)S(1)}, f32[1032,768]{1,0:T(8,128)S(1)}, bf16[1024,512]{1,0:T(8,128)(2,1)S(1)}, f32[1024,768]{1,0:T(8,128)S(1)}, f32[1...) custom-call(f32[8,768]{1,0:T(8,128)S(1)} %combine.5.refs_0_, ...), custom_call_target="tpu_custom_call" | custom-call | flops 5000000000 | bytes 1 | tf_op jit(solution)/shard_map/middle/pallas_call | solution.py:46
  64.8 1.8 collective-permute-start.25
  66.6 2.1 %collective-permute-start.23 = (f32[8,768]{1,0:T(8,128)S(1)}, f32[8,768]{1,0:T(8,128)S(1)}, u32[]{:S(2)}, u32[]{:S(2)}) collective-permute-start(f32[8,768]{1,0:T(8,128)S(1)} %combine.6.refs_1_.refs_0_), channel_id=1, source_target_pairs={{0,3},{1,2},{2,1},{3,0},{4,7},{5,6},{6,5},{7,4},{8,11},{9,10},{10,... | collective-permute-start | bytes 73736 | tf_op jit(solution)/shard_map/ppermute | solution.py:932
  70.1 1.6 collective-permute-start.29
  71.6 3.1 %adjoint1.1 = (f32[1024,512]{1,0:T(8,128)S(1)}, f32[768,512]{1,0:T(8,128)S(1)}, f32[8,128]{1,0:T(8,128)S(1)}, f32[16,128]{1,0:T(8,128)S(1)}) custom-call(f32[8,768]{1,0:T(8,128)S(1)} %combine.6.refs_1_.refs_0_, f32[8,768]{1,0:T(8,128)S(1)} %collective-permute-done.23.refs_1_, f32[8,768]{1,0:T(8,128)S(1)} %collective-permute-done.24.refs_2_, ...), custom_call_target="tpu_custom_call" | custom-call | flops 5000000000 | bytes 1 | tf_op jit(solution)/shard_map/adjoint1/pallas_call | solution.py:46
  76.0 1.2 collective-permute-start.31
  78.9 1.9 %collective-permute-done.29.refs_1_ = f32[320,512]{1,0:T(8,128)S(1)} collective-permute-done((f32[320,512]{1,0:T(8,128)S(1)}, f32[320,512]{1,0:T(8,128)S(1)}, u32[]{:S(2)}, u32[]{:S(2)}) %collective-permute-start.29) | collective-permute-done | bytes 655392 | tf_op jit(solution)/shard_map/ppermute | solution.py:937
  80.9 1.3 collective-permute-done.28.refs_1_
  84.3 1.8 collective-permute-start.32
  87.1 1.5 emit.1
  89.3 3.8 %collective-permute-done.35.refs_1_ = f32[160,512]{1,0:T(8,128)S(1)} collective-permute-done((f32[160,512]{1,0:T(8,128)S(1)}, f32[160,512]{1,0:T(8,128)S(1)}, u32[]{:S(2)}, u32[]{:S(2)}) %collective-permute-start.35) | collective-permute-done | bytes 327712 | tf_op jit(solution)/shard_map/ppermute | solution.py:937
  93.2 4.2 %lower.1 = (f32[1024,512]{1,0:T(8,128)S(1)}, bf16[1024,512]{1,0:T(8,128)(2,1)S(1)}, f32[1024,768]{1,0:T(8,128)S(1)}, f32[512,512]{1,0:T(8,128)S(1)}, f32[768,512...) custom-call(f32[16,128]{1,0:T(8,128)S(1)} %add.45.refs_2_.refs_0_, ...), custom_call_target="tpu_custom_call" | custom-call | flops 5000000000 | bytes 1 | tf_op jit(solution)/shard_map/lower/pallas_call | solution.py:46
  99.5 1.6 collective-permute-start.40
  101.1 1.2 collective-permute-start.43
  102.3 2.2 %collective-permute-done.40.src_ref = f32[8,768]{1,0:T(8,128)S(1)} collective-permute-done((f32[8,768]{1,0:T(8,128)S(1)}, f32[8,768]{1,0:T(8,128)S(1)}, u32[]{:S(2)}, u32[]{:S(2)}) %collective-permute-start.40) | collective-permute-done | bytes 24608 | tf_op jit(solution)/shard_map/ppermute | solution.py:932
  104.6 2.1 %collective-permute-start.38 = (f32[8,768]{1,0:T(8,128)S(1)}, f32[8,768]{1,0:T(8,128)S(1)}, u32[]{:S(2)}, u32[]{:S(2)}) collective-permute-start(f32[8,768]{1,0:T(8,128)S(1)} %combine.7.refs_1_.refs_0_), channel_id=1, source_target_pairs={{0,3},{1,2},{2,1},{3,0},{4,7},{5,6},{6,5},{7,4},{8,11},{9,10},{10,... | collective-permute-start | bytes 73736 | tf_op jit(solution)/shard_map/ppermute | solution.py:932
  106.7 1.3 collective-permute-start.47
  108.9 2.0 %adjoint0.1 = (bf16[1024,768]{1,0:T(8,128)(2,1)S(1)}, f32[768,512]{1,0:T(8,128)S(1)}, f32[8,128]{1,0:T(8,128)S(1)}) custom-call(f32[8,768]{1,0:T(8,128)S(1)} %combine.7.refs_1_.refs_0_, f32[8,768]{1,0:T(8,128)S(1)} %collective-permute-done.38.refs_1_, f32[8,768]{1,0:T(8,128)S(1)} %collective-permute-done.39.refs_2_, f32[8,768]{1,0:T(8,128)S(1)} %copy.41.refs_3_, ...), custom_call_target="tpu_custom_call" | custom-call | flops 5000000000 | bytes 1 | tf_op jit(solution)/shard_map/adjoint0/pallas_call | solution.py:46
  111.5 2.0 %collective-permute-start.53 = (f32[80,512]{1,0:T(8,128)S(1)}, f32[80,512]{1,0:T(8,128)S(1)}, u32[]{:S(2)}, u32[]{:S(2)}) collective-permute-start(f32[80,512]{1,0:T(8,128)S(1)} %add.46.refs_2_.refs_0_), channel_id=1, source_target_pairs={{0,4},{1,5},{2,6},{3,7},{4,0},{5,1},{6,2},{7,3},{8,12},{9,13},{10,... | collective-permute-start | bytes 491528 | tf_op jit(solution)/shard_map/ppermute | solution.py:932
  113.5 1.5 collective-permute-start.46
  115.0 1.2 back.1
  116.5 3.3 %collective-permute-done.48.refs_1_ = f32[128,512]{1,0:T(8,128)S(1)} collective-permute-done((f32[128,512]{1,0:T(8,128)S(1)}, f32[128,512]{1,0:T(8,128)S(1)}, u32[]{:S(2)}, u32[]{:S(2)}) %collective-permute-start.48) | collective-permute-done | bytes 262176 | tf_op jit(solution)/shard_map/ppermute | solution.py:932
  121.4 2.5 %collective-permute-start.59 = (f32[48,512]{1,0:T(8,128)S(1)}, f32[48,512]{1,0:T(8,128)S(1)}, u32[]{:S(2)}, u32[]{:S(2)}) collective-permute-start(f32[48,512]{1,0:T(8,128)S(1)} %get-tuple-element.181.refs_2_), channel_id=1, source_target_pairs={{0,2},{1,3},{2,0},{3,1},{4,6},{5,7},{6,4},{7,5},{8,10},{9,11},{10,... | collective-permute-start | bytes 294920 | tf_op jit(solution)/shard_map/ppermute | solution.py:932
  124.0 5.2 %collective-permute-done.52.refs_1_ = f32[192,512]{1,0:T(8,128)S(1)} collective-permute-done((f32[192,512]{1,0:T(8,128)S(1)}, f32[192,512]{1,0:T(8,128)S(1)}, u32[]{:S(2)}, u32[]{:S(2)}) %collective-permute-start.52) | collective-permute-done | bytes 393248 | tf_op jit(solution)/shard_map/ppermute | solution.py:937
  129.5 1.3 collective-permute-start.56
  130.8 2.1 %collective-permute-start.55 = (f32[48,512]{1,0:T(8,128)S(1)}, f32[48,512]{1,0:T(8,128)S(1)}, u32[]{:S(2)}, u32[]{:S(2)}) collective-permute-start(f32[48,512]{1,0:T(8,128)S(1)} %get-tuple-element.185.refs_2_), channel_id=1, source_target_pairs={{0,2},{1,3},{2,0},{3,1},{4,6},{5,7},{6,4},{7,5},{8,10},{9,11},{10,... | collective-permute-start | bytes 294920 | tf_op jit(solution)/shard_map/ppermute | solution.py:932
  133.4 1.4 collective-permute-done.57.refs_1_
  135.7 1.6 collective-permute-start.61
  137.3 1.6 collective-permute-start.63
  140.0 2.7 %collective-permute-done.64.refs_1_ = f32[48,512]{1,0:T(8,128)S(1)} collective-permute-done((f32[48,512]{1,0:T(8,128)S(1)}, f32[48,512]{1,0:T(8,128)S(1)}, u32[]{:S(2)}, u32[]{:S(2)}) %collective-permute-start.64) | collective-permute-done | bytes 98336 | tf_op jit(solution)/shard_map/ppermute | solution.py:932
  143.7 1.4 collective-permute-start.69
  145.2 2.4 %collective-permute-start.72 = (f32[64,512]{1,0:T(8,128)S(1)}, f32[64,512]{1,0:T(8,128)S(1)}, u32[]{:S(2)}, u32[]{:S(2)}) collective-permute-start(f32[64,512]{1,0:T(8,128)S(1)} %add.56.refs_2_.refs_0_), channel_id=1, source_target_pairs={{0,16},{1,9},{2,18},{3,11},{4,20},{5,13},{6,22},{7,15},{8,24},{9,1... | collective-permute-start | bytes 393224 | tf_op jit(solution)/shard_map/ppermute | solution.py:937
  147.9 1.7 collective-permute-start.80
  149.9 2.4 %collective-permute-done.69.refs_1_ = f32[48,512]{1,0:T(8,128)S(1)} collective-permute-done((f32[48,512]{1,0:T(8,128)S(1)}, f32[48,512]{1,0:T(8,128)S(1)}, u32[]{:S(2)}, u32[]{:S(2)}) %collective-permute-start.69) | collective-permute-done | bytes 98336 | tf_op jit(solution)/shard_map/ppermute | solution.py:932
  153.2 2.2 %collective-permute-done.71.refs_1_ = f32[48,512]{1,0:T(8,128)S(1)} collective-permute-done((f32[48,512]{1,0:T(8,128)S(1)}, f32[48,512]{1,0:T(8,128)S(1)}, u32[]{:S(2)}, u32[]{:S(2)}) %collective-permute-start.71) | collective-permute-done | bytes 98336 | tf_op jit(solution)/shard_map/ppermute | solution.py:932
  156.0 1.4 collective-permute-done.70.refs_1_
  157.4 1.6 collective-permute-start.75
  161.3 3.1 %leave.1 = (f32[4,256,512]{2,1,0:T(8,128)}, f32[2,512]{1,0:T(2,128)}, f32[2,512]{1,0:T(2,128)}, f32[2,512]{1,0:T(2,128)}, f32[2,512]{1,0:T(2,128)}, /*index=5*/f...) custom-call(f32[64,128]{1,0:T(8,128)S(1)} %add.61.refs_0_.refs_12_, ...), custom_call_target="tpu_custom_call" | custom-call | flops 5000000000 | bytes 1 | tf_op jit(solution)/shard_map/leave/pallas_call | solution.py:46
  164.5 1.4 collective-permute-start.78
  166.5 1.7 collective-permute-done.73.refs_1_
  168.3 1.4 collective-permute-start.76
  170.6 2.7 %collective-permute-done.78.refs_1_ = f32[192,512]{1,0:T(8,128)S(1)} collective-permute-done((f32[192,512]{1,0:T(8,128)S(1)}, f32[192,512]{1,0:T(8,128)S(1)}, u32[]{:S(2)}, u32[]{:S(2)}) %collective-permute-start.78) | collective-permute-done | bytes 393248 | tf_op jit(solution)/shard_map/ppermute | solution.py:937
  174.1 3.4 %collective-permute-done.76.refs_1_ = f32[192,512]{1,0:T(8,128)S(1)} collective-permute-done((f32[192,512]{1,0:T(8,128)S(1)}, f32[192,512]{1,0:T(8,128)S(1)}, u32[]{:S(2)}, u32[]{:S(2)}) %collective-permute-start.76) | collective-permute-done | bytes 393248 | tf_op jit(solution)/shard_map/ppermute | solution.py:937
  177.8 2.1 %place.3 = (f32[2,512,512]{2,1,0:T(8,128)}, f32[2,768,512]{2,1,0:T(8,128)}, f32[2,512,768]{2,1,0:T(8,128)}, f32[8,128]{1,0:T(8,128)S(1)}) custom-call(f32[640,512]{1,0:T(8,128)S(1)} %join.23.refs_2_.refs_0_, f32[640,512]{1,0:T(8,128)S(1)} %collective-permute-done.82.refs_1_, f32[384,512]{1,0:T(8,128)S(1)} %join.24.refs_2_, ...), custom_call_target="tpu_custom_call" | custom-call | flops 5000000000 | bytes 1 | tf_op jit(solution)/shard_map/place/pallas_call | solution.py:46
  180.0 1.6 place.4
  181.6 1.9 %place.5 = (f32[2,512,768]{2,1,0:T(8,128)}, f32[8,128]{1,0:T(8,128)}) custom-call(f32[384,512]{1,0:T(8,128)S(1)} %join.27.refs_4_.refs_0_, f32[384,512]{1,0:T(8,128)S(1)} %collective-permute-done.81.refs_1_, f32[2,512,768]{2,1,0:T(8,128)} %get-tuple-element.199.refs_2_, f32[8,128]{1,0:T(8,128)S(1)} %get-tuple-element.203.refs_3_), custom_call_target="tpu_custom_call", output_to_operand_aliasing={{0}: (2, {})} | custom-call | flops 5000000000 | bytes 1 | tf_op jit(solution)/shard_map/place/pallas_call | solution.py:46
  (227 shorter events, 45.3 us)
Async XLA Ops:
  6.3 5.0 %collective-permute-start.1 = (f32[24,128]{1,0:T(8,128)S(1)}, f32[24,128]{1,0:T(8,128)S(1)}, u32[]{:S(2)}, u32[]{:S(2)}) collective-permute-start(f32[24,128]{1,0:T(8,128)S(1)} %add.31.refs_0_), channel_id=1, source_target_pairs={{0,25},{1,24},{2,27},{3,26},{4,29},{5,28},{6,31},{7,30},{8,17},{9,... | collective-permute-start | bytes 36872 | tf_op jit(solution)/shard_map/ppermute | solution.py:932
  13.2 5.1 %collective-permute-start.4 = (f32[24,128]{1,0:T(8,128)S(1)}, f32[24,128]{1,0:T(8,128)S(1)}, u32[]{:S(2)}, u32[]{:S(2)}) collective-permute-start(f32[24,128]{1,0:T(8,128)S(1)} %add.33.refs_0_), channel_id=1, source_target_pairs={{0,7},{1,6},{2,5},{3,4},{4,3},{5,2},{6,1},{7,0},{8,15},{9,14},{10,... | collective-permute-start | bytes 36872 | tf_op jit(solution)/shard_map/ppermute | solution.py:932
  23.7 5.2 %collective-permute-start.10 = (f32[8,768]{1,0:T(8,128)S(1)}, f32[8,768]{1,0:T(8,128)S(1)}, u32[]{:S(2)}, u32[]{:S(2)}) collective-permute-start(f32[8,768]{1,0:T(8,128)S(1)} %combine.4.refs_0_), channel_id=1, source_target_pairs={{0,7},{1,6},{2,5},{3,4},{4,3},{5,2},{6,1},{7,0},{8,15},{9,14},{10,... | collective-permute-start | bytes 73736 | tf_op jit(solution)/shard_map/ppermute | solution.py:932
  25.3 5.1 %collective-permute-start.9 = (f32[8,768]{1,0:T(8,128)S(1)}, f32[8,768]{1,0:T(8,128)S(1)}, u32[]{:S(2)}, u32[]{:S(2)}) collective-permute-start(f32[8,768]{1,0:T(8,128)S(1)} %combine.4.refs_0_), channel_id=1, source_target_pairs={{0,5},{1,4},{2,7},{3,6},{4,1},{5,0},{6,3},{7,2},{8,13},{9,12},{10,... | collective-permute-start | bytes 73736 | tf_op jit(solution)/shard_map/ppermute | solution.py:932
  40.7 4.9 %collective-permute-start.15 = (f32[16,128]{1,0:T(8,128)S(1)}, f32[16,128]{1,0:T(8,128)S(1)}, u32[]{:S(2)}, u32[]{:S(2)}) collective-permute-start(f32[16,128]{1,0:T(8,128)S(1)} %add.38.refs_0_), channel_id=1, source_target_pairs={{0,7},{1,6},{2,5},{3,4},{4,3},{5,2},{6,1},{7,0},{8,15},{9,14},{10,... | collective-permute-start | bytes 24584 | tf_op jit(solution)/shard_map/ppermute | solution.py:932
  49.2 5.2 %collective-permute-start.21 = (f32[8,768]{1,0:T(8,128)S(1)}, f32[8,768]{1,0:T(8,128)S(1)}, u32[]{:S(2)}, u32[]{:S(2)}) collective-permute-start(f32[8,768]{1,0:T(8,128)S(1)} %combine.5.refs_0_), channel_id=1, source_target_pairs={{0,7},{1,6},{2,5},{3,4},{4,3},{5,2},{6,1},{7,0},{8,15},{9,14},{10,... | collective-permute-start | bytes 73736 | tf_op jit(solution)/shard_map/ppermute | solution.py:932
  64.4 5.5 %collective-permute-start.26 = (f32[640,512]{1,0:T(8,128)S(1)}, f32[640,512]{1,0:T(8,128)S(1)}, u32[]{:S(2)}, u32[]{:S(2)}) collective-permute-start(f32[640,512]{1,0:T(8,128)S(1)} %split.5.refs_2_), channel_id=1, source_target_pairs={{0,1},{1,0},{2,3},{3,2},{4,5},{5,4},{6,7},{7,6},{8,9},{9,8},{10,11... | collective-permute-start | bytes 3932168 | tf_op jit(solution)/shard_map/ppermute | solution.py:932
  64.8 5.0 %collective-permute-start.25 = (f32[8,768]{1,0:T(8,128)S(1)}, f32[8,768]{1,0:T(8,128)S(1)}, u32[]{:S(2)}, u32[]{:S(2)}) collective-permute-start(f32[8,768]{1,0:T(8,128)S(1)} %combine.6.refs_1_.refs_0_), channel_id=1, source_target_pairs={{0,7},{1,6},{2,5},{3,4},{4,3},{5,2},{6,1},{7,0},{8,15},{9,14},{10,... | collective-permute-start | bytes 73736 | tf_op jit(solution)/shard_map/ppermute | solution.py:932
  66.6 5.0 %collective-permute-start.24 = (f32[8,768]{1,0:T(8,128)S(1)}, f32[8,768]{1,0:T(8,128)S(1)}, u32[]{:S(2)}, u32[]{:S(2)}) collective-permute-start(f32[8,768]{1,0:T(8,128)S(1)} %combine.6.refs_1_.refs_0_), channel_id=1, source_target_pairs={{0,5},{1,4},{2,7},{3,6},{4,1},{5,0},{6,3},{7,2},{8,13},{9,12},{10,... | collective-permute-start | bytes 73736 | tf_op jit(solution)/shard_map/ppermute | solution.py:932
  66.6 5.0 %collective-permute-start.23 = (f32[8,768]{1,0:T(8,128)S(1)}, f32[8,768]{1,0:T(8,128)S(1)}, u32[]{:S(2)}, u32[]{:S(2)}) collective-permute-start(f32[8,768]{1,0:T(8,128)S(1)} %combine.6.refs_1_.refs_0_), channel_id=1, source_target_pairs={{0,3},{1,2},{2,1},{3,0},{4,7},{5,6},{6,5},{7,4},{8,11},{9,10},{10,... | collective-permute-start | bytes 73736 | tf_op jit(solution)/shard_map/ppermute | solution.py:932
  70.1 10.7 %collective-permute-start.29 = (f32[320,512]{1,0:T(8,128)S(1)}, f32[320,512]{1,0:T(8,128)S(1)}, u32[]{:S(2)}, u32[]{:S(2)}) collective-permute-start(f32[320,512]{1,0:T(8,128)S(1)} %get-tuple-element.141.refs_20_), channel_id=1, source_target_pairs={{0,8},{1,17},{2,10},{3,19},{4,12},{5,21},{6,14},{7,23},{8,0},{9,25... | collective-permute-start | bytes 1966088 | tf_op jit(solution)/shard_map/ppermute | solution.py:937
  75.0 14.2 %collective-permute-start.36 = (f32[384,512]{1,0:T(8,128)S(1)}, f32[384,512]{1,0:T(8,128)S(1)}, u32[]{:S(2)}, u32[]{:S(2)}) collective-permute-start(f32[384,512]{1,0:T(8,128)S(1)} %split.6.refs_2_), channel_id=1, source_target_pairs={{0,1},{1,0},{2,3},{3,2},{4,5},{5,4},{6,7},{7,6},{8,9},{9,8},{10,11... | collective-permute-start | bytes 2359304 | tf_op jit(solution)/shard_map/ppermute | solution.py:932
  76.0 6.2 %collective-permute-start.31 = (f32[16,128]{1,0:T(8,128)S(1)}, f32[16,128]{1,0:T(8,128)S(1)}, u32[]{:S(2)}, u32[]{:S(2)}) collective-permute-start(f32[16,128]{1,0:T(8,128)S(1)} %add.41.refs_2_.refs_0_), channel_id=1, source_target_pairs={{0,9},{1,8},{2,11},{3,10},{4,13},{5,12},{6,15},{7,14},{8,1},{9,0},... | collective-permute-start | bytes 24584 | tf_op jit(solution)/shard_map/ppermute | solution.py:932
  77.2 4.9 %collective-permute-start.30 = (f32[16,128]{1,0:T(8,128)S(1)}, f32[16,128]{1,0:T(8,128)S(1)}, u32[]{:S(2)}, u32[]{:S(2)}) collective-permute-start(f32[16,128]{1,0:T(8,128)S(1)} %add.41.refs_2_.refs_0_), channel_id=1, source_target_pairs={{0,17},{1,16},{2,19},{3,18},{4,21},{5,20},{6,23},{7,22},{8,25},{9,... | collective-permute-start | bytes 24584 | tf_op jit(solution)/shard_map/ppermute | solution.py:932
  82.2 7.0 %collective-permute-start.34 = (f32[16,128]{1,0:T(8,128)S(1)}, f32[16,128]{1,0:T(8,128)S(1)}, u32[]{:S(2)}, u32[]{:S(2)}) collective-permute-start(f32[16,128]{1,0:T(8,128)S(1)} %add.43.refs_1_.refs_0_), channel_id=1, source_target_pairs={{0,3},{1,2},{2,1},{3,0},{4,7},{5,6},{6,5},{7,4},{8,11},{9,10},{10,... | collective-permute-start | bytes 24584 | tf_op jit(solution)/shard_map/ppermute | solution.py:932
  83.1 6.1 %collective-permute-start.33 = (f32[16,128]{1,0:T(8,128)S(1)}, f32[16,128]{1,0:T(8,128)S(1)}, u32[]{:S(2)}, u32[]{:S(2)}) collective-permute-start(f32[16,128]{1,0:T(8,128)S(1)} %add.43.refs_1_.refs_0_), channel_id=1, source_target_pairs={{0,5},{1,4},{2,7},{3,6},{4,1},{5,0},{6,3},{7,2},{8,13},{9,12},{10,... | collective-permute-start | bytes 24584 | tf_op jit(solution)/shard_map/ppermute | solution.py:932
  84.3 4.9 %collective-permute-start.32 = (f32[16,128]{1,0:T(8,128)S(1)}, f32[16,128]{1,0:T(8,128)S(1)}, u32[]{:S(2)}, u32[]{:S(2)}) collective-permute-start(f32[16,128]{1,0:T(8,128)S(1)} %add.43.refs_1_.refs_0_), channel_id=1, source_target_pairs={{0,7},{1,6},{2,5},{3,4},{4,3},{5,2},{6,1},{7,0},{8,15},{9,14},{10,... | collective-permute-start | bytes 24584 | tf_op jit(solution)/shard_map/ppermute | solution.py:932
  86.1 7.1 %collective-permute-start.35 = (f32[160,512]{1,0:T(8,128)S(1)}, f32[160,512]{1,0:T(8,128)S(1)}, u32[]{:S(2)}, u32[]{:S(2)}) collective-permute-start(f32[160,512]{1,0:T(8,128)S(1)} %get-tuple-element.145.refs_2_), channel_id=1, source_target_pairs={{0,16},{1,9},{2,18},{3,11},{4,20},{5,13},{6,22},{7,15},{8,24},{9,1... | collective-permute-start | bytes 983048 | tf_op jit(solution)/shard_map/ppermute | solution.py:937
  98.8 5.7 %collective-permute-start.42 = (f32[384,512]{1,0:T(8,128)S(1)}, f32[384,512]{1,0:T(8,128)S(1)}, u32[]{:S(2)}, u32[]{:S(2)}) collective-permute-start(f32[384,512]{1,0:T(8,128)S(1)} %split.7.refs_1_), channel_id=1, source_target_pairs={{0,1},{1,0},{2,3},{3,2},{4,5},{5,4},{6,7},{7,6},{8,9},{9,8},{10,11... | collective-permute-start | bytes 2359304 | tf_op jit(solution)/shard_map/ppermute | solution.py:932
  99.1 7.7 %collective-permute-start.41 = (f32[256,512]{1,0:T(8,128)S(1)}, f32[256,512]{1,0:T(8,128)S(1)}, u32[]{:S(2)}, u32[]{:S(2)}) collective-permute-start(f32[256,512]{1,0:T(8,128)S(1)} %split.8.refs_2_), channel_id=1, source_target_pairs={{0,1},{1,0},{2,3},{3,2},{4,5},{5,4},{6,7},{7,6},{8,9},{9,8},{10,11... | collective-permute-start | bytes 1572872 | tf_op jit(solution)/shard_map/ppermute | solution.py:932
  99.5 5.0 %collective-permute-start.40 = (f32[8,768]{1,0:T(8,128)S(1)}, f32[8,768]{1,0:T(8,128)S(1)}, u32[]{:S(2)}, u32[]{:S(2)}) collective-permute-start(f32[8,768]{1,0:T(8,128)S(1)} %combine.7.refs_1_.refs_0_), channel_id=1, source_target_pairs={{0,7},{1,6},{2,5},{3,4},{4,3},{5,2},{6,1},{7,0},{8,15},{9,14},{10,... | collective-permute-start | bytes 73736 | tf_op jit(solution)/shard_map/ppermute | solution.py:932
  101.1 12.4 %collective-permute-start.43 = (f32[192,512]{1,0:T(8,128)S(1)}, f32[192,512]{1,0:T(8,128)S(1)}, u32[]{:S(2)}, u32[]{:S(2)}) collective-permute-start(f32[192,512]{1,0:T(8,128)S(1)} %get-tuple-element.155.refs_2_), channel_id=1, source_target_pairs={{0,8},{1,17},{2,10},{3,19},{4,12},{5,21},{6,14},{7,23},{8,0},{9,25... | collective-permute-start | bytes 1179656 | tf_op jit(solution)/shard_map/ppermute | solution.py:937
  102.3 9.1 %collective-permute-start.44 = (f32[80,512]{1,0:T(8,128)S(1)}, f32[80,512]{1,0:T(8,128)S(1)}, u32[]{:S(2)}, u32[]{:S(2)}) collective-permute-start(f32[80,512]{1,0:T(8,128)S(1)} %get-tuple-element.156.refs_18_), channel_id=1, source_target_pairs={{0,2},{1,3},{2,0},{3,1},{4,6},{5,7},{6,4},{7,5},{8,10},{9,11},{10,... | collective-permute-start | bytes 491528 | tf_op jit(solution)/shard_map/ppermute | solution.py:932
  104.6 4.4 %collective-permute-start.38 = (f32[8,768]{1,0:T(8,128)S(1)}, f32[8,768]{1,0:T(8,128)S(1)}, u32[]{:S(2)}, u32[]{:S(2)}) collective-permute-start(f32[8,768]{1,0:T(8,128)S(1)} %combine.7.refs_1_.refs_0_), channel_id=1, source_target_pairs={{0,3},{1,2},{2,1},{3,0},{4,7},{5,6},{6,5},{7,4},{8,11},{9,10},{10,... | collective-permute-start | bytes 73736 | tf_op jit(solution)/shard_map/ppermute | solution.py:932
  106.7 14.2 %collective-permute-start.47 = (f32[192,512]{1,0:T(8,128)S(1)}, f32[192,512]{1,0:T(8,128)S(1)}, u32[]{:S(2)}, u32[]{:S(2)}) collective-permute-start(f32[192,512]{1,0:T(8,128)S(1)} %get-tuple-element.162.refs_2_), channel_id=1, source_target_pairs={{0,8},{1,17},{2,10},{3,19},{4,12},{5,21},{6,14},{7,23},{8,0},{9,25... | collective-permute-start | bytes 1179656 | tf_op jit(solution)/shard_map/ppermute | solution.py:937
  108.8 11.0 %collective-permute-start.48 = (f32[128,512]{1,0:T(8,128)S(1)}, f32[128,512]{1,0:T(8,128)S(1)}, u32[]{:S(2)}, u32[]{:S(2)}) collective-permute-start(f32[128,512]{1,0:T(8,128)S(1)} %get-tuple-element.163.refs_14_), channel_id=1, source_target_pairs={{0,2},{1,3},{2,0},{3,1},{4,6},{5,7},{6,4},{7,5},{8,10},{9,11},{10,... | collective-permute-start | bytes 786440 | tf_op jit(solution)/shard_map/ppermute | solution.py:932
  111.0 5.3 %collective-permute-start.49 = (f32[384,512]{1,0:T(8,128)S(1)}, f32[384,512]{1,0:T(8,128)S(1)}, u32[]{:S(2)}, u32[]{:S(2)}) collective-permute-start(f32[384,512]{1,0:T(8,128)S(1)} %split.9.refs_2_), channel_id=1, source_target_pairs={{0,1},{1,0},{2,3},{3,2},{4,5},{5,4},{6,7},{7,6},{8,9},{9,8},{10,11... | collective-permute-start | bytes 2359304 | tf_op jit(solution)/shard_map/ppermute | solution.py:932
  111.5 12.4 %collective-permute-start.53 = (f32[80,512]{1,0:T(8,128)S(1)}, f32[80,512]{1,0:T(8,128)S(1)}, u32[]{:S(2)}, u32[]{:S(2)}) collective-permute-start(f32[80,512]{1,0:T(8,128)S(1)} %add.46.refs_2_.refs_0_), channel_id=1, source_target_pairs={{0,4},{1,5},{2,6},{3,7},{4,0},{5,1},{6,2},{7,3},{8,12},{9,13},{10,... | collective-permute-start | bytes 491528 | tf_op jit(solution)/shard_map/ppermute | solution.py:932
  113.5 7.6 %collective-permute-start.46 = (f32[96,512]{1,0:T(8,128)S(1)}, f32[96,512]{1,0:T(8,128)S(1)}, u32[]{:S(2)}, u32[]{:S(2)}) collective-permute-start(f32[96,512]{1,0:T(8,128)S(1)} %get-tuple-element.173.refs_11_), channel_id=1, source_target_pairs={{0,16},{1,9},{2,18},{3,11},{4,20},{5,13},{6,22},{7,15},{8,24},{9,1... | collective-permute-start | bytes 589832 | tf_op jit(solution)/shard_map/ppermute | solution.py:937
  116.3 5.1 %collective-permute-start.45 = (f32[64,128]{1,0:T(8,128)S(1)}, f32[64,128]{1,0:T(8,128)S(1)}, u32[]{:S(2)}, u32[]{:S(2)}) collective-permute-start(f32[64,128]{1,0:T(8,128)S(1)} %get-tuple-element.174.refs_2_.refs_0_), channel_id=1, source_target_pairs={{0,1},{1,0},{2,3},{3,2},{4,5},{5,4},{6,7},{7,6},{8,9},{9,8},{10,11... | collective-permute-start | bytes 98312 | tf_op jit(solution)/shard_map/ppermute | solution.py:932
  119.8 9.4 %collective-permute-start.52 = (f32[192,512]{1,0:T(8,128)S(1)}, f32[192,512]{1,0:T(8,128)S(1)}, u32[]{:S(2)}, u32[]{:S(2)}) collective-permute-start(f32[192,512]{1,0:T(8,128)S(1)} %get-tuple-element.178.refs_2_), channel_id=1, source_target_pairs={{0,8},{1,17},{2,10},{3,19},{4,12},{5,21},{6,14},{7,23},{8,0},{9,25... | collective-permute-start | bytes 1179656 | tf_op jit(solution)/shard_map/ppermute | solution.py:937
  120.9 12.1 %collective-permute-start.58 = (f32[64,512]{1,0:T(8,128)S(1)}, f32[64,512]{1,0:T(8,128)S(1)}, u32[]{:S(2)}, u32[]{:S(2)}) collective-permute-start(f32[64,512]{1,0:T(8,128)S(1)} %get-tuple-element.179.refs_2_), channel_id=1, source_target_pairs={{0,4},{1,5},{2,6},{3,7},{4,0},{5,1},{6,2},{7,3},{8,12},{9,13},{10,... | collective-permute-start | bytes 393224 | tf_op jit(solution)/shard_map/ppermute | solution.py:932
  121.1 8.4 %collective-permute-start.51 = (f32[96,512]{1,0:T(8,128)S(1)}, f32[96,512]{1,0:T(8,128)S(1)}, u32[]{:S(2)}, u32[]{:S(2)}) collective-permute-start(f32[96,512]{1,0:T(8,128)S(1)} %get-tuple-element.180.refs_2_), channel_id=1, source_target_pairs={{0,16},{1,9},{2,18},{3,11},{4,20},{5,13},{6,22},{7,15},{8,24},{9,1... | collective-permute-start | bytes 589832 | tf_op jit(solution)/shard_map/ppermute | solution.py:937
  121.4 11.5 %collective-permute-start.59 = (f32[48,512]{1,0:T(8,128)S(1)}, f32[48,512]{1,0:T(8,128)S(1)}, u32[]{:S(2)}, u32[]{:S(2)}) collective-permute-start(f32[48,512]{1,0:T(8,128)S(1)} %get-tuple-element.181.refs_2_), channel_id=1, source_target_pairs={{0,2},{1,3},{2,0},{3,1},{4,6},{5,7},{6,4},{7,5},{8,10},{9,11},{10,... | collective-permute-start | bytes 294920 | tf_op jit(solution)/shard_map/ppermute | solution.py:932
  123.9 6.9 %collective-permute-start.50 = (f32[64,128]{1,0:T(8,128)S(1)}, f32[64,128]{1,0:T(8,128)S(1)}, u32[]{:S(2)}, u32[]{:S(2)}) collective-permute-start(f32[64,128]{1,0:T(8,128)S(1)} %add.47.refs_2_.refs_0_), channel_id=1, source_target_pairs={{0,9},{1,8},{2,11},{3,10},{4,13},{5,12},{6,15},{7,14},{8,1},{9,0},... | collective-permute-start | bytes 98312 | tf_op jit(solution)/shard_map/ppermute | solution.py:932
  129.2 5.6 %collective-permute-start.57 = (f32[80,512]{1,0:T(8,128)S(1)}, f32[80,512]{1,0:T(8,128)S(1)}, u32[]{:S(2)}, u32[]{:S(2)}) collective-permute-start(f32[80,512]{1,0:T(8,128)S(1)} %add.48.refs_2_.refs_0_), channel_id=1, source_target_pairs={{0,2},{1,3},{2,0},{3,1},{4,6},{5,7},{6,4},{7,5},{8,10},{9,11},{10,... | collective-permute-start | bytes 491528 | tf_op jit(solution)/shard_map/ppermute | solution.py:932
  129.5 6.2 %collective-permute-start.56 = (f32[96,512]{1,0:T(8,128)S(1)}, f32[96,512]{1,0:T(8,128)S(1)}, u32[]{:S(2)}, u32[]{:S(2)}) collective-permute-start(f32[96,512]{1,0:T(8,128)S(1)} %get-tuple-element.184.refs_2_), channel_id=1, source_target_pairs={{0,16},{1,9},{2,18},{3,11},{4,20},{5,13},{6,22},{7,15},{8,24},{9,1... | collective-permute-start | bytes 589832 | tf_op jit(solution)/shard_map/ppermute | solution.py:937
  130.8 6.5 %collective-permute-start.55 = (f32[48,512]{1,0:T(8,128)S(1)}, f32[48,512]{1,0:T(8,128)S(1)}, u32[]{:S(2)}, u32[]{:S(2)}) collective-permute-start(f32[48,512]{1,0:T(8,128)S(1)} %get-tuple-element.185.refs_2_), channel_id=1, source_target_pairs={{0,2},{1,3},{2,0},{3,1},{4,6},{5,7},{6,4},{7,5},{8,10},{9,11},{10,... | collective-permute-start | bytes 294920 | tf_op jit(solution)/shard_map/ppermute | solution.py:932
  132.9 6.0 %collective-permute-start.54 = (f32[64,128]{1,0:T(8,128)S(1)}, f32[64,128]{1,0:T(8,128)S(1)}, u32[]{:S(2)}, u32[]{:S(2)}) collective-permute-start(f32[64,128]{1,0:T(8,128)S(1)} %add.49.refs_2_.refs_0_), channel_id=1, source_target_pairs={{0,17},{1,16},{2,19},{3,18},{4,21},{5,20},{6,23},{7,22},{8,25},{9,... | collective-permute-start | bytes 98312 | tf_op jit(solution)/shard_map/ppermute | solution.py:932
  133.0 9.6 %collective-permute-start.64 = (f32[48,512]{1,0:T(8,128)S(1)}, f32[48,512]{1,0:T(8,128)S(1)}, u32[]{:S(2)}, u32[]{:S(2)}) collective-permute-start(f32[48,512]{1,0:T(8,128)S(1)} %add.50.refs_2_.refs_0_), channel_id=1, source_target_pairs={{0,4},{1,5},{2,6},{3,7},{4,0},{5,1},{6,2},{7,3},{8,12},{9,13},{10,... | collective-permute-start | bytes 294920 | tf_op jit(solution)/shard_map/ppermute | solution.py:932
  134.8 8.9 %collective-permute-start.62 = (f32[64,512]{1,0:T(8,128)S(1)}, f32[64,512]{1,0:T(8,128)S(1)}, u32[]{:S(2)}, u32[]{:S(2)}) collective-permute-start(f32[64,512]{1,0:T(8,128)S(1)} %add.51.refs_2_.refs_0_), channel_id=1, source_target_pairs={{0,8},{1,17},{2,10},{3,19},{4,12},{5,21},{6,14},{7,23},{8,0},{9,25... | collective-permute-start | bytes 393224 | tf_op jit(solution)/shard_map/ppermute | solution.py:937
  135.7 9.5 %collective-permute-start.61 = (f32[160,512]{1,0:T(8,128)S(1)}, f32[160,512]{1,0:T(8,128)S(1)}, u32[]{:S(2)}, u32[]{:S(2)}) collective-permute-start(f32[160,512]{1,0:T(8,128)S(1)} %join.14.refs_2_.refs_0_), channel_id=1, source_target_pairs={{0,16},{1,9},{2,18},{3,11},{4,20},{5,13},{6,22},{7,15},{8,24},{9,1... | collective-permute-start | bytes 983048 | tf_op jit(solution)/shard_map/ppermute | solution.py:937
  137.3 6.3 %collective-permute-start.63 = (f32[48,512]{1,0:T(8,128)S(1)}, f32[48,512]{1,0:T(8,128)S(1)}, u32[]{:S(2)}, u32[]{:S(2)}) collective-permute-start(f32[48,512]{1,0:T(8,128)S(1)} %get-tuple-element.190.refs_2_), channel_id=1, source_target_pairs={{0,2},{1,3},{2,0},{3,1},{4,6},{5,7},{6,4},{7,5},{8,10},{9,11},{10,... | collective-permute-start | bytes 294920 | tf_op jit(solution)/shard_map/ppermute | solution.py:932
  139.0 10.7 %collective-permute-start.67 = (f32[48,512]{1,0:T(8,128)S(1)}, f32[48,512]{1,0:T(8,128)S(1)}, u32[]{:S(2)}, u32[]{:S(2)}) collective-permute-start(f32[48,512]{1,0:T(8,128)S(1)} %add.52.refs_2_.refs_0_), channel_id=1, source_target_pairs={{0,4},{1,5},{2,6},{3,7},{4,0},{5,1},{6,2},{7,3},{8,12},{9,13},{10,... | collective-permute-start | bytes 294920 | tf_op jit(solution)/shard_map/ppermute | solution.py:932
  142.7 5.2 %collective-permute-start.60 = (f32[64,128]{1,0:T(8,128)S(1)}, f32[64,128]{1,0:T(8,128)S(1)}, u32[]{:S(2)}, u32[]{:S(2)}) collective-permute-start(f32[64,128]{1,0:T(8,128)S(1)} %add.53.refs_2_.refs_0_), channel_id=1, source_target_pairs={{0,3},{1,2},{2,1},{3,0},{4,7},{5,6},{6,5},{7,4},{8,11},{9,10},{10,... | collective-permute-start | bytes 98312 | tf_op jit(solution)/shard_map/ppermute | solution.py:932
  143.7 6.0 %collective-permute-start.66 = (f32[48,512]{1,0:T(8,128)S(1)}, f32[48,512]{1,0:T(8,128)S(1)}, u32[]{:S(2)}, u32[]{:S(2)}) collective-permute-start(f32[48,512]{1,0:T(8,128)S(1)} %add.54.refs_2_.refs_0_), channel_id=1, source_target_pairs={{0,2},{1,3},{2,0},{3,1},{4,6},{5,7},{6,4},{7,5},{8,10},{9,11},{10,... | collective-permute-start | bytes 294920 | tf_op jit(solution)/shard_map/ppermute | solution.py:932
  143.7 8.5 %collective-permute-start.69 = (f32[48,512]{1,0:T(8,128)S(1)}, f32[48,512]{1,0:T(8,128)S(1)}, u32[]{:S(2)}, u32[]{:S(2)}) collective-permute-start(f32[48,512]{1,0:T(8,128)S(1)} %add.55.refs_2_.refs_0_), channel_id=1, source_target_pairs={{0,4},{1,5},{2,6},{3,7},{4,0},{5,1},{6,2},{7,3},{8,12},{9,13},{10,... | collective-permute-start | bytes 294920 | tf_op jit(solution)/shard_map/ppermute | solution.py:932
  145.2 7.5 %collective-permute-start.72 = (f32[64,512]{1,0:T(8,128)S(1)}, f32[64,512]{1,0:T(8,128)S(1)}, u32[]{:S(2)}, u32[]{:S(2)}) collective-permute-start(f32[64,512]{1,0:T(8,128)S(1)} %add.56.refs_2_.refs_0_), channel_id=1, source_target_pairs={{0,16},{1,9},{2,18},{3,11},{4,20},{5,13},{6,22},{7,15},{8,24},{9,1... | collective-permute-start | bytes 393224 | tf_op jit(solution)/shard_map/ppermute | solution.py:937
  147.9 21.8 %collective-permute-start.80 = (f32[320,512]{1,0:T(8,128)S(1)}, f32[320,512]{1,0:T(8,128)S(1)}, u32[]{:S(2)}, u32[]{:S(2)}) collective-permute-start(f32[320,512]{1,0:T(8,128)S(1)} %join.15.refs_2_.refs_0_), channel_id=1, source_target_pairs={{0,8},{1,17},{2,10},{3,19},{4,12},{5,21},{6,14},{7,23},{8,0},{9,25... | collective-permute-start | bytes 1966088 | tf_op jit(solution)/shard_map/ppermute | solution.py:937
  149.6 11.0 %collective-permute-start.65 = (f32[64,128]{1,0:T(8,128)S(1)}, f32[64,128]{1,0:T(8,128)S(1)}, u32[]{:S(2)}, u32[]{:S(2)}) collective-permute-start(f32[64,128]{1,0:T(8,128)S(1)} %add.57.refs_2_.refs_0_), channel_id=1, source_target_pairs={{0,5},{1,4},{2,7},{3,6},{4,1},{5,0},{6,3},{7,2},{8,13},{9,12},{10,... | collective-permute-start | bytes 98312 | tf_op jit(solution)/shard_map/ppermute | solution.py:932
  149.8 5.7 %collective-permute-start.71 = (f32[48,512]{1,0:T(8,128)S(1)}, f32[48,512]{1,0:T(8,128)S(1)}, u32[]{:S(2)}, u32[]{:S(2)}) collective-permute-start(f32[48,512]{1,0:T(8,128)S(1)} %add.58.refs_2_.refs_0_), channel_id=1, source_target_pairs={{0,2},{1,3},{2,0},{3,1},{4,6},{5,7},{6,4},{7,5},{8,10},{9,11},{10,... | collective-permute-start | bytes 294920 | tf_op jit(solution)/shard_map/ppermute | solution.py:932
  152.3 7.3 %collective-permute-start.68 = (f32[96,512]{1,0:T(8,128)S(1)}, f32[96,512]{1,0:T(8,128)S(1)}, u32[]{:S(2)}, u32[]{:S(2)}) collective-permute-start(f32[96,512]{1,0:T(8,128)S(1)} %join.16.refs_2_.refs_0_), channel_id=1, source_target_pairs={{0,16},{1,9},{2,18},{3,11},{4,20},{5,13},{6,22},{7,15},{8,24},{9,1... | collective-permute-start | bytes 589832 | tf_op jit(solution)/shard_map/ppermute | solution.py:937
  152.7 4.7 %collective-permute-start.70 = (f32[48,512]{1,0:T(8,128)S(1)}, f32[48,512]{1,0:T(8,128)S(1)}, u32[]{:S(2)}, u32[]{:S(2)}) collective-permute-start(f32[48,512]{1,0:T(8,128)S(1)} %add.59.refs_2_.refs_0_), channel_id=1, source_target_pairs={{0,2},{1,3},{2,0},{3,1},{4,6},{5,7},{6,4},{7,5},{8,10},{9,11},{10,... | collective-permute-start | bytes 294920 | tf_op jit(solution)/shard_map/ppermute | solution.py:932
  155.5 10.5 %collective-permute-start.74 = (f32[64,512]{1,0:T(8,128)S(1)}, f32[64,512]{1,0:T(8,128)S(1)}, u32[]{:S(2)}, u32[]{:S(2)}) collective-permute-start(f32[64,512]{1,0:T(8,128)S(1)} %add.60.refs_2_.refs_0_), channel_id=1, source_target_pairs={{0,4},{1,5},{2,6},{3,7},{4,0},{5,1},{6,2},{7,3},{8,12},{9,13},{10,... | collective-permute-start | bytes 393224 | tf_op jit(solution)/shard_map/ppermute | solution.py:932
  157.4 7.1 %collective-permute-start.75 = (f32[96,512]{1,0:T(8,128)S(1)}, f32[96,512]{1,0:T(8,128)S(1)}, u32[]{:S(2)}, u32[]{:S(2)}) collective-permute-start(f32[96,512]{1,0:T(8,128)S(1)} %join.17.refs_2_.refs_0_), channel_id=1, source_target_pairs={{0,16},{1,9},{2,18},{3,11},{4,20},{5,13},{6,22},{7,15},{8,24},{9,1... | collective-permute-start | bytes 589832 | tf_op jit(solution)/shard_map/ppermute | solution.py:937
  159.6 8.6 %collective-permute-start.73 = (f32[96,512]{1,0:T(8,128)S(1)}, f32[96,512]{1,0:T(8,128)S(1)}, u32[]{:S(2)}, u32[]{:S(2)}) collective-permute-start(f32[96,512]{1,0:T(8,128)S(1)} %join.18.refs_2_.refs_0_), channel_id=1, source_target_pairs={{0,16},{1,9},{2,18},{3,11},{4,20},{5,13},{6,22},{7,15},{8,24},{9,1... | collective-permute-start | bytes 589832 | tf_op jit(solution)/shard_map/ppermute | solution.py:937
  160.6 9.3 %collective-permute-start.79 = (f32[192,512]{1,0:T(8,128)S(1)}, f32[192,512]{1,0:T(8,128)S(1)}, u32[]{:S(2)}, u32[]{:S(2)}) collective-permute-start(f32[192,512]{1,0:T(8,128)S(1)} %join.19.refs_2_.refs_0_), channel_id=1, source_target_pairs={{0,8},{1,17},{2,10},{3,19},{4,12},{5,21},{6,14},{7,23},{8,0},{9,25... | collective-permute-start | bytes 1179656 | tf_op jit(solution)/shard_map/ppermute | solution.py:937
  164.5 8.7 %collective-permute-start.78 = (f32[192,512]{1,0:T(8,128)S(1)}, f32[192,512]{1,0:T(8,128)S(1)}, u32[]{:S(2)}, u32[]{:S(2)}) collective-permute-start(f32[192,512]{1,0:T(8,128)S(1)} %join.20.refs_2_.refs_0_), channel_id=1, source_target_pairs={{0,8},{1,17},{2,10},{3,19},{4,12},{5,21},{6,14},{7,23},{8,0},{9,25... | collective-permute-start | bytes 1179656 | tf_op jit(solution)/shard_map/ppermute | solution.py:937
  166.0 7.8 %collective-permute-start.77 = (f32[128,512]{1,0:T(8,128)S(1)}, f32[128,512]{1,0:T(8,128)S(1)}, u32[]{:S(2)}, u32[]{:S(2)}) collective-permute-start(f32[128,512]{1,0:T(8,128)S(1)} %join.21.refs_2_.refs_0_), channel_id=1, source_target_pairs={{0,2},{1,3},{2,0},{3,1},{4,6},{5,7},{6,4},{7,5},{8,10},{9,11},{10,... | collective-permute-start | bytes 786440 | tf_op jit(solution)/shard_map/ppermute | solution.py:932
  168.3 9.2 %collective-permute-start.76 = (f32[192,512]{1,0:T(8,128)S(1)}, f32[192,512]{1,0:T(8,128)S(1)}, u32[]{:S(2)}, u32[]{:S(2)}) collective-permute-start(f32[192,512]{1,0:T(8,128)S(1)} %join.22.refs_2_.refs_0_), channel_id=1, source_target_pairs={{0,8},{1,17},{2,10},{3,19},{4,12},{5,21},{6,14},{7,23},{8,0},{9,25... | collective-permute-start | bytes 1179656 | tf_op jit(solution)/shard_map/ppermute | solution.py:937
  169.8 8.0 %collective-permute-start.82 = (f32[640,512]{1,0:T(8,128)S(1)}, f32[640,512]{1,0:T(8,128)S(1)}, u32[]{:S(2)}, u32[]{:S(2)}) collective-permute-start(f32[640,512]{1,0:T(8,128)S(1)} %join.23.refs_2_.refs_0_), channel_id=1, source_target_pairs={{0,1},{1,0},{2,3},{3,2},{4,5},{5,4},{6,7},{7,6},{8,9},{9,8},{10,11... | collective-permute-start | bytes 3932168 | tf_op jit(solution)/shard_map/ppermute | solution.py:932
  170.0 7.8 %collective-permute-start.83 = (f32[384,512]{1,0:T(8,128)S(1)}, f32[384,512]{1,0:T(8,128)S(1)}, u32[]{:S(2)}, u32[]{:S(2)}) collective-permute-start(f32[384,512]{1,0:T(8,128)S(1)} %join.24.refs_2_), channel_id=1, source_target_pairs={{0,1},{1,0},{2,3},{3,2},{4,5},{5,4},{6,7},{7,6},{8,9},{9,8},{10,11... | collective-permute-start | bytes 2359304 | tf_op jit(solution)/shard_map/ppermute | solution.py:932
  173.4 6.6 %collective-permute-start.84 = (f32[384,512]{1,0:T(8,128)S(1)}, f32[384,512]{1,0:T(8,128)S(1)}, u32[]{:S(2)}, u32[]{:S(2)}) collective-permute-start(f32[384,512]{1,0:T(8,128)S(1)} %join.25.refs_2_.refs_0_), channel_id=1, source_target_pairs={{0,1},{1,0},{2,3},{3,2},{4,5},{5,4},{6,7},{7,6},{8,9},{9,8},{10,11... | collective-permute-start | bytes 2359304 | tf_op jit(solution)/shard_map/ppermute | solution.py:932
  173.9 6.0 %collective-permute-start.85 = (f32[256,512]{1,0:T(8,128)S(1)}, f32[256,512]{1,0:T(8,128)S(1)}, u32[]{:S(2)}, u32[]{:S(2)}) collective-permute-start(f32[256,512]{1,0:T(8,128)S(1)} %join.26.refs_2_), channel_id=1, source_target_pairs={{0,1},{1,0},{2,3},{3,2},{4,5},{5,4},{6,7},{7,6},{8,9},{9,8},{10,11... | collective-permute-start | bytes 1572872 | tf_op jit(solution)/shard_map/ppermute | solution.py:932
  (37 other events, 115.8 us)
